TPU v7x, 32 devices: a whole 2x2x4 slice. The times are simulated.
32 devices in a mesh: seq: 8 (over z, y), head: 4 (over x, core).
Axes of the slice: x: 2, y: 2, z: 4, core: 2. Of those that a mesh axis runs over, the one named last changes fastest.
Arguments:
- queries: bfloat16 [2048, 4096], P(('seq', 'head')), may hold values from -1 to 1
- keys: bfloat16 [2048, 1024], P(('seq', 'head')), may hold values from -2.5 to 2.5
- values: bfloat16 [2048, 1024], P(('seq', 'head')), may hold values from -3 to 3
- outputs_saved: bfloat16 [2048, 4096], P(('seq', 'head')), may hold values from -3 to 3
- grad_out: bfloat16 [2048, 4096], P(('seq', 'head')), may hold values from -3 to 3
- lse: float32 [2048, 32], P('seq', 'head'), may hold values from 2.5 to 4
- block_lists: int32 [16, 32, 4], P(None, 'head'), may hold values from 0 to 31, as said below
Outputs:
- grad_queries: bfloat16 [2048, 4096], P(('seq', 'head'))
- grad_keys: bfloat16 [2048, 1024], P(('seq', 'head'))
- grad_values: bfloat16 [2048, 1024], P(('seq', 'head'))
Inputs may be any that keep to these rules, and one draw needn't show every extreme that they name: `block_lists`: key block j lies in sequence shard j // 4. No query block lists a key block of its own sequence shard. For the query blocks of one sequence shard and the 8 query heads held by one device along `head`, at most 10 listed block lies in any one other sequence shard; a few shards are listed far more often than the others.
All inputs are finite; a program needn't handle non-finite values.
Results may differ from a plain program's by a relative error of at most 0.011.
Values may be sent and summed in bfloat16 or wider, within the bound.
No kernel may reach another device: no remote copies, remote signals or barrier semaphores. Data moves between devices by JAX's collectives and lax.ppermute only.
A program may use at most 128 MiB of HBM per device.

v0:
```python
import math

import jax
import jax.numpy as jnp
from jax import lax
from jax.sharding import PartitionSpec as P

HD = 128
QB = 128
KB = 64
NSEL = 4
GROUP = 4


def remote_terms(q_rows, o_grad, lse_rows, delta_rows, k_rows, v_rows):
    scaling = HD ** (-0.5)
    logit_scores = (
        jnp.einsum("nkd,nqd->nkq", k_rows, q_rows, preferred_element_type=jnp.float32) * scaling
    )
    probability = jnp.exp(logit_scores - lse_rows[:, None, :])
    grad_prob = jnp.einsum("nkd,nqd->nkq", v_rows, o_grad, preferred_element_type=jnp.float32)
    score_gradient = probability * (grad_prob - delta_rows[:, None, :])
    prob_low = probability.astype(jnp.bfloat16)
    score_low = score_gradient.astype(jnp.bfloat16)
    dq_part = (
        jnp.einsum("nkq,nkd->nqd", score_low, k_rows, preferred_element_type=jnp.float32) * scaling
    )
    dk_part = (
        jnp.einsum("nkq,nqd->nkd", score_low, q_rows, preferred_element_type=jnp.float32) * scaling
    )
    dv_part = jnp.einsum("nkq,nqd->nkd", prob_low, o_grad, preferred_element_type=jnp.float32)
    return (
        dq_part.astype(jnp.bfloat16),
        dk_part.astype(jnp.bfloat16),
        dv_part.astype(jnp.bfloat16),
    )


def in_groups(handler, arrays, slot_count):
    group_size = math.gcd(slot_count, 16)
    shaped = tuple(
        (
            entry.reshape((slot_count // group_size, group_size) + entry.shape[1:])
            for entry in arrays
        )
    )
    results = lax.map(lambda fragments: handler(*fragments), shaped)
    return tuple((entry.reshape((slot_count,) + entry.shape[2:]) for entry in results))


def own_terms(q_five, do_five, k_four, v_four, lse_four, delta_four):
    scaling = HD ** (-0.5)
    block_rows = q_five.shape[1]
    causal = lax.broadcasted_iota(jnp.int32, (block_rows, block_rows), 0) <= lax.broadcasted_iota(
        jnp.int32, (block_rows, block_rows), 1
    )
    logit_scores = (
        jnp.einsum("bshd,bqhgd->bhgsq", k_four, q_five, preferred_element_type=jnp.float32)
        * scaling
    )
    probability = jnp.where(
        causal, jnp.exp(logit_scores - lse_four[:, :, :, None, :]), jnp.float32(0.0)
    )
    grad_prob = jnp.einsum("bshd,bqhgd->bhgsq", v_four, do_five, preferred_element_type=jnp.float32)
    score_gradient = probability * (grad_prob - delta_four[:, :, :, None, :])
    prob_low = probability.astype(jnp.bfloat16)
    score_low = score_gradient.astype(jnp.bfloat16)
    dq_own = (
        jnp.einsum("bhgsq,bshd->bqhgd", score_low, k_four, preferred_element_type=jnp.float32)
        * scaling
    )
    dk_own = (
        jnp.einsum("bhgsq,bqhgd->bshd", score_low, q_five, preferred_element_type=jnp.float32)
        * scaling
    )
    dv_own = jnp.einsum("bhgsq,bqhgd->bshd", prob_low, do_five, preferred_element_type=jnp.float32)
    return (dq_own, dk_own, dv_own)


def body(queries, keys, values, outputs_saved, grad_out, lse, block_lists):
    heads_here = lse.shape[1]
    q_head, do_head, o_head, k_head, v_head = (
        lax.all_to_all(queries, "head", split_axis=1, concat_axis=0, tiled=True),
        lax.all_to_all(grad_out, "head", split_axis=1, concat_axis=0, tiled=True),
        lax.all_to_all(outputs_saved, "head", split_axis=1, concat_axis=0, tiled=True),
        lax.all_to_all(keys, "head", split_axis=1, concat_axis=0, tiled=True),
        lax.all_to_all(values, "head", split_axis=1, concat_axis=0, tiled=True),
    )
    products = do_head.astype(jnp.float32) * o_head.astype(jnp.float32)
    delta_head = jnp.sum(products.reshape(q_head.shape[0], heads_here, HD), axis=-1)
    token_count = q_head.shape[0]
    kv_here = k_head.shape[1] // HD
    blocks_here = token_count // QB
    key_count = token_count // KB
    q_five = q_head.reshape(blocks_here, QB, kv_here, GROUP, HD)
    do_five = do_head.reshape(blocks_here, QB, kv_here, GROUP, HD)
    k_four = k_head.reshape(blocks_here, QB, kv_here, HD)
    v_four = v_head.reshape(blocks_here, QB, kv_here, HD)
    lse_four = lse.reshape(blocks_here, QB, kv_here, GROUP).transpose(0, 2, 3, 1)
    delta_four = delta_head.reshape(blocks_here, QB, kv_here, GROUP).transpose(0, 2, 3, 1)
    dq_own, dk_own, dv_own = own_terms(q_five, do_five, k_four, v_four, lse_four, delta_four)
    neighbour_count = lax.axis_size("seq")
    seq_here = lax.axis_index("seq")
    per_peer = block_lists.reshape(neighbour_count, -1)
    request_count = per_peer.shape[1]
    capacity = (request_count + neighbour_count - 2) // (neighbour_count - 1)
    slot_count = neighbour_count * capacity
    owner_of = per_peer // key_count
    order_ids = jnp.arange(request_count, dtype=jnp.int32)
    earlier = (owner_of[:, :, None] == owner_of[:, None, :]) & (
        order_ids[None, :] < order_ids[:, None]
    )[None, :, :]
    position = jnp.sum(earlier.astype(jnp.int32), axis=2)
    mine_owner = lax.dynamic_index_in_dim(owner_of, seq_here, 0, keepdims=False)
    mine_position = lax.dynamic_index_in_dim(position, seq_here, 0, keepdims=False)
    slots = mine_owner * capacity + mine_position
    hits = (
        (owner_of == seq_here)[:, :, None]
        & (position[:, :, None] == jnp.arange(capacity, dtype=jnp.int32)[None, None, :])
    ).astype(jnp.int32)
    slot_used = jnp.sum(hits, axis=1).reshape(-1)
    local_block = jnp.sum(hits * (per_peer % key_count)[:, :, None], axis=1).reshape(-1)
    head_of_request = order_ids % (heads_here * NSEL) // NSEL
    kv_slot = jnp.sum(hits * (head_of_request // GROUP)[None, :, None], axis=1).reshape(-1)
    unit_index = local_block * kv_here + kv_slot
    selector = (
        (jnp.arange(key_count * kv_here, dtype=jnp.int32)[:, None] == unit_index[None, :])
        & (slot_used[None, :] > 0)
    ).astype(jnp.bfloat16)
    q_pairs = (
        q_head.reshape(blocks_here, QB, heads_here, HD).transpose(0, 2, 1, 3).reshape(-1, QB, HD)
    )
    do_pairs = (
        do_head.reshape(blocks_here, QB, heads_here, HD).transpose(0, 2, 1, 3).reshape(-1, QB, HD)
    )
    lse_pairs = lse.reshape(blocks_here, QB, heads_here).transpose(0, 2, 1).reshape(-1, QB)
    delta_pairs = delta_head.reshape(blocks_here, QB, heads_here).transpose(0, 2, 1).reshape(-1, QB)
    pair_index = order_ids // NSEL
    key_blocks = k_head.reshape(key_count, KB, kv_here, HD)
    value_blocks = v_head.reshape(key_count, KB, kv_here, HD)
    send_rows = jnp.concatenate([q_pairs, do_pairs], axis=-1)[pair_index]
    send_stats = jnp.stack([lse_pairs, delta_pairs], axis=1)[pair_index]
    row_buffer = jnp.zeros((slot_count, QB, 2 * HD), jnp.bfloat16).at[slots].set(send_rows)
    stat_buffer = jnp.zeros((slot_count, 2, QB), jnp.float32).at[slots].set(send_stats)
    arrived = lax.all_to_all(row_buffer, "seq", split_axis=0, concat_axis=0, tiled=True)
    arrived_stats = lax.all_to_all(stat_buffer, "seq", split_axis=0, concat_axis=0, tiled=True)
    k_rows = key_blocks[local_block, :, kv_slot]
    v_rows = value_blocks[local_block, :, kv_slot]
    dq_slots, dk_slots, dv_slots = in_groups(
        remote_terms,
        (
            arrived[..., :HD],
            arrived[..., HD:],
            arrived_stats[:, 0],
            arrived_stats[:, 1],
            k_rows,
            v_rows,
        ),
        slot_count,
    )
    returned = lax.all_to_all(dq_slots, "seq", split_axis=0, concat_axis=0, tiled=True)
    dq_requests = returned[slots]
    dkv_parts = jnp.concatenate([dk_slots, dv_slots], axis=-1)
    unit_sums = jnp.dot(
        selector, dkv_parts.reshape(slot_count, -1), preferred_element_type=jnp.float32
    )
    unit_sums = unit_sums.reshape(key_count, kv_here, KB, 2 * HD).transpose(0, 2, 1, 3)
    listed_k = unit_sums[..., :HD].reshape(token_count, kv_here * HD)
    listed_v = unit_sums[..., HD:].reshape(token_count, kv_here * HD)
    grad_k = (dk_own.reshape(token_count, kv_here * HD) + listed_k).astype(jnp.bfloat16)
    grad_v = (dv_own.reshape(token_count, kv_here * HD) + listed_v).astype(jnp.bfloat16)
    dq_listed = (
        dq_requests.astype(jnp.float32)
        .reshape(blocks_here, heads_here, NSEL, QB, HD)
        .sum(axis=2)
        .transpose(0, 2, 1, 3)
    )
    grad_q = (
        (dq_own.reshape(blocks_here, QB, heads_here, HD) + dq_listed)
        .astype(jnp.bfloat16)
        .reshape(token_count, heads_here * HD)
    )
    grad_queries, grad_keys, grad_values = (
        lax.all_to_all(grad_q, "head", split_axis=0, concat_axis=1, tiled=True),
        lax.all_to_all(grad_k, "head", split_axis=0, concat_axis=1, tiled=True),
        lax.all_to_all(grad_v, "head", split_axis=0, concat_axis=1, tiled=True),
    )
    return (grad_queries, grad_keys, grad_values)


def solution(mesh):
    in_specs = (
        P(("seq", "head"), None),
        P(("seq", "head"), None),
        P(("seq", "head"), None),
        P(("seq", "head"), None),
        P(("seq", "head"), None),
        P("seq", "head"),
        P(None, "head", None),
    )
    out_specs = (P(("seq", "head"), None), P(("seq", "head"), None), P(("seq", "head"), None))
    return jax.shard_map(body, mesh=mesh, in_specs=in_specs, out_specs=out_specs, check_vma=False)
```

profile of v0, /device:TPU:0, one launch (start us, length us, event | category | flops | bytes accessed | tf_op | source)
XLA Modules:
  0.0 349.7 jit_solution(15596597919189710943)
XLA Ops:
  0.7 1.9 copy.227
  2.6 4.3 %all-to-all-start.2 = ((bf16[64,4,1024]{2,0,1:T(8,128)(2,1)}), bf16[64,4,1024]{2,0,1:T(8,128)(2,1)S(1)}, u32[]{:S(2)}, u32[]{:S(2)}) async-start(bf16[64,4,1024]{2,0,1:T(8,128)(2,1)} %bitcast.202), calls=%async_computation.2 | async-start | bytes 1048576 | tf_op jit(solution)/shard_map/all_to_all | solution.py:84
  6.9 1.9 copy.226
  8.8 7.0 %all-to-all-done.2 = bf16[64,4,1024]{2,0,1:T(8,128)(2,1)S(1)} async-done(((bf16[64,4,1024]{2,0,1:T(8,128)(2,1)}), bf16[64,4,1024]{2,0,1:T(8,128)(2,1)S(1)}, u32[]{:S(2)}, u32[]{:S(2)}) %all-to-all-start.2) | async-done | bytes 524320 | tf_op jit(solution)/shard_map/all_to_all | solution.py:84
  15.8 3.5 all-to-all-start.4
  20.7 7.4 %all-to-all-done.4 = bf16[64,4,1024]{2,0,1:T(8,128)(2,1)S(1)} async-done(((bf16[64,4,1024]{2,0,1:T(8,128)(2,1)}), bf16[64,4,1024]{2,0,1:T(8,128)(2,1)S(1)}, u32[]{:S(2)}, u32[]{:S(2)}) %all-to-all-start.4) | async-done | bytes 524320 | tf_op jit(solution)/shard_map/all_to_all | solution.py:85
  28.1 3.5 all-to-all-start
  33.2 7.1 %all-to-all-done = bf16[64,4,1024]{2,0,1:T(8,128)(2,1)S(1)} async-done(((bf16[64,4,1024]{2,0,1:T(8,128)(2,1)}), bf16[64,4,1024]{2,0,1:T(8,128)(2,1)S(1)}, u32[]{:S(2)}, u32[]{:S(2)}) %all-to-all-start) | async-done | bytes 524320 | tf_op jit(solution)/shard_map/all_to_all | solution.py:83
  40.4 3.3 all-to-all-start.1
  46.1 2.2 all-to-all-done.1
  48.3 3.3 all-to-all-start.3
  53.0 6.9 %scatter_fusion.1 = f32[80,2,128]{2,1,0:T(2,128)} fusion(f32[80,2,128]{2,1,0:T(2,128)} %broadcast_in_dim.27, s32[64]{0:T(128)S(1)} %get-tuple-element.94, f32[64,2,128]{2,1,0:T(2,128)S(1)} %gather_fusion.2), kind=kCustom, calls=%fused_computation.6 | custom fusion | bytes 196864 | tf_op jit(solution)/shard_map/scatter | solution.py:144
  59.8 6.5 %all-to-all-start.6 = ((f32[80,2,128]{2,1,0:T(2,128)}), f32[80,2,128]{2,1,0:T(2,128)S(1)}, u32[]{:S(2)}, u32[]{:S(2)}) async-start(f32[80,2,128]{2,1,0:T(2,128)} %scatter_fusion.1), calls=%async_computation.6 | async-start | bytes 163840 | tf_op jit(solution)/shard_map/all_to_all | solution.py:146
  67.8 2.8 gather_fusion.1
  70.5 3.0 broadcast_in_dim.26
  73.6 12.1 %scatter_fusion = bf16[80,128,256]{2,1,0:T(8,128)(2,1)} fusion(bf16[80,128,256]{2,1,0:T(8,128)(2,1)} %broadcast_in_dim.26, s32[64]{0:T(128)S(1)} %get-tuple-element.94, bf16[64,128,256]{2,1,0:T(8,128)(2,1)} %gather_fusion.1), kind=kCustom, calls=%fused_computation.5 | custom fusion | bytes 12583168 | tf_op jit(solution)/shard_map/scatter | solution.py:143
  85.7 6.0 %all-to-all-start.5 = ((bf16[80,128,256]{2,1,0:T(8,128)(2,1)}), bf16[80,128,256]{2,1,0:T(8,128)(2,1)}, u32[]{:S(2)}, u32[]{:S(2)}) async-start(bf16[80,128,256]{2,1,0:T(8,128)(2,1)} %scatter_fusion), calls=%async_computation.5 | async-start | bytes 10485760 | tf_op jit(solution)/shard_map/all_to_all | solution.py:145
  92.9 2.3 gather_fusion
  95.2 2.3 gather_fusion.3
  98.2 109.2 %all-to-all-done.5 = bf16[80,128,256]{2,1,0:T(8,128)(2,1)} async-done(((bf16[80,128,256]{2,1,0:T(8,128)(2,1)}), bf16[80,128,256]{2,1,0:T(8,128)(2,1)}, u32[]{:S(2)}, u32[]{:S(2)}) %all-to-all-start.5) | async-done | bytes 5242912 | tf_op jit(solution)/shard_map/all_to_all | solution.py:145
  207.4 5.6 %fusion.70 = (bf16[80,128,128]{2,1,0:T(8,128)(2,1)}, bf16[80,128,128]{2,1,0:T(8,128)(2,1)S(1)}) fusion(bf16[80,128,256]{2,1,0:T(8,128)(2,1)} %all-to-all-done.5), kind=kLoop, calls=%fused_computation.143 | loop fusion | bytes 10485760 | tf_op jit(solution)/shard_map/slice | solution.py:153
  213.0 44.2 %while.14 = (s32[]{:T(128)}, bf16[5,16,128,128]{3,2,1,0:T(8,128)(2,1)}, bf16[5,16,64,128]{3,2,1,0:T(8,128)(2,1)}, bf16[5,16,64,128]{3,2,1,0:T(8,128)(2,1)}, bf16...) while((s32[]{:T(128)}, ...), condition=%wide.region_7.8_spmd, body=%wide.region_6.7_spmd.sunk | while | flops 169476096 | bytes 6345841 | solution.py:47
  213.7 1.4 fusion.104
  215.2 1.6 fusion.105
  216.8 2.1 fusion.106
  219.9 2.0 fusion.108
  222.6 1.4 fusion.104
  224.0 1.6 fusion.105
  225.6 2.1 fusion.106
  228.7 2.0 fusion.108
  231.4 1.4 fusion.104
  232.8 1.6 fusion.105
  234.4 2.1 fusion.106
  237.5 2.0 fusion.108
  240.2 1.4 fusion.104
  241.7 1.6 fusion.105
  243.3 2.1 fusion.106
  246.4 2.0 fusion.108
  249.1 1.4 fusion.104
  250.5 1.6 fusion.105
  252.1 2.2 fusion.106
  255.3 2.0 fusion.108
  257.3 3.9 %all-to-all-start.7 = ((bf16[80,128,128]{2,1,0:T(8,128)(2,1)}), bf16[80,128,128]{2,1,0:T(8,128)(2,1)S(1)}, u32[]{:S(2)}, u32[]{:S(2)}) async-start(bf16[80,128,128]{2,1,0:T(8,128)(2,1)} %bitcast.245), calls=%async_computation.7 | async-start | bytes 5242880 | tf_op jit(solution)/shard_map/all_to_all | solution.py:161
  265.3 2.2 reshape.468
  267.5 1.2 reshape.471
  268.7 1.6 fusion.39
  272.5 1.2 reshape.496
  273.7 1.6 fusion.40
  276.1 1.4 fusion.43
  277.9 2.3 convolution_multiply_fusion.3
  280.2 2.2 pad_maximum_fusion
  282.4 1.6 fusion.41
  285.7 1.2 reshape.497
  286.8 1.9 copy.160
  288.7 1.9 reshape.495
  291.2 1.6 add_convert_fusion.1
  292.9 27.9 %all-to-all-done.7 = bf16[80,128,128]{2,1,0:T(8,128)(2,1)S(1)} async-done(((bf16[80,128,128]{2,1,0:T(8,128)(2,1)}), bf16[80,128,128]{2,1,0:T(8,128)(2,1)S(1)}, u32[]{:S(2)}, u32[]{:S(2)}) %all-to-all-start.7) | async-done | bytes 2621472 | tf_op jit(solution)/shard_map/all_to_all | solution.py:161
  320.8 3.3 all-to-all-start.10
  324.1 2.3 gather_fusion.4
  326.4 2.1 convert_reduce_fusion
  328.7 3.3 all-to-all-start.9
  333.5 3.1 all-to-all-done.9
  336.6 3.5 all-to-all-start.8
  341.4 7.5 %all-to-all-done.8 = bf16[4,64,1024]{2,1,0:T(8,128)(2,1)S(1)} async-done(((bf16[4,64,1024]{2,1,0:T(8,128)(2,1)}), bf16[4,64,1024]{2,1,0:T(8,128)(2,1)S(1)}, u32[]{:S(2)}, u32[]{:S(2)}) %all-to-all-start.8) | async-done | bytes 524320 | tf_op jit(solution)/shard_map/all_to_all | solution.py:184
  (111 shorter events, 32.2 us)
Async XLA Ops:
  0.6 18.6 %copy-start.10 = (s32[16,8,4]{0,2,1:T(4,128)S(1)}, s32[16,8,4]{0,2,1:T(4,128)}, u32[]{:S(2)}) copy-start(s32[16,8,4]{0,2,1:T(4,128)} %param.15) | copy-start | bytes 6148
  0.6 18.9 %copy-start.6 = (bf16[64,4096]{1,0:T(8,128)(2,1)S(1)}, bf16[64,4096]{1,0:T(8,128)(2,1)}, u32[]{:S(2)}) copy-start(bf16[64,4096]{1,0:T(8,128)(2,1)} %param.9) | copy-start | bytes 1572868
  2.6 29.0 %copy-start.7 = (bf16[64,1024]{1,0:T(8,128)(2,1)S(1)}, bf16[64,1024]{1,0:T(8,128)(2,1)}, u32[]{:S(2)}) copy-start(bf16[64,1024]{1,0:T(8,128)(2,1)} %param.10) | copy-start | bytes 393220
  2.6 29.7 %copy-start.8 = (bf16[64,1024]{1,0:T(8,128)(2,1)S(1)}, bf16[64,1024]{1,0:T(8,128)(2,1)}, u32[]{:S(2)}) copy-start(bf16[64,1024]{1,0:T(8,128)(2,1)} %param.11) | copy-start | bytes 393220
  2.6 13.2 %all-to-all-start.2 = ((bf16[64,4,1024]{2,0,1:T(8,128)(2,1)}), bf16[64,4,1024]{2,0,1:T(8,128)(2,1)S(1)}, u32[]{:S(2)}, u32[]{:S(2)}) async-start(bf16[64,4,1024]{2,0,1:T(8,128)(2,1)} %bitcast.202), calls=%async_computation.2 | async-start | bytes 1048576 | tf_op jit(solution)/shard_map/all_to_all | solution.py:84
  15.8 12.3 %all-to-all-start.4 = ((bf16[64,4,1024]{2,0,1:T(8,128)(2,1)}), bf16[64,4,1024]{2,0,1:T(8,128)(2,1)S(1)}, u32[]{:S(2)}, u32[]{:S(2)}) async-start(bf16[64,4,1024]{2,0,1:T(8,128)(2,1)} %bitcast.201), calls=%async_computation.4 | async-start | bytes 1048576 | tf_op jit(solution)/shard_map/all_to_all | solution.py:85
  28.1 12.3 %all-to-all-start = ((bf16[64,4,1024]{2,0,1:T(8,128)(2,1)}), bf16[64,4,1024]{2,0,1:T(8,128)(2,1)S(1)}, u32[]{:S(2)}, u32[]{:S(2)}) async-start(bf16[64,4,1024]{2,0,1:T(8,128)(2,1)} %bitcast.203), calls=%async_computation | async-start | bytes 1048576 | tf_op jit(solution)/shard_map/all_to_all | solution.py:83
  31.6 42.0 %copy-start.11 = (s32[64]{0:T(128)}, s32[64]{0:T(128)S(1)}, u32[]{:S(2)}) copy-start(s32[64]{0:T(128)S(1)} %get-tuple-element.94) | copy-start | bytes 772
  40.4 5.6 %copy-start.2 = (bf16[64,4,1024]{2,0,1:T(8,128)(2,1)}, bf16[64,4,1024]{2,0,1:T(8,128)(2,1)S(1)}, u32[]{:S(2)}) copy-start(bf16[64,4,1024]{2,0,1:T(8,128)(2,1)S(1)} %all-to-all-done) | copy-start | bytes 1572868
  40.4 7.9 %all-to-all-start.1 = ((bf16[64,4,256]{2,0,1:T(8,128)(2,1)}), bf16[64,4,256]{2,0,1:T(8,128)(2,1)S(1)}, u32[]{:S(2)}, u32[]{:S(2)}) async-start(bf16[64,4,256]{2,0,1:T(8,128)(2,1)} %bitcast.205), calls=%async_computation.1 | async-start | bytes 262144 | tf_op jit(solution)/shard_map/all_to_all | solution.py:86
  44.5 7.1 %copy-start.13 = (f32[256,8]{0,1:T(8,128)S(1)}, f32[256,8]{0,1:T(8,128)}, u32[]{:S(2)}) copy-start(f32[256,8]{0,1:T(8,128)} %param.14) | copy-start | bytes 24580
  45.6 21.8 %copy-start.5 = (bf16[2,8,128,128]{3,1,2,0:T(8,128)(2,1)S(1)}, bf16[2,8,128,128]{3,1,2,0:T(8,128)(2,1)}, u32[]{:S(2)}) copy-start(bf16[2,8,128,128]{3,1,2,0:T(8,128)(2,1)} %bitcast_bitcast_fusion.4) | copy-start | bytes 1572868
  48.3 11.5 %all-to-all-start.3 = ((bf16[64,4,256]{2,0,1:T(8,128)(2,1)}), bf16[64,4,256]{2,0,1:T(8,128)(2,1)S(1)}, u32[]{:S(2)}, u32[]{:S(2)}) async-start(bf16[64,4,256]{2,0,1:T(8,128)(2,1)} %bitcast.204), calls=%async_computation.3 | async-start | bytes 262144 | tf_op jit(solution)/shard_map/all_to_all | solution.py:87
  59.8 25.8 %all-to-all-start.6 = ((f32[80,2,128]{2,1,0:T(2,128)}), f32[80,2,128]{2,1,0:T(2,128)S(1)}, u32[]{:S(2)}, u32[]{:S(2)}) async-start(f32[80,2,128]{2,1,0:T(2,128)} %scatter_fusion.1), calls=%async_computation.6 | async-start | bytes 163840 | tf_op jit(solution)/shard_map/all_to_all | solution.py:146
  85.7 121.7 %all-to-all-start.5 = ((bf16[80,128,256]{2,1,0:T(8,128)(2,1)}), bf16[80,128,256]{2,1,0:T(8,128)(2,1)}, u32[]{:S(2)}, u32[]{:S(2)}) async-start(bf16[80,128,256]{2,1,0:T(8,128)(2,1)} %scatter_fusion), calls=%async_computation.5 | async-start | bytes 10485760 | tf_op jit(solution)/shard_map/all_to_all | solution.py:145
  257.3 4.7 %copy-start.9 = (s32[8,10]{0,1:T(8,128)S(1)}, s32[8,10]{0,1:T(8,128)}, u32[]{:S(2)}) copy-start(s32[8,10]{0,1:T(8,128)} %get-tuple-element.60) | copy-start | bytes 964
  257.3 6.1 %copy-start.12 = (s32[64]{0:T(128)S(1)}, s32[64]{0:T(128)}, u32[]{:S(2)}) copy-start(s32[64]{0:T(128)} %copy-done.11) | copy-start | bytes 772
  257.3 63.5 %all-to-all-start.7 = ((bf16[80,128,128]{2,1,0:T(8,128)(2,1)}), bf16[80,128,128]{2,1,0:T(8,128)(2,1)S(1)}, u32[]{:S(2)}, u32[]{:S(2)}) async-start(bf16[80,128,128]{2,1,0:T(8,128)(2,1)} %bitcast.245), calls=%async_computation.7 | async-start | bytes 5242880 | tf_op jit(solution)/shard_map/all_to_all | solution.py:161
  261.2 7.4 %copy-start.14 = (f32[256,8]{0,1:T(8,128)S(1)}, f32[256,8]{0,1:T(8,128)}, u32[]{:S(2)}) copy-start(f32[256,8]{0,1:T(8,128)} %param.14) | copy-start | bytes 24580
  268.7 2.6 copy-start
  270.3 1.0 copy-start.3
  275.3 0.8 copy-start.1
  280.2 2.2 copy-start.15
  280.2 2.2 copy-start.16
  280.2 2.2 copy-start.17
  320.8 7.9 %all-to-all-start.10 = ((bf16[4,64,256]{2,1,0:T(8,128)(2,1)}), bf16[4,64,256]{2,1,0:T(8,128)(2,1)S(1)}, u32[]{:S(2)}, u32[]{:S(2)}) async-start(bf16[4,64,256]{2,1,0:T(8,128)(2,1)} %add_convert_fusion), calls=%async_computation.10 | async-start | bytes 262144 | tf_op jit(solution)/shard_map/all_to_all | solution.py:186
  326.4 5.7 %copy-start.4 = (f32[2,2,4,128,128]{4,3,2,1,0:T(8,128)S(1)}, f32[2,2,4,128,128]{4,3,2,1,0:T(8,128)}, u32[]{:S(2)}) copy-start(f32[2,2,4,128,128]{4,3,2,1,0:T(8,128)} %convolution_multiply_fusion.3) | copy-start | bytes 3145732
  328.7 7.9 %all-to-all-start.9 = ((bf16[4,64,256]{2,1,0:T(8,128)(2,1)}), bf16[4,64,256]{2,1,0:T(8,128)(2,1)S(1)}, u32[]{:S(2)}, u32[]{:S(2)}) async-start(bf16[4,64,256]{2,1,0:T(8,128)(2,1)} %add_convert_fusion.1), calls=%async_computation.9 | async-start | bytes 262144 | tf_op jit(solution)/shard_map/all_to_all | solution.py:185
  336.6 12.3 %all-to-all-start.8 = ((bf16[4,64,1024]{2,1,0:T(8,128)(2,1)}), bf16[4,64,1024]{2,1,0:T(8,128)(2,1)S(1)}, u32[]{:S(2)}, u32[]{:S(2)}) async-start(bf16[4,64,1024]{2,1,0:T(8,128)(2,1)} %all_to_all.122), calls=%async_computation.8 | async-start | bytes 1048576 | tf_op jit(solution)/shard_map/all_to_all | solution.py:184
where the time goes:
time: 352 us; the launch traced here: 350 us
  waiting for transfers between devices  172 us (49%)
  local copies, waits for them, and re-layouts  72.6 us (21%)
  matrix products  49.4 us (14%)
  starting transfers between devices  44.5 us (13%)
  other arithmetic  10.5 us (3%)
    all_to_all x1, waiting for transfers between devices, body(): lax.all_to_all(row_buffer, 'seq', split_axis=0, concat_axis=0, tiled=True)  109 us
    all_to_all x1, waiting for transfers between devices, body(): lax.all_to_all(dq_slots, 'seq', split_axis=0, concat_axis=0, tiled=True)  27.9 us
    scatter x1, local copies, waits for them, and re-layouts, body(): jnp.zeros((slot_count, QB, 2 * HD), jnp.bfloat16).at[slots].set(send_rows)  12.1 us
    dot_general x5, matrix products, remote_terms(): jnp.einsum('nkq,nkd->nqd', score_low, k_rows, preferred_element_type=jnp....  10.6 us
    dot_general x5, matrix products, remote_terms(): jnp.einsum('nkq,nqd->nkd', prob_low, o_grad, preferred_element_type=jnp.f...  10.1 us
    dot_general x5, matrix products, remote_terms(): jnp.einsum('nkd,nqd->nkq', v_rows, o_grad, preferred_element_type=jnp.flo...  7.95 us
    all_to_all x1, waiting for transfers between devices, body(): lax.all_to_all(grad_q, 'head', split_axis=0, concat_axis=1, tiled=True)  7.48 us
    all_to_all x1, waiting for transfers between devices, body(): lax.all_to_all(outputs_saved, 'head', split_axis=1, concat_axis=0, tiled=...  7.37 us
  transfers between devices with their start and end apart: 11, of which 9 were waited for; matrix products, arithmetic and copies ran while one was open for 22% of the time, Pallas kernels for 0%

commit v1 on v0

v1 whole, which is shorter than its diff:
```python
import functools

import jax
import jax.numpy as jnp
from jax import lax
from jax.experimental import pallas as pl
from jax.experimental.pallas import tpu as pltpu
from jax.sharding import PartitionSpec as P

HD = 128
QB = 128
KB = 64
NSEL = 4
GROUP = 4
SCALE = HD ** (-0.5)
STAT = 16

VMEM = pl.BlockSpec(memory_space=pltpu.VMEM)
SMEM = pl.BlockSpec(memory_space=pltpu.SMEM)
NT = (((1,), (1,)), ((), ()))
TN = (((0,), (0,)), ((), ()))
PARAMS = pltpu.CompilerParams(vmem_limit_bytes=48 * 1024 * 1024)


def dot(a, b, dims=(((1,), (0,)), ((), ()))):
    return lax.dot_general(a, b, dims, preferred_element_type=jnp.float32)


def pack_kv_kernel(k_ref, v_ref, out_ref):
    for g in range(out_ref.shape[0]):
        cols = slice(g * HD, (g + 1) * HD)
        out_ref[g, :, :HD] = k_ref[:, cols]
        out_ref[g, :, HD:] = v_ref[:, cols]


def pack_kv(keys, values):
    tokens, width = keys.shape
    return pl.pallas_call(
        pack_kv_kernel,
        out_shape=jax.ShapeDtypeStruct((width // HD, tokens, 2 * HD), jnp.bfloat16),
        in_specs=[VMEM, VMEM],
        out_specs=VMEM,
        compiler_params=PARAMS,
    )(keys, values)


def three_pieces(x):
    hi = x.astype(jnp.bfloat16)
    rest = x - hi.astype(jnp.float32)
    mid = rest.astype(jnp.bfloat16)
    low = (rest - mid.astype(jnp.float32)).astype(jnp.bfloat16)
    return hi, mid, low


def pack_q_kernel(q_ref, do_ref, o_ref, out_ref):
    peers, rows, _ = out_ref.shape
    heads = (rows - STAT) // KB
    lane = lax.broadcasted_iota(jnp.int32, (KB, HD), 1)
    delta = jnp.zeros((KB, HD), jnp.float32)
    for t in range(peers):
        for h in range(heads):
            head = t * heads + h
            cols = slice(head * HD, (head + 1) * HD)
            do = do_ref[:, cols]
            out_ref[t, h * KB : (h + 1) * KB, :HD] = q_ref[:, cols]
            out_ref[t, h * KB : (h + 1) * KB, HD:] = do
            products = do.astype(jnp.float32) * o_ref[:, cols].astype(jnp.float32)
            total = jnp.sum(products, axis=-1, keepdims=True)
            delta = jnp.where(lane == head, total, delta)
    by_head = delta.T
    for t in range(peers):
        hi, mid, low = three_pieces(by_head[t * heads : (t + 1) * heads])
        base = heads * KB
        zero = jnp.zeros((heads, HD - KB), jnp.bfloat16)
        first = jnp.concatenate([hi, zero, mid, zero], axis=1)
        second = jnp.concatenate([low, zero, zero, jnp.zeros_like(low)], axis=1)
        out_ref[t, base : base + STAT, :] = jnp.concatenate([first, second], axis=0)


def pack_q(queries, grad_out, outputs_saved, peers):
    tokens, width = queries.shape
    heads = width // HD // peers
    return pl.pallas_call(
        pack_q_kernel,
        out_shape=jax.ShapeDtypeStruct((peers, heads * tokens + STAT, 2 * HD), jnp.bfloat16),
        in_specs=[VMEM] * 3,
        out_specs=VMEM,
        compiler_params=PARAMS,
    )(queries, grad_out, outputs_saved)


def attend_kernel(
    slot_ref, kv_ref, own_kv_ref, qdo_ref, lse_ref, dq_ref, part_ref, own_ref, sums, stats
):
    peers, rows, _ = qdo_ref.shape
    heads = (rows - STAT) // KB
    kv_heads = heads // GROUP
    blocks = peers * KB // QB
    base = heads * KB
    sums[...] = jnp.zeros_like(sums)
    own_ref[...] = jnp.zeros_like(own_ref)
    lse = lse_ref[...].T
    pieces = []
    for t in range(peers):
        first = qdo_ref[t, base : base + heads, :].astype(jnp.float32)
        second = qdo_ref[t, base + heads : base + 2 * heads, :].astype(jnp.float32)
        pieces.append(first[:, :KB] + first[:, HD : HD + KB] + second[:, :KB])
    delta = jnp.concatenate(pieces, axis=1)
    stats[0] = lse
    stats[1] = delta
    key_row = lax.broadcasted_iota(jnp.int32, (QB, QB), 0)
    query_row = lax.broadcasted_iota(jnp.int32, (QB, QB), 1)
    causal = key_row <= query_row
    for b in range(blocks):
        for h in range(heads):
            g = h // GROUP
            rows_h = slice(h * KB, (h + 1) * KB)
            q = jnp.concatenate([qdo_ref[2 * b + i, rows_h, :HD] for i in range(2)], axis=0)
            do = jnp.concatenate([qdo_ref[2 * b + i, rows_h, HD:] for i in range(2)], axis=0)
            slots = [slot_ref[(b * heads + h) * NSEL + n] for n in range(NSEL)]
            own = [(2 * b + i) * kv_heads + g for i in range(2)]
            listed = [kv_ref[s] for s in slots] + [own_kv_ref[u] for u in own]
            kv = jnp.concatenate(listed, axis=0)
            k = kv[:, :HD]
            v = kv[:, HD:]
            lse_row = stats[0, h : h + 1, b * QB : (b + 1) * QB]
            delta_row = stats[1, h : h + 1, b * QB : (b + 1) * QB]
            prob = jnp.exp(dot(k, q, NT) * SCALE - lse_row)
            own_prob = jnp.where(causal, prob[NSEL * KB :], 0.0)
            prob = jnp.concatenate([prob[: NSEL * KB], own_prob], axis=0)
            score = (prob * (dot(v, do, NT) - delta_row)).astype(jnp.bfloat16)
            prob = prob.astype(jnp.bfloat16)
            dq = dot(score, k, TN) * SCALE
            for i in range(2):
                dq_ref[2 * b + i, :, h * HD : (h + 1) * HD] = dq[i * KB : (i + 1) * KB].astype(
                    jnp.bfloat16
                )
            dk = dot(score, q) * SCALE
            dv = dot(prob, do)
            for n in range(NSEL):
                part = slice(n * KB, (n + 1) * KB)
                sums[slots[n], :, :HD] += dk[part]
                sums[slots[n], :, HD:] += dv[part]
            for i in range(2):
                part = slice((NSEL + i) * KB, (NSEL + i + 1) * KB)
                own_ref[own[i], :, :HD] += dk[part]
                own_ref[own[i], :, HD:] += dv[part]
    part_ref[...] = sums[...].astype(jnp.bfloat16)


def attend(slots, kv_slots, own_kv, qdo, lse):
    peers, rows, _ = qdo.shape
    heads = (rows - STAT) // KB
    return pl.pallas_call(
        attend_kernel,
        out_shape=(
            jax.ShapeDtypeStruct((peers, KB, heads * HD), jnp.bfloat16),
            jax.ShapeDtypeStruct(kv_slots.shape, jnp.bfloat16),
            jax.ShapeDtypeStruct(own_kv.shape, jnp.float32),
        ),
        in_specs=[SMEM, VMEM, VMEM, VMEM, VMEM],
        out_specs=(VMEM, VMEM, VMEM),
        scratch_shapes=[
            pltpu.VMEM(kv_slots.shape, jnp.float32),
            pltpu.VMEM((2, heads, peers * KB), jnp.float32),
        ],
        compiler_params=PARAMS,
    )(slots, kv_slots, own_kv, qdo, lse)


def unpack_kernel(dq_ref, dkv_ref, gq_ref, gk_ref, gv_ref):
    peers, _, width = dq_ref.shape
    for t in range(peers):
        gq_ref[:, t * width : (t + 1) * width] = dq_ref[t]
    for g in range(dkv_ref.shape[0]):
        gk_ref[:, g * HD : (g + 1) * HD] = dkv_ref[g, :, :HD]
        gv_ref[:, g * HD : (g + 1) * HD] = dkv_ref[g, :, HD:]


def unpack(dq, dkv):
    peers, tokens, width = dq.shape
    kv_heads = dkv.shape[0]
    return pl.pallas_call(
        unpack_kernel,
        out_shape=(
            jax.ShapeDtypeStruct((tokens, peers * width), jnp.bfloat16),
            jax.ShapeDtypeStruct((tokens, kv_heads * HD), jnp.bfloat16),
            jax.ShapeDtypeStruct((tokens, kv_heads * HD), jnp.bfloat16),
        ),
        in_specs=[VMEM, VMEM],
        out_specs=(VMEM, VMEM, VMEM),
        compiler_params=PARAMS,
    )(dq, dkv)


def body(queries, keys, values, outputs_saved, grad_out, lse, block_lists):
    peers = lax.axis_size("head")
    shards = lax.axis_size("seq")
    me = lax.axis_index("seq")
    heads = lse.shape[1]
    kv_heads = heads // GROUP
    key_count = peers
    units = key_count * kv_heads

    own_kv = lax.all_to_all(pack_kv(keys, values), "head", 0, 0, tiled=True)

    per_peer = block_lists.reshape(shards, -1)
    requests = per_peer.shape[1]
    order = jnp.arange(requests, dtype=jnp.int32)
    group_of = order % (heads * NSEL) // (NSEL * GROUP)
    capacity = -(-requests // (shards - 1))
    dense = units <= capacity

    if dense:
        kv_slots = lax.all_gather(own_kv, "seq", axis=0, tiled=True)
        mine = lax.dynamic_index_in_dim(per_peer, me, 0, keepdims=False)
        slots = mine * kv_heads + group_of
    else:
        owner = per_peer // key_count
        earlier = (owner[:, :, None] == owner[:, None, :]) & (order[None, :] < order[:, None])
        position = jnp.sum(earlier.astype(jnp.int32), axis=2)
        slots = lax.dynamic_index_in_dim(owner * capacity + position, me, 0, keepdims=False)
        hits = (owner == me)[:, :, None] & (position[:, :, None] == jnp.arange(capacity))
        hits = hits.astype(jnp.int32)
        used = jnp.sum(hits, axis=1).reshape(-1)
        wanted = (per_peer % key_count) * kv_heads + group_of[None, :]
        wanted = jnp.sum(hits * wanted[:, :, None], axis=1).reshape(-1)
        kv_slots = lax.all_to_all(own_kv[wanted], "seq", 0, 0, tiled=True)

    packed = pack_q(queries, grad_out, outputs_saved, peers)
    qdo = lax.all_to_all(packed, "head", 0, 0, tiled=True)
    dq, parts, own = attend(slots, kv_slots, own_kv, qdo, lse)
    dq = lax.all_to_all(dq, "head", 0, 0, tiled=True)

    if dense:
        total = lax.psum_scatter(parts, "seq", scatter_dimension=0, tiled=True)
        total = total.astype(jnp.float32) + own
    else:
        parts = lax.all_to_all(parts, "seq", 0, 0, tiled=True)
        chosen = (jnp.arange(units)[:, None] == wanted[None, :]) & (used[None, :] > 0)
        total = jnp.dot(
            chosen.astype(jnp.bfloat16),
            parts.reshape(parts.shape[0], -1),
            preferred_element_type=jnp.float32,
        )
        total = total.reshape(own.shape) + own
    dkv = lax.all_to_all(total.astype(jnp.bfloat16), "head", 0, 0, tiled=True)
    return unpack(dq, dkv)


def solution(mesh):
    rows = P(("seq", "head"), None)
    in_specs = (rows, rows, rows, rows, rows, P("seq", "head"), P(None, "head", None))
    return jax.shard_map(
        body, mesh=mesh, in_specs=in_specs, out_specs=(rows, rows, rows), check_vma=False
    )
```

time: 352 us -> 162 us (0.46)
  waiting for transfers between devices: 172 us -> 104 us
  local copies, waits for them, and re-layouts: 72.6 us -> 5.28 us
  matrix products: 49.4 us -> 0 us
  starting transfers between devices: 44.5 us -> 7.08 us
  blocking collectives: 0 us -> 18.7 us
  between operations: 1.08 us -> 14.1 us
  Pallas kernels: 0 us -> 10.7 us
  other arithmetic: 10.5 us -> 1.02 us
    all_to_all x11 -> x2, waiting for transfers between devices: 172 us -> 14.3 us  [the longest x1 14.3 us: body(): qdo = lax.all_to_all(packed, 'head', 0, 0, tiled=True)]
    reduce_scatter x0 -> x1, waiting for transfers between devices: none -> 62.8 us  [body(): total = lax.psum_scatter(parts, 'seq', scatter_dimension=0, tiled=True)]
    dot_general x31 -> x0, matrix products: 49.4 us -> none  [the longest x5 10.6 us: remote_terms(): jnp.einsum('nkq,nkd->nqd', score_low, k_rows, preferred_element_type=jnp....]
    all_to_all x11 -> x2, starting transfers between devices: 44.5 us -> 7 us  [the longest x1 3.52 us: body(): qdo = lax.all_to_all(packed, 'head', 0, 0, tiled=True)]
    all_gather x0 -> x1, waiting for transfers between devices: none -> 27.3 us  [body(): kv_slots = lax.all_gather(own_kv, 'seq', axis=0, tiled=True)]
    scatter x2 -> x0, local copies, waits for them, and re-layouts: 19 us -> none  [the longest x1 12.1 us: body(): jnp.zeros((slot_count, QB, 2 * HD), jnp.bfloat16).at[slots].set(send_rows)]
    all_to_all x0 -> x2, blocking collectives: none -> 18.7 us  [the longest x1 10.2 us: body(): own_kv = lax.all_to_all(pack_kv(keys, values), 'head', 0, 0, tiled=True)]
    pallas_call x0 -> x4, Pallas kernels: none -> 10.7 us  [the longest x1 8.29 us: attend(): pl.pallas_call(attend_kernel, out_shape=(jax.ShapeDtypeStruct((peers, KB,...]
  transfers between devices with their start and end apart: 11 -> 4, of which waited for: 9 -> 3; matrix products, arithmetic and copies ran while one was open for 22% -> 1% of each run, Pallas kernels for 0% -> 1%
where the time goes in v1:
time: 162 us; the launch traced here: 161 us
  waiting for transfers between devices  104 us (64%)
  blocking collectives  18.7 us (12%)
  between operations  14.1 us (9%)
  Pallas kernels  10.7 us (7%)
  starting transfers between devices  7.08 us (4%)
  local copies, waits for them, and re-layouts  5.28 us (3%)
    reduce_scatter x1, waiting for transfers between devices, body(): total = lax.psum_scatter(parts, 'seq', scatter_dimension=0, tiled=True)  62.8 us
    all_gather x1, waiting for transfers between devices, body(): kv_slots = lax.all_gather(own_kv, 'seq', axis=0, tiled=True)  27.3 us
    all_to_all x1, waiting for transfers between devices, body(): qdo = lax.all_to_all(packed, 'head', 0, 0, tiled=True)  14.3 us
    all_to_all x1, blocking collectives, body(): own_kv = lax.all_to_all(pack_kv(keys, values), 'head', 0, 0, tiled=True)  10.2 us
    all_to_all x1, blocking collectives, body(): dkv = lax.all_to_all(total.astype(jnp.bfloat16), 'head', 0, 0, tiled=True)  8.57 us
    pallas_call x1, Pallas kernels, attend(): pl.pallas_call(attend_kernel, out_shape=(jax.ShapeDtypeStruct((peers, KB,...  8.29 us
    unnamed x18, local copies, waits for them, and re-layouts  5.18 us
    all_to_all x1, starting transfers between devices, body(): qdo = lax.all_to_all(packed, 'head', 0, 0, tiled=True)  3.52 us
  transfers between devices with their start and end apart: 4, of which 3 were waited for; matrix products, arithmetic and copies ran while one was open for 1% of the time, Pallas kernels for 1%

profile of v1, /device:TPU:0, one launch (start us, length us, event | category | flops | bytes accessed | tf_op | source)
XLA Modules:
  0.0 161.4 jit_solution(9181297240082715127)
XLA Ops:
  7.2 0.0 all-gather.2.cloned.1.call-start
  7.2 0.0 copy-start.4
  7.2 0.9 copy-done.4
  8.1 0.0 copy-start.5
  8.1 0.9 copy-done.5
  9.1 10.2 %all_to_all.20.own_kv_ref = bf16[8,64,256]{2,1,0:T(8,128)(2,1)} all-to-all(bf16[8,64,256]{2,1,0:T(8,128)(2,1)S(1)} %shard_map.94), channel_id=1, replica_groups=mesh['seq'=8,'head'=4] {'head'}, dimensions={0} | all-to-all | bytes 524288 | tf_op jit(solution)/shard_map/all_to_all | solution.py:205
  19.2 0.0 all-gather.2.cloned.1.call-update
  19.2 0.0 copy-start.1
  19.3 1.0 copy-done.1
  20.3 0.0 copy-start.2
  20.3 1.0 copy-done.2
  21.3 0.0 copy-start.3
  21.3 1.0 copy-done.3
  22.4 0.0 copy-start.6
  22.4 0.0 copy-start.7
  22.4 0.0 copy-start
  22.4 1.4 shard_map.95
  23.8 3.5 %all-to-all-start.1 = ((bf16[4,528,256]{2,1,0:T(8,128)(2,1)}), bf16[4,528,256]{2,1,0:T(8,128)(2,1)S(1)}, u32[]{:S(2)}, u32[]{:S(2)}) async-start(bf16[4,528,256]{2,1,0:T(8,128)(2,1)} %shard_map.95), calls=%async_computation.1 | async-start | bytes 2162688 | tf_op jit(solution)/shard_map/all_to_all | solution.py:231
  27.3 0.0 reduce-scatter.2.cloned.1.call-start
  27.4 0.0 copy-done.6
  27.4 0.1 copy.13
  27.5 0.1 reshape.11
  27.6 0.0 copy-done.7
  27.6 0.1 copy.14.lse_ref
  27.8 14.3 %all-to-all-done.1.qdo_ref = bf16[4,528,256]{2,1,0:T(8,128)(2,1)S(1)} async-done(((bf16[4,528,256]{2,1,0:T(8,128)(2,1)}), bf16[4,528,256]{2,1,0:T(8,128)(2,1)S(1)}, u32[]{:S(2)}, u32[]{:S(2)}) %all-to-all-start.1) | async-done | bytes 1081376 | tf_op jit(solution)/shard_map/all_to_all | solution.py:231
  42.1 27.3 %all-gather.2.cloned.1.call-done.kv_ref = bf16[64,64,256]{2,1,0:T(8,128)(2,1)} async-done(((bf16[8,64,256]{2,1,0:T(8,128)(2,1)}), bf16[64,64,256]{2,1,0:T(8,128)(2,1)}) %all-gather.2.cloned.1.call-update) | async-done | bytes 2097168 | tf_op jit(solution)/shard_map/all_gather | solution.py:215
  69.4 0.0 copy-done
  69.4 8.3 %shard_map.96 = (bf16[4,64,1024]{2,1,0:T(8,128)(2,1)}, bf16[64,64,256]{2,1,0:T(8,128)(2,1)}, f32[8,64,256]{2,1,0:T(8,128)S(1)}) custom-call(s32[64]{0:T(128)S(1)} %bitcast_add_fusion.slot_ref, bf16[64,64,256]{2,1,0:T(8,128)(2,1)} %all-gather.2.cloned.1.call-done.kv_ref, bf16[8,64,256]{2,1,0:T(8,128)(2,1)S(1)} %copy-done, ...), custom_call_target="tpu_custom_call" | custom-call | tf_op jit(solution)/shard_map/pallas_call | solution.py:154
  77.7 0.0 reduce-scatter.2.cloned.1.call-update
  77.7 3.5 %all-to-all-start.2 = ((bf16[4,64,1024]{2,1,0:T(8,128)(2,1)}), bf16[4,64,1024]{2,1,0:T(8,128)(2,1)S(1)}, u32[]{:S(2)}, u32[]{:S(2)}) async-start(bf16[4,64,1024]{2,1,0:T(8,128)(2,1)} %get-tuple-element.6), calls=%async_computation.2 | async-start | bytes 1048576 | tf_op jit(solution)/shard_map/all_to_all | solution.py:233
  81.2 62.8 %reduce-scatter.2.cloned.1.call-done = bf16[8,64,256]{2,1,0:T(8,128)(2,1)} async-done(((bf16[64,64,256]{2,1,0:T(8,128)(2,1)}), bf16[8,64,256]{2,1,0:T(8,128)(2,1)}) %reduce-scatter.2.cloned.1.call-update) | async-done | bytes 262160 | tf_op jit(solution)/shard_map/reduce_scatter | solution.py:236
  144.0 1.0 add_convert_fusion
  145.1 0.0 all-to-all-done.2.dq_ref
  145.1 8.6 %all_to_all.21.dkv_ref = bf16[8,64,256]{2,1,0:T(8,128)(2,1)S(1)} all-to-all(bf16[8,64,256]{2,1,0:T(8,128)(2,1)S(1)} %add_convert_fusion), channel_id=1, replica_groups=mesh['seq'=8,'head'=4] {'head'}, dimensions={0} | all-to-all | bytes 524288 | tf_op jit(solution)/shard_map/all_to_all | solution.py:247
  153.6 1.0 shard_map.97
  (2 shorter events, 0.1 us)
Async XLA Ops:
  7.2 62.3 %all-gather.2.cloned.1.call-start = ((), (), s32[]{:S(2)}) async-start(), calls=%async_computation.5 | async-start | bytes 2359296 | tf_op jit(solution)/shard_map/all_gather | solution.py:215
  7.2 0.9 copy-start.4
  8.1 0.9 copy-start.5
  19.2 1.0 copy-start.1
  20.3 1.0 copy-start.2
  21.3 1.0 copy-start.3
  22.4 5.0 %copy-start.6 = (s32[16,8,4]{0,2,1:T(4,128)S(1)}, s32[16,8,4]{0,2,1:T(4,128)}, u32[]{:S(2)}) copy-start(s32[16,8,4]{0,2,1:T(4,128)} %param.13) | copy-start | bytes 6148
  22.4 5.2 %copy-start.7 = (f32[256,8]{0,1:T(8,128)S(1)}, f32[256,8]{0,1:T(8,128)}, u32[]{:S(2)}) copy-start(f32[256,8]{0,1:T(8,128)} %param.12) | copy-start | bytes 24580
  22.4 47.0 %copy-start = (bf16[8,64,256]{2,1,0:T(8,128)(2,1)S(1)}, bf16[8,64,256]{2,1,0:T(8,128)(2,1)}, u32[]{:S(2)}) copy-start(bf16[8,64,256]{2,1,0:T(8,128)(2,1)} %all_to_all.20.own_kv_ref) | copy-start | bytes 786436
  23.8 18.3 %all-to-all-start.1 = ((bf16[4,528,256]{2,1,0:T(8,128)(2,1)}), bf16[4,528,256]{2,1,0:T(8,128)(2,1)S(1)}, u32[]{:S(2)}, u32[]{:S(2)}) async-start(bf16[4,528,256]{2,1,0:T(8,128)(2,1)} %shard_map.95), calls=%async_computation.1 | async-start | bytes 2162688 | tf_op jit(solution)/shard_map/all_to_all | solution.py:231
  27.3 116.7 %reduce-scatter.2.cloned.1.call-start = ((), (), s32[]{:S(2)}) async-start(), calls=%async_computation.6 | async-start | bytes 2359296 | tf_op jit(solution)/shard_map/reduce_scatter | solution.py:236
  77.7 67.3 %all-to-all-start.2 = ((bf16[4,64,1024]{2,1,0:T(8,128)(2,1)}), bf16[4,64,1024]{2,1,0:T(8,128)(2,1)S(1)}, u32[]{:S(2)}, u32[]{:S(2)}) async-start(bf16[4,64,1024]{2,1,0:T(8,128)(2,1)} %get-tuple-element.6), calls=%async_computation.2 | async-start | bytes 1048576 | tf_op jit(solution)/shard_map/all_to_all | solution.py:233
Sparse Core Ops, SparseCore 0:
  19.4 50.0 all-gather.1
  77.9 66.1 reduce-scatter.1

commit v2 on v1

v2 whole, which is shorter than its diff:
```python
import functools

import jax
import jax.numpy as jnp
from jax import lax
from jax.experimental import pallas as pl
from jax.experimental.pallas import tpu as pltpu
from jax.sharding import PartitionSpec as P

HD = 128
QB = 128
KB = 64
NSEL = 4
GROUP = 4
SCALE = HD ** (-0.5)
STAT = 16

VMEM = pl.BlockSpec(memory_space=pltpu.VMEM)
ANY = pl.BlockSpec(memory_space=pl.ANY)
HBM = pl.BlockSpec(memory_space=pltpu.HBM)
SMEM = pl.BlockSpec(memory_space=pltpu.SMEM)
NT = (((1,), (1,)), ((), ()))
TN = (((0,), (0,)), ((), ()))
PARAMS = pltpu.CompilerParams(vmem_limit_bytes=24 * 1024 * 1024)


def dot(a, b, dims=(((1,), (0,)), ((), ()))):
    return lax.dot_general(a, b, dims, preferred_element_type=jnp.float32)


def lanes(index, width):
    return pl.ds(pl.multiple_of(index * width, width), width)


def run_copies(pairs, sems):
    copies = [
        pltpu.make_async_copy(source, target, sems.at[i])
        for i, (source, target) in enumerate(pairs)
    ]
    for copy in copies:
        copy.start()
    return copies


def pack_kv_kernel(peers, me_ref, k_ref, v_ref, *refs):
    out_refs, sems = refs[:peers], refs[peers]
    kv_heads = out_refs[0].shape[0]
    pairs = []
    for c, out_ref in reversed(list(enumerate(out_refs))):
        for g in range(kv_heads):
            cols = lanes((me_ref[0] ^ c) * kv_heads + g, HD)
            pairs.append((k_ref.at[:, cols], out_ref.at[g, :, pl.ds(0, HD)]))
            pairs.append((v_ref.at[:, cols], out_ref.at[g, :, pl.ds(HD, HD)]))
    for copy in run_copies(pairs, sems):
        copy.wait()


def pack_kv(me, keys, values, peers):
    tokens, width = keys.shape
    kv_heads = width // HD // peers
    piece = jax.ShapeDtypeStruct((kv_heads, tokens, 2 * HD), jnp.bfloat16)
    return pl.pallas_call(
        functools.partial(pack_kv_kernel, peers),
        out_shape=(piece,) * peers,
        in_specs=[SMEM, HBM, HBM],
        out_specs=(VMEM,) * peers,
        scratch_shapes=[pltpu.SemaphoreType.DMA((2 * peers * kv_heads,))],
        compiler_params=PARAMS,
    )(me, keys, values)


def three_pieces(x):
    hi = x.astype(jnp.bfloat16)
    rest = x - hi.astype(jnp.float32)
    mid = rest.astype(jnp.bfloat16)
    low = (rest - mid.astype(jnp.float32)).astype(jnp.bfloat16)
    return hi, mid, low


def pack_q_kernel(peers, me_ref, q_any, do_any, o_any, *refs):
    out_refs = refs[:peers]
    q_ref, do_ref, o_ref, sems = refs[peers:]
    for copy in run_copies([(q_any, q_ref), (do_any, do_ref), (o_any, o_ref)], sems):
        copy.wait()
    heads = (out_refs[0].shape[0] - STAT) // KB
    lane = lax.broadcasted_iota(jnp.int32, (KB, HD), 1)
    delta = jnp.zeros((KB, HD), jnp.float32)
    for c, out_ref in enumerate(out_refs):
        for h in range(heads):
            cols = lanes((me_ref[0] ^ c) * heads + h, HD)
            do = do_ref[:, cols]
            out_ref[h * KB : (h + 1) * KB, :HD] = q_ref[:, cols]
            out_ref[h * KB : (h + 1) * KB, HD:] = do
            products = do.astype(jnp.float32) * o_ref[:, cols].astype(jnp.float32)
            total = jnp.sum(products, axis=-1, keepdims=True)
            delta = jnp.where(lane == c * heads + h, total, delta)
    by_head = delta.T
    for c, out_ref in enumerate(out_refs):
        hi, mid, low = three_pieces(by_head[c * heads : (c + 1) * heads])
        base = heads * KB
        zero = jnp.zeros((heads, HD - KB), jnp.bfloat16)
        first = jnp.concatenate([hi, zero, mid, zero], axis=1)
        second = jnp.concatenate([low, zero, zero, jnp.zeros_like(low)], axis=1)
        out_ref[base : base + STAT, :] = jnp.concatenate([first, second], axis=0)


def pack_q(me, queries, grad_out, outputs_saved, peers):
    tokens, width = queries.shape
    heads = width // HD // peers
    piece = jax.ShapeDtypeStruct((heads * tokens + STAT, 2 * HD), jnp.bfloat16)
    return pl.pallas_call(
        functools.partial(pack_q_kernel, peers),
        out_shape=(piece,) * peers,
        in_specs=[SMEM] + [HBM] * 3,
        out_specs=(VMEM,) * peers,
        scratch_shapes=[pltpu.VMEM(queries.shape, jnp.bfloat16)] * 3
        + [pltpu.SemaphoreType.DMA((3,))],
        compiler_params=PARAMS,
    )(me, queries, grad_out, outputs_saved)


def query_rows(qdo, c, h):
    rows = slice(h * KB, (h + 1) * KB)
    pair = (qdo[c], qdo[c ^ 1])
    q = jnp.concatenate([ref[rows, :HD] for ref in pair], axis=0)
    do = jnp.concatenate([ref[rows, HD:] for ref in pair], axis=0)
    return q, do


def own_kernel(peers, me_ref, own_kv_ref, stats_ref, *refs):
    qdo = refs[:peers]
    listed_refs = refs[peers : 2 * peers]
    dq_refs, own_ref = refs[2 * peers : 3 * peers], refs[3 * peers]
    heads = (qdo[0].shape[0] - STAT) // KB
    kv_heads = heads // GROUP
    key_row = lax.broadcasted_iota(jnp.int32, (QB, QB), 0)
    query_row = lax.broadcasted_iota(jnp.int32, (QB, QB), 1)
    swapped = jnp.where((me_ref[0] & 1) == 1, KB, 0)
    causal = (key_row ^ swapped) <= (query_row ^ swapped)
    for c in range(0, peers, 2):
        for g in range(kv_heads):
            own = [(c + i) * kv_heads + g for i in range(2)]
            kv = jnp.concatenate([own_kv_ref[u] for u in own], axis=0)
            k = kv[:, :HD]
            v = kv[:, HD:]
            dk = jnp.zeros((QB, HD), jnp.float32)
            dv = jnp.zeros((QB, HD), jnp.float32)
            for h in range(g * GROUP, (g + 1) * GROUP):
                q, do = query_rows(qdo, c, h)
                lse_row = stats_ref[0, h : h + 1, c * KB : c * KB + QB]
                delta_row = stats_ref[1, h : h + 1, c * KB : c * KB + QB]
                prob = jnp.where(causal, jnp.exp(dot(k, q, NT) * SCALE - lse_row), 0.0)
                score = (prob * (dot(v, do, NT) - delta_row)).astype(jnp.bfloat16)
                dq = dot(score, k, TN) * SCALE
                cols = slice(h * HD, (h + 1) * HD)
                for i in range(2):
                    part = listed_refs[c + i][:, cols] + dq[i * KB : (i + 1) * KB]
                    dq_refs[c + i][:, cols] = part.astype(jnp.bfloat16)
                dk += dot(score, q)
                dv += dot(prob.astype(jnp.bfloat16), do)
            for i in range(2):
                own_ref[own[i], :, :HD] = dk[i * KB : (i + 1) * KB] * SCALE
                own_ref[own[i], :, HD:] = dv[i * KB : (i + 1) * KB]


def own_terms(me, own_kv, stats, qdo, listed):
    peers = len(qdo)
    piece = jax.ShapeDtypeStruct(listed[0].shape, jnp.bfloat16)
    outs = pl.pallas_call(
        functools.partial(own_kernel, peers),
        out_shape=(piece,) * peers + (jax.ShapeDtypeStruct(own_kv.shape, jnp.float32),),
        in_specs=[SMEM] + [VMEM] * (2 + 2 * peers),
        out_specs=(VMEM,) * (peers + 1),
        compiler_params=PARAMS,
        cost_estimate=pl.CostEstimate(
            flops=335_000_000, bytes_accessed=4_000_000, transcendentals=260_000
        ),
    )(me, own_kv, stats, *qdo, *listed)
    return outs[:peers], outs[peers]


def row_stats(me, qdo, lse_ref, stats_ref):
    peers = len(qdo)
    heads = (qdo[0].shape[0] - STAT) // KB
    base = heads * KB
    lse_blocks = [lse_ref[:, c * KB : (c + 1) * KB] for c in range(peers)]
    for c in range(peers):
        first = qdo[c][base : base + heads, :].astype(jnp.float32)
        second = qdo[c][base + heads : base + 2 * heads, :].astype(jnp.float32)
        delta = first[:, :KB] + first[:, HD : HD + KB] + second[:, :KB]
        lse_here = lse_blocks[0]
        for t in range(1, peers):
            lse_here = jnp.where((me ^ c) == t, lse_blocks[t], lse_here)
        stats_ref[0, :, c * KB : (c + 1) * KB] = lse_here
        stats_ref[1, :, c * KB : (c + 1) * KB] = delta


def listed_kernel(peers, pieces, me_ref, slot_ref, lse_ref, *refs):
    qdo = refs[:peers]
    kv_refs = refs[peers : peers + pieces]
    outs = refs[peers + pieces : -3]
    stats_ref, dq_refs, part_refs = outs[0], outs[1 : peers + 1], outs[peers + 1 :]
    kv, sums, sems = refs[-3:]
    spans = []
    first = 0
    for ref in kv_refs:
        spans.append(pl.ds(first, ref.shape[0]))
        first += ref.shape[0]
    copies = run_copies([(ref, kv.at[span]) for ref, span in zip(kv_refs, spans)], sems)
    row_stats(me_ref[0], qdo, lse_ref, stats_ref)
    heads = (qdo[0].shape[0] - STAT) // KB
    sums[...] = jnp.zeros_like(sums)
    for copy in copies:
        copy.wait()
    for c in range(0, peers, 2):
        for h in range(heads):
            q, do = query_rows(qdo, c, h)
            slots = [slot_ref[(c // 2 * heads + h) * NSEL + n] for n in range(NSEL)]
            rows_kv = jnp.concatenate([kv[s] for s in slots], axis=0)
            k = rows_kv[:, :HD]
            v = rows_kv[:, HD:]
            lse_row = stats_ref[0, h : h + 1, c * KB : c * KB + QB]
            delta_row = stats_ref[1, h : h + 1, c * KB : c * KB + QB]
            prob = jnp.exp(dot(k, q, NT) * SCALE - lse_row)
            score = (prob * (dot(v, do, NT) - delta_row)).astype(jnp.bfloat16)
            dq = dot(score, k, TN) * SCALE
            cols = slice(h * HD, (h + 1) * HD)
            for i in range(2):
                dq_refs[c + i][:, cols] = dq[i * KB : (i + 1) * KB]
            dk = dot(score, q) * SCALE
            dv = dot(prob.astype(jnp.bfloat16), do)
            for n in range(NSEL):
                part = slice(n * KB, (n + 1) * KB)
                sums[slots[n], :, :HD] += dk[part]
                sums[slots[n], :, HD:] += dv[part]
    for part_ref, span in zip(part_refs, spans):
        part_ref[...] = sums[span].astype(part_ref.dtype)


def listed_terms(me, slots, lse, qdo, kv_pieces, part_types):
    peers = len(qdo)
    pieces = len(kv_pieces)
    units = sum(piece.shape[0] for piece in kv_pieces)
    whole = (units,) + kv_pieces[0].shape[1:]
    heads, tokens = lse.shape
    outs = pl.pallas_call(
        functools.partial(listed_kernel, peers, pieces),
        out_shape=(
            jax.ShapeDtypeStruct((2, heads, tokens), jnp.float32),
            *[jax.ShapeDtypeStruct((KB, heads * HD), jnp.float32)] * peers,
            *[jax.ShapeDtypeStruct(p.shape, kind) for p, kind in zip(kv_pieces, part_types)],
        ),
        in_specs=[SMEM, SMEM] + [VMEM] * (1 + peers) + [ANY] * pieces,
        out_specs=(VMEM,) * (1 + peers + pieces),
        scratch_shapes=[
            pltpu.VMEM(whole, jnp.bfloat16),
            pltpu.VMEM(whole, jnp.float32),
            pltpu.SemaphoreType.DMA((pieces,)),
        ],
        compiler_params=PARAMS,
        cost_estimate=pl.CostEstimate(
            flops=671_000_000, bytes_accessed=8_000_000, transcendentals=530_000
        ),
    )(me, slots, lse, *qdo, *kv_pieces)
    return outs[0], outs[1 : peers + 1], outs[peers + 1 :]


def add_kernel(*refs):
    *terms, out_ref = refs
    total = terms[0][...].astype(jnp.float32)
    for ref in terms[1:]:
        total = total + ref[...].astype(jnp.float32)
    out_ref[...] = total.astype(out_ref.dtype)


def add_rounded(*terms):
    return pl.pallas_call(
        add_kernel,
        out_shape=jax.ShapeDtypeStruct(terms[0].shape, jnp.bfloat16),
        in_specs=[VMEM] * len(terms),
        out_specs=VMEM,
        compiler_params=PARAMS,
    )(*terms)


def total_kernel(kv_heads, own_ref, *refs):
    peers = own_ref.shape[0] // kv_heads
    arrived, out_refs = refs[:-peers], refs[-peers:]
    for c, out_ref in enumerate(out_refs):
        part = slice(c * kv_heads, (c + 1) * kv_heads)
        total = own_ref[part]
        for ref in arrived:
            total = total + ref[part].astype(jnp.float32)
        out_ref[...] = total.astype(jnp.bfloat16)


def total_rounded(own, arrived, kv_heads):
    peers = own.shape[0] // kv_heads
    piece = jax.ShapeDtypeStruct((kv_heads,) + own.shape[1:], jnp.bfloat16)
    return pl.pallas_call(
        functools.partial(total_kernel, kv_heads),
        out_shape=(piece,) * peers,
        in_specs=[VMEM] * (1 + len(arrived)),
        out_specs=(VMEM,) * peers,
        compiler_params=PARAMS,
    )(own, *arrived)


def unpack_kernel(peers, me_ref, *refs):
    dq_refs, dkv_refs = refs[:peers], refs[peers : 2 * peers]
    gq_ref, gk_ref, gv_ref = refs[2 * peers :]
    width = dq_refs[0].shape[1]
    kv_heads = dkv_refs[0].shape[0]
    for c in range(peers):
        source = me_ref[0] ^ c
        gq_ref[:, lanes(source, width)] = dq_refs[c][...]
        for g in range(kv_heads):
            cols = lanes(source * kv_heads + g, HD)
            gk_ref[:, cols] = dkv_refs[c][g, :, :HD]
            gv_ref[:, cols] = dkv_refs[c][g, :, HD:]


def unpack(me, dq, dkv):
    peers = len(dq)
    tokens, width = dq[0].shape
    kv_width = dkv[0].shape[0] * peers * HD
    return pl.pallas_call(
        functools.partial(unpack_kernel, peers),
        out_shape=(
            jax.ShapeDtypeStruct((tokens, peers * width), jnp.bfloat16),
            jax.ShapeDtypeStruct((tokens, kv_width), jnp.bfloat16),
            jax.ShapeDtypeStruct((tokens, kv_width), jnp.bfloat16),
        ),
        in_specs=[SMEM] + [VMEM] * (2 * peers),
        out_specs=(VMEM,) * 3,
        compiler_params=PARAMS,
    )(me, *dq, *dkv)


def exchange(pieces):
    peers = len(pieces)
    moved = [
        lax.ppermute(pieces[c], "head", [(h, h ^ c) for h in range(peers)])
        for c in range(1, peers)
    ]
    return [pieces[0]] + moved


def body(queries, keys, values, outputs_saved, grad_out, lse, block_lists):
    peers = lax.axis_size("head")
    shards = lax.axis_size("seq")
    me = lax.axis_index("seq")
    head_me = lax.axis_index("head")
    me_ref = head_me.astype(jnp.int32).reshape(1)
    heads = lse.shape[1]
    kv_heads = heads // GROUP
    key_count = peers
    units = key_count * kv_heads

    own_kv = jnp.concatenate(exchange(pack_kv(me_ref, keys, values, peers)), axis=0)

    per_peer = block_lists.reshape(shards, -1)
    requests = per_peer.shape[1]
    order = jnp.arange(requests, dtype=jnp.int32)
    group_of = order % (heads * NSEL) // (NSEL * GROUP)
    block_turn = jnp.where(head_me >= peers // 2, requests // 2, 0)
    capacity = -(-requests // (shards - 1))
    dense = units <= capacity and shards == 8

    if dense:
        far = shards // 2
        swap = [(s, s ^ 1) for s in range(shards)]
        ahead = [(s, (s + 2) % shards) for s in range(shards)]
        back = [(s, (s - 2) % shards) for s in range(shards)]
        mine = lax.dynamic_index_in_dim(per_peer, me, 0, keepdims=False)
        owner = mine // key_count
        apart = (me // 2 - owner // 2) % far
        crossed = (me ^ owner) & 1
        piece = jnp.where(crossed == 1, far - 1 + (apart + 1) % far, apart - 1)
        slots = piece * units + (mine % key_count ^ head_me) * kv_heads + group_of
        slots = jnp.roll(slots, block_turn)
        later_me, own_kv, slots = lax.optimization_barrier((me_ref, own_kv, slots))
        q_pieces = list(pack_q(later_me, queries, grad_out, outputs_saved, peers))
        same1 = lax.ppermute(own_kv, "seq", ahead)
        cross0 = lax.ppermute(own_kv, "seq", swap)
        held, q_pieces[0] = lax.optimization_barrier((own_kv, q_pieces[0]))
        qdo = exchange(q_pieces)
        same3 = lax.ppermute(held, "seq", back)
        cross3 = lax.ppermute(cross0, "seq", back)
        same2 = lax.ppermute(same1, "seq", ahead)
        cross1 = lax.ppermute(same1, "seq", swap)
        held, cross1, qdo[1:] = lax.optimization_barrier((same2, cross1, qdo[1:]))
        cross2 = lax.ppermute(held, "seq", swap)
        kv_pieces = [same1, same2, same3, cross3, cross0, cross1, cross2]
        wide, low = jnp.float32, jnp.bfloat16
        part_types = [wide, wide, low, low, wide, low, low]
    else:
        owner = per_peer // key_count
        earlier = (owner[:, :, None] == owner[:, None, :]) & (order[None, :] < order[:, None])
        position = jnp.sum(earlier.astype(jnp.int32), axis=2)
        slots = lax.dynamic_index_in_dim(owner * capacity + position, me, 0, keepdims=False)
        hits = (owner == me)[:, :, None] & (position[:, :, None] == jnp.arange(capacity))
        hits = hits.astype(jnp.int32)
        used = jnp.sum(hits, axis=1).reshape(-1)
        wanted = (per_peer % key_count ^ head_me) * kv_heads + group_of[None, :]
        wanted = jnp.sum(hits * wanted[:, :, None], axis=1).reshape(-1)
        kv_pieces = [lax.all_to_all(own_kv[wanted], "seq", 0, 0, tiled=True)]
        part_types = [jnp.bfloat16]
        slots = jnp.roll(slots, block_turn)
        qdo = exchange(pack_q(me_ref, queries, grad_out, outputs_saved, peers))

    stats, listed, parts = listed_terms(me_ref, slots, lse.T, qdo, kv_pieces, part_types)
    dq, own = own_terms(me_ref, own_kv, stats, qdo, listed)

    if dense:
        stay1, stay2, away3, leave3, leave0, leave1, leave2 = parts
        came2 = lax.ppermute(leave2, "seq", swap)
        came3 = lax.ppermute(leave3, "seq", ahead)
        came1 = lax.ppermute(leave1, "seq", swap)
        hop = lax.ppermute(add_rounded(stay2, came2), "seq", back)
        away3, came3 = lax.optimization_barrier((away3, came3))
        turned = lax.ppermute(away3, "seq", ahead)
        near, came1 = lax.optimization_barrier((add_rounded(leave0, came3), came1))
        came0 = lax.ppermute(near, "seq", swap)
        hop, dq = lax.optimization_barrier((hop, list(dq)))
        side = add_rounded(stay1, came1, hop)
        arrived = [turned, came0, lax.ppermute(side, "seq", back)]
    else:
        parts = lax.all_to_all(parts[0], "seq", 0, 0, tiled=True)
        chosen = (jnp.arange(units)[:, None] == wanted[None, :]) & (used[None, :] > 0)
        total = jnp.dot(
            chosen.astype(jnp.bfloat16),
            parts.reshape(parts.shape[0], -1),
            preferred_element_type=jnp.float32,
        )
        arrived = [total.reshape(own.shape)]
    dq = exchange(dq)
    dkv = exchange(total_rounded(own, arrived, kv_heads))
    return unpack(me_ref, dq, dkv)


def solution(mesh):
    rows = P(("seq", "head"), None)
    in_specs = (rows, rows, rows, rows, rows, P("seq", "head"), P(None, "head", None))
    return jax.shard_map(
        body, mesh=mesh, in_specs=in_specs, out_specs=(rows, rows, rows), check_vma=False
    )
```

time: 162 us -> 87.8 us (0.54)
  waiting for transfers between devices: 104 us -> 31 us
  starting transfers between devices: 7.08 us -> 38.8 us
  blocking collectives: 18.7 us -> 0 us
  between operations: 14.1 us -> 0.79 us
    reduce_scatter x1 -> x0, waiting for transfers between devices: 62.8 us -> none  [body(): total = lax.psum_scatter(parts, 'seq', scatter_dimension=0, tiled=True)]
    ppermute x0 -> x26, starting transfers between devices: none -> 38.8 us  [the longest x1 11 us: body(): turned = lax.ppermute(away3, 'seq', ahead)]
    ppermute x0 -> x26, waiting for transfers between devices: none -> 31 us  [the longest x12 9.78 us: exchange(): lax.ppermute(pieces[c], 'head', [(h, h ^ c) for h in range(peers)])]
    all_gather x1 -> x0, waiting for transfers between devices: 27.3 us -> none  [body(): kv_slots = lax.all_gather(own_kv, 'seq', axis=0, tiled=True)]
    all_to_all x2 -> x0, blocking collectives: 18.7 us -> none  [the longest x1 10.2 us: body(): own_kv = lax.all_to_all(pack_kv(keys, values), 'head', 0, 0, tiled=True)]
    all_to_all x2 -> x0, waiting for transfers between devices: 14.3 us -> none  [the longest x1 14.3 us: body(): qdo = lax.all_to_all(packed, 'head', 0, 0, tiled=True)]
    all_to_all x2 -> x0, starting transfers between devices: 7 us -> none  [the longest x1 3.52 us: body(): qdo = lax.all_to_all(packed, 'head', 0, 0, tiled=True)]
    pallas_call x4 -> x9, Pallas kernels: 10.7 us -> 11.8 us  [the longest x1 5.69 us: listed_terms(): pl.pallas_call(functools.partial(listed_kernel, peers, pieces), out_shape...]
  transfers between devices with their start and end apart: 4 -> 26, of which waited for: 3 -> 13; matrix products, arithmetic and copies ran while one was open for 1% -> 1% of each run, Pallas kernels for 1% -> 6%
where the time goes in v2:
time: 87.8 us; the launch traced here: 87.5 us
  starting transfers between devices  38.8 us (44%)
  waiting for transfers between devices  31 us (35%)
  Pallas kernels  11.8 us (13%)
  local copies, waits for them, and re-layouts  4.96 us (6%)
    ppermute x1, starting transfers between devices, body(): turned = lax.ppermute(away3, 'seq', ahead)  11 us
    ppermute x12, waiting for transfers between devices, exchange(): lax.ppermute(pieces[c], 'head', [(h, h ^ c) for h in range(peers)])  9.78 us
    ppermute x12, starting transfers between devices, exchange(): lax.ppermute(pieces[c], 'head', [(h, h ^ c) for h in range(peers)])  8.88 us
    ppermute x1, waiting for transfers between devices, body(): came2 = lax.ppermute(leave2, 'seq', swap)  6.34 us
    pallas_call x1, Pallas kernels, listed_terms(): pl.pallas_call(functools.partial(listed_kernel, peers, pieces), out_shape...  5.69 us
    unnamed x13, local copies, waits for them, and re-layouts  4.79 us
    pallas_call x1, Pallas kernels, own_terms(): pl.pallas_call(functools.partial(own_kernel, peers), out_shape=(piece,) *...  3.84 us
    ppermute x1, starting transfers between devices, body(): same3 = lax.ppermute(held, 'seq', back)  3.82 us
  transfers between devices with their start and end apart: 26, of which 13 were waited for; matrix products, arithmetic and copies ran while one was open for 1% of the time, Pallas kernels for 6%

profile of v2, /device:TPU:0, one launch (start us, length us, event | category | flops | bytes accessed | tf_op | source)
XLA Modules:
  0.0 87.5 jit_solution(12076081785766961220)
XLA Ops:
  0.7 1.0 %copy-done.3 = bf16[64,1024]{1,0:T(8,128)(2,1)S(1)} copy-done((bf16[64,1024]{1,0:T(8,128)(2,1)S(1)}, bf16[64,1024]{1,0:T(8,128)(2,1)}, u32[]{:S(2)}) %copy-start.3) | copy-done | bytes 131096
  1.6 0.9 %copy-done.4 = bf16[64,1024]{1,0:T(8,128)(2,1)S(1)} copy-done((bf16[64,1024]{1,0:T(8,128)(2,1)S(1)}, bf16[64,1024]{1,0:T(8,128)(2,1)}, u32[]{:S(2)}) %copy-start.4) | copy-done | bytes 131096
  2.5 0.3 shard_map.94
  2.8 0.5 collective-permute-start
  3.3 2.6 %collective-permute-start.1 = (bf16[2,64,256]{2,1,0:T(8,128)(2,1)S(1)}, bf16[2,64,256]{2,1,0:T(8,128)(2,1)S(1)}, u32[]{:S(2)}, u32[]{:S(2)}) collective-permute-start(bf16[2,64,256]{2,1,0:T(8,128)(2,1)S(1)} %get-tuple-element.53), channel_id=1, source_target_pairs={{0,2},{1,3},{2,0},{3,1},{4,6},{5,7},{6,4},{7,5},{8,10},{9,11},{10,... | collective-permute-start | bytes 196616 | tf_op jit(solution)/shard_map/ppermute | solution.py:343
  5.9 0.1 collective-permute-start.2
  5.9 0.8 copy.10
  6.8 0.1 reshape.13
  6.9 0.1 pad_add_fusion
  7.0 0.1 dynamic_slice.9.slot_ref
  7.1 0.0 collective-permute-done
  7.1 1.5 %collective-permute-done.1 = bf16[2,64,256]{2,1,0:T(8,128)(2,1)S(1)} collective-permute-done((bf16[2,64,256]{2,1,0:T(8,128)(2,1)S(1)}, bf16[2,64,256]{2,1,0:T(8,128)(2,1)S(1)}, u32[]{:S(2)}, u32[]{:S(2)}) %collective-permute-start.1) | collective-permute-done | bytes 65568 | tf_op jit(solution)/shard_map/ppermute | solution.py:343
  8.5 1.4 %collective-permute-done.2 = bf16[2,64,256]{2,1,0:T(8,128)(2,1)S(1)} collective-permute-done((bf16[2,64,256]{2,1,0:T(8,128)(2,1)S(1)}, bf16[2,64,256]{2,1,0:T(8,128)(2,1)S(1)}, u32[]{:S(2)}, u32[]{:S(2)}) %collective-permute-start.2) | collective-permute-done | bytes 65568 | tf_op jit(solution)/shard_map/ppermute | solution.py:343
  9.9 1.6 %collective-permute-start.3 = (bf16[8,64,256]{2,1,0:T(8,128)(2,1)S(1)}, bf16[8,64,256]{2,1,0:T(8,128)(2,1)S(1)}, u32[]{:S(2)}, u32[]{:S(2)}) collective-permute-start(bf16[8,64,256]{2,1,0:T(8,128)(2,1)S(1)} %pad_maximum_fusion.own_kv_ref), channel_id=1, source_target_pairs={{0,8},{4,12},{8,16},{12,20},{16,24},{20,28},{24,0},{28,4},{1,9},{5... | collective-permute-start | bytes 786440 | tf_op jit(solution)/shard_map/ppermute | solution.py:384
  11.6 1.5 %collective-permute-start.10 = (bf16[8,64,256]{2,1,0:T(8,128)(2,1)S(1)}, bf16[8,64,256]{2,1,0:T(8,128)(2,1)S(1)}, u32[]{:S(2)}, u32[]{:S(2)}) collective-permute-start(bf16[8,64,256]{2,1,0:T(8,128)(2,1)S(1)} %pad_maximum_fusion.own_kv_ref), channel_id=1, source_target_pairs={{0,4},{4,0},{8,12},{12,8},{16,20},{20,16},{24,28},{28,24},{1,5},{5... | collective-permute-start | bytes 786440 | tf_op jit(solution)/shard_map/ppermute | solution.py:385
  13.1 1.0 %copy-done.1 = bf16[64,4096]{1,0:T(8,128)(2,1)S(1)} copy-done((bf16[64,4096]{1,0:T(8,128)(2,1)S(1)}, bf16[64,4096]{1,0:T(8,128)(2,1)}, u32[]{:S(2)}) %copy-start.1) | copy-done | bytes 524312
  14.1 1.0 %copy-done.2 = bf16[64,4096]{1,0:T(8,128)(2,1)S(1)} copy-done((bf16[64,4096]{1,0:T(8,128)(2,1)S(1)}, bf16[64,4096]{1,0:T(8,128)(2,1)}, u32[]{:S(2)}) %copy-start.2) | copy-done | bytes 524312
  15.2 0.8 shard_map.95
  15.9 0.0 copy-start.5
  16.0 0.1 collective-permute-start.6
  16.0 1.4 %collective-permute-start.7 = (bf16[528,256]{1,0:T(8,128)(2,1)S(1)}, bf16[528,256]{1,0:T(8,128)(2,1)S(1)}, u32[]{:S(2)}, u32[]{:S(2)}) collective-permute-start(bf16[528,256]{1,0:T(8,128)(2,1)S(1)} %get-tuple-element.61), channel_id=1, source_target_pairs={{0,2},{1,3},{2,0},{3,1},{4,6},{5,7},{6,4},{7,5},{8,10},{9,11},{10,... | collective-permute-start | bytes 811016 | tf_op jit(solution)/shard_map/ppermute | solution.py:343
  17.4 0.5 collective-permute-start.8
  17.9 2.3 %collective-permute-done.3.refs_4_ = bf16[8,64,256]{2,1,0:T(8,128)(2,1)S(1)} collective-permute-done((bf16[8,64,256]{2,1,0:T(8,128)(2,1)S(1)}, bf16[8,64,256]{2,1,0:T(8,128)(2,1)S(1)}, u32[]{:S(2)}, u32[]{:S(2)}) %collective-permute-start.3) | collective-permute-done | bytes 262176 | tf_op jit(solution)/shard_map/ppermute | solution.py:384
  20.2 1.5 %collective-permute-start.5 = (bf16[8,64,256]{2,1,0:T(8,128)(2,1)S(1)}, bf16[8,64,256]{2,1,0:T(8,128)(2,1)S(1)}, u32[]{:S(2)}, u32[]{:S(2)}) collective-permute-start(bf16[8,64,256]{2,1,0:T(8,128)(2,1)S(1)} %collective-permute-done.3.refs_4_), channel_id=1, source_target_pairs={{0,4},{4,0},{8,12},{12,8},{16,20},{20,16},{24,28},{28,24},{1,5},{5... | collective-permute-start | bytes 786440 | tf_op jit(solution)/shard_map/ppermute | solution.py:391
  21.8 0.0 collective-permute-done.10.refs_8_
  21.8 0.0 collective-permute-start.4
  21.8 0.0 collective-permute-done.6.refs_1_
  21.8 3.8 %collective-permute-start.9 = (bf16[8,64,256]{2,1,0:T(8,128)(2,1)S(1)}, bf16[8,64,256]{2,1,0:T(8,128)(2,1)S(1)}, u32[]{:S(2)}, u32[]{:S(2)}) collective-permute-start(bf16[8,64,256]{2,1,0:T(8,128)(2,1)S(1)} %pad_maximum_fusion.own_kv_ref), channel_id=1, source_target_pairs={{0,24},{4,28},{8,0},{12,4},{16,8},{20,12},{24,16},{28,20},{1,25},{... | collective-permute-start | bytes 786440 | tf_op jit(solution)/shard_map/ppermute | solution.py:388
  25.6 0.0 collective-permute-done.7.refs_2_
  25.6 2.0 %collective-permute-start.11 = (bf16[8,64,256]{2,1,0:T(8,128)(2,1)S(1)}, bf16[8,64,256]{2,1,0:T(8,128)(2,1)S(1)}, u32[]{:S(2)}, u32[]{:S(2)}) collective-permute-start(bf16[8,64,256]{2,1,0:T(8,128)(2,1)S(1)} %collective-permute-done.10.refs_8_), channel_id=1, source_target_pairs={{0,24},{4,28},{8,0},{12,4},{16,8},{20,12},{24,16},{28,20},{1,25},{... | collective-permute-start | bytes 786440 | tf_op jit(solution)/shard_map/ppermute | solution.py:389
  27.6 2.6 %collective-permute-done.8.refs_3_ = bf16[528,256]{1,0:T(8,128)(2,1)S(1)} collective-permute-done((bf16[528,256]{1,0:T(8,128)(2,1)S(1)}, bf16[528,256]{1,0:T(8,128)(2,1)S(1)}, u32[]{:S(2)}, u32[]{:S(2)}) %collective-permute-start.8) | collective-permute-done | bytes 270368 | tf_op jit(solution)/shard_map/ppermute | solution.py:343
  30.3 0.0 collective-permute-done.5.refs_9_
  30.3 2.5 %collective-permute-done.4.refs_5_ = bf16[8,64,256]{2,1,0:T(8,128)(2,1)S(1)} collective-permute-done((bf16[8,64,256]{2,1,0:T(8,128)(2,1)S(1)}, bf16[8,64,256]{2,1,0:T(8,128)(2,1)S(1)}, u32[]{:S(2)}, u32[]{:S(2)}) %collective-permute-start.4) | collective-permute-done | bytes 262176 | tf_op jit(solution)/shard_map/ppermute | solution.py:390
  32.8 0.5 collective-permute-start.12
  33.3 3.4 %collective-permute-done.9.refs_6_ = bf16[8,64,256]{2,1,0:T(8,128)(2,1)S(1)} collective-permute-done((bf16[8,64,256]{2,1,0:T(8,128)(2,1)S(1)}, bf16[8,64,256]{2,1,0:T(8,128)(2,1)S(1)}, u32[]{:S(2)}, u32[]{:S(2)}) %collective-permute-start.9) | collective-permute-done | bytes 262176 | tf_op jit(solution)/shard_map/ppermute | solution.py:388
  36.7 3.7 %collective-permute-done.11.refs_7_ = bf16[8,64,256]{2,1,0:T(8,128)(2,1)S(1)} collective-permute-done((bf16[8,64,256]{2,1,0:T(8,128)(2,1)S(1)}, bf16[8,64,256]{2,1,0:T(8,128)(2,1)S(1)}, u32[]{:S(2)}, u32[]{:S(2)}) %collective-permute-start.11) | collective-permute-done | bytes 262176 | tf_op jit(solution)/shard_map/ppermute | solution.py:389
  40.4 0.0 collective-permute-done.12.refs_10_
  40.4 5.7 %shard_map.96 = (f32[2,8,256]{2,1,0:T(8,128)S(1)}, f32[64,1024]{1,0:T(8,128)S(1)}, f32[64,1024]{1,0:T(8,128)S(1)}, f32[64,1024]{1,0:T(8,128)S(1)}, f32[64,1024]{...) custom-call(s32[1]{0:T(128)} %bitcast.me_ref, ...), custom_call_target="tpu_custom_call" | custom-call | flops 671000000 | bytes 8000000 | tf_op jit(solution)/shard_map/pallas_call | solution.py:246
  46.1 0.6 collective-permute-start.13
  46.7 1.6 %collective-permute-start.18 = (bf16[8,64,256]{2,1,0:T(8,128)(2,1)S(1)}, bf16[8,64,256]{2,1,0:T(8,128)(2,1)S(1)}, u32[]{:S(2)}, u32[]{:S(2)}) collective-permute-start(bf16[8,64,256]{2,1,0:T(8,128)(2,1)S(1)} %get-tuple-element.86), channel_id=1, source_target_pairs={{0,8},{4,12},{8,16},{12,20},{16,24},{20,28},{24,0},{28,4},{1,9},{5... | collective-permute-start | bytes 786440 | tf_op jit(solution)/shard_map/ppermute | solution.py:418
  48.3 0.8 collective-permute-start.20
  49.1 6.3 %collective-permute-done.13.refs_1_ = bf16[8,64,256]{2,1,0:T(8,128)(2,1)S(1)} collective-permute-done((bf16[8,64,256]{2,1,0:T(8,128)(2,1)S(1)}, bf16[8,64,256]{2,1,0:T(8,128)(2,1)S(1)}, u32[]{:S(2)}, u32[]{:S(2)}) %collective-permute-start.13) | collective-permute-done | bytes 262176 | tf_op jit(solution)/shard_map/ppermute | solution.py:417
  55.5 2.1 %collective-permute-start.14 = (bf16[8,64,256]{2,1,0:T(8,128)(2,1)S(1)}, bf16[8,64,256]{2,1,0:T(8,128)(2,1)S(1)}, u32[]{:S(2)}, u32[]{:S(2)}) collective-permute-start(bf16[8,64,256]{2,1,0:T(8,128)(2,1)S(1)} %shard_map.97), channel_id=1, source_target_pairs={{0,24},{4,28},{8,0},{12,4},{16,8},{20,12},{24,16},{28,20},{1,25},{... | collective-permute-start | bytes 786440 | tf_op jit(solution)/shard_map/ppermute | solution.py:420
  57.5 0.0 collective-permute-done.18.refs_1_
  57.5 11.0 %collective-permute-start.19 = (bf16[8,64,256]{2,1,0:T(8,128)(2,1)S(1)}, bf16[8,64,256]{2,1,0:T(8,128)(2,1)S(1)}, u32[]{:S(2)}, u32[]{:S(2)}) collective-permute-start(bf16[8,64,256]{2,1,0:T(8,128)(2,1)S(1)} %get-tuple-element.87), channel_id=1, source_target_pairs={{0,8},{4,12},{8,16},{12,20},{16,24},{20,28},{24,0},{28,4},{1,9},{5... | collective-permute-start | bytes 786440 | tf_op jit(solution)/shard_map/ppermute | solution.py:422
  68.6 3.8 %shard_map.98 = (bf16[64,1024]{1,0:T(8,128)(2,1)S(1)}, bf16[64,1024]{1,0:T(8,128)(2,1)S(1)}, bf16[64,1024]{1,0:T(8,128)(2,1)S(1)}, bf16[64,1024]{1,0:T(8,128)(2,1)S(1)}, f32[8,64,256]{2,1,0:T(8,128)S(1)}) custom-call(s32[1]{0:T(128)} %bitcast.me_ref, bf16[8,64,256]{2,1,0:T(8,128)(2,1)S(1)} %pad_maximum_fusion.own_kv_ref, ...), custom_call_target="tpu_custom_call" | custom-call | flops 335000000 | bytes 4000000 | tf_op jit(solution)/shard_map/pallas_call | solution.py:169
  72.5 0.7 collective-permute-start.21
  73.2 0.1 shard_map.100
  73.3 2.1 %collective-permute-start.22 = (bf16[8,64,256]{2,1,0:T(8,128)(2,1)S(1)}, bf16[8,64,256]{2,1,0:T(8,128)(2,1)S(1)}, u32[]{:S(2)}, u32[]{:S(2)}) collective-permute-start(bf16[8,64,256]{2,1,0:T(8,128)(2,1)S(1)} %shard_map.100), channel_id=1, source_target_pairs={{0,24},{4,28},{8,0},{12,4},{16,8},{20,12},{24,16},{28,20},{1,25},{... | collective-permute-start | bytes 786440 | tf_op jit(solution)/shard_map/ppermute | solution.py:427
  75.4 1.4 %collective-permute-start.16 = (bf16[64,1024]{1,0:T(8,128)(2,1)S(1)}, bf16[64,1024]{1,0:T(8,128)(2,1)S(1)}, u32[]{:S(2)}, u32[]{:S(2)}) collective-permute-start(bf16[64,1024]{1,0:T(8,128)(2,1)S(1)} %get-tuple-element.82), channel_id=1, source_target_pairs={{0,2},{1,3},{2,0},{3,1},{4,6},{5,7},{6,4},{7,5},{8,10},{9,11},{10,... | collective-permute-start | bytes 393224 | tf_op jit(solution)/shard_map/ppermute | solution.py:343
  76.8 0.5 collective-permute-start.17
  77.3 1.7 %collective-permute-done.21.refs_1_ = bf16[8,64,256]{2,1,0:T(8,128)(2,1)S(1)} collective-permute-done((bf16[8,64,256]{2,1,0:T(8,128)(2,1)S(1)}, bf16[8,64,256]{2,1,0:T(8,128)(2,1)S(1)}, u32[]{:S(2)}, u32[]{:S(2)}) %collective-permute-start.21) | collective-permute-done | bytes 262176 | tf_op jit(solution)/shard_map/ppermute | solution.py:424
  78.9 1.2 %collective-permute-done.22.refs_2_ = bf16[8,64,256]{2,1,0:T(8,128)(2,1)S(1)} collective-permute-done((bf16[8,64,256]{2,1,0:T(8,128)(2,1)S(1)}, bf16[8,64,256]{2,1,0:T(8,128)(2,1)S(1)}, u32[]{:S(2)}, u32[]{:S(2)}) %collective-permute-start.22) | collective-permute-done | bytes 262176 | tf_op jit(solution)/shard_map/ppermute | solution.py:427
  80.1 0.1 shard_map.101
  80.3 0.1 collective-permute-start.23
  80.4 1.4 %collective-permute-start.24 = (bf16[2,64,256]{2,1,0:T(8,128)(2,1)S(1)}, bf16[2,64,256]{2,1,0:T(8,128)(2,1)S(1)}, u32[]{:S(2)}, u32[]{:S(2)}) collective-permute-start(bf16[2,64,256]{2,1,0:T(8,128)(2,1)S(1)} %get-tuple-element.97), channel_id=1, source_target_pairs={{0,2},{1,3},{2,0},{3,1},{4,6},{5,7},{6,4},{7,5},{8,10},{9,11},{10,... | collective-permute-start | bytes 196616 | tf_op jit(solution)/shard_map/ppermute | solution.py:343
  81.8 0.0 collective-permute-done.15.refs_1_
  81.8 0.5 collective-permute-start.25
  82.2 0.0 collective-permute-done.16.refs_2_
  82.2 1.5 %collective-permute-done.17.refs_3_ = bf16[64,1024]{1,0:T(8,128)(2,1)S(1)} collective-permute-done((bf16[64,1024]{1,0:T(8,128)(2,1)S(1)}, bf16[64,1024]{1,0:T(8,128)(2,1)S(1)}, u32[]{:S(2)}, u32[]{:S(2)}) %collective-permute-start.17) | collective-permute-done | bytes 131104 | tf_op jit(solution)/shard_map/ppermute | solution.py:343
  83.7 0.0 collective-permute-done.23.refs_5_
  83.7 2.2 %collective-permute-done.24.refs_6_ = bf16[2,64,256]{2,1,0:T(8,128)(2,1)S(1)} collective-permute-done((bf16[2,64,256]{2,1,0:T(8,128)(2,1)S(1)}, bf16[2,64,256]{2,1,0:T(8,128)(2,1)S(1)}, u32[]{:S(2)}, u32[]{:S(2)}) %collective-permute-start.24) | collective-permute-done | bytes 65568 | tf_op jit(solution)/shard_map/ppermute | solution.py:343
  85.9 0.6 collective-permute-done.25.refs_7_
  86.5 1.0 %shard_map.102 = (bf16[64,4096]{1,0:T(8,128)(2,1)}, bf16[64,1024]{1,0:T(8,128)(2,1)}, bf16[64,1024]{1,0:T(8,128)(2,1)}) custom-call(s32[1]{0:T(128)} %bitcast.me_ref, bf16[64,1024]{1,0:T(8,128)(2,1)S(1)} %get-tuple-element.80.refs_0_, bf16[64,1024]{1,0:T(8,128)(2,1)S(1)} %collective-permute-done.15.refs_1_, ...), custom_call_target="tpu_custom_call" | custom-call | tf_op jit(solution)/shard_map/pallas_call | solution.py:327
  (15 shorter events, 0.2 us)
Async XLA Ops:
  0.6 12.5 %copy-start = (bf16[64,4096]{1,0:T(8,128)(2,1)S(1)}, bf16[64,4096]{1,0:T(8,128)(2,1)}, u32[]{:S(2)}) copy-start(bf16[64,4096]{1,0:T(8,128)(2,1)} %q_any.1) | copy-start | bytes 1572868
  0.6 1.0 %copy-start.3 = (bf16[64,1024]{1,0:T(8,128)(2,1)S(1)}, bf16[64,1024]{1,0:T(8,128)(2,1)}, u32[]{:S(2)}) copy-start(bf16[64,1024]{1,0:T(8,128)(2,1)} %k_ref.1) | copy-start | bytes 393220
  1.6 0.9 %copy-start.4 = (bf16[64,1024]{1,0:T(8,128)(2,1)S(1)}, bf16[64,1024]{1,0:T(8,128)(2,1)}, u32[]{:S(2)}) copy-start(bf16[64,1024]{1,0:T(8,128)(2,1)} %v_ref.1) | copy-start | bytes 393220
  2.8 4.3 %collective-permute-start = (bf16[2,64,256]{2,1,0:T(8,128)(2,1)S(1)}, bf16[2,64,256]{2,1,0:T(8,128)(2,1)S(1)}, u32[]{:S(2)}, u32[]{:S(2)}) collective-permute-start(bf16[2,64,256]{2,1,0:T(8,128)(2,1)S(1)} %get-tuple-element.52), channel_id=1, source_target_pairs={{0,1},{1,0},{2,3},{3,2},{4,5},{5,4},{6,7},{7,6},{8,9},{9,8},{10,11... | collective-permute-start | bytes 196616 | tf_op jit(solution)/shard_map/ppermute | solution.py:343
  3.3 5.3 %collective-permute-start.1 = (bf16[2,64,256]{2,1,0:T(8,128)(2,1)S(1)}, bf16[2,64,256]{2,1,0:T(8,128)(2,1)S(1)}, u32[]{:S(2)}, u32[]{:S(2)}) collective-permute-start(bf16[2,64,256]{2,1,0:T(8,128)(2,1)S(1)} %get-tuple-element.53), channel_id=1, source_target_pairs={{0,2},{1,3},{2,0},{3,1},{4,6},{5,7},{6,4},{7,5},{8,10},{9,11},{10,... | collective-permute-start | bytes 196616 | tf_op jit(solution)/shard_map/ppermute | solution.py:343
  5.9 4.0 %collective-permute-start.2 = (bf16[2,64,256]{2,1,0:T(8,128)(2,1)S(1)}, bf16[2,64,256]{2,1,0:T(8,128)(2,1)S(1)}, u32[]{:S(2)}, u32[]{:S(2)}) collective-permute-start(bf16[2,64,256]{2,1,0:T(8,128)(2,1)S(1)} %get-tuple-element.54), channel_id=1, source_target_pairs={{0,3},{1,2},{2,1},{3,0},{4,7},{5,6},{6,5},{7,4},{8,11},{9,10},{10,... | collective-permute-start | bytes 196616 | tf_op jit(solution)/shard_map/ppermute | solution.py:343
  9.9 10.3 %collective-permute-start.3 = (bf16[8,64,256]{2,1,0:T(8,128)(2,1)S(1)}, bf16[8,64,256]{2,1,0:T(8,128)(2,1)S(1)}, u32[]{:S(2)}, u32[]{:S(2)}) collective-permute-start(bf16[8,64,256]{2,1,0:T(8,128)(2,1)S(1)} %pad_maximum_fusion.own_kv_ref), channel_id=1, source_target_pairs={{0,8},{4,12},{8,16},{12,20},{16,24},{20,28},{24,0},{28,4},{1,9},{5... | collective-permute-start | bytes 786440 | tf_op jit(solution)/shard_map/ppermute | solution.py:384
  11.6 10.2 %collective-permute-start.10 = (bf16[8,64,256]{2,1,0:T(8,128)(2,1)S(1)}, bf16[8,64,256]{2,1,0:T(8,128)(2,1)S(1)}, u32[]{:S(2)}, u32[]{:S(2)}) collective-permute-start(bf16[8,64,256]{2,1,0:T(8,128)(2,1)S(1)} %pad_maximum_fusion.own_kv_ref), channel_id=1, source_target_pairs={{0,4},{4,0},{8,12},{12,8},{16,20},{20,16},{24,28},{28,24},{1,5},{5... | collective-permute-start | bytes 786440 | tf_op jit(solution)/shard_map/ppermute | solution.py:385
  13.1 1.0 %copy-start.1 = (bf16[64,4096]{1,0:T(8,128)(2,1)S(1)}, bf16[64,4096]{1,0:T(8,128)(2,1)}, u32[]{:S(2)}) copy-start(bf16[64,4096]{1,0:T(8,128)(2,1)} %do_any.1) | copy-start | bytes 1572868
  14.1 1.0 %copy-start.2 = (bf16[64,4096]{1,0:T(8,128)(2,1)S(1)}, bf16[64,4096]{1,0:T(8,128)(2,1)}, u32[]{:S(2)}) copy-start(bf16[64,4096]{1,0:T(8,128)(2,1)} %o_any.1) | copy-start | bytes 1572868
  15.9 24.5 %copy-start.5 = (f32[256,8]{0,1:T(8,128)S(1)}, f32[256,8]{0,1:T(8,128)}, u32[]{:S(2)}) copy-start(f32[256,8]{0,1:T(8,128)} %param.12) | copy-start | bytes 24580
  16.0 5.8 %collective-permute-start.6 = (bf16[528,256]{1,0:T(8,128)(2,1)S(1)}, bf16[528,256]{1,0:T(8,128)(2,1)S(1)}, u32[]{:S(2)}, u32[]{:S(2)}) collective-permute-start(bf16[528,256]{1,0:T(8,128)(2,1)S(1)} %get-tuple-element.60), channel_id=1, source_target_pairs={{0,1},{1,0},{2,3},{3,2},{4,5},{5,4},{6,7},{7,6},{8,9},{9,8},{10,11... | collective-permute-start | bytes 811016 | tf_op jit(solution)/shard_map/ppermute | solution.py:343
  16.0 9.6 %collective-permute-start.7 = (bf16[528,256]{1,0:T(8,128)(2,1)S(1)}, bf16[528,256]{1,0:T(8,128)(2,1)S(1)}, u32[]{:S(2)}, u32[]{:S(2)}) collective-permute-start(bf16[528,256]{1,0:T(8,128)(2,1)S(1)} %get-tuple-element.61), channel_id=1, source_target_pairs={{0,2},{1,3},{2,0},{3,1},{4,6},{5,7},{6,4},{7,5},{8,10},{9,11},{10,... | collective-permute-start | bytes 811016 | tf_op jit(solution)/shard_map/ppermute | solution.py:343
  17.4 12.8 %collective-permute-start.8 = (bf16[528,256]{1,0:T(8,128)(2,1)S(1)}, bf16[528,256]{1,0:T(8,128)(2,1)S(1)}, u32[]{:S(2)}, u32[]{:S(2)}) collective-permute-start(bf16[528,256]{1,0:T(8,128)(2,1)S(1)} %get-tuple-element.62), channel_id=1, source_target_pairs={{0,3},{1,2},{2,1},{3,0},{4,7},{5,6},{6,5},{7,4},{8,11},{9,10},{10,... | collective-permute-start | bytes 811016 | tf_op jit(solution)/shard_map/ppermute | solution.py:343
  20.2 10.0 %collective-permute-start.5 = (bf16[8,64,256]{2,1,0:T(8,128)(2,1)S(1)}, bf16[8,64,256]{2,1,0:T(8,128)(2,1)S(1)}, u32[]{:S(2)}, u32[]{:S(2)}) collective-permute-start(bf16[8,64,256]{2,1,0:T(8,128)(2,1)S(1)} %collective-permute-done.3.refs_4_), channel_id=1, source_target_pairs={{0,4},{4,0},{8,12},{12,8},{16,20},{20,16},{24,28},{28,24},{1,5},{5... | collective-permute-start | bytes 786440 | tf_op jit(solution)/shard_map/ppermute | solution.py:391
  21.8 11.0 %collective-permute-start.4 = (bf16[8,64,256]{2,1,0:T(8,128)(2,1)S(1)}, bf16[8,64,256]{2,1,0:T(8,128)(2,1)S(1)}, u32[]{:S(2)}, u32[]{:S(2)}) collective-permute-start(bf16[8,64,256]{2,1,0:T(8,128)(2,1)S(1)} %collective-permute-done.3.refs_4_), channel_id=1, source_target_pairs={{0,8},{4,12},{8,16},{12,20},{16,24},{20,28},{24,0},{28,4},{1,9},{5... | collective-permute-start | bytes 786440 | tf_op jit(solution)/shard_map/ppermute | solution.py:390
  21.8 14.9 %collective-permute-start.9 = (bf16[8,64,256]{2,1,0:T(8,128)(2,1)S(1)}, bf16[8,64,256]{2,1,0:T(8,128)(2,1)S(1)}, u32[]{:S(2)}, u32[]{:S(2)}) collective-permute-start(bf16[8,64,256]{2,1,0:T(8,128)(2,1)S(1)} %pad_maximum_fusion.own_kv_ref), channel_id=1, source_target_pairs={{0,24},{4,28},{8,0},{12,4},{16,8},{20,12},{24,16},{28,20},{1,25},{... | collective-permute-start | bytes 786440 | tf_op jit(solution)/shard_map/ppermute | solution.py:388
  25.6 14.8 %collective-permute-start.11 = (bf16[8,64,256]{2,1,0:T(8,128)(2,1)S(1)}, bf16[8,64,256]{2,1,0:T(8,128)(2,1)S(1)}, u32[]{:S(2)}, u32[]{:S(2)}) collective-permute-start(bf16[8,64,256]{2,1,0:T(8,128)(2,1)S(1)} %collective-permute-done.10.refs_8_), channel_id=1, source_target_pairs={{0,24},{4,28},{8,0},{12,4},{16,8},{20,12},{24,16},{28,20},{1,25},{... | collective-permute-start | bytes 786440 | tf_op jit(solution)/shard_map/ppermute | solution.py:389
  32.8 7.6 %collective-permute-start.12 = (bf16[8,64,256]{2,1,0:T(8,128)(2,1)S(1)}, bf16[8,64,256]{2,1,0:T(8,128)(2,1)S(1)}, u32[]{:S(2)}, u32[]{:S(2)}) collective-permute-start(bf16[8,64,256]{2,1,0:T(8,128)(2,1)S(1)} %collective-permute-done.4.refs_5_), channel_id=1, source_target_pairs={{0,4},{4,0},{8,12},{12,8},{16,20},{20,16},{24,28},{28,24},{1,5},{5... | collective-permute-start | bytes 786440 | tf_op jit(solution)/shard_map/ppermute | solution.py:393
  46.1 9.3 %collective-permute-start.13 = (bf16[8,64,256]{2,1,0:T(8,128)(2,1)S(1)}, bf16[8,64,256]{2,1,0:T(8,128)(2,1)S(1)}, u32[]{:S(2)}, u32[]{:S(2)}) collective-permute-start(bf16[8,64,256]{2,1,0:T(8,128)(2,1)S(1)} %get-tuple-element.70), channel_id=1, source_target_pairs={{0,4},{4,0},{8,12},{12,8},{16,20},{20,16},{24,28},{28,24},{1,5},{5... | collective-permute-start | bytes 786440 | tf_op jit(solution)/shard_map/ppermute | solution.py:417
  46.7 10.8 %collective-permute-start.18 = (bf16[8,64,256]{2,1,0:T(8,128)(2,1)S(1)}, bf16[8,64,256]{2,1,0:T(8,128)(2,1)S(1)}, u32[]{:S(2)}, u32[]{:S(2)}) collective-permute-start(bf16[8,64,256]{2,1,0:T(8,128)(2,1)S(1)} %get-tuple-element.86), channel_id=1, source_target_pairs={{0,8},{4,12},{8,16},{12,20},{16,24},{20,28},{24,0},{28,4},{1,9},{5... | collective-permute-start | bytes 786440 | tf_op jit(solution)/shard_map/ppermute | solution.py:418
  48.3 24.2 %collective-permute-start.20 = (bf16[8,64,256]{2,1,0:T(8,128)(2,1)S(1)}, bf16[8,64,256]{2,1,0:T(8,128)(2,1)S(1)}, u32[]{:S(2)}, u32[]{:S(2)}) collective-permute-start(bf16[8,64,256]{2,1,0:T(8,128)(2,1)S(1)} %get-tuple-element.90), channel_id=1, source_target_pairs={{0,4},{4,0},{8,12},{12,8},{16,20},{20,16},{24,28},{28,24},{1,5},{5... | collective-permute-start | bytes 786440 | tf_op jit(solution)/shard_map/ppermute | solution.py:419
  55.5 17.7 %collective-permute-start.14 = (bf16[8,64,256]{2,1,0:T(8,128)(2,1)S(1)}, bf16[8,64,256]{2,1,0:T(8,128)(2,1)S(1)}, u32[]{:S(2)}, u32[]{:S(2)}) collective-permute-start(bf16[8,64,256]{2,1,0:T(8,128)(2,1)S(1)} %shard_map.97), channel_id=1, source_target_pairs={{0,24},{4,28},{8,0},{12,4},{16,8},{20,12},{24,16},{28,20},{1,25},{... | collective-permute-start | bytes 786440 | tf_op jit(solution)/shard_map/ppermute | solution.py:420
  57.5 19.3 %collective-permute-start.19 = (bf16[8,64,256]{2,1,0:T(8,128)(2,1)S(1)}, bf16[8,64,256]{2,1,0:T(8,128)(2,1)S(1)}, u32[]{:S(2)}, u32[]{:S(2)}) collective-permute-start(bf16[8,64,256]{2,1,0:T(8,128)(2,1)S(1)} %get-tuple-element.87), channel_id=1, source_target_pairs={{0,8},{4,12},{8,16},{12,20},{16,24},{20,28},{24,0},{28,4},{1,9},{5... | collective-permute-start | bytes 786440 | tf_op jit(solution)/shard_map/ppermute | solution.py:422
  72.5 6.4 %collective-permute-start.21 = (bf16[8,64,256]{2,1,0:T(8,128)(2,1)S(1)}, bf16[8,64,256]{2,1,0:T(8,128)(2,1)S(1)}, u32[]{:S(2)}, u32[]{:S(2)}) collective-permute-start(bf16[8,64,256]{2,1,0:T(8,128)(2,1)S(1)} %shard_map.99), channel_id=1, source_target_pairs={{0,4},{4,0},{8,12},{12,8},{16,20},{20,16},{24,28},{28,24},{1,5},{5... | collective-permute-start | bytes 786440 | tf_op jit(solution)/shard_map/ppermute | solution.py:424
  73.3 6.9 %collective-permute-start.22 = (bf16[8,64,256]{2,1,0:T(8,128)(2,1)S(1)}, bf16[8,64,256]{2,1,0:T(8,128)(2,1)S(1)}, u32[]{:S(2)}, u32[]{:S(2)}) collective-permute-start(bf16[8,64,256]{2,1,0:T(8,128)(2,1)S(1)} %shard_map.100), channel_id=1, source_target_pairs={{0,24},{4,28},{8,0},{12,4},{16,8},{20,12},{24,16},{28,20},{1,25},{... | collective-permute-start | bytes 786440 | tf_op jit(solution)/shard_map/ppermute | solution.py:427
  75.4 6.4 %collective-permute-start.15 = (bf16[64,1024]{1,0:T(8,128)(2,1)S(1)}, bf16[64,1024]{1,0:T(8,128)(2,1)S(1)}, u32[]{:S(2)}, u32[]{:S(2)}) collective-permute-start(bf16[64,1024]{1,0:T(8,128)(2,1)S(1)} %get-tuple-element.81), channel_id=1, source_target_pairs={{0,1},{1,0},{2,3},{3,2},{4,5},{5,4},{6,7},{7,6},{8,9},{9,8},{10,11... | collective-permute-start | bytes 393224 | tf_op jit(solution)/shard_map/ppermute | solution.py:343
  75.4 6.8 %collective-permute-start.16 = (bf16[64,1024]{1,0:T(8,128)(2,1)S(1)}, bf16[64,1024]{1,0:T(8,128)(2,1)S(1)}, u32[]{:S(2)}, u32[]{:S(2)}) collective-permute-start(bf16[64,1024]{1,0:T(8,128)(2,1)S(1)} %get-tuple-element.82), channel_id=1, source_target_pairs={{0,2},{1,3},{2,0},{3,1},{4,6},{5,7},{6,4},{7,5},{8,10},{9,11},{10,... | collective-permute-start | bytes 393224 | tf_op jit(solution)/shard_map/ppermute | solution.py:343
  76.8 6.9 %collective-permute-start.17 = (bf16[64,1024]{1,0:T(8,128)(2,1)S(1)}, bf16[64,1024]{1,0:T(8,128)(2,1)S(1)}, u32[]{:S(2)}, u32[]{:S(2)}) collective-permute-start(bf16[64,1024]{1,0:T(8,128)(2,1)S(1)} %get-tuple-element.83), channel_id=1, source_target_pairs={{0,3},{1,2},{2,1},{3,0},{4,7},{5,6},{6,5},{7,4},{8,11},{9,10},{10,... | collective-permute-start | bytes 393224 | tf_op jit(solution)/shard_map/ppermute | solution.py:343
  80.3 3.5 %collective-permute-start.23 = (bf16[2,64,256]{2,1,0:T(8,128)(2,1)S(1)}, bf16[2,64,256]{2,1,0:T(8,128)(2,1)S(1)}, u32[]{:S(2)}, u32[]{:S(2)}) collective-permute-start(bf16[2,64,256]{2,1,0:T(8,128)(2,1)S(1)} %get-tuple-element.96), channel_id=1, source_target_pairs={{0,1},{1,0},{2,3},{3,2},{4,5},{5,4},{6,7},{7,6},{8,9},{9,8},{10,11... | collective-permute-start | bytes 196616 | tf_op jit(solution)/shard_map/ppermute | solution.py:343
  80.4 5.5 %collective-permute-start.24 = (bf16[2,64,256]{2,1,0:T(8,128)(2,1)S(1)}, bf16[2,64,256]{2,1,0:T(8,128)(2,1)S(1)}, u32[]{:S(2)}, u32[]{:S(2)}) collective-permute-start(bf16[2,64,256]{2,1,0:T(8,128)(2,1)S(1)} %get-tuple-element.97), channel_id=1, source_target_pairs={{0,2},{1,3},{2,0},{3,1},{4,6},{5,7},{6,4},{7,5},{8,10},{9,11},{10,... | collective-permute-start | bytes 196616 | tf_op jit(solution)/shard_map/ppermute | solution.py:343
  81.8 4.8 %collective-permute-start.25 = (bf16[2,64,256]{2,1,0:T(8,128)(2,1)S(1)}, bf16[2,64,256]{2,1,0:T(8,128)(2,1)S(1)}, u32[]{:S(2)}, u32[]{:S(2)}) collective-permute-start(bf16[2,64,256]{2,1,0:T(8,128)(2,1)S(1)} %get-tuple-element.98), channel_id=1, source_target_pairs={{0,3},{1,2},{2,1},{3,0},{4,7},{5,6},{6,5},{7,4},{8,11},{9,10},{10,... | collective-permute-start | bytes 196616 | tf_op jit(solution)/shard_map/ppermute | solution.py:343

commit v3 on v2

--- a/solution.py
+++ b/solution.py
@@ -78,8 +78,10 @@
 
 
 def pack_q_kernel(peers, me_ref, q_any, do_any, o_any, *refs):
-    out_refs = refs[:peers]
-    q_ref, do_ref, o_ref, sems = refs[peers:]
+    half = peers // 2
+    rows = refs[0].shape[0]
+    out_refs = refs[:half] + tuple(refs[half].at[i * rows : (i + 1) * rows] for i in range(half))
+    q_ref, do_ref, o_ref, sems = refs[half + 1 :]
     for copy in run_copies([(q_any, q_ref), (do_any, do_ref), (o_any, o_ref)], sems):
         copy.wait()
     heads = (out_refs[0].shape[0] - STAT) // KB
@@ -107,12 +109,15 @@
 def pack_q(me, queries, grad_out, outputs_saved, peers):
     tokens, width = queries.shape
     heads = width // HD // peers
-    piece = jax.ShapeDtypeStruct((heads * tokens + STAT, 2 * HD), jnp.bfloat16)
+    half = peers // 2
+    rows = heads * tokens + STAT
+    piece = jax.ShapeDtypeStruct((rows, 2 * HD), jnp.bfloat16)
+    far = jax.ShapeDtypeStruct((half * rows, 2 * HD), jnp.bfloat16)
     return pl.pallas_call(
         functools.partial(pack_q_kernel, peers),
-        out_shape=(piece,) * peers,
+        out_shape=(piece,) * half + (far,),
         in_specs=[SMEM] + [HBM] * 3,
-        out_specs=(VMEM,) * peers,
+        out_specs=(VMEM,) * (half + 1),
         scratch_shapes=[pltpu.VMEM(queries.shape, jnp.bfloat16)] * 3
         + [pltpu.SemaphoreType.DMA((3,))],
         compiler_params=PARAMS,
@@ -283,32 +288,32 @@
     )(*terms)
 
 
-def total_kernel(kv_heads, own_ref, *refs):
-    peers = own_ref.shape[0] // kv_heads
-    arrived, out_refs = refs[:-peers], refs[-peers:]
+def add_blocks_kernel(terms, *refs):
+    term_refs, out_refs = refs[:terms], refs[terms:]
     for c, out_ref in enumerate(out_refs):
-        part = slice(c * kv_heads, (c + 1) * kv_heads)
-        total = own_ref[part]
-        for ref in arrived:
+        size = out_ref.shape[0]
+        part = slice(c * size, (c + 1) * size)
+        total = term_refs[0][part].astype(jnp.float32)
+        for ref in term_refs[1:]:
             total = total + ref[part].astype(jnp.float32)
-        out_ref[...] = total.astype(jnp.bfloat16)
-
-
-def total_rounded(own, arrived, kv_heads):
-    peers = own.shape[0] // kv_heads
-    piece = jax.ShapeDtypeStruct((kv_heads,) + own.shape[1:], jnp.bfloat16)
+        out_ref[...] = total.astype(out_ref.dtype)
+
+
+def add_blocks(kv_heads, *terms):
+    peers = terms[0].shape[0] // kv_heads
+    piece = jax.ShapeDtypeStruct((kv_heads,) + terms[0].shape[1:], jnp.bfloat16)
     return pl.pallas_call(
-        functools.partial(total_kernel, kv_heads),
+        functools.partial(add_blocks_kernel, len(terms)),
         out_shape=(piece,) * peers,
-        in_specs=[VMEM] * (1 + len(arrived)),
+        in_specs=[VMEM] * len(terms),
         out_specs=(VMEM,) * peers,
         compiler_params=PARAMS,
-    )(own, *arrived)
-
-
-def unpack_kernel(peers, me_ref, *refs):
-    dq_refs, dkv_refs = refs[:peers], refs[peers : 2 * peers]
-    gq_ref, gk_ref, gv_ref = refs[2 * peers :]
+    )(*terms)
+
+
+def unpack_kernel(peers, sets, me_ref, *refs):
+    dq_refs, dkv_refs = refs[:peers], refs[peers : peers * (1 + sets)]
+    gq_ref, gk_ref, gv_ref = refs[peers * (1 + sets) :]
     width = dq_refs[0].shape[1]
     kv_heads = dkv_refs[0].shape[0]
     for c in range(peers):
@@ -316,25 +321,30 @@
         gq_ref[:, lanes(source, width)] = dq_refs[c][...]
         for g in range(kv_heads):
             cols = lanes(source * kv_heads + g, HD)
-            gk_ref[:, cols] = dkv_refs[c][g, :, :HD]
-            gv_ref[:, cols] = dkv_refs[c][g, :, HD:]
+            total = dkv_refs[c][g].astype(jnp.float32)
+            for i in range(1, sets):
+                total = total + dkv_refs[i * peers + c][g].astype(jnp.float32)
+            total = total.astype(jnp.bfloat16)
+            gk_ref[:, cols] = total[:, :HD]
+            gv_ref[:, cols] = total[:, HD:]
 
 
 def unpack(me, dq, dkv):
     peers = len(dq)
     tokens, width = dq[0].shape
-    kv_width = dkv[0].shape[0] * peers * HD
+    kv_width = dkv[0][0].shape[0] * peers * HD
+    flat = [piece for pieces in dkv for piece in pieces]
     return pl.pallas_call(
-        functools.partial(unpack_kernel, peers),
+        functools.partial(unpack_kernel, peers, len(dkv)),
         out_shape=(
             jax.ShapeDtypeStruct((tokens, peers * width), jnp.bfloat16),
             jax.ShapeDtypeStruct((tokens, kv_width), jnp.bfloat16),
             jax.ShapeDtypeStruct((tokens, kv_width), jnp.bfloat16),
         ),
-        in_specs=[SMEM] + [VMEM] * (2 * peers),
+        in_specs=[SMEM] + [VMEM] * (peers + len(flat)),
         out_specs=(VMEM,) * 3,
         compiler_params=PARAMS,
-    )(me, *dq, *dkv)
+    )(me, *dq, *flat)
 
 
 def exchange(pieces):
@@ -344,6 +354,15 @@
         for c in range(1, peers)
     ]
     return [pieces[0]] + moved
+
+
+def exchange_rows(here, near, far):
+    rows = here.shape[0]
+    flip = [(h, h ^ 1) for h in range(4)]
+    across = [(h, h ^ 2) for h in range(4)]
+    far = lax.ppermute(far, "head", across)
+    near = lax.ppermute(near, "head", flip)
+    return [here, near, far[:rows], lax.ppermute(far[rows:], "head", flip)]
 
 
 def body(queries, keys, values, outputs_saved, grad_out, lse, block_lists):
@@ -357,7 +376,8 @@
     key_count = peers
     units = key_count * kv_heads
 
-    own_kv = jnp.concatenate(exchange(pack_kv(me_ref, keys, values, peers)), axis=0)
+    kv_pack = pack_kv(me_ref, keys, values, peers)
+    own_kv = jnp.concatenate(exchange(kv_pack), axis=0)
 
     per_peer = block_lists.reshape(shards, -1)
     requests = per_peer.shape[1]
@@ -372,6 +392,19 @@
         swap = [(s, s ^ 1) for s in range(shards)]
         ahead = [(s, (s + 2) % shards) for s in range(shards)]
         back = [(s, (s - 2) % shards) for s in range(shards)]
+        later_me, _ = lax.optimization_barrier((me_ref, kv_pack))
+        q_pieces = pack_q(later_me, queries, grad_out, outputs_saved, peers)
+        own_kv, q_pieces = lax.optimization_barrier((own_kv, q_pieces))
+        qdo = exchange_rows(*q_pieces)
+        same1 = lax.ppermute(own_kv, "seq", ahead)
+        cross0 = lax.ppermute(own_kv, "seq", swap)
+        same3 = lax.ppermute(own_kv, "seq", back)
+        same2 = lax.ppermute(same1, "seq", ahead)
+        cross1 = lax.ppermute(same1, "seq", swap)
+        cross3 = lax.ppermute(same3, "seq", swap)
+        held, cross0, cross1 = lax.optimization_barrier((same2, cross0, cross1))
+        cross2 = lax.ppermute(held, "seq", swap)
+        per_peer, cross0 = lax.optimization_barrier((per_peer, cross0))
         mine = lax.dynamic_index_in_dim(per_peer, me, 0, keepdims=False)
         owner = mine // key_count
         apart = (me // 2 - owner // 2) % far
@@ -379,18 +412,6 @@
         piece = jnp.where(crossed == 1, far - 1 + (apart + 1) % far, apart - 1)
         slots = piece * units + (mine % key_count ^ head_me) * kv_heads + group_of
         slots = jnp.roll(slots, block_turn)
-        later_me, own_kv, slots = lax.optimization_barrier((me_ref, own_kv, slots))
-        q_pieces = list(pack_q(later_me, queries, grad_out, outputs_saved, peers))
-        same1 = lax.ppermute(own_kv, "seq", ahead)
-        cross0 = lax.ppermute(own_kv, "seq", swap)
-        held, q_pieces[0] = lax.optimization_barrier((own_kv, q_pieces[0]))
-        qdo = exchange(q_pieces)
-        same3 = lax.ppermute(held, "seq", back)
-        cross3 = lax.ppermute(cross0, "seq", back)
-        same2 = lax.ppermute(same1, "seq", ahead)
-        cross1 = lax.ppermute(same1, "seq", swap)
-        held, cross1, qdo[1:] = lax.optimization_barrier((same2, cross1, qdo[1:]))
-        cross2 = lax.ppermute(held, "seq", swap)
         kv_pieces = [same1, same2, same3, cross3, cross0, cross1, cross2]
         wide, low = jnp.float32, jnp.bfloat16
         part_types = [wide, wide, low, low, wide, low, low]
@@ -407,24 +428,23 @@
         kv_pieces = [lax.all_to_all(own_kv[wanted], "seq", 0, 0, tiled=True)]
         part_types = [jnp.bfloat16]
         slots = jnp.roll(slots, block_turn)
-        qdo = exchange(pack_q(me_ref, queries, grad_out, outputs_saved, peers))
+        qdo = exchange_rows(*pack_q(me_ref, queries, grad_out, outputs_saved, peers))
 
     stats, listed, parts = listed_terms(me_ref, slots, lse.T, qdo, kv_pieces, part_types)
     dq, own = own_terms(me_ref, own_kv, stats, qdo, listed)
 
     if dense:
         stay1, stay2, away3, leave3, leave0, leave1, leave2 = parts
+        came3 = lax.ppermute(jnp.concatenate([leave3, away3], axis=0), "seq", ahead)
         came2 = lax.ppermute(leave2, "seq", swap)
-        came3 = lax.ppermute(leave3, "seq", ahead)
         came1 = lax.ppermute(leave1, "seq", swap)
         hop = lax.ppermute(add_rounded(stay2, came2), "seq", back)
-        away3, came3 = lax.optimization_barrier((away3, came3))
-        turned = lax.ppermute(away3, "seq", ahead)
-        near, came1 = lax.optimization_barrier((add_rounded(leave0, came3), came1))
+        came3, dq = lax.optimization_barrier((came3, list(dq)))
+        dq = exchange(dq)
+        near, came1 = lax.optimization_barrier((add_rounded(leave0, came3[:units]), came1))
         came0 = lax.ppermute(near, "seq", swap)
-        hop, dq = lax.optimization_barrier((hop, list(dq)))
-        side = add_rounded(stay1, came1, hop)
-        arrived = [turned, came0, lax.ppermute(side, "seq", back)]
+        side = lax.ppermute(add_rounded(stay1, came1, hop), "seq", back)
+        dkv = [exchange(add_blocks(kv_heads, own, came3[units:], came0, side))]
     else:
         parts = lax.all_to_all(parts[0], "seq", 0, 0, tiled=True)
         chosen = (jnp.arange(units)[:, None] == wanted[None, :]) & (used[None, :] > 0)
@@ -433,9 +453,8 @@
             parts.reshape(parts.shape[0], -1),
             preferred_element_type=jnp.float32,
         )
-        arrived = [total.reshape(own.shape)]
-    dq = exchange(dq)
-    dkv = exchange(total_rounded(own, arrived, kv_heads))
+        dq = exchange(dq)
+        dkv = [exchange(add_blocks(kv_heads, own, total.reshape(own.shape)))]
     return unpack(me_ref, dq, dkv)
 
 

time: 87.8 us -> 83.5 us (0.951)
  starting transfers between devices: 38.8 us -> 28.6 us
  waiting for transfers between devices: 31 us -> 35 us
  local copies, waits for them, and re-layouts: 4.96 us -> 6.72 us
    ppermute x5 -> x7, starting transfers between devices: 20.6 us -> 11.3 us  [the longest x1 3.39 us: body(): came3 = lax.ppermute(jnp.concatenate([leave3, away3], axis=0), 'seq', ahead)]
    ppermute x12 -> x9, waiting for transfers between devices: 9.78 us -> 3.78 us  [exchange(): lax.ppermute(pieces[c], 'head', [(h, h ^ c) for h in range(peers)])]
    ppermute x1, waiting for transfers between devices: 0.01 us -> 5.21 us  [body(): cross2 = lax.ppermute(held, 'seq', swap)]
    ppermute x1, waiting for transfers between devices: 2.34 us -> 5.65 us  [body(): same1 = lax.ppermute(own_kv, 'seq', ahead)]
    ppermute x5 -> x7, waiting for transfers between devices: 8.31 us -> 5.43 us  [the longest x1 3.48 us: body(): side = lax.ppermute(add_rounded(stay1, came1, hop), 'seq', back)]
    ppermute x1, waiting for transfers between devices: 2.54 us -> 4.97 us  [body(): same2 = lax.ppermute(same1, 'seq', ahead)]
    ppermute x1, waiting for transfers between devices: 0.01 us -> 1.98 us  [body(): hop = lax.ppermute(add_rounded(stay2, came2), 'seq', back)]
    ppermute x12 -> x9, starting transfers between devices: 8.88 us -> 6.95 us  [exchange(): lax.ppermute(pieces[c], 'head', [(h, h ^ c) for h in range(peers)])]
  transfers between devices with their start and end apart: 26 -> 25, of which waited for: 13 -> 13; matrix products, arithmetic and copies ran while one was open for 1% -> 1% of each run, Pallas kernels for 6% -> 6%
where the time goes in v3:
time: 83.5 us; the launch traced here: 83.1 us
  waiting for transfers between devices  35 us (42%)
  starting transfers between devices  28.6 us (34%)
  Pallas kernels  11.8 us (14%)
  local copies, waits for them, and re-layouts  6.72 us (8%)
    ppermute x1, waiting for transfers between devices, body(): came2 = lax.ppermute(leave2, 'seq', swap)  7.22 us
    ppermute x9, starting transfers between devices, exchange(): lax.ppermute(pieces[c], 'head', [(h, h ^ c) for h in range(peers)])  6.95 us
    unnamed x15, local copies, waits for them, and re-layouts  5.78 us
    pallas_call x1, Pallas kernels, listed_terms(): pl.pallas_call(functools.partial(listed_kernel, peers, pieces), out_shape...  5.69 us
    ppermute x1, waiting for transfers between devices, body(): same1 = lax.ppermute(own_kv, 'seq', ahead)  5.65 us
    ppermute x1, waiting for transfers between devices, body(): cross2 = lax.ppermute(held, 'seq', swap)  5.21 us
    ppermute x1, waiting for transfers between devices, body(): same2 = lax.ppermute(same1, 'seq', ahead)  4.97 us
    pallas_call x1, Pallas kernels, own_terms(): pl.pallas_call(functools.partial(own_kernel, peers), out_shape=(piece,) *...  3.84 us
  transfers between devices with their start and end apart: 25, of which 13 were waited for; matrix products, arithmetic and copies ran while one was open for 1% of the time, Pallas kernels for 6%

profile of v3, /device:TPU:0, one launch (start us, length us, event | category | flops | bytes accessed | tf_op | source)
XLA Modules:
  0.0 83.1 jit_solution(1312929148784835007)
XLA Ops:
  0.6 0.9 %copy-done.3 = bf16[64,1024]{1,0:T(8,128)(2,1)S(1)} copy-done((bf16[64,1024]{1,0:T(8,128)(2,1)S(1)}, bf16[64,1024]{1,0:T(8,128)(2,1)}, u32[]{:S(2)}) %copy-start.3) | copy-done | bytes 131096
  1.5 0.9 %copy-done.4 = bf16[64,1024]{1,0:T(8,128)(2,1)S(1)} copy-done((bf16[64,1024]{1,0:T(8,128)(2,1)S(1)}, bf16[64,1024]{1,0:T(8,128)(2,1)}, u32[]{:S(2)}) %copy-start.4) | copy-done | bytes 131096
  2.4 0.3 shard_map.94
  2.7 0.5 collective-permute-start
  3.2 2.6 %collective-permute-start.1 = (bf16[2,64,256]{2,1,0:T(8,128)(2,1)S(1)}, bf16[2,64,256]{2,1,0:T(8,128)(2,1)S(1)}, u32[]{:S(2)}, u32[]{:S(2)}) collective-permute-start(bf16[2,64,256]{2,1,0:T(8,128)(2,1)S(1)} %get-tuple-element.50), channel_id=1, source_target_pairs={{0,2},{1,3},{2,0},{3,1},{4,6},{5,7},{6,4},{7,5},{8,10},{9,11},{10,... | collective-permute-start | bytes 196616 | tf_op jit(solution)/shard_map/ppermute | solution.py:353
  5.8 0.1 collective-permute-start.2
  5.9 1.0 %copy-done = bf16[64,4096]{1,0:T(8,128)(2,1)S(1)} copy-done((bf16[64,4096]{1,0:T(8,128)(2,1)S(1)}, bf16[64,4096]{1,0:T(8,128)(2,1)}, u32[]{:S(2)}) %copy-start) | copy-done | bytes 524312
  6.9 1.0 %copy-done.1 = bf16[64,4096]{1,0:T(8,128)(2,1)S(1)} copy-done((bf16[64,4096]{1,0:T(8,128)(2,1)S(1)}, bf16[64,4096]{1,0:T(8,128)(2,1)}, u32[]{:S(2)}) %copy-start.1) | copy-done | bytes 524312
  7.9 1.0 %copy-done.2 = bf16[64,4096]{1,0:T(8,128)(2,1)S(1)} copy-done((bf16[64,4096]{1,0:T(8,128)(2,1)S(1)}, bf16[64,4096]{1,0:T(8,128)(2,1)}, u32[]{:S(2)}) %copy-start.2) | copy-done | bytes 524312
  9.0 0.8 shard_map.95
  9.7 0.0 collective-permute-done
  9.8 0.0 collective-permute-done.1
  9.8 0.1 collective-permute-done.2
  9.9 1.7 %collective-permute-start.8 = (bf16[1056,256]{1,0:T(8,128)(2,1)S(1)}, bf16[1056,256]{1,0:T(8,128)(2,1)S(1)}, u32[]{:S(2)}, u32[]{:S(2)}) collective-permute-start(bf16[1056,256]{1,0:T(8,128)(2,1)S(1)} %get-tuple-element.61), channel_id=1, source_target_pairs={{0,2},{1,3},{2,0},{3,1},{4,6},{5,7},{6,4},{7,5},{8,10},{9,11},{10,... | collective-permute-start | bytes 1622024 | tf_op jit(solution)/shard_map/ppermute | solution.py:363
  11.6 1.6 %collective-permute-start.3 = (bf16[8,64,256]{2,1,0:T(8,128)(2,1)S(1)}, bf16[8,64,256]{2,1,0:T(8,128)(2,1)S(1)}, u32[]{:S(2)}, u32[]{:S(2)}) collective-permute-start(bf16[8,64,256]{2,1,0:T(8,128)(2,1)S(1)} %pad_maximum_fusion.1.own_kv_ref), channel_id=1, source_target_pairs={{0,8},{4,12},{8,16},{12,20},{16,24},{20,28},{24,0},{28,4},{1,9},{5... | collective-permute-start | bytes 786440 | tf_op jit(solution)/shard_map/ppermute | solution.py:399
  13.2 2.2 %collective-permute-start.10 = (bf16[8,64,256]{2,1,0:T(8,128)(2,1)S(1)}, bf16[8,64,256]{2,1,0:T(8,128)(2,1)S(1)}, u32[]{:S(2)}, u32[]{:S(2)}) collective-permute-start(bf16[8,64,256]{2,1,0:T(8,128)(2,1)S(1)} %pad_maximum_fusion.1.own_kv_ref), channel_id=1, source_target_pairs={{0,24},{4,28},{8,0},{12,4},{16,8},{20,12},{24,16},{28,20},{1,25},{... | collective-permute-start | bytes 786440 | tf_op jit(solution)/shard_map/ppermute | solution.py:401
  15.4 1.5 %collective-permute-start.5 = (bf16[8,64,256]{2,1,0:T(8,128)(2,1)S(1)}, bf16[8,64,256]{2,1,0:T(8,128)(2,1)S(1)}, u32[]{:S(2)}, u32[]{:S(2)}) collective-permute-start(bf16[8,64,256]{2,1,0:T(8,128)(2,1)S(1)} %pad_maximum_fusion.1.own_kv_ref), channel_id=1, source_target_pairs={{0,4},{4,0},{8,12},{12,8},{16,20},{20,16},{24,28},{28,24},{1,5},{5... | collective-permute-start | bytes 786440 | tf_op jit(solution)/shard_map/ppermute | solution.py:400
  17.0 5.7 %collective-permute-done.3.refs_4_ = bf16[8,64,256]{2,1,0:T(8,128)(2,1)S(1)} collective-permute-done((bf16[8,64,256]{2,1,0:T(8,128)(2,1)S(1)}, bf16[8,64,256]{2,1,0:T(8,128)(2,1)S(1)}, u32[]{:S(2)}, u32[]{:S(2)}) %collective-permute-start.3) | collective-permute-done | bytes 262176 | tf_op jit(solution)/shard_map/ppermute | solution.py:399
  22.6 1.5 %collective-permute-start.6 = (bf16[8,64,256]{2,1,0:T(8,128)(2,1)S(1)}, bf16[8,64,256]{2,1,0:T(8,128)(2,1)S(1)}, u32[]{:S(2)}, u32[]{:S(2)}) collective-permute-start(bf16[8,64,256]{2,1,0:T(8,128)(2,1)S(1)} %collective-permute-done.3.refs_4_), channel_id=1, source_target_pairs={{0,4},{4,0},{8,12},{12,8},{16,20},{20,16},{24,28},{28,24},{1,5},{5... | collective-permute-start | bytes 786440 | tf_op jit(solution)/shard_map/ppermute | solution.py:403
  24.1 0.0 collective-permute-start.4
  24.1 0.3 collective-permute-done.8
  24.4 0.0 collective-permute-start.7
  24.4 0.7 fusion.8
  25.1 1.7 %collective-permute-done.10.refs_6_ = bf16[8,64,256]{2,1,0:T(8,128)(2,1)S(1)} collective-permute-done((bf16[8,64,256]{2,1,0:T(8,128)(2,1)S(1)}, bf16[8,64,256]{2,1,0:T(8,128)(2,1)S(1)}, u32[]{:S(2)}, u32[]{:S(2)}) %collective-permute-start.10) | collective-permute-done | bytes 262176 | tf_op jit(solution)/shard_map/ppermute | solution.py:401
  26.8 0.0 collective-permute-start.9
  26.8 1.7 %collective-permute-start.11 = (bf16[8,64,256]{2,1,0:T(8,128)(2,1)S(1)}, bf16[8,64,256]{2,1,0:T(8,128)(2,1)S(1)}, u32[]{:S(2)}, u32[]{:S(2)}) collective-permute-start(bf16[8,64,256]{2,1,0:T(8,128)(2,1)S(1)} %collective-permute-done.10.refs_6_), channel_id=1, source_target_pairs={{0,4},{4,0},{8,12},{12,8},{16,20},{20,16},{24,28},{28,24},{1,5},{5... | collective-permute-start | bytes 786440 | tf_op jit(solution)/shard_map/ppermute | solution.py:404
  28.5 0.8 collective-permute-done.6.refs_9_
  29.3 5.0 %collective-permute-done.4.refs_5_ = bf16[8,64,256]{2,1,0:T(8,128)(2,1)S(1)} collective-permute-done((bf16[8,64,256]{2,1,0:T(8,128)(2,1)S(1)}, bf16[8,64,256]{2,1,0:T(8,128)(2,1)S(1)}, u32[]{:S(2)}, u32[]{:S(2)}) %collective-permute-start.4) | collective-permute-done | bytes 262176 | tf_op jit(solution)/shard_map/ppermute | solution.py:402
  34.3 0.5 collective-permute-start.12
  34.8 0.7 copy-done.6
  35.5 0.1 copy.10
  35.6 0.1 reshape.13
  35.7 0.0 copy-start.5
  35.8 0.1 pad_add_fusion
  35.9 0.1 dynamic_slice.9.slot_ref
  36.0 5.2 %collective-permute-done.12.refs_10_ = bf16[8,64,256]{2,1,0:T(8,128)(2,1)S(1)} collective-permute-done((bf16[8,64,256]{2,1,0:T(8,128)(2,1)S(1)}, bf16[8,64,256]{2,1,0:T(8,128)(2,1)S(1)}, u32[]{:S(2)}, u32[]{:S(2)}) %collective-permute-start.12) | collective-permute-done | bytes 262176 | tf_op jit(solution)/shard_map/ppermute | solution.py:406
  41.2 0.0 collective-permute-done.9.refs_3_
  41.2 5.7 %shard_map.96 = (f32[2,8,256]{2,1,0:T(8,128)S(1)}, f32[64,1024]{1,0:T(8,128)S(1)}, f32[64,1024]{1,0:T(8,128)S(1)}, f32[64,1024]{1,0:T(8,128)S(1)}, f32[64,1024]{...) custom-call(s32[1]{0:T(128)} %bitcast.me_ref, ...), custom_call_target="tpu_custom_call" | custom-call | flops 671000000 | bytes 8000000 | tf_op jit(solution)/shard_map/pallas_call | solution.py:251
  46.9 3.4 %collective-permute-start.13 = (bf16[16,64,256]{2,1,0:T(8,128)(2,1)S(1)}, bf16[16,64,256]{2,1,0:T(8,128)(2,1)S(1)}, u32[]{:S(2)}, u32[]{:S(2)}) collective-permute-start(bf16[16,64,256]{2,1,0:T(8,128)(2,1)S(1)} %pad_maximum_fusion), channel_id=1, source_target_pairs={{0,8},{4,12},{8,16},{12,20},{16,24},{20,28},{24,0},{28,4},{1,9},{5... | collective-permute-start | bytes 1572872 | tf_op jit(solution)/shard_map/ppermute | solution.py:438
  50.3 0.5 collective-permute-start.19
  50.8 1.5 %collective-permute-start.17 = (bf16[8,64,256]{2,1,0:T(8,128)(2,1)S(1)}, bf16[8,64,256]{2,1,0:T(8,128)(2,1)S(1)}, u32[]{:S(2)}, u32[]{:S(2)}) collective-permute-start(bf16[8,64,256]{2,1,0:T(8,128)(2,1)S(1)} %get-tuple-element.83), channel_id=1, source_target_pairs={{0,4},{4,0},{8,12},{12,8},{16,20},{20,16},{24,28},{28,24},{1,5},{5... | collective-permute-start | bytes 786440 | tf_op jit(solution)/shard_map/ppermute | solution.py:440
  52.3 7.2 %collective-permute-done.19.refs_1_ = bf16[8,64,256]{2,1,0:T(8,128)(2,1)S(1)} collective-permute-done((bf16[8,64,256]{2,1,0:T(8,128)(2,1)S(1)}, bf16[8,64,256]{2,1,0:T(8,128)(2,1)S(1)}, u32[]{:S(2)}, u32[]{:S(2)}) %collective-permute-start.19) | collective-permute-done | bytes 262176 | tf_op jit(solution)/shard_map/ppermute | solution.py:439
  59.6 1.6 %collective-permute-start.20 = (bf16[8,64,256]{2,1,0:T(8,128)(2,1)S(1)}, bf16[8,64,256]{2,1,0:T(8,128)(2,1)S(1)}, u32[]{:S(2)}, u32[]{:S(2)}) collective-permute-start(bf16[8,64,256]{2,1,0:T(8,128)(2,1)S(1)} %shard_map.99), channel_id=1, source_target_pairs={{0,24},{4,28},{8,0},{12,4},{16,8},{20,12},{24,16},{28,20},{1,25},{... | collective-permute-start | bytes 786440 | tf_op jit(solution)/shard_map/ppermute | solution.py:441
  61.2 3.8 %shard_map.97 = (bf16[64,1024]{1,0:T(8,128)(2,1)S(1)}, bf16[64,1024]{1,0:T(8,128)(2,1)S(1)}, bf16[64,1024]{1,0:T(8,128)(2,1)S(1)}, bf16[64,1024]{1,0:T(8,128)(2,1)S(1)}, f32[8,64,256]{2,1,0:T(8,128)S(1)}) custom-call(s32[1]{0:T(128)} %bitcast.me_ref, bf16[8,64,256]{2,1,0:T(8,128)(2,1)S(1)} %pad_maximum_fusion.1.own_kv_ref, ...), custom_call_target="tpu_custom_call" | custom-call | flops 335000000 | bytes 4000000 | tf_op jit(solution)/shard_map/pallas_call | solution.py:174
  65.1 0.0 collective-permute-done.13
  65.2 1.6 %collective-permute-start.18 = (bf16[8,64,256]{2,1,0:T(8,128)(2,1)S(1)}, bf16[8,64,256]{2,1,0:T(8,128)(2,1)S(1)}, u32[]{:S(2)}, u32[]{:S(2)}) collective-permute-start(bf16[8,64,256]{2,1,0:T(8,128)(2,1)S(1)} %shard_map.98), channel_id=1, source_target_pairs={{0,4},{4,0},{8,12},{12,8},{16,20},{20,16},{24,28},{28,24},{1,5},{5... | collective-permute-start | bytes 786440 | tf_op jit(solution)/shard_map/ppermute | solution.py:445
  66.8 2.0 %collective-permute-done.20.refs_2_ = bf16[8,64,256]{2,1,0:T(8,128)(2,1)S(1)} collective-permute-done((bf16[8,64,256]{2,1,0:T(8,128)(2,1)S(1)}, bf16[8,64,256]{2,1,0:T(8,128)(2,1)S(1)}, u32[]{:S(2)}, u32[]{:S(2)}) %collective-permute-start.20) | collective-permute-done | bytes 262176 | tf_op jit(solution)/shard_map/ppermute | solution.py:441
  68.8 0.1 shard_map.100
  68.9 2.2 %collective-permute-start.21 = (bf16[8,64,256]{2,1,0:T(8,128)(2,1)S(1)}, bf16[8,64,256]{2,1,0:T(8,128)(2,1)S(1)}, u32[]{:S(2)}, u32[]{:S(2)}) collective-permute-start(bf16[8,64,256]{2,1,0:T(8,128)(2,1)S(1)} %shard_map.100), channel_id=1, source_target_pairs={{0,24},{4,28},{8,0},{12,4},{16,8},{20,12},{24,16},{28,20},{1,25},{... | collective-permute-start | bytes 786440 | tf_op jit(solution)/shard_map/ppermute | solution.py:446
  71.0 0.0 collective-permute-start.14
  71.0 0.5 collective-permute-start.15
  71.6 1.3 %collective-permute-start.16 = (bf16[64,1024]{1,0:T(8,128)(2,1)S(1)}, bf16[64,1024]{1,0:T(8,128)(2,1)S(1)}, u32[]{:S(2)}, u32[]{:S(2)}) collective-permute-start(bf16[64,1024]{1,0:T(8,128)(2,1)S(1)} %get-tuple-element.79), channel_id=1, source_target_pairs={{0,3},{1,2},{2,1},{3,0},{4,7},{5,6},{6,5},{7,4},{8,11},{9,10},{10,... | collective-permute-start | bytes 393224 | tf_op jit(solution)/shard_map/ppermute | solution.py:353
  72.9 0.0 collective-permute-done.18.refs_2_
  72.9 3.5 %collective-permute-done.21.refs_3_ = bf16[8,64,256]{2,1,0:T(8,128)(2,1)S(1)} collective-permute-done((bf16[8,64,256]{2,1,0:T(8,128)(2,1)S(1)}, bf16[8,64,256]{2,1,0:T(8,128)(2,1)S(1)}, u32[]{:S(2)}, u32[]{:S(2)}) %collective-permute-start.21) | collective-permute-done | bytes 262176 | tf_op jit(solution)/shard_map/ppermute | solution.py:446
  76.4 0.1 shard_map.101
  76.5 0.1 collective-permute-start.22
  76.6 0.6 collective-permute-start.23
  77.2 0.0 collective-permute-done.14.refs_1_
  77.2 1.3 %collective-permute-start.24 = (bf16[2,64,256]{2,1,0:T(8,128)(2,1)S(1)}, bf16[2,64,256]{2,1,0:T(8,128)(2,1)S(1)}, u32[]{:S(2)}, u32[]{:S(2)}) collective-permute-start(bf16[2,64,256]{2,1,0:T(8,128)(2,1)S(1)} %get-tuple-element.92), channel_id=1, source_target_pairs={{0,3},{1,2},{2,1},{3,0},{4,7},{5,6},{6,5},{7,4},{8,11},{9,10},{10,... | collective-permute-start | bytes 196616 | tf_op jit(solution)/shard_map/ppermute | solution.py:353
  78.5 0.0 collective-permute-done.15.refs_2_
  78.5 0.9 %collective-permute-done.16.refs_3_ = bf16[64,1024]{1,0:T(8,128)(2,1)S(1)} collective-permute-done((bf16[64,1024]{1,0:T(8,128)(2,1)S(1)}, bf16[64,1024]{1,0:T(8,128)(2,1)S(1)}, u32[]{:S(2)}, u32[]{:S(2)}) %collective-permute-start.16) | collective-permute-done | bytes 131104 | tf_op jit(solution)/shard_map/ppermute | solution.py:353
  79.4 2.2 %collective-permute-done.23.refs_6_ = bf16[2,64,256]{2,1,0:T(8,128)(2,1)S(1)} collective-permute-done((bf16[2,64,256]{2,1,0:T(8,128)(2,1)S(1)}, bf16[2,64,256]{2,1,0:T(8,128)(2,1)S(1)}, u32[]{:S(2)}, u32[]{:S(2)}) %collective-permute-start.23) | collective-permute-done | bytes 65568 | tf_op jit(solution)/shard_map/ppermute | solution.py:353
  81.6 0.6 collective-permute-done.24.refs_7_
  82.2 1.0 %shard_map.102 = (bf16[64,4096]{1,0:T(8,128)(2,1)}, bf16[64,1024]{1,0:T(8,128)(2,1)}, bf16[64,1024]{1,0:T(8,128)(2,1)}) custom-call(s32[1]{0:T(128)} %bitcast.me_ref, bf16[64,1024]{1,0:T(8,128)(2,1)S(1)} %get-tuple-element.76.refs_0_, bf16[64,1024]{1,0:T(8,128)(2,1)S(1)} %collective-permute-done.14.refs_1_, ...), custom_call_target="tpu_custom_call" | custom-call | tf_op jit(solution)/shard_map/pallas_call | solution.py:337
  (18 shorter events, 0.3 us)
Async XLA Ops:
  0.6 0.9 %copy-start.3 = (bf16[64,1024]{1,0:T(8,128)(2,1)S(1)}, bf16[64,1024]{1,0:T(8,128)(2,1)}, u32[]{:S(2)}) copy-start(bf16[64,1024]{1,0:T(8,128)(2,1)} %k_ref.1) | copy-start | bytes 393220
  1.5 0.9 %copy-start.4 = (bf16[64,1024]{1,0:T(8,128)(2,1)S(1)}, bf16[64,1024]{1,0:T(8,128)(2,1)}, u32[]{:S(2)}) copy-start(bf16[64,1024]{1,0:T(8,128)(2,1)} %v_ref.1) | copy-start | bytes 393220
  2.7 7.0 %collective-permute-start = (bf16[2,64,256]{2,1,0:T(8,128)(2,1)S(1)}, bf16[2,64,256]{2,1,0:T(8,128)(2,1)S(1)}, u32[]{:S(2)}, u32[]{:S(2)}) collective-permute-start(bf16[2,64,256]{2,1,0:T(8,128)(2,1)S(1)} %get-tuple-element.49), channel_id=1, source_target_pairs={{0,1},{1,0},{2,3},{3,2},{4,5},{5,4},{6,7},{7,6},{8,9},{9,8},{10,11... | collective-permute-start | bytes 196616 | tf_op jit(solution)/shard_map/ppermute | solution.py:353
  3.2 6.5 %collective-permute-start.1 = (bf16[2,64,256]{2,1,0:T(8,128)(2,1)S(1)}, bf16[2,64,256]{2,1,0:T(8,128)(2,1)S(1)}, u32[]{:S(2)}, u32[]{:S(2)}) collective-permute-start(bf16[2,64,256]{2,1,0:T(8,128)(2,1)S(1)} %get-tuple-element.50), channel_id=1, source_target_pairs={{0,2},{1,3},{2,0},{3,1},{4,6},{5,7},{6,4},{7,5},{8,10},{9,11},{10,... | collective-permute-start | bytes 196616 | tf_op jit(solution)/shard_map/ppermute | solution.py:353
  5.8 4.0 %collective-permute-start.2 = (bf16[2,64,256]{2,1,0:T(8,128)(2,1)S(1)}, bf16[2,64,256]{2,1,0:T(8,128)(2,1)S(1)}, u32[]{:S(2)}, u32[]{:S(2)}) collective-permute-start(bf16[2,64,256]{2,1,0:T(8,128)(2,1)S(1)} %get-tuple-element.51), channel_id=1, source_target_pairs={{0,3},{1,2},{2,1},{3,0},{4,7},{5,6},{6,5},{7,4},{8,11},{9,10},{10,... | collective-permute-start | bytes 196616 | tf_op jit(solution)/shard_map/ppermute | solution.py:353
  5.9 1.0 %copy-start = (bf16[64,4096]{1,0:T(8,128)(2,1)S(1)}, bf16[64,4096]{1,0:T(8,128)(2,1)}, u32[]{:S(2)}) copy-start(bf16[64,4096]{1,0:T(8,128)(2,1)} %q_any.1) | copy-start | bytes 1572868
  6.9 1.0 %copy-start.1 = (bf16[64,4096]{1,0:T(8,128)(2,1)S(1)}, bf16[64,4096]{1,0:T(8,128)(2,1)}, u32[]{:S(2)}) copy-start(bf16[64,4096]{1,0:T(8,128)(2,1)} %do_any.1) | copy-start | bytes 1572868
  7.9 1.0 %copy-start.2 = (bf16[64,4096]{1,0:T(8,128)(2,1)S(1)}, bf16[64,4096]{1,0:T(8,128)(2,1)}, u32[]{:S(2)}) copy-start(bf16[64,4096]{1,0:T(8,128)(2,1)} %o_any.1) | copy-start | bytes 1572868
  9.9 14.5 %collective-permute-start.8 = (bf16[1056,256]{1,0:T(8,128)(2,1)S(1)}, bf16[1056,256]{1,0:T(8,128)(2,1)S(1)}, u32[]{:S(2)}, u32[]{:S(2)}) collective-permute-start(bf16[1056,256]{1,0:T(8,128)(2,1)S(1)} %get-tuple-element.61), channel_id=1, source_target_pairs={{0,2},{1,3},{2,0},{3,1},{4,6},{5,7},{6,4},{7,5},{8,10},{9,11},{10,... | collective-permute-start | bytes 1622024 | tf_op jit(solution)/shard_map/ppermute | solution.py:363
  11.6 11.0 %collective-permute-start.3 = (bf16[8,64,256]{2,1,0:T(8,128)(2,1)S(1)}, bf16[8,64,256]{2,1,0:T(8,128)(2,1)S(1)}, u32[]{:S(2)}, u32[]{:S(2)}) collective-permute-start(bf16[8,64,256]{2,1,0:T(8,128)(2,1)S(1)} %pad_maximum_fusion.1.own_kv_ref), channel_id=1, source_target_pairs={{0,8},{4,12},{8,16},{12,20},{16,24},{20,28},{24,0},{28,4},{1,9},{5... | collective-permute-start | bytes 786440 | tf_op jit(solution)/shard_map/ppermute | solution.py:399
  13.2 13.6 %collective-permute-start.10 = (bf16[8,64,256]{2,1,0:T(8,128)(2,1)S(1)}, bf16[8,64,256]{2,1,0:T(8,128)(2,1)S(1)}, u32[]{:S(2)}, u32[]{:S(2)}) collective-permute-start(bf16[8,64,256]{2,1,0:T(8,128)(2,1)S(1)} %pad_maximum_fusion.1.own_kv_ref), channel_id=1, source_target_pairs={{0,24},{4,28},{8,0},{12,4},{16,8},{20,12},{24,16},{28,20},{1,25},{... | collective-permute-start | bytes 786440 | tf_op jit(solution)/shard_map/ppermute | solution.py:401
  15.4 11.4 %collective-permute-start.5 = (bf16[8,64,256]{2,1,0:T(8,128)(2,1)S(1)}, bf16[8,64,256]{2,1,0:T(8,128)(2,1)S(1)}, u32[]{:S(2)}, u32[]{:S(2)}) collective-permute-start(bf16[8,64,256]{2,1,0:T(8,128)(2,1)S(1)} %pad_maximum_fusion.1.own_kv_ref), channel_id=1, source_target_pairs={{0,4},{4,0},{8,12},{12,8},{16,20},{20,16},{24,28},{28,24},{1,5},{5... | collective-permute-start | bytes 786440 | tf_op jit(solution)/shard_map/ppermute | solution.py:400
  22.6 6.7 %collective-permute-start.6 = (bf16[8,64,256]{2,1,0:T(8,128)(2,1)S(1)}, bf16[8,64,256]{2,1,0:T(8,128)(2,1)S(1)}, u32[]{:S(2)}, u32[]{:S(2)}) collective-permute-start(bf16[8,64,256]{2,1,0:T(8,128)(2,1)S(1)} %collective-permute-done.3.refs_4_), channel_id=1, source_target_pairs={{0,4},{4,0},{8,12},{12,8},{16,20},{20,16},{24,28},{28,24},{1,5},{5... | collective-permute-start | bytes 786440 | tf_op jit(solution)/shard_map/ppermute | solution.py:403
  24.1 10.1 %collective-permute-start.4 = (bf16[8,64,256]{2,1,0:T(8,128)(2,1)S(1)}, bf16[8,64,256]{2,1,0:T(8,128)(2,1)S(1)}, u32[]{:S(2)}, u32[]{:S(2)}) collective-permute-start(bf16[8,64,256]{2,1,0:T(8,128)(2,1)S(1)} %collective-permute-done.3.refs_4_), channel_id=1, source_target_pairs={{0,8},{4,12},{8,16},{12,20},{16,24},{20,28},{24,0},{28,4},{1,9},{5... | collective-permute-start | bytes 786440 | tf_op jit(solution)/shard_map/ppermute | solution.py:402
  24.4 11.6 %collective-permute-start.7 = (bf16[528,256]{1,0:T(8,128)(2,1)S(1)}, bf16[528,256]{1,0:T(8,128)(2,1)S(1)}, u32[]{:S(2)}, u32[]{:S(2)}) collective-permute-start(bf16[528,256]{1,0:T(8,128)(2,1)S(1)} %get-tuple-element.60), channel_id=1, source_target_pairs={{0,1},{1,0},{2,3},{3,2},{4,5},{5,4},{6,7},{7,6},{8,9},{9,8},{10,11... | collective-permute-start | bytes 811016 | tf_op jit(solution)/shard_map/ppermute | solution.py:364
  26.8 14.3 %collective-permute-start.9 = (bf16[528,256]{1,0:T(8,128)(2,1)}, bf16[528,256]{1,0:T(8,128)(2,1)S(1)}, u32[]{:S(2)}, u32[]{:S(2)}) collective-permute-start(bf16[528,256]{1,0:T(8,128)(2,1)} %get-tuple-element.93), channel_id=1, source_target_pairs={{0,1},{1,0},{2,3},{3,2},{4,5},{5,4},{6,7},{7,6},{8,9},{9,8},{10,11... | collective-permute-start | bytes 811016 | tf_op jit(solution)/shard_map/ppermute | solution.py:365
  26.8 9.1 %collective-permute-start.11 = (bf16[8,64,256]{2,1,0:T(8,128)(2,1)S(1)}, bf16[8,64,256]{2,1,0:T(8,128)(2,1)S(1)}, u32[]{:S(2)}, u32[]{:S(2)}) collective-permute-start(bf16[8,64,256]{2,1,0:T(8,128)(2,1)S(1)} %collective-permute-done.10.refs_6_), channel_id=1, source_target_pairs={{0,4},{4,0},{8,12},{12,8},{16,20},{20,16},{24,28},{28,24},{1,5},{5... | collective-permute-start | bytes 786440 | tf_op jit(solution)/shard_map/ppermute | solution.py:404
  34.3 6.9 %collective-permute-start.12 = (bf16[8,64,256]{2,1,0:T(8,128)(2,1)S(1)}, bf16[8,64,256]{2,1,0:T(8,128)(2,1)S(1)}, u32[]{:S(2)}, u32[]{:S(2)}) collective-permute-start(bf16[8,64,256]{2,1,0:T(8,128)(2,1)S(1)} %collective-permute-done.4.refs_5_), channel_id=1, source_target_pairs={{0,4},{4,0},{8,12},{12,8},{16,20},{20,16},{24,28},{28,24},{1,5},{5... | collective-permute-start | bytes 786440 | tf_op jit(solution)/shard_map/ppermute | solution.py:406
  34.8 0.7 copy-start.6
  35.7 5.4 %copy-start.5 = (f32[256,8]{0,1:T(8,128)S(1)}, f32[256,8]{0,1:T(8,128)}, u32[]{:S(2)}) copy-start(f32[256,8]{0,1:T(8,128)} %param.12) | copy-start | bytes 24580
  46.9 18.2 %collective-permute-start.13 = (bf16[16,64,256]{2,1,0:T(8,128)(2,1)S(1)}, bf16[16,64,256]{2,1,0:T(8,128)(2,1)S(1)}, u32[]{:S(2)}, u32[]{:S(2)}) collective-permute-start(bf16[16,64,256]{2,1,0:T(8,128)(2,1)S(1)} %pad_maximum_fusion), channel_id=1, source_target_pairs={{0,8},{4,12},{8,16},{12,20},{16,24},{20,28},{24,0},{28,4},{1,9},{5... | collective-permute-start | bytes 1572872 | tf_op jit(solution)/shard_map/ppermute | solution.py:438
  50.3 9.2 %collective-permute-start.19 = (bf16[8,64,256]{2,1,0:T(8,128)(2,1)S(1)}, bf16[8,64,256]{2,1,0:T(8,128)(2,1)S(1)}, u32[]{:S(2)}, u32[]{:S(2)}) collective-permute-start(bf16[8,64,256]{2,1,0:T(8,128)(2,1)S(1)} %get-tuple-element.88), channel_id=1, source_target_pairs={{0,4},{4,0},{8,12},{12,8},{16,20},{20,16},{24,28},{28,24},{1,5},{5... | collective-permute-start | bytes 786440 | tf_op jit(solution)/shard_map/ppermute | solution.py:439
  50.8 14.4 %collective-permute-start.17 = (bf16[8,64,256]{2,1,0:T(8,128)(2,1)S(1)}, bf16[8,64,256]{2,1,0:T(8,128)(2,1)S(1)}, u32[]{:S(2)}, u32[]{:S(2)}) collective-permute-start(bf16[8,64,256]{2,1,0:T(8,128)(2,1)S(1)} %get-tuple-element.83), channel_id=1, source_target_pairs={{0,4},{4,0},{8,12},{12,8},{16,20},{20,16},{24,28},{28,24},{1,5},{5... | collective-permute-start | bytes 786440 | tf_op jit(solution)/shard_map/ppermute | solution.py:440
  59.6 9.2 %collective-permute-start.20 = (bf16[8,64,256]{2,1,0:T(8,128)(2,1)S(1)}, bf16[8,64,256]{2,1,0:T(8,128)(2,1)S(1)}, u32[]{:S(2)}, u32[]{:S(2)}) collective-permute-start(bf16[8,64,256]{2,1,0:T(8,128)(2,1)S(1)} %shard_map.99), channel_id=1, source_target_pairs={{0,24},{4,28},{8,0},{12,4},{16,8},{20,12},{24,16},{28,20},{1,25},{... | collective-permute-start | bytes 786440 | tf_op jit(solution)/shard_map/ppermute | solution.py:441
  65.2 7.7 %collective-permute-start.18 = (bf16[8,64,256]{2,1,0:T(8,128)(2,1)S(1)}, bf16[8,64,256]{2,1,0:T(8,128)(2,1)S(1)}, u32[]{:S(2)}, u32[]{:S(2)}) collective-permute-start(bf16[8,64,256]{2,1,0:T(8,128)(2,1)S(1)} %shard_map.98), channel_id=1, source_target_pairs={{0,4},{4,0},{8,12},{12,8},{16,20},{20,16},{24,28},{28,24},{1,5},{5... | collective-permute-start | bytes 786440 | tf_op jit(solution)/shard_map/ppermute | solution.py:445
  68.9 7.5 %collective-permute-start.21 = (bf16[8,64,256]{2,1,0:T(8,128)(2,1)S(1)}, bf16[8,64,256]{2,1,0:T(8,128)(2,1)S(1)}, u32[]{:S(2)}, u32[]{:S(2)}) collective-permute-start(bf16[8,64,256]{2,1,0:T(8,128)(2,1)S(1)} %shard_map.100), channel_id=1, source_target_pairs={{0,24},{4,28},{8,0},{12,4},{16,8},{20,12},{24,16},{28,20},{1,25},{... | collective-permute-start | bytes 786440 | tf_op jit(solution)/shard_map/ppermute | solution.py:446
  71.0 6.2 %collective-permute-start.14 = (bf16[64,1024]{1,0:T(8,128)(2,1)S(1)}, bf16[64,1024]{1,0:T(8,128)(2,1)S(1)}, u32[]{:S(2)}, u32[]{:S(2)}) collective-permute-start(bf16[64,1024]{1,0:T(8,128)(2,1)S(1)} %get-tuple-element.77), channel_id=1, source_target_pairs={{0,1},{1,0},{2,3},{3,2},{4,5},{5,4},{6,7},{7,6},{8,9},{9,8},{10,11... | collective-permute-start | bytes 393224 | tf_op jit(solution)/shard_map/ppermute | solution.py:353
  71.0 7.4 %collective-permute-start.15 = (bf16[64,1024]{1,0:T(8,128)(2,1)S(1)}, bf16[64,1024]{1,0:T(8,128)(2,1)S(1)}, u32[]{:S(2)}, u32[]{:S(2)}) collective-permute-start(bf16[64,1024]{1,0:T(8,128)(2,1)S(1)} %get-tuple-element.78), channel_id=1, source_target_pairs={{0,2},{1,3},{2,0},{3,1},{4,6},{5,7},{6,4},{7,5},{8,10},{9,11},{10,... | collective-permute-start | bytes 393224 | tf_op jit(solution)/shard_map/ppermute | solution.py:353
  71.6 7.8 %collective-permute-start.16 = (bf16[64,1024]{1,0:T(8,128)(2,1)S(1)}, bf16[64,1024]{1,0:T(8,128)(2,1)S(1)}, u32[]{:S(2)}, u32[]{:S(2)}) collective-permute-start(bf16[64,1024]{1,0:T(8,128)(2,1)S(1)} %get-tuple-element.79), channel_id=1, source_target_pairs={{0,3},{1,2},{2,1},{3,0},{4,7},{5,6},{6,5},{7,4},{8,11},{9,10},{10,... | collective-permute-start | bytes 393224 | tf_op jit(solution)/shard_map/ppermute | solution.py:353
  76.5 2.9 %collective-permute-start.22 = (bf16[2,64,256]{2,1,0:T(8,128)(2,1)S(1)}, bf16[2,64,256]{2,1,0:T(8,128)(2,1)S(1)}, u32[]{:S(2)}, u32[]{:S(2)}) collective-permute-start(bf16[2,64,256]{2,1,0:T(8,128)(2,1)S(1)} %get-tuple-element.90), channel_id=1, source_target_pairs={{0,1},{1,0},{2,3},{3,2},{4,5},{5,4},{6,7},{7,6},{8,9},{9,8},{10,11... | collective-permute-start | bytes 196616 | tf_op jit(solution)/shard_map/ppermute | solution.py:353
  76.6 5.0 %collective-permute-start.23 = (bf16[2,64,256]{2,1,0:T(8,128)(2,1)S(1)}, bf16[2,64,256]{2,1,0:T(8,128)(2,1)S(1)}, u32[]{:S(2)}, u32[]{:S(2)}) collective-permute-start(bf16[2,64,256]{2,1,0:T(8,128)(2,1)S(1)} %get-tuple-element.91), channel_id=1, source_target_pairs={{0,2},{1,3},{2,0},{3,1},{4,6},{5,7},{6,4},{7,5},{8,10},{9,11},{10,... | collective-permute-start | bytes 196616 | tf_op jit(solution)/shard_map/ppermute | solution.py:353
  77.2 5.0 %collective-permute-start.24 = (bf16[2,64,256]{2,1,0:T(8,128)(2,1)S(1)}, bf16[2,64,256]{2,1,0:T(8,128)(2,1)S(1)}, u32[]{:S(2)}, u32[]{:S(2)}) collective-permute-start(bf16[2,64,256]{2,1,0:T(8,128)(2,1)S(1)} %get-tuple-element.92), channel_id=1, source_target_pairs={{0,3},{1,2},{2,1},{3,0},{4,7},{5,6},{6,5},{7,4},{8,11},{9,10},{10,... | collective-permute-start | bytes 196616 | tf_op jit(solution)/shard_map/ppermute | solution.py:353

commit v4 on v3

--- a/solution.py
+++ b/solution.py
@@ -21,6 +21,7 @@
 SMEM = pl.BlockSpec(memory_space=pltpu.SMEM)
 NT = (((1,), (1,)), ((), ()))
 TN = (((0,), (0,)), ((), ()))
+PACK_PARAMS = pltpu.CompilerParams(vmem_limit_bytes=60 * 1024 * 1024)
 PARAMS = pltpu.CompilerParams(vmem_limit_bytes=24 * 1024 * 1024)
 
 
@@ -65,7 +66,7 @@
         in_specs=[SMEM, HBM, HBM],
         out_specs=(VMEM,) * peers,
         scratch_shapes=[pltpu.SemaphoreType.DMA((2 * peers * kv_heads,))],
-        compiler_params=PARAMS,
+        compiler_params=PACK_PARAMS,
     )(me, keys, values)
 
 
@@ -120,7 +121,7 @@
         out_specs=(VMEM,) * (half + 1),
         scratch_shapes=[pltpu.VMEM(queries.shape, jnp.bfloat16)] * 3
         + [pltpu.SemaphoreType.DMA((3,))],
-        compiler_params=PARAMS,
+        compiler_params=PACK_PARAMS,
     )(me, queries, grad_out, outputs_saved)
 
 
@@ -200,120 +201,102 @@
         stats_ref[1, :, c * KB : (c + 1) * KB] = delta
 
 
-def listed_kernel(peers, pieces, me_ref, slot_ref, lse_ref, *refs):
-    qdo = refs[:peers]
-    kv_refs = refs[peers : peers + pieces]
-    outs = refs[peers + pieces : -3]
+def listed_kernel(peers, me_ref, slot_ref, lse_ref, kv, *refs):
+    qdo, outs, sums = refs[:peers], refs[peers:-1], refs[-1]
     stats_ref, dq_refs, part_refs = outs[0], outs[1 : peers + 1], outs[peers + 1 :]
-    kv, sums, sems = refs[-3:]
-    spans = []
-    first = 0
-    for ref in kv_refs:
-        spans.append(pl.ds(first, ref.shape[0]))
-        first += ref.shape[0]
-    copies = run_copies([(ref, kv.at[span]) for ref, span in zip(kv_refs, spans)], sems)
     row_stats(me_ref[0], qdo, lse_ref, stats_ref)
     heads = (qdo[0].shape[0] - STAT) // KB
     sums[...] = jnp.zeros_like(sums)
-    for copy in copies:
-        copy.wait()
+
+    def scores(c, h):
+        q, do = query_rows(qdo, c, h)
+        slots = [slot_ref[(c // 2 * heads + h) * NSEL + n] for n in range(NSEL)]
+        rows_kv = jnp.concatenate([kv[s] for s in slots], axis=0)
+        k = rows_kv[:, :HD]
+        v = rows_kv[:, HD:]
+        lse_row = stats_ref[0, h : h + 1, c * KB : c * KB + QB]
+        delta_row = stats_ref[1, h : h + 1, c * KB : c * KB + QB]
+        prob = jnp.exp(dot(k, q, NT) * SCALE - lse_row)
+        score = (prob * (dot(v, do, NT) - delta_row)).astype(jnp.bfloat16)
+        return c, h, slots, q, do, k, prob.astype(jnp.bfloat16), score
+
+    def gradients(c, h, slots, q, do, k, prob, score):
+        dq = dot(score, k, TN) * SCALE
+        cols = slice(h * HD, (h + 1) * HD)
+        for i in range(2):
+            dq_refs[c + i][:, cols] = dq[i * KB : (i + 1) * KB]
+        dk = dot(score, q) * SCALE
+        dv = dot(prob, do)
+        for n in range(NSEL):
+            part = slice(n * KB, (n + 1) * KB)
+            sums[slots[n], :, :HD] += dk[part]
+            sums[slots[n], :, HD:] += dv[part]
+
+    waiting = []
     for c in range(0, peers, 2):
         for h in range(heads):
-            q, do = query_rows(qdo, c, h)
-            slots = [slot_ref[(c // 2 * heads + h) * NSEL + n] for n in range(NSEL)]
-            rows_kv = jnp.concatenate([kv[s] for s in slots], axis=0)
-            k = rows_kv[:, :HD]
-            v = rows_kv[:, HD:]
-            lse_row = stats_ref[0, h : h + 1, c * KB : c * KB + QB]
-            delta_row = stats_ref[1, h : h + 1, c * KB : c * KB + QB]
-            prob = jnp.exp(dot(k, q, NT) * SCALE - lse_row)
-            score = (prob * (dot(v, do, NT) - delta_row)).astype(jnp.bfloat16)
-            dq = dot(score, k, TN) * SCALE
-            cols = slice(h * HD, (h + 1) * HD)
-            for i in range(2):
-                dq_refs[c + i][:, cols] = dq[i * KB : (i + 1) * KB]
-            dk = dot(score, q) * SCALE
-            dv = dot(prob.astype(jnp.bfloat16), do)
-            for n in range(NSEL):
-                part = slice(n * KB, (n + 1) * KB)
-                sums[slots[n], :, :HD] += dk[part]
-                sums[slots[n], :, HD:] += dv[part]
-    for part_ref, span in zip(part_refs, spans):
-        part_ref[...] = sums[span].astype(part_ref.dtype)
-
-
-def listed_terms(me, slots, lse, qdo, kv_pieces, part_types):
+            waiting.append(scores(c, h))
+            if len(waiting) > 2:
+                gradients(*waiting.pop(0))
+    for state in waiting:
+        gradients(*state)
+    first = 0
+    for part_ref in part_refs:
+        part_ref[...] = sums[first : first + part_ref.shape[0]].astype(part_ref.dtype)
+        first += part_ref.shape[0]
+
+
+def listed_terms(me, slots, lse, kv, qdo, parts):
     peers = len(qdo)
-    pieces = len(kv_pieces)
-    units = sum(piece.shape[0] for piece in kv_pieces)
-    whole = (units,) + kv_pieces[0].shape[1:]
     heads, tokens = lse.shape
     outs = pl.pallas_call(
-        functools.partial(listed_kernel, peers, pieces),
+        functools.partial(listed_kernel, peers),
         out_shape=(
             jax.ShapeDtypeStruct((2, heads, tokens), jnp.float32),
             *[jax.ShapeDtypeStruct((KB, heads * HD), jnp.float32)] * peers,
-            *[jax.ShapeDtypeStruct(p.shape, kind) for p, kind in zip(kv_pieces, part_types)],
+            *[jax.ShapeDtypeStruct((units,) + kv.shape[1:], kind) for units, kind in parts],
         ),
-        in_specs=[SMEM, SMEM] + [VMEM] * (1 + peers) + [ANY] * pieces,
-        out_specs=(VMEM,) * (1 + peers + pieces),
-        scratch_shapes=[
-            pltpu.VMEM(whole, jnp.bfloat16),
-            pltpu.VMEM(whole, jnp.float32),
-            pltpu.SemaphoreType.DMA((pieces,)),
-        ],
+        in_specs=[SMEM, SMEM] + [VMEM] * (2 + peers),
+        out_specs=(VMEM,) * (1 + peers + len(parts)),
+        scratch_shapes=[pltpu.VMEM(kv.shape, jnp.float32)],
         compiler_params=PARAMS,
         cost_estimate=pl.CostEstimate(
             flops=671_000_000, bytes_accessed=8_000_000, transcendentals=530_000
         ),
-    )(me, slots, lse, *qdo, *kv_pieces)
+    )(me, slots, lse, kv, *qdo)
     return outs[0], outs[1 : peers + 1], outs[peers + 1 :]
 
 
-def add_kernel(*refs):
-    *terms, out_ref = refs
-    total = terms[0][...].astype(jnp.float32)
-    for ref in terms[1:]:
-        total = total + ref[...].astype(jnp.float32)
-    out_ref[...] = total.astype(out_ref.dtype)
-
-
-def add_rounded(*terms):
-    return pl.pallas_call(
-        add_kernel,
-        out_shape=jax.ShapeDtypeStruct(terms[0].shape, jnp.bfloat16),
-        in_specs=[VMEM] * len(terms),
-        out_specs=VMEM,
+def add_kernel(firsts, *refs):
+    terms, out_refs = refs[: len(firsts)], refs[len(firsts) :]
+    done = 0
+    for out_ref in out_refs:
+        size = out_ref.shape[0]
+        total = None
+        for ref, first in zip(terms, firsts):
+            part = ref[first + done : first + done + size].astype(jnp.float32)
+            total = part if total is None else total + part
+        out_ref[...] = total.astype(out_ref.dtype)
+        done += size
+
+
+def add_rounded(units, *terms, cuts=1):
+    terms = [term if isinstance(term, tuple) else (term, 0) for term in terms]
+    arrays = [array for array, _ in terms]
+    piece = jax.ShapeDtypeStruct((units // cuts,) + arrays[0].shape[1:], jnp.bfloat16)
+    outs = pl.pallas_call(
+        functools.partial(add_kernel, [first for _, first in terms]),
+        out_shape=(piece,) * cuts,
+        in_specs=[VMEM] * len(arrays),
+        out_specs=(VMEM,) * cuts,
         compiler_params=PARAMS,
-    )(*terms)
-
-
-def add_blocks_kernel(terms, *refs):
-    term_refs, out_refs = refs[:terms], refs[terms:]
-    for c, out_ref in enumerate(out_refs):
-        size = out_ref.shape[0]
-        part = slice(c * size, (c + 1) * size)
-        total = term_refs[0][part].astype(jnp.float32)
-        for ref in term_refs[1:]:
-            total = total + ref[part].astype(jnp.float32)
-        out_ref[...] = total.astype(out_ref.dtype)
-
-
-def add_blocks(kv_heads, *terms):
-    peers = terms[0].shape[0] // kv_heads
-    piece = jax.ShapeDtypeStruct((kv_heads,) + terms[0].shape[1:], jnp.bfloat16)
-    return pl.pallas_call(
-        functools.partial(add_blocks_kernel, len(terms)),
-        out_shape=(piece,) * peers,
-        in_specs=[VMEM] * len(terms),
-        out_specs=(VMEM,) * peers,
-        compiler_params=PARAMS,
-    )(*terms)
-
-
-def unpack_kernel(peers, sets, me_ref, *refs):
-    dq_refs, dkv_refs = refs[:peers], refs[peers : peers * (1 + sets)]
-    gq_ref, gk_ref, gv_ref = refs[peers * (1 + sets) :]
+    )(*arrays)
+    return outs if cuts > 1 else outs[0]
+
+
+def unpack_kernel(peers, me_ref, *refs):
+    dq_refs, dkv_refs = refs[:peers], refs[peers : 2 * peers]
+    gq_ref, gk_ref, gv_ref = refs[2 * peers :]
     width = dq_refs[0].shape[1]
     kv_heads = dkv_refs[0].shape[0]
     for c in range(peers):
@@ -321,30 +304,25 @@
         gq_ref[:, lanes(source, width)] = dq_refs[c][...]
         for g in range(kv_heads):
             cols = lanes(source * kv_heads + g, HD)
-            total = dkv_refs[c][g].astype(jnp.float32)
-            for i in range(1, sets):
-                total = total + dkv_refs[i * peers + c][g].astype(jnp.float32)
-            total = total.astype(jnp.bfloat16)
-            gk_ref[:, cols] = total[:, :HD]
-            gv_ref[:, cols] = total[:, HD:]
+            gk_ref[:, cols] = dkv_refs[c][g, :, :HD]
+            gv_ref[:, cols] = dkv_refs[c][g, :, HD:]
 
 
 def unpack(me, dq, dkv):
     peers = len(dq)
     tokens, width = dq[0].shape
-    kv_width = dkv[0][0].shape[0] * peers * HD
-    flat = [piece for pieces in dkv for piece in pieces]
+    kv_width = dkv[0].shape[0] * peers * HD
     return pl.pallas_call(
-        functools.partial(unpack_kernel, peers, len(dkv)),
+        functools.partial(unpack_kernel, peers),
         out_shape=(
             jax.ShapeDtypeStruct((tokens, peers * width), jnp.bfloat16),
             jax.ShapeDtypeStruct((tokens, kv_width), jnp.bfloat16),
             jax.ShapeDtypeStruct((tokens, kv_width), jnp.bfloat16),
         ),
-        in_specs=[SMEM] + [VMEM] * (peers + len(flat)),
+        in_specs=[SMEM] + [VMEM] * (2 * peers),
         out_specs=(VMEM,) * 3,
         compiler_params=PARAMS,
-    )(me, *dq, *flat)
+    )(me, *dq, *dkv)
 
 
 def exchange(pieces):
@@ -394,7 +372,15 @@
         back = [(s, (s - 2) % shards) for s in range(shards)]
         later_me, _ = lax.optimization_barrier((me_ref, kv_pack))
         q_pieces = pack_q(later_me, queries, grad_out, outputs_saved, peers)
-        own_kv, q_pieces = lax.optimization_barrier((own_kv, q_pieces))
+        own_kv, q_pieces, per_peer = lax.optimization_barrier((own_kv, q_pieces, per_peer))
+        mine = lax.dynamic_index_in_dim(per_peer, me, 0, keepdims=False)
+        owner = mine // key_count
+        apart = (me // 2 - owner // 2) % far
+        crossed = (me ^ owner) & 1
+        piece = jnp.where(crossed == 1, far - 1 + (apart + 1) % far, apart - 1)
+        slots = piece * units + (mine % key_count ^ head_me) * kv_heads + group_of
+        slots = jnp.roll(slots, block_turn)
+        q_pieces, slots = lax.optimization_barrier((q_pieces, slots))
         qdo = exchange_rows(*q_pieces)
         same1 = lax.ppermute(own_kv, "seq", ahead)
         cross0 = lax.ppermute(own_kv, "seq", swap)
@@ -402,19 +388,15 @@
         same2 = lax.ppermute(same1, "seq", ahead)
         cross1 = lax.ppermute(same1, "seq", swap)
         cross3 = lax.ppermute(same3, "seq", swap)
-        held, cross0, cross1 = lax.optimization_barrier((same2, cross0, cross1))
+        held, cross1 = lax.optimization_barrier((same2, cross1))
         cross2 = lax.ppermute(held, "seq", swap)
-        per_peer, cross0 = lax.optimization_barrier((per_peer, cross0))
-        mine = lax.dynamic_index_in_dim(per_peer, me, 0, keepdims=False)
-        owner = mine // key_count
-        apart = (me // 2 - owner // 2) % far
-        crossed = (me ^ owner) & 1
-        piece = jnp.where(crossed == 1, far - 1 + (apart + 1) % far, apart - 1)
-        slots = piece * units + (mine % key_count ^ head_me) * kv_heads + group_of
-        slots = jnp.roll(slots, block_turn)
-        kv_pieces = [same1, same2, same3, cross3, cross0, cross1, cross2]
+        kv_all = jnp.zeros((7 * units,) + own_kv.shape[1:], jnp.bfloat16)
+        arriving = [(same1, 0), (cross0, 4), (cross1, 5), (same2, 1), (same3, 2)]
+        for array, at in arriving + [(cross2, 6), (cross3, 3)]:
+            kv_all = lax.dynamic_update_slice_in_dim(kv_all, array, at * units, 0)
         wide, low = jnp.float32, jnp.bfloat16
-        part_types = [wide, wide, low, low, wide, low, low]
+        part_types = [(1, wide), (1, wide), (2, low), (1, wide), (1, low), (1, low)]
+        part_types = [(count * units, kind) for count, kind in part_types]
     else:
         owner = per_peer // key_count
         earlier = (owner[:, :, None] == owner[:, None, :]) & (order[None, :] < order[:, None])
@@ -425,26 +407,26 @@
         used = jnp.sum(hits, axis=1).reshape(-1)
         wanted = (per_peer % key_count ^ head_me) * kv_heads + group_of[None, :]
         wanted = jnp.sum(hits * wanted[:, :, None], axis=1).reshape(-1)
-        kv_pieces = [lax.all_to_all(own_kv[wanted], "seq", 0, 0, tiled=True)]
-        part_types = [jnp.bfloat16]
+        kv_all = lax.all_to_all(own_kv[wanted], "seq", 0, 0, tiled=True)
+        part_types = [(kv_all.shape[0], jnp.bfloat16)]
         slots = jnp.roll(slots, block_turn)
         qdo = exchange_rows(*pack_q(me_ref, queries, grad_out, outputs_saved, peers))
 
-    stats, listed, parts = listed_terms(me_ref, slots, lse.T, qdo, kv_pieces, part_types)
+    stats, listed, parts = listed_terms(me_ref, slots, lse.T, kv_all, qdo, part_types)
     dq, own = own_terms(me_ref, own_kv, stats, qdo, listed)
 
     if dense:
-        stay1, stay2, away3, leave3, leave0, leave1, leave2 = parts
-        came3 = lax.ppermute(jnp.concatenate([leave3, away3], axis=0), "seq", ahead)
+        stay1, stay2, away3, leave0, leave1, leave2 = parts
         came2 = lax.ppermute(leave2, "seq", swap)
+        came3 = lax.ppermute(away3, "seq", ahead)
         came1 = lax.ppermute(leave1, "seq", swap)
-        hop = lax.ppermute(add_rounded(stay2, came2), "seq", back)
+        hop = lax.ppermute(add_rounded(units, stay2, came2), "seq", back)
         came3, dq = lax.optimization_barrier((came3, list(dq)))
         dq = exchange(dq)
-        near, came1 = lax.optimization_barrier((add_rounded(leave0, came3[:units]), came1))
+        near, came1 = lax.optimization_barrier((add_rounded(units, leave0, (came3, units)), came1))
         came0 = lax.ppermute(near, "seq", swap)
-        side = lax.ppermute(add_rounded(stay1, came1, hop), "seq", back)
-        dkv = [exchange(add_blocks(kv_heads, own, came3[units:], came0, side))]
+        side = lax.ppermute(add_rounded(units, stay1, came1, hop), "seq", back)
+        dkv = exchange(add_rounded(units, own, came3, came0, side, cuts=peers))
     else:
         parts = lax.all_to_all(parts[0], "seq", 0, 0, tiled=True)
         chosen = (jnp.arange(units)[:, None] == wanted[None, :]) & (used[None, :] > 0)
@@ -454,7 +436,7 @@
             preferred_element_type=jnp.float32,
         )
         dq = exchange(dq)
-        dkv = [exchange(add_blocks(kv_heads, own, total.reshape(own.shape)))]
+        dkv = exchange(add_rounded(units, own, total.reshape(own.shape), cuts=peers))
     return unpack(me_ref, dq, dkv)
 
 

time: 83.5 us -> 83 us (level)
  waiting for transfers between devices: 35 us -> 40.7 us
  local copies, waits for them, and re-layouts: 6.72 us -> 1.38 us
  starting transfers between devices: 28.6 us -> 26.6 us
  Pallas kernels: 11.8 us -> 12.9 us
    unnamed x15 -> x9, local copies, waits for them, and re-layouts: 5.78 us -> 0.86 us
    ppermute x1, waiting for transfers between devices: 0.75 us -> 4.65 us  [body(): cross1 = lax.ppermute(same1, 'seq', swap)]
    ppermute x1, waiting for transfers between devices: 5.65 us -> 9.38 us  [body(): same1 = lax.ppermute(own_kv, 'seq', ahead)]
    ppermute x1, waiting for transfers between devices: 4.97 us -> 1.98 us  [body(): same2 = lax.ppermute(same1, 'seq', ahead)]
    pallas_call x6, Pallas kernels: 6.97 us -> 4.4 us  [the longest x1 3.1 us: listed_terms(): pl.pallas_call(functools.partial(listed_kernel, peers), out_shape=(jax.Sh...]
    ppermute x1, waiting for transfers between devices: 5.21 us -> 7.48 us  [body(): cross2 = lax.ppermute(held, 'seq', swap)]
    pallas_call x1, Pallas kernels: 0.75 us -> 2.96 us  [pack_q(): pl.pallas_call(functools.partial(pack_q_kernel, peers), out_shape=(piece,...]
    ppermute x3, starting transfers between devices: 7.2 us -> 5.1 us  [the longest x1 2.26 us: body(): hop = lax.ppermute(add_rounded(units, stay2, came2), 'seq', back)]
  transfers between devices with their start and end apart: 25 -> 25, of which waited for: 13 -> 11; matrix products, arithmetic and copies ran while one was open for 1% -> 2% of each run, Pallas kernels for 6% -> 9%
where the time goes in v4:
time: 83 us; the launch traced here: 82.7 us
  waiting for transfers between devices  40.7 us (49%)
  starting transfers between devices  26.6 us (32%)
  Pallas kernels  12.9 us (16%)
  local copies, waits for them, and re-layouts  1.38 us (2%)
  between operations  0.93 us (1%)
    ppermute x1, waiting for transfers between devices, body(): same1 = lax.ppermute(own_kv, 'seq', ahead)  9.38 us
    ppermute x1, waiting for transfers between devices, body(): cross2 = lax.ppermute(held, 'seq', swap)  7.48 us
    ppermute x1, waiting for transfers between devices, body(): came2 = lax.ppermute(leave2, 'seq', swap)  7.22 us
    ppermute x9, starting transfers between devices, exchange(): lax.ppermute(pieces[c], 'head', [(h, h ^ c) for h in range(peers)])  6.95 us
    ppermute x1, waiting for transfers between devices, body(): cross1 = lax.ppermute(same1, 'seq', swap)  4.65 us
    ppermute x1, waiting for transfers between devices, body(): side = lax.ppermute(add_rounded(units, stay1, came1, hop), 'seq', back)  4.21 us
    ppermute x9, waiting for transfers between devices, exchange(): lax.ppermute(pieces[c], 'head', [(h, h ^ c) for h in range(peers)])  4.04 us
    pallas_call x1, Pallas kernels, own_terms(): pl.pallas_call(functools.partial(own_kernel, peers), out_shape=(piece,) *...  3.84 us
  transfers between devices with their start and end apart: 25, of which 11 were waited for; matrix products, arithmetic and copies ran while one was open for 2% of the time, Pallas kernels for 9%

profile of v4, /device:TPU:0, one launch (start us, length us, event | category | flops | bytes accessed | tf_op | source)
XLA Modules:
  0.0 82.7 jit_solution(14408831198717763758)
XLA Ops:
  0.6 1.7 %shard_map.94 = (bf16[2,64,256]{2,1,0:T(8,128)(2,1)}, bf16[2,64,256]{2,1,0:T(8,128)(2,1)}, bf16[2,64,256]{2,1,0:T(8,128)(2,1)}, bf16[2,64,256]{2,1,0:T(8,128)(2,1)}) custom-call(s32[1]{0:T(128)} %bitcast.me_ref, bf16[64,1024]{1,0:T(8,128)(2,1)} %k_ref.1, bf16[64,1024]{1,0:T(8,128)(2,1)} %v_ref.1), custom_call_target="tpu_custom_call" | custom-call | tf_op jit(solution)/shard_map/pallas_call | solution.py:63
  2.4 0.0 copy-start.2
  2.4 0.5 collective-permute-start
  2.9 2.6 %collective-permute-start.1 = (bf16[2,64,256]{2,1,0:T(8,128)(2,1)}, bf16[2,64,256]{2,1,0:T(8,128)(2,1)S(1)}, u32[]{:S(2)}, u32[]{:S(2)}) collective-permute-start(bf16[2,64,256]{2,1,0:T(8,128)(2,1)} %get-tuple-element.51), channel_id=1, source_target_pairs={{0,2},{1,3},{2,0},{3,1},{4,6},{5,7},{6,4},{7,5},{8,10},{9,11},{10,... | collective-permute-start | bytes 196616 | tf_op jit(solution)/shard_map/ppermute | solution.py:331
  5.5 0.1 collective-permute-start.2
  5.5 0.8 %copy.10 = s32[16,8,4]{2,1,0:T(8,128)S(1)} copy(s32[16,8,4]{0,2,1:T(4,128)} %param.13) | data formatting | bytes 4096 | tf_op args[6]
  6.4 0.1 reshape.13
  6.5 3.0 %shard_map.95 = (bf16[528,256]{1,0:T(8,128)(2,1)}, bf16[528,256]{1,0:T(8,128)(2,1)}, bf16[1056,256]{1,0:T(8,128)(2,1)}) custom-call(s32[1]{0:T(128)} %bitcast.me_ref, bf16[64,4096]{1,0:T(8,128)(2,1)} %q_any.1, bf16[64,4096]{1,0:T(8,128)(2,1)} %do_any.1, bf16[64,4096]{1,0:T(8,128)(2,1)} %o_any.1), custom_call_target="tpu_custom_call" | custom-call | tf_op jit(solution)/shard_map/pallas_call | solution.py:117
  9.5 0.0 collective-permute-done
  9.5 0.0 collective-permute-done.1
  9.5 0.3 collective-permute-done.2
  9.9 3.7 %collective-permute-start.7 = (bf16[8,64,256]{2,1,0:T(8,128)(2,1)S(1)}, bf16[8,64,256]{2,1,0:T(8,128)(2,1)S(1)}, u32[]{:S(2)}, u32[]{:S(2)}) collective-permute-start(bf16[8,64,256]{2,1,0:T(8,128)(2,1)S(1)} %pad_maximum_fusion.own_kv_ref), channel_id=1, source_target_pairs={{0,24},{4,28},{8,0},{12,4},{16,8},{20,12},{24,16},{28,20},{1,25},{... | collective-permute-start | bytes 786440 | tf_op jit(solution)/shard_map/ppermute | solution.py:387
  13.5 1.5 %collective-permute-start.4 = (bf16[8,64,256]{2,1,0:T(8,128)(2,1)S(1)}, bf16[8,64,256]{2,1,0:T(8,128)(2,1)S(1)}, u32[]{:S(2)}, u32[]{:S(2)}) collective-permute-start(bf16[8,64,256]{2,1,0:T(8,128)(2,1)S(1)} %pad_maximum_fusion.own_kv_ref), channel_id=1, source_target_pairs={{0,4},{4,0},{8,12},{12,8},{16,20},{20,16},{24,28},{28,24},{1,5},{5... | collective-permute-start | bytes 786440 | tf_op jit(solution)/shard_map/ppermute | solution.py:386
  15.0 0.0 collective-permute-start.3
  15.1 0.1 pad_add_fusion
  15.2 0.1 dynamic_slice.9.slot_ref
  15.2 1.4 %collective-permute-start.11 = (bf16[1056,256]{1,0:T(8,128)(2,1)}, bf16[1056,256]{1,0:T(8,128)(2,1)S(1)}, u32[]{:S(2)}, u32[]{:S(2)}) collective-permute-start(bf16[1056,256]{1,0:T(8,128)(2,1)} %get-tuple-element.67), channel_id=1, source_target_pairs={{0,2},{1,3},{2,0},{3,1},{4,6},{5,7},{6,4},{7,5},{8,10},{9,11},{10,... | collective-permute-start | bytes 1622024 | tf_op jit(solution)/shard_map/ppermute | solution.py:341
  16.7 9.4 %collective-permute-done.3 = bf16[8,64,256]{2,1,0:T(8,128)(2,1)S(1)} collective-permute-done((bf16[8,64,256]{2,1,0:T(8,128)(2,1)S(1)}, bf16[8,64,256]{2,1,0:T(8,128)(2,1)S(1)}, u32[]{:S(2)}, u32[]{:S(2)}) %collective-permute-start.3) | collective-permute-done | bytes 262176 | tf_op jit(solution)/shard_map/ppermute | solution.py:385
  26.0 1.5 %collective-permute-start.6 = (bf16[8,64,256]{2,1,0:T(8,128)(2,1)S(1)}, bf16[8,64,256]{2,1,0:T(8,128)(2,1)S(1)}, u32[]{:S(2)}, u32[]{:S(2)}) collective-permute-start(bf16[8,64,256]{2,1,0:T(8,128)(2,1)S(1)} %collective-permute-done.3), channel_id=1, source_target_pairs={{0,4},{4,0},{8,12},{12,8},{16,20},{20,16},{24,28},{28,24},{1,5},{5... | collective-permute-start | bytes 786440 | tf_op jit(solution)/shard_map/ppermute | solution.py:389
  27.6 1.6 %collective-permute-start.5 = (bf16[8,64,256]{2,1,0:T(8,128)(2,1)S(1)}, bf16[8,64,256]{2,1,0:T(8,128)(2,1)S(1)}, u32[]{:S(2)}, u32[]{:S(2)}) collective-permute-start(bf16[8,64,256]{2,1,0:T(8,128)(2,1)S(1)} %collective-permute-done.3), channel_id=1, source_target_pairs={{0,8},{4,12},{8,16},{12,20},{16,24},{20,28},{24,0},{28,4},{1,9},{5... | collective-permute-start | bytes 786440 | tf_op jit(solution)/shard_map/ppermute | solution.py:388
  29.2 0.2 dynamic_update_slice.21
  29.4 0.0 collective-permute-done.7
  29.4 0.1 collective-permute-start.10
  29.5 0.0 collective-permute-done.4
  29.5 0.6 collective-permute-start.9
  30.1 0.0 copy-start
  30.1 0.0 copy-start.1
  30.1 4.7 %collective-permute-done.6 = bf16[8,64,256]{2,1,0:T(8,128)(2,1)S(1)} collective-permute-done((bf16[8,64,256]{2,1,0:T(8,128)(2,1)S(1)}, bf16[8,64,256]{2,1,0:T(8,128)(2,1)S(1)}, u32[]{:S(2)}, u32[]{:S(2)}) %collective-permute-start.6) | collective-permute-done | bytes 262176 | tf_op jit(solution)/shard_map/ppermute | solution.py:389
  34.8 2.0 %collective-permute-done.5 = bf16[8,64,256]{2,1,0:T(8,128)(2,1)S(1)} collective-permute-done((bf16[8,64,256]{2,1,0:T(8,128)(2,1)S(1)}, bf16[8,64,256]{2,1,0:T(8,128)(2,1)S(1)}, u32[]{:S(2)}, u32[]{:S(2)}) %collective-permute-start.5) | collective-permute-done | bytes 262176 | tf_op jit(solution)/shard_map/ppermute | solution.py:388
  36.8 0.5 collective-permute-start.8
  37.3 0.0 collective-permute-done.11
  37.4 0.1 collective-permute-start.12
  37.5 7.5 %collective-permute-done.8 = bf16[8,64,256]{2,1,0:T(8,128)(2,1)S(1)} collective-permute-done((bf16[8,64,256]{2,1,0:T(8,128)(2,1)S(1)}, bf16[8,64,256]{2,1,0:T(8,128)(2,1)S(1)}, u32[]{:S(2)}, u32[]{:S(2)}) %collective-permute-start.8) | collective-permute-done | bytes 262176 | tf_op jit(solution)/shard_map/ppermute | solution.py:392
  45.0 0.0 collective-permute-done.9
  45.0 0.0 collective-permute-done.10.refs_1_
  45.0 0.0 collective-permute-done.12.refs_3_
  45.1 3.1 %shard_map.96 = (f32[2,8,256]{2,1,0:T(8,128)S(1)}, f32[64,1024]{1,0:T(8,128)S(1)}, f32[64,1024]{1,0:T(8,128)S(1)}, f32[64,1024]{1,0:T(8,128)S(1)}, f32[64,1024]{...) custom-call(s32[1]{0:T(128)} %bitcast.me_ref, ...), custom_call_target="tpu_custom_call" | custom-call | flops 671000000 | bytes 8000000 | tf_op jit(solution)/shard_map/pallas_call | solution.py:252
  48.2 1.7 %collective-permute-start.13 = (bf16[16,64,256]{2,1,0:T(8,128)(2,1)S(1)}, bf16[16,64,256]{2,1,0:T(8,128)(2,1)S(1)}, u32[]{:S(2)}, u32[]{:S(2)}) collective-permute-start(bf16[16,64,256]{2,1,0:T(8,128)(2,1)S(1)} %get-tuple-element.68), channel_id=1, source_target_pairs={{0,8},{4,12},{8,16},{12,20},{16,24},{20,28},{24,0},{28,4},{1,9},{5... | collective-permute-start | bytes 1572872 | tf_op jit(solution)/shard_map/ppermute | solution.py:421
  49.8 1.5 %collective-permute-start.19 = (bf16[8,64,256]{2,1,0:T(8,128)(2,1)S(1)}, bf16[8,64,256]{2,1,0:T(8,128)(2,1)S(1)}, u32[]{:S(2)}, u32[]{:S(2)}) collective-permute-start(bf16[8,64,256]{2,1,0:T(8,128)(2,1)S(1)} %get-tuple-element.90), channel_id=1, source_target_pairs={{0,4},{4,0},{8,12},{12,8},{16,20},{20,16},{24,28},{28,24},{1,5},{5... | collective-permute-start | bytes 786440 | tf_op jit(solution)/shard_map/ppermute | solution.py:420
  51.4 0.5 collective-permute-start.17
  51.9 7.2 %collective-permute-done.19.refs_1_ = bf16[8,64,256]{2,1,0:T(8,128)(2,1)S(1)} collective-permute-done((bf16[8,64,256]{2,1,0:T(8,128)(2,1)S(1)}, bf16[8,64,256]{2,1,0:T(8,128)(2,1)S(1)}, u32[]{:S(2)}, u32[]{:S(2)}) %collective-permute-start.19) | collective-permute-done | bytes 262176 | tf_op jit(solution)/shard_map/ppermute | solution.py:420
  59.1 2.3 %collective-permute-start.20 = (bf16[8,64,256]{2,1,0:T(8,128)(2,1)S(1)}, bf16[8,64,256]{2,1,0:T(8,128)(2,1)S(1)}, u32[]{:S(2)}, u32[]{:S(2)}) collective-permute-start(bf16[8,64,256]{2,1,0:T(8,128)(2,1)S(1)} %shard_map.99), channel_id=1, source_target_pairs={{0,24},{4,28},{8,0},{12,4},{16,8},{20,12},{24,16},{28,20},{1,25},{... | collective-permute-start | bytes 786440 | tf_op jit(solution)/shard_map/ppermute | solution.py:423
  61.4 3.8 %shard_map.97 = (bf16[64,1024]{1,0:T(8,128)(2,1)S(1)}, bf16[64,1024]{1,0:T(8,128)(2,1)S(1)}, bf16[64,1024]{1,0:T(8,128)(2,1)S(1)}, bf16[64,1024]{1,0:T(8,128)(2,1)S(1)}, f32[8,64,256]{2,1,0:T(8,128)S(1)}) custom-call(s32[1]{0:T(128)} %bitcast.me_ref, bf16[8,64,256]{2,1,0:T(8,128)(2,1)S(1)} %pad_maximum_fusion.own_kv_ref, ...), custom_call_target="tpu_custom_call" | custom-call | flops 335000000 | bytes 4000000 | tf_op jit(solution)/shard_map/pallas_call | solution.py:175
  65.2 0.0 collective-permute-done.13.refs_1_
  65.2 0.1 shard_map.98
  65.3 1.6 %collective-permute-start.18 = (bf16[8,64,256]{2,1,0:T(8,128)(2,1)S(1)}, bf16[8,64,256]{2,1,0:T(8,128)(2,1)S(1)}, u32[]{:S(2)}, u32[]{:S(2)}) collective-permute-start(bf16[8,64,256]{2,1,0:T(8,128)(2,1)S(1)} %shard_map.98), channel_id=1, source_target_pairs={{0,4},{4,0},{8,12},{12,8},{16,20},{20,16},{24,28},{28,24},{1,5},{5... | collective-permute-start | bytes 786440 | tf_op jit(solution)/shard_map/ppermute | solution.py:427
  66.9 1.6 %collective-permute-done.20.refs_2_ = bf16[8,64,256]{2,1,0:T(8,128)(2,1)S(1)} collective-permute-done((bf16[8,64,256]{2,1,0:T(8,128)(2,1)S(1)}, bf16[8,64,256]{2,1,0:T(8,128)(2,1)S(1)}, u32[]{:S(2)}, u32[]{:S(2)}) %collective-permute-start.20) | collective-permute-done | bytes 262176 | tf_op jit(solution)/shard_map/ppermute | solution.py:423
  68.5 0.1 shard_map.100
  68.6 1.2 %collective-permute-start.21 = (bf16[8,64,256]{2,1,0:T(8,128)(2,1)S(1)}, bf16[8,64,256]{2,1,0:T(8,128)(2,1)S(1)}, u32[]{:S(2)}, u32[]{:S(2)}) collective-permute-start(bf16[8,64,256]{2,1,0:T(8,128)(2,1)S(1)} %shard_map.100), channel_id=1, source_target_pairs={{0,24},{4,28},{8,0},{12,4},{16,8},{20,12},{24,16},{28,20},{1,25},{... | collective-permute-start | bytes 786440 | tf_op jit(solution)/shard_map/ppermute | solution.py:428
  69.8 0.0 collective-permute-start.14
  69.8 1.7 %collective-permute-start.15 = (bf16[64,1024]{1,0:T(8,128)(2,1)S(1)}, bf16[64,1024]{1,0:T(8,128)(2,1)S(1)}, u32[]{:S(2)}, u32[]{:S(2)}) collective-permute-start(bf16[64,1024]{1,0:T(8,128)(2,1)S(1)} %get-tuple-element.80), channel_id=1, source_target_pairs={{0,2},{1,3},{2,0},{3,1},{4,6},{5,7},{6,4},{7,5},{8,10},{9,11},{10,... | collective-permute-start | bytes 393224 | tf_op jit(solution)/shard_map/ppermute | solution.py:331
  71.4 0.2 collective-permute-start.16
  71.6 0.1 collective-permute-done.18.refs_2_
  71.8 4.2 %collective-permute-done.21.refs_3_ = bf16[8,64,256]{2,1,0:T(8,128)(2,1)S(1)} collective-permute-done((bf16[8,64,256]{2,1,0:T(8,128)(2,1)S(1)}, bf16[8,64,256]{2,1,0:T(8,128)(2,1)S(1)}, u32[]{:S(2)}, u32[]{:S(2)}) %collective-permute-start.21) | collective-permute-done | bytes 262176 | tf_op jit(solution)/shard_map/ppermute | solution.py:428
  76.0 0.1 shard_map.101
  76.1 0.1 collective-permute-start.22
  76.2 1.5 %collective-permute-start.23 = (bf16[2,64,256]{2,1,0:T(8,128)(2,1)S(1)}, bf16[2,64,256]{2,1,0:T(8,128)(2,1)S(1)}, u32[]{:S(2)}, u32[]{:S(2)}) collective-permute-start(bf16[2,64,256]{2,1,0:T(8,128)(2,1)S(1)} %get-tuple-element.93), channel_id=1, source_target_pairs={{0,2},{1,3},{2,0},{3,1},{4,6},{5,7},{6,4},{7,5},{8,10},{9,11},{10,... | collective-permute-start | bytes 196616 | tf_op jit(solution)/shard_map/ppermute | solution.py:331
  77.7 0.0 collective-permute-done.14.refs_1_
  77.7 0.4 collective-permute-start.24
  78.1 0.0 collective-permute-done.15.refs_2_
  78.1 0.0 collective-permute-done.16.refs_3_
  78.1 2.6 %collective-permute-done.23.refs_6_ = bf16[2,64,256]{2,1,0:T(8,128)(2,1)S(1)} collective-permute-done((bf16[2,64,256]{2,1,0:T(8,128)(2,1)S(1)}, bf16[2,64,256]{2,1,0:T(8,128)(2,1)S(1)}, u32[]{:S(2)}, u32[]{:S(2)}) %collective-permute-start.23) | collective-permute-done | bytes 65568 | tf_op jit(solution)/shard_map/ppermute | solution.py:331
  80.7 1.0 %collective-permute-done.24.refs_7_ = bf16[2,64,256]{2,1,0:T(8,128)(2,1)S(1)} collective-permute-done((bf16[2,64,256]{2,1,0:T(8,128)(2,1)S(1)}, bf16[2,64,256]{2,1,0:T(8,128)(2,1)S(1)}, u32[]{:S(2)}, u32[]{:S(2)}) %collective-permute-start.24) | collective-permute-done | bytes 65568 | tf_op jit(solution)/shard_map/ppermute | solution.py:331
  81.8 1.0 %shard_map.102 = (bf16[64,4096]{1,0:T(8,128)(2,1)}, bf16[64,1024]{1,0:T(8,128)(2,1)}, bf16[64,1024]{1,0:T(8,128)(2,1)}) custom-call(s32[1]{0:T(128)} %bitcast.me_ref, bf16[64,1024]{1,0:T(8,128)(2,1)S(1)} %get-tuple-element.78.refs_0_, bf16[64,1024]{1,0:T(8,128)(2,1)S(1)} %collective-permute-done.14.refs_1_, ...), custom_call_target="tpu_custom_call" | custom-call | tf_op jit(solution)/shard_map/pallas_call | solution.py:315
  (17 shorter events, 0.3 us)
Async XLA Ops:
  2.4 7.4 %copy-start.2 = (bf16[2,64,256]{2,1,0:T(8,128)(2,1)S(1)}, bf16[2,64,256]{2,1,0:T(8,128)(2,1)}, u32[]{:S(2)}) copy-start(bf16[2,64,256]{2,1,0:T(8,128)(2,1)} %get-tuple-element.49) | copy-start | bytes 196612
  2.4 7.1 %collective-permute-start = (bf16[2,64,256]{2,1,0:T(8,128)(2,1)}, bf16[2,64,256]{2,1,0:T(8,128)(2,1)S(1)}, u32[]{:S(2)}, u32[]{:S(2)}) collective-permute-start(bf16[2,64,256]{2,1,0:T(8,128)(2,1)} %get-tuple-element.50), channel_id=1, source_target_pairs={{0,1},{1,0},{2,3},{3,2},{4,5},{5,4},{6,7},{7,6},{8,9},{9,8},{10,11... | collective-permute-start | bytes 196616 | tf_op jit(solution)/shard_map/ppermute | solution.py:331
  2.9 6.6 %collective-permute-start.1 = (bf16[2,64,256]{2,1,0:T(8,128)(2,1)}, bf16[2,64,256]{2,1,0:T(8,128)(2,1)S(1)}, u32[]{:S(2)}, u32[]{:S(2)}) collective-permute-start(bf16[2,64,256]{2,1,0:T(8,128)(2,1)} %get-tuple-element.51), channel_id=1, source_target_pairs={{0,2},{1,3},{2,0},{3,1},{4,6},{5,7},{6,4},{7,5},{8,10},{9,11},{10,... | collective-permute-start | bytes 196616 | tf_op jit(solution)/shard_map/ppermute | solution.py:331
  5.5 4.3 %collective-permute-start.2 = (bf16[2,64,256]{2,1,0:T(8,128)(2,1)}, bf16[2,64,256]{2,1,0:T(8,128)(2,1)S(1)}, u32[]{:S(2)}, u32[]{:S(2)}) collective-permute-start(bf16[2,64,256]{2,1,0:T(8,128)(2,1)} %get-tuple-element.52), channel_id=1, source_target_pairs={{0,3},{1,2},{2,1},{3,0},{4,7},{5,6},{6,5},{7,4},{8,11},{9,10},{10,... | collective-permute-start | bytes 196616 | tf_op jit(solution)/shard_map/ppermute | solution.py:331
  9.5 19.9 %copy-start.3 = (bf16[528,256]{1,0:T(8,128)(2,1)S(1)}, bf16[528,256]{1,0:T(8,128)(2,1)}, u32[]{:S(2)}) copy-start(bf16[528,256]{1,0:T(8,128)(2,1)} %get-tuple-element.66) | copy-start | bytes 811012
  9.9 19.5 %collective-permute-start.7 = (bf16[8,64,256]{2,1,0:T(8,128)(2,1)S(1)}, bf16[8,64,256]{2,1,0:T(8,128)(2,1)S(1)}, u32[]{:S(2)}, u32[]{:S(2)}) collective-permute-start(bf16[8,64,256]{2,1,0:T(8,128)(2,1)S(1)} %pad_maximum_fusion.own_kv_ref), channel_id=1, source_target_pairs={{0,24},{4,28},{8,0},{12,4},{16,8},{20,12},{24,16},{28,20},{1,25},{... | collective-permute-start | bytes 786440 | tf_op jit(solution)/shard_map/ppermute | solution.py:387
  13.5 16.0 %collective-permute-start.4 = (bf16[8,64,256]{2,1,0:T(8,128)(2,1)S(1)}, bf16[8,64,256]{2,1,0:T(8,128)(2,1)S(1)}, u32[]{:S(2)}, u32[]{:S(2)}) collective-permute-start(bf16[8,64,256]{2,1,0:T(8,128)(2,1)S(1)} %pad_maximum_fusion.own_kv_ref), channel_id=1, source_target_pairs={{0,4},{4,0},{8,12},{12,8},{16,20},{20,16},{24,28},{28,24},{1,5},{5... | collective-permute-start | bytes 786440 | tf_op jit(solution)/shard_map/ppermute | solution.py:386
  15.0 11.0 %collective-permute-start.3 = (bf16[8,64,256]{2,1,0:T(8,128)(2,1)S(1)}, bf16[8,64,256]{2,1,0:T(8,128)(2,1)S(1)}, u32[]{:S(2)}, u32[]{:S(2)}) collective-permute-start(bf16[8,64,256]{2,1,0:T(8,128)(2,1)S(1)} %pad_maximum_fusion.own_kv_ref), channel_id=1, source_target_pairs={{0,8},{4,12},{8,16},{12,20},{16,24},{20,28},{24,0},{28,4},{1,9},{5... | collective-permute-start | bytes 786440 | tf_op jit(solution)/shard_map/ppermute | solution.py:385
  15.2 22.1 %collective-permute-start.11 = (bf16[1056,256]{1,0:T(8,128)(2,1)}, bf16[1056,256]{1,0:T(8,128)(2,1)S(1)}, u32[]{:S(2)}, u32[]{:S(2)}) collective-permute-start(bf16[1056,256]{1,0:T(8,128)(2,1)} %get-tuple-element.67), channel_id=1, source_target_pairs={{0,2},{1,3},{2,0},{3,1},{4,6},{5,7},{6,4},{7,5},{8,10},{9,11},{10,... | collective-permute-start | bytes 1622024 | tf_op jit(solution)/shard_map/ppermute | solution.py:341
  26.0 8.7 %collective-permute-start.6 = (bf16[8,64,256]{2,1,0:T(8,128)(2,1)S(1)}, bf16[8,64,256]{2,1,0:T(8,128)(2,1)S(1)}, u32[]{:S(2)}, u32[]{:S(2)}) collective-permute-start(bf16[8,64,256]{2,1,0:T(8,128)(2,1)S(1)} %collective-permute-done.3), channel_id=1, source_target_pairs={{0,4},{4,0},{8,12},{12,8},{16,20},{20,16},{24,28},{28,24},{1,5},{5... | collective-permute-start | bytes 786440 | tf_op jit(solution)/shard_map/ppermute | solution.py:389
  27.6 9.2 %collective-permute-start.5 = (bf16[8,64,256]{2,1,0:T(8,128)(2,1)S(1)}, bf16[8,64,256]{2,1,0:T(8,128)(2,1)S(1)}, u32[]{:S(2)}, u32[]{:S(2)}) collective-permute-start(bf16[8,64,256]{2,1,0:T(8,128)(2,1)S(1)} %collective-permute-done.3), channel_id=1, source_target_pairs={{0,8},{4,12},{8,16},{12,20},{16,24},{20,28},{24,0},{28,4},{1,9},{5... | collective-permute-start | bytes 786440 | tf_op jit(solution)/shard_map/ppermute | solution.py:388
  29.4 15.6 %collective-permute-start.10 = (bf16[528,256]{1,0:T(8,128)(2,1)S(1)}, bf16[528,256]{1,0:T(8,128)(2,1)S(1)}, u32[]{:S(2)}, u32[]{:S(2)}) collective-permute-start(bf16[528,256]{1,0:T(8,128)(2,1)S(1)} %copy-done.3), channel_id=1, source_target_pairs={{0,1},{1,0},{2,3},{3,2},{4,5},{5,4},{6,7},{7,6},{8,9},{9,8},{10,11... | collective-permute-start | bytes 811016 | tf_op jit(solution)/shard_map/ppermute | solution.py:342
  29.5 15.5 %collective-permute-start.9 = (bf16[8,64,256]{2,1,0:T(8,128)(2,1)S(1)}, bf16[8,64,256]{2,1,0:T(8,128)(2,1)S(1)}, u32[]{:S(2)}, u32[]{:S(2)}) collective-permute-start(bf16[8,64,256]{2,1,0:T(8,128)(2,1)S(1)} %collective-permute-done.7), channel_id=1, source_target_pairs={{0,4},{4,0},{8,12},{12,8},{16,20},{20,16},{24,28},{28,24},{1,5},{5... | collective-permute-start | bytes 786440 | tf_op jit(solution)/shard_map/ppermute | solution.py:390
  30.1 14.9 %copy-start = (bf16[528,256]{1,0:T(8,128)(2,1)S(1)}, bf16[528,256]{1,0:T(8,128)(2,1)}, u32[]{:S(2)}) copy-start(bf16[528,256]{1,0:T(8,128)(2,1)} %get-tuple-element.65.refs_0_) | copy-start | bytes 811012
  30.1 14.9 %copy-start.1 = (f32[256,8]{0,1:T(8,128)S(1)}, f32[256,8]{0,1:T(8,128)}, u32[]{:S(2)}) copy-start(f32[256,8]{0,1:T(8,128)} %param.12) | copy-start | bytes 24580
  36.8 8.2 %collective-permute-start.8 = (bf16[8,64,256]{2,1,0:T(8,128)(2,1)S(1)}, bf16[8,64,256]{2,1,0:T(8,128)(2,1)S(1)}, u32[]{:S(2)}, u32[]{:S(2)}) collective-permute-start(bf16[8,64,256]{2,1,0:T(8,128)(2,1)S(1)} %collective-permute-done.5), channel_id=1, source_target_pairs={{0,4},{4,0},{8,12},{12,8},{16,20},{20,16},{24,28},{28,24},{1,5},{5... | collective-permute-start | bytes 786440 | tf_op jit(solution)/shard_map/ppermute | solution.py:392
  37.4 7.7 %collective-permute-start.12 = (bf16[528,256]{1,0:T(8,128)(2,1)S(1)}, bf16[528,256]{1,0:T(8,128)(2,1)S(1)}, u32[]{:S(2)}, u32[]{:S(2)}) collective-permute-start(bf16[528,256]{1,0:T(8,128)(2,1)S(1)} %get-tuple-element.95), channel_id=1, source_target_pairs={{0,1},{1,0},{2,3},{3,2},{4,5},{5,4},{6,7},{7,6},{8,9},{9,8},{10,11... | collective-permute-start | bytes 811016 | tf_op jit(solution)/shard_map/ppermute | solution.py:343
  48.2 17.1 %collective-permute-start.13 = (bf16[16,64,256]{2,1,0:T(8,128)(2,1)S(1)}, bf16[16,64,256]{2,1,0:T(8,128)(2,1)S(1)}, u32[]{:S(2)}, u32[]{:S(2)}) collective-permute-start(bf16[16,64,256]{2,1,0:T(8,128)(2,1)S(1)} %get-tuple-element.68), channel_id=1, source_target_pairs={{0,8},{4,12},{8,16},{12,20},{16,24},{20,28},{24,0},{28,4},{1,9},{5... | collective-permute-start | bytes 1572872 | tf_op jit(solution)/shard_map/ppermute | solution.py:421
  49.8 9.2 %collective-permute-start.19 = (bf16[8,64,256]{2,1,0:T(8,128)(2,1)S(1)}, bf16[8,64,256]{2,1,0:T(8,128)(2,1)S(1)}, u32[]{:S(2)}, u32[]{:S(2)}) collective-permute-start(bf16[8,64,256]{2,1,0:T(8,128)(2,1)S(1)} %get-tuple-element.90), channel_id=1, source_target_pairs={{0,4},{4,0},{8,12},{12,8},{16,20},{20,16},{24,28},{28,24},{1,5},{5... | collective-permute-start | bytes 786440 | tf_op jit(solution)/shard_map/ppermute | solution.py:420
  51.4 14.0 %collective-permute-start.17 = (bf16[8,64,256]{2,1,0:T(8,128)(2,1)S(1)}, bf16[8,64,256]{2,1,0:T(8,128)(2,1)S(1)}, u32[]{:S(2)}, u32[]{:S(2)}) collective-permute-start(bf16[8,64,256]{2,1,0:T(8,128)(2,1)S(1)} %get-tuple-element.85), channel_id=1, source_target_pairs={{0,4},{4,0},{8,12},{12,8},{16,20},{20,16},{24,28},{28,24},{1,5},{5... | collective-permute-start | bytes 786440 | tf_op jit(solution)/shard_map/ppermute | solution.py:422
  59.1 9.4 %collective-permute-start.20 = (bf16[8,64,256]{2,1,0:T(8,128)(2,1)S(1)}, bf16[8,64,256]{2,1,0:T(8,128)(2,1)S(1)}, u32[]{:S(2)}, u32[]{:S(2)}) collective-permute-start(bf16[8,64,256]{2,1,0:T(8,128)(2,1)S(1)} %shard_map.99), channel_id=1, source_target_pairs={{0,24},{4,28},{8,0},{12,4},{16,8},{20,12},{24,16},{28,20},{1,25},{... | collective-permute-start | bytes 786440 | tf_op jit(solution)/shard_map/ppermute | solution.py:423
  65.3 6.4 %collective-permute-start.18 = (bf16[8,64,256]{2,1,0:T(8,128)(2,1)S(1)}, bf16[8,64,256]{2,1,0:T(8,128)(2,1)S(1)}, u32[]{:S(2)}, u32[]{:S(2)}) collective-permute-start(bf16[8,64,256]{2,1,0:T(8,128)(2,1)S(1)} %shard_map.98), channel_id=1, source_target_pairs={{0,4},{4,0},{8,12},{12,8},{16,20},{20,16},{24,28},{28,24},{1,5},{5... | collective-permute-start | bytes 786440 | tf_op jit(solution)/shard_map/ppermute | solution.py:427
  68.6 7.4 %collective-permute-start.21 = (bf16[8,64,256]{2,1,0:T(8,128)(2,1)S(1)}, bf16[8,64,256]{2,1,0:T(8,128)(2,1)S(1)}, u32[]{:S(2)}, u32[]{:S(2)}) collective-permute-start(bf16[8,64,256]{2,1,0:T(8,128)(2,1)S(1)} %shard_map.100), channel_id=1, source_target_pairs={{0,24},{4,28},{8,0},{12,4},{16,8},{20,12},{24,16},{28,20},{1,25},{... | collective-permute-start | bytes 786440 | tf_op jit(solution)/shard_map/ppermute | solution.py:428
  69.8 7.9 %collective-permute-start.14 = (bf16[64,1024]{1,0:T(8,128)(2,1)S(1)}, bf16[64,1024]{1,0:T(8,128)(2,1)S(1)}, u32[]{:S(2)}, u32[]{:S(2)}) collective-permute-start(bf16[64,1024]{1,0:T(8,128)(2,1)S(1)} %get-tuple-element.79), channel_id=1, source_target_pairs={{0,1},{1,0},{2,3},{3,2},{4,5},{5,4},{6,7},{7,6},{8,9},{9,8},{10,11... | collective-permute-start | bytes 393224 | tf_op jit(solution)/shard_map/ppermute | solution.py:331
  69.8 8.3 %collective-permute-start.15 = (bf16[64,1024]{1,0:T(8,128)(2,1)S(1)}, bf16[64,1024]{1,0:T(8,128)(2,1)S(1)}, u32[]{:S(2)}, u32[]{:S(2)}) collective-permute-start(bf16[64,1024]{1,0:T(8,128)(2,1)S(1)} %get-tuple-element.80), channel_id=1, source_target_pairs={{0,2},{1,3},{2,0},{3,1},{4,6},{5,7},{6,4},{7,5},{8,10},{9,11},{10,... | collective-permute-start | bytes 393224 | tf_op jit(solution)/shard_map/ppermute | solution.py:331
  71.4 6.7 %collective-permute-start.16 = (bf16[64,1024]{1,0:T(8,128)(2,1)S(1)}, bf16[64,1024]{1,0:T(8,128)(2,1)S(1)}, u32[]{:S(2)}, u32[]{:S(2)}) collective-permute-start(bf16[64,1024]{1,0:T(8,128)(2,1)S(1)} %get-tuple-element.81), channel_id=1, source_target_pairs={{0,3},{1,2},{2,1},{3,0},{4,7},{5,6},{6,5},{7,4},{8,11},{9,10},{10,... | collective-permute-start | bytes 393224 | tf_op jit(solution)/shard_map/ppermute | solution.py:331
  76.1 2.0 %collective-permute-start.22 = (bf16[2,64,256]{2,1,0:T(8,128)(2,1)S(1)}, bf16[2,64,256]{2,1,0:T(8,128)(2,1)S(1)}, u32[]{:S(2)}, u32[]{:S(2)}) collective-permute-start(bf16[2,64,256]{2,1,0:T(8,128)(2,1)S(1)} %get-tuple-element.92), channel_id=1, source_target_pairs={{0,1},{1,0},{2,3},{3,2},{4,5},{5,4},{6,7},{7,6},{8,9},{9,8},{10,11... | collective-permute-start | bytes 196616 | tf_op jit(solution)/shard_map/ppermute | solution.py:331
  76.2 4.5 %collective-permute-start.23 = (bf16[2,64,256]{2,1,0:T(8,128)(2,1)S(1)}, bf16[2,64,256]{2,1,0:T(8,128)(2,1)S(1)}, u32[]{:S(2)}, u32[]{:S(2)}) collective-permute-start(bf16[2,64,256]{2,1,0:T(8,128)(2,1)S(1)} %get-tuple-element.93), channel_id=1, source_target_pairs={{0,2},{1,3},{2,0},{3,1},{4,6},{5,7},{6,4},{7,5},{8,10},{9,11},{10,... | collective-permute-start | bytes 196616 | tf_op jit(solution)/shard_map/ppermute | solution.py:331
  77.7 4.1 %collective-permute-start.24 = (bf16[2,64,256]{2,1,0:T(8,128)(2,1)S(1)}, bf16[2,64,256]{2,1,0:T(8,128)(2,1)S(1)}, u32[]{:S(2)}, u32[]{:S(2)}) collective-permute-start(bf16[2,64,256]{2,1,0:T(8,128)(2,1)S(1)} %get-tuple-element.94), channel_id=1, source_target_pairs={{0,3},{1,2},{2,1},{3,0},{4,7},{5,6},{6,5},{7,4},{8,11},{9,10},{10,... | collective-permute-start | bytes 196616 | tf_op jit(solution)/shard_map/ppermute | solution.py:331

commit v5 on v4

--- a/solution.py
+++ b/solution.py
@@ -136,7 +136,9 @@
 def own_kernel(peers, me_ref, own_kv_ref, stats_ref, *refs):
     qdo = refs[:peers]
     listed_refs = refs[peers : 2 * peers]
-    dq_refs, own_ref = refs[2 * peers : 3 * peers], refs[3 * peers]
+    half = peers // 2
+    *dq_refs, far_ref, own_ref = refs[2 * peers :]
+    dq_refs += [far_ref.at[i * KB : (i + 1) * KB] for i in range(half)]
     heads = (qdo[0].shape[0] - STAT) // KB
     kv_heads = heads // GROUP
     key_row = lax.broadcasted_iota(jnp.int32, (QB, QB), 0)
@@ -171,18 +173,21 @@
 
 def own_terms(me, own_kv, stats, qdo, listed):
     peers = len(qdo)
-    piece = jax.ShapeDtypeStruct(listed[0].shape, jnp.bfloat16)
+    half = peers // 2
+    rows, width = listed[0].shape
+    piece = jax.ShapeDtypeStruct((rows, width), jnp.bfloat16)
+    far = jax.ShapeDtypeStruct((half * rows, width), jnp.bfloat16)
     outs = pl.pallas_call(
         functools.partial(own_kernel, peers),
-        out_shape=(piece,) * peers + (jax.ShapeDtypeStruct(own_kv.shape, jnp.float32),),
+        out_shape=(piece,) * half + (far, jax.ShapeDtypeStruct(own_kv.shape, jnp.float32)),
         in_specs=[SMEM] + [VMEM] * (2 + 2 * peers),
-        out_specs=(VMEM,) * (peers + 1),
+        out_specs=(VMEM,) * (half + 2),
         compiler_params=PARAMS,
         cost_estimate=pl.CostEstimate(
             flops=335_000_000, bytes_accessed=4_000_000, transcendentals=260_000
         ),
     )(me, own_kv, stats, *qdo, *listed)
-    return outs[:peers], outs[peers]
+    return list(outs[:-1]), outs[-1]
 
 
 def row_stats(me, qdo, lse_ref, stats_ref):
@@ -280,49 +285,61 @@
         done += size
 
 
-def add_rounded(units, *terms, cuts=1):
+def add_rounded(units, *terms, cuts=1, kind=jnp.bfloat16, bytes_moved=2_000_000):
     terms = [term if isinstance(term, tuple) else (term, 0) for term in terms]
     arrays = [array for array, _ in terms]
-    piece = jax.ShapeDtypeStruct((units // cuts,) + arrays[0].shape[1:], jnp.bfloat16)
+    piece = jax.ShapeDtypeStruct((units // cuts,) + arrays[0].shape[1:], kind)
     outs = pl.pallas_call(
         functools.partial(add_kernel, [first for _, first in terms]),
         out_shape=(piece,) * cuts,
         in_specs=[VMEM] * len(arrays),
         out_specs=(VMEM,) * cuts,
         compiler_params=PARAMS,
+        cost_estimate=pl.CostEstimate(
+            flops=2_000_000, bytes_accessed=bytes_moved, transcendentals=0
+        ),
     )(*arrays)
     return outs if cuts > 1 else outs[0]
 
 
-def unpack_kernel(peers, me_ref, *refs):
-    dq_refs, dkv_refs = refs[:peers], refs[peers : 2 * peers]
-    gq_ref, gk_ref, gv_ref = refs[2 * peers :]
-    width = dq_refs[0].shape[1]
-    kv_heads = dkv_refs[0].shape[0]
+def unpack_q_kernel(peers, me_ref, *refs):
+    gq_ref = refs[peers]
+    width = refs[0].shape[1]
     for c in range(peers):
-        source = me_ref[0] ^ c
-        gq_ref[:, lanes(source, width)] = dq_refs[c][...]
+        gq_ref[:, lanes(me_ref[0] ^ c, width)] = refs[c][...]
+
+
+def unpack_kv_kernel(peers, me_ref, *refs):
+    gk_ref, gv_ref = refs[peers:]
+    kv_heads = refs[0].shape[0]
+    for c in range(peers):
         for g in range(kv_heads):
-            cols = lanes(source * kv_heads + g, HD)
-            gk_ref[:, cols] = dkv_refs[c][g, :, :HD]
-            gv_ref[:, cols] = dkv_refs[c][g, :, HD:]
+            cols = lanes((me_ref[0] ^ c) * kv_heads + g, HD)
+            gk_ref[:, cols] = refs[c][g, :, :HD]
+            gv_ref[:, cols] = refs[c][g, :, HD:]
 
 
 def unpack(me, dq, dkv):
     peers = len(dq)
     tokens, width = dq[0].shape
     kv_width = dkv[0].shape[0] * peers * HD
-    return pl.pallas_call(
-        functools.partial(unpack_kernel, peers),
-        out_shape=(
-            jax.ShapeDtypeStruct((tokens, peers * width), jnp.bfloat16),
-            jax.ShapeDtypeStruct((tokens, kv_width), jnp.bfloat16),
-            jax.ShapeDtypeStruct((tokens, kv_width), jnp.bfloat16),
-        ),
-        in_specs=[SMEM] + [VMEM] * (2 * peers),
-        out_specs=(VMEM,) * 3,
+    spec = [SMEM] + [VMEM] * peers
+    grad_q = pl.pallas_call(
+        functools.partial(unpack_q_kernel, peers),
+        out_shape=jax.ShapeDtypeStruct((tokens, peers * width), jnp.bfloat16),
+        in_specs=spec,
+        out_specs=VMEM,
         compiler_params=PARAMS,
-    )(me, *dq, *dkv)
+    )(me, *dq)
+    grad_q, dkv[0] = lax.optimization_barrier((grad_q, dkv[0]))
+    grad_k, grad_v = pl.pallas_call(
+        functools.partial(unpack_kv_kernel, peers),
+        out_shape=(jax.ShapeDtypeStruct((tokens, kv_width), jnp.bfloat16),) * 2,
+        in_specs=spec,
+        out_specs=(VMEM, VMEM),
+        compiler_params=PARAMS,
+    )(me, *dkv)
+    return grad_q, grad_k, grad_v
 
 
 def exchange(pieces):
@@ -370,9 +387,14 @@
         swap = [(s, s ^ 1) for s in range(shards)]
         ahead = [(s, (s + 2) % shards) for s in range(shards)]
         back = [(s, (s - 2) % shards) for s in range(shards)]
-        later_me, _ = lax.optimization_barrier((me_ref, kv_pack))
+        same1 = lax.ppermute(own_kv, "seq", ahead)
+        cross0 = lax.ppermute(own_kv, "seq", swap)
+        later_me, held = lax.optimization_barrier((me_ref, own_kv))
         q_pieces = pack_q(later_me, queries, grad_out, outputs_saved, peers)
-        own_kv, q_pieces, per_peer = lax.optimization_barrier((own_kv, q_pieces, per_peer))
+        held, q_pieces = lax.optimization_barrier((held, q_pieces))
+        same3 = lax.ppermute(held, "seq", back)
+        qdo = exchange_rows(*q_pieces)
+        per_peer, same1 = lax.optimization_barrier((per_peer, same1))
         mine = lax.dynamic_index_in_dim(per_peer, me, 0, keepdims=False)
         owner = mine // key_count
         apart = (me // 2 - owner // 2) % far
@@ -380,11 +402,6 @@
         piece = jnp.where(crossed == 1, far - 1 + (apart + 1) % far, apart - 1)
         slots = piece * units + (mine % key_count ^ head_me) * kv_heads + group_of
         slots = jnp.roll(slots, block_turn)
-        q_pieces, slots = lax.optimization_barrier((q_pieces, slots))
-        qdo = exchange_rows(*q_pieces)
-        same1 = lax.ppermute(own_kv, "seq", ahead)
-        cross0 = lax.ppermute(own_kv, "seq", swap)
-        same3 = lax.ppermute(own_kv, "seq", back)
         same2 = lax.ppermute(same1, "seq", ahead)
         cross1 = lax.ppermute(same1, "seq", swap)
         cross3 = lax.ppermute(same3, "seq", swap)
@@ -420,13 +437,16 @@
         came2 = lax.ppermute(leave2, "seq", swap)
         came3 = lax.ppermute(away3, "seq", ahead)
         came1 = lax.ppermute(leave1, "seq", swap)
+        came2, dq = lax.optimization_barrier((came2, dq))
         hop = lax.ppermute(add_rounded(units, stay2, came2), "seq", back)
-        came3, dq = lax.optimization_barrier((came3, list(dq)))
-        dq = exchange(dq)
-        near, came1 = lax.optimization_barrier((add_rounded(units, leave0, (came3, units)), came1))
+        near = add_rounded(units, leave0, (came3, units))
+        near, dq = lax.optimization_barrier((near, dq))
         came0 = lax.ppermute(near, "seq", swap)
+        base = add_rounded(units, own, came3, came0, kind=jnp.float32, bytes_moved=16_000_000)
+        hop, dq[1:2] = lax.optimization_barrier((hop, dq[1:2]))
         side = lax.ppermute(add_rounded(units, stay1, came1, hop), "seq", back)
-        dkv = exchange(add_rounded(units, own, came3, came0, side, cuts=peers))
+        dq = exchange_rows(*dq)
+        dkv = exchange(add_rounded(units, base, side, cuts=peers))
     else:
         parts = lax.all_to_all(parts[0], "seq", 0, 0, tiled=True)
         chosen = (jnp.arange(units)[:, None] == wanted[None, :]) & (used[None, :] > 0)
@@ -435,7 +455,7 @@
             parts.reshape(parts.shape[0], -1),
             preferred_element_type=jnp.float32,
         )
-        dq = exchange(dq)
+        dq = exchange_rows(*dq)
         dkv = exchange(add_rounded(units, own, total.reshape(own.shape), cuts=peers))
     return unpack(me_ref, dq, dkv)
 

time: 83 us -> 80.1 us (0.965)
  waiting for transfers between devices: 40.7 us -> 35.8 us
  starting transfers between devices: 26.6 us -> 27.9 us
    ppermute x1, waiting for transfers between devices: 9.38 us -> 0.39 us  [body(): same1 = lax.ppermute(own_kv, 'seq', ahead)]
    ppermute x1, waiting for transfers between devices: 4.65 us -> 0.01 us  [body(): cross1 = lax.ppermute(same1, 'seq', swap)]
    ppermute x1, waiting for transfers between devices: 0.01 us -> 4.01 us  [body(): came3 = lax.ppermute(away3, 'seq', ahead)]
    ppermute x1, waiting for transfers between devices: 7.22 us -> 3.47 us  [body(): came2 = lax.ppermute(leave2, 'seq', swap)]
    ppermute x1, waiting for transfers between devices: 0.01 us -> 3.46 us  [body(): same3 = lax.ppermute(held, 'seq', back)]
    ppermute x1, waiting for transfers between devices: 1.98 us -> 4.4 us  [body(): same2 = lax.ppermute(same1, 'seq', ahead)]
    ppermute x9 -> x6, waiting for transfers between devices: 4.04 us -> 6.17 us  [exchange(): lax.ppermute(pieces[c], 'head', [(h, h ^ c) for h in range(peers)])]
    ppermute x9 -> x6, starting transfers between devices: 6.95 us -> 5.08 us  [exchange(): lax.ppermute(pieces[c], 'head', [(h, h ^ c) for h in range(peers)])]
  transfers between devices with their start and end apart: 25 -> 25, of which waited for: 11 -> 13; matrix products, arithmetic and copies ran while one was open for 2% -> 2% of each run, Pallas kernels for 9% -> 10%
where the time goes in v5:
time: 80.1 us; the launch traced here: 79.8 us
  waiting for transfers between devices  35.8 us (45%)
  starting transfers between devices  27.9 us (35%)
  Pallas kernels  13.6 us (17%)
  local copies, waits for them, and re-layouts  1.55 us (2%)
  between operations  0.9 us (1%)
    ppermute x1, waiting for transfers between devices, body(): cross2 = lax.ppermute(held, 'seq', swap)  6.96 us
    ppermute x6, waiting for transfers between devices, exchange(): lax.ppermute(pieces[c], 'head', [(h, h ^ c) for h in range(peers)])  6.17 us
    ppermute x1, waiting for transfers between devices, body(): side = lax.ppermute(add_rounded(units, stay1, came1, hop), 'seq', back)  5.6 us
    ppermute x6, starting transfers between devices, exchange(): lax.ppermute(pieces[c], 'head', [(h, h ^ c) for h in range(peers)])  5.08 us
    ppermute x1, waiting for transfers between devices, body(): same2 = lax.ppermute(same1, 'seq', ahead)  4.4 us
    ppermute x1, waiting for transfers between devices, body(): came3 = lax.ppermute(away3, 'seq', ahead)  4.01 us
    pallas_call x1, Pallas kernels, own_terms(): pl.pallas_call(functools.partial(own_kernel, peers), out_shape=(piece,) *...  3.84 us
    ppermute x1, waiting for transfers between devices, body(): came2 = lax.ppermute(leave2, 'seq', swap)  3.47 us
  transfers between devices with their start and end apart: 25, of which 13 were waited for; matrix products, arithmetic and copies ran while one was open for 2% of the time, Pallas kernels for 10%

profile of v5, /device:TPU:0, one launch (start us, length us, event | category | flops | bytes accessed | tf_op | source)
XLA Modules:
  0.0 79.8 jit_solution(15686065096647430117)
XLA Ops:
  0.6 1.7 %shard_map.94 = (bf16[2,64,256]{2,1,0:T(8,128)(2,1)}, bf16[2,64,256]{2,1,0:T(8,128)(2,1)}, bf16[2,64,256]{2,1,0:T(8,128)(2,1)}, bf16[2,64,256]{2,1,0:T(8,128)(2,1)}) custom-call(s32[1]{0:T(128)} %bitcast.me_ref, bf16[64,1024]{1,0:T(8,128)(2,1)} %k_ref.1, bf16[64,1024]{1,0:T(8,128)(2,1)} %v_ref.1), custom_call_target="tpu_custom_call" | custom-call | tf_op jit(solution)/shard_map/pallas_call | solution.py:63
  2.4 0.5 collective-permute-start
  2.9 2.6 %collective-permute-start.1 = (bf16[2,64,256]{2,1,0:T(8,128)(2,1)}, bf16[2,64,256]{2,1,0:T(8,128)(2,1)S(1)}, u32[]{:S(2)}, u32[]{:S(2)}) collective-permute-start(bf16[2,64,256]{2,1,0:T(8,128)(2,1)} %get-tuple-element.55), channel_id=1, source_target_pairs={{0,2},{1,3},{2,0},{3,1},{4,6},{5,7},{6,4},{7,5},{8,10},{9,11},{10,... | collective-permute-start | bytes 196616 | tf_op jit(solution)/shard_map/ppermute | solution.py:348
  5.5 0.1 collective-permute-start.2
  5.5 0.8 %constant_dynamic-update-slice_fusion.3 = bf16[8,64,256]{2,1,0:T(8,128)(2,1)S(1)} fusion(bf16[2,64,256]{2,1,0:T(8,128)(2,1)} %get-tuple-element.53), kind=kLoop, calls=%fused_computation.3 | loop fusion | bytes 131072
  6.4 0.0 collective-permute-done
  6.4 2.0 %collective-permute-done.1 = bf16[2,64,256]{2,1,0:T(8,128)(2,1)S(1)} collective-permute-done((bf16[2,64,256]{2,1,0:T(8,128)(2,1)}, bf16[2,64,256]{2,1,0:T(8,128)(2,1)S(1)}, u32[]{:S(2)}, u32[]{:S(2)}) %collective-permute-start.1) | collective-permute-done | bytes 65568 | tf_op jit(solution)/shard_map/ppermute | solution.py:348
  8.4 1.4 %collective-permute-done.2 = bf16[2,64,256]{2,1,0:T(8,128)(2,1)S(1)} collective-permute-done((bf16[2,64,256]{2,1,0:T(8,128)(2,1)}, bf16[2,64,256]{2,1,0:T(8,128)(2,1)S(1)}, u32[]{:S(2)}, u32[]{:S(2)}) %collective-permute-start.2) | collective-permute-done | bytes 65568 | tf_op jit(solution)/shard_map/ppermute | solution.py:348
  9.8 1.6 %collective-permute-start.3 = (bf16[8,64,256]{2,1,0:T(8,128)(2,1)S(1)}, bf16[8,64,256]{2,1,0:T(8,128)(2,1)S(1)}, u32[]{:S(2)}, u32[]{:S(2)}) collective-permute-start(bf16[8,64,256]{2,1,0:T(8,128)(2,1)S(1)} %constant_dynamic-update-slice_fusion.own_kv_ref), channel_id=1, source_target_pairs={{0,8},{4,12},{8,16},{12,20},{16,24},{20,28},{24,0},{28,4},{1,9},{5... | collective-permute-start | bytes 786440 | tf_op jit(solution)/shard_map/ppermute | solution.py:390
  11.4 1.5 %collective-permute-start.4 = (bf16[8,64,256]{2,1,0:T(8,128)(2,1)S(1)}, bf16[8,64,256]{2,1,0:T(8,128)(2,1)S(1)}, u32[]{:S(2)}, u32[]{:S(2)}) collective-permute-start(bf16[8,64,256]{2,1,0:T(8,128)(2,1)S(1)} %constant_dynamic-update-slice_fusion.own_kv_ref), channel_id=1, source_target_pairs={{0,4},{4,0},{8,12},{12,8},{16,20},{20,16},{24,28},{28,24},{1,5},{5... | collective-permute-start | bytes 786440 | tf_op jit(solution)/shard_map/ppermute | solution.py:391
  12.9 3.0 %shard_map.95 = (bf16[528,256]{1,0:T(8,128)(2,1)}, bf16[528,256]{1,0:T(8,128)(2,1)}, bf16[1056,256]{1,0:T(8,128)(2,1)}) custom-call(s32[1]{0:T(128)} %bitcast.me_ref, bf16[64,4096]{1,0:T(8,128)(2,1)} %q_any.1, bf16[64,4096]{1,0:T(8,128)(2,1)} %do_any.1, bf16[64,4096]{1,0:T(8,128)(2,1)} %o_any.1), custom_call_target="tpu_custom_call" | custom-call | tf_op jit(solution)/shard_map/pallas_call | solution.py:117
  15.9 2.3 %collective-permute-start.7 = (bf16[8,64,256]{2,1,0:T(8,128)(2,1)S(1)}, bf16[8,64,256]{2,1,0:T(8,128)(2,1)S(1)}, u32[]{:S(2)}, u32[]{:S(2)}) collective-permute-start(bf16[8,64,256]{2,1,0:T(8,128)(2,1)S(1)} %constant_dynamic-update-slice_fusion.own_kv_ref), channel_id=1, source_target_pairs={{0,24},{4,28},{8,0},{12,4},{16,8},{20,12},{24,16},{28,20},{1,25},{... | collective-permute-start | bytes 786440 | tf_op jit(solution)/shard_map/ppermute | solution.py:395
  18.2 0.1 copy.10
  18.3 0.1 reshape.13
  18.4 1.3 %collective-permute-start.11 = (bf16[1056,256]{1,0:T(8,128)(2,1)}, bf16[1056,256]{1,0:T(8,128)(2,1)S(1)}, u32[]{:S(2)}, u32[]{:S(2)}) collective-permute-start(bf16[1056,256]{1,0:T(8,128)(2,1)} %get-tuple-element.69), channel_id=1, source_target_pairs={{0,2},{1,3},{2,0},{3,1},{4,6},{5,7},{6,4},{7,5},{8,10},{9,11},{10,... | collective-permute-start | bytes 1622024 | tf_op jit(solution)/shard_map/ppermute | solution.py:358
  19.8 0.4 collective-permute-done.3
  20.2 2.1 %collective-permute-start.6 = (bf16[8,64,256]{2,1,0:T(8,128)(2,1)S(1)}, bf16[8,64,256]{2,1,0:T(8,128)(2,1)S(1)}, u32[]{:S(2)}, u32[]{:S(2)}) collective-permute-start(bf16[8,64,256]{2,1,0:T(8,128)(2,1)S(1)} %collective-permute-done.3), channel_id=1, source_target_pairs={{0,4},{4,0},{8,12},{12,8},{16,20},{20,16},{24,28},{28,24},{1,5},{5... | collective-permute-start | bytes 786440 | tf_op jit(solution)/shard_map/ppermute | solution.py:406
  22.3 0.0 collective-permute-start.5
  22.3 0.2 dynamic_update_slice.21
  22.5 0.1 pad_add_fusion
  22.6 0.1 dynamic_slice.9.slot_ref
  22.7 0.0 collective-permute-start.10
  22.7 3.5 %collective-permute-done.7 = bf16[8,64,256]{2,1,0:T(8,128)(2,1)S(1)} collective-permute-done((bf16[8,64,256]{2,1,0:T(8,128)(2,1)S(1)}, bf16[8,64,256]{2,1,0:T(8,128)(2,1)S(1)}, u32[]{:S(2)}, u32[]{:S(2)}) %collective-permute-start.7) | collective-permute-done | bytes 262176 | tf_op jit(solution)/shard_map/ppermute | solution.py:395
  26.2 1.7 %collective-permute-start.9 = (bf16[8,64,256]{2,1,0:T(8,128)(2,1)S(1)}, bf16[8,64,256]{2,1,0:T(8,128)(2,1)S(1)}, u32[]{:S(2)}, u32[]{:S(2)}) collective-permute-start(bf16[8,64,256]{2,1,0:T(8,128)(2,1)S(1)} %collective-permute-done.7), channel_id=1, source_target_pairs={{0,4},{4,0},{8,12},{12,8},{16,20},{20,16},{24,28},{28,24},{1,5},{5... | collective-permute-start | bytes 786440 | tf_op jit(solution)/shard_map/ppermute | solution.py:407
  27.9 0.0 copy-start
  27.9 0.0 copy-start.1
  27.9 0.0 collective-permute-done.6
  28.0 4.4 %collective-permute-done.5 = bf16[8,64,256]{2,1,0:T(8,128)(2,1)S(1)} collective-permute-done((bf16[8,64,256]{2,1,0:T(8,128)(2,1)S(1)}, bf16[8,64,256]{2,1,0:T(8,128)(2,1)S(1)}, u32[]{:S(2)}, u32[]{:S(2)}) %collective-permute-start.5) | collective-permute-done | bytes 262176 | tf_op jit(solution)/shard_map/ppermute | solution.py:405
  32.4 0.4 collective-permute-start.8
  32.9 0.1 collective-permute-start.12
  33.0 7.0 %collective-permute-done.8 = bf16[8,64,256]{2,1,0:T(8,128)(2,1)S(1)} collective-permute-done((bf16[8,64,256]{2,1,0:T(8,128)(2,1)S(1)}, bf16[8,64,256]{2,1,0:T(8,128)(2,1)S(1)}, u32[]{:S(2)}, u32[]{:S(2)}) %collective-permute-start.8) | collective-permute-done | bytes 262176 | tf_op jit(solution)/shard_map/ppermute | solution.py:409
  40.0 0.0 collective-permute-done.9
  40.0 0.0 collective-permute-done.10.refs_1_
  40.0 0.0 collective-permute-done.12.refs_3_
  40.0 3.1 %shard_map.96 = (f32[2,8,256]{2,1,0:T(8,128)S(1)}, f32[64,1024]{1,0:T(8,128)S(1)}, f32[64,1024]{1,0:T(8,128)S(1)}, f32[64,1024]{1,0:T(8,128)S(1)}, f32[64,1024]{...) custom-call(s32[1]{0:T(128)} %bitcast.me_ref, ...), custom_call_target="tpu_custom_call" | custom-call | flops 671000000 | bytes 8000000 | tf_op jit(solution)/shard_map/pallas_call | solution.py:257
  43.1 2.3 %collective-permute-start.13 = (bf16[16,64,256]{2,1,0:T(8,128)(2,1)S(1)}, bf16[16,64,256]{2,1,0:T(8,128)(2,1)S(1)}, u32[]{:S(2)}, u32[]{:S(2)}) collective-permute-start(bf16[16,64,256]{2,1,0:T(8,128)(2,1)S(1)} %get-tuple-element.71), channel_id=1, source_target_pairs={{0,8},{4,12},{8,16},{12,20},{16,24},{20,28},{24,0},{28,4},{1,9},{5... | collective-permute-start | bytes 1572872 | tf_op jit(solution)/shard_map/ppermute | solution.py:438
  45.5 0.3 collective-permute-start.14
  45.7 3.8 %shard_map.98 = (bf16[64,1024]{1,0:T(8,128)(2,1)S(1)}, bf16[64,1024]{1,0:T(8,128)(2,1)S(1)}, bf16[128,1024]{1,0:T(8,128)(2,1)S(1)}, f32[8,64,256]{2,1,0:T(8,128)S(1)}) custom-call(s32[1]{0:T(128)} %bitcast.me_ref, bf16[8,64,256]{2,1,0:T(8,128)(2,1)S(1)} %constant_dynamic-update-slice_fusion.own_kv_ref, f32[2,8,256]{2,1,0:T(8,128)S(1)} %get-tuple-element.73.stats_ref, ...), custom_call_target="tpu_custom_call" | custom-call | flops 335000000 | bytes 4000000 | tf_op jit(solution)/shard_map/pallas_call | solution.py:180
  49.6 3.5 %collective-permute-done.14.refs_1_ = bf16[8,64,256]{2,1,0:T(8,128)(2,1)S(1)} collective-permute-done((bf16[8,64,256]{2,1,0:T(8,128)(2,1)S(1)}, bf16[8,64,256]{2,1,0:T(8,128)(2,1)S(1)}, u32[]{:S(2)}, u32[]{:S(2)}) %collective-permute-start.14) | collective-permute-done | bytes 262176 | tf_op jit(solution)/shard_map/ppermute | solution.py:437
  53.1 0.1 shard_map.99
  53.1 1.5 %collective-permute-start.15 = (bf16[8,64,256]{2,1,0:T(8,128)(2,1)S(1)}, bf16[8,64,256]{2,1,0:T(8,128)(2,1)S(1)}, u32[]{:S(2)}, u32[]{:S(2)}) collective-permute-start(bf16[8,64,256]{2,1,0:T(8,128)(2,1)S(1)} %shard_map.99), channel_id=1, source_target_pairs={{0,24},{4,28},{8,0},{12,4},{16,8},{20,12},{24,16},{28,20},{1,25},{... | collective-permute-start | bytes 786440 | tf_op jit(solution)/shard_map/ppermute | solution.py:441
  54.6 1.2 %collective-permute-start.20 = (bf16[8,64,256]{2,1,0:T(8,128)(2,1)S(1)}, bf16[8,64,256]{2,1,0:T(8,128)(2,1)S(1)}, u32[]{:S(2)}, u32[]{:S(2)}) collective-permute-start(bf16[8,64,256]{2,1,0:T(8,128)(2,1)S(1)} %get-tuple-element.93), channel_id=1, source_target_pairs={{0,4},{4,0},{8,12},{12,8},{16,20},{20,16},{24,28},{28,24},{1,5},{5... | collective-permute-start | bytes 786440 | tf_op jit(solution)/shard_map/ppermute | solution.py:439
  55.8 4.0 %collective-permute-done.13.refs_1_ = bf16[16,64,256]{2,1,0:T(8,128)(2,1)S(1)} collective-permute-done((bf16[16,64,256]{2,1,0:T(8,128)(2,1)S(1)}, bf16[16,64,256]{2,1,0:T(8,128)(2,1)S(1)}, u32[]{:S(2)}, u32[]{:S(2)}) %collective-permute-start.13) | collective-permute-done | bytes 524320 | tf_op jit(solution)/shard_map/ppermute | solution.py:438
  59.9 0.1 shard_map.97
  59.9 1.5 %collective-permute-start.17 = (bf16[128,1024]{1,0:T(8,128)(2,1)S(1)}, bf16[128,1024]{1,0:T(8,128)(2,1)S(1)}, u32[]{:S(2)}, u32[]{:S(2)}) collective-permute-start(bf16[128,1024]{1,0:T(8,128)(2,1)S(1)} %get-tuple-element.89), channel_id=1, source_target_pairs={{0,2},{1,3},{2,0},{3,1},{4,6},{5,7},{6,4},{7,5},{8,10},{9,11},{10,... | collective-permute-start | bytes 786440 | tf_op jit(solution)/shard_map/ppermute | solution.py:358
  61.4 2.0 %collective-permute-start.19 = (bf16[8,64,256]{2,1,0:T(8,128)(2,1)S(1)}, bf16[8,64,256]{2,1,0:T(8,128)(2,1)S(1)}, u32[]{:S(2)}, u32[]{:S(2)}) collective-permute-start(bf16[8,64,256]{2,1,0:T(8,128)(2,1)S(1)} %shard_map.97), channel_id=1, source_target_pairs={{0,4},{4,0},{8,12},{12,8},{16,20},{20,16},{24,28},{28,24},{1,5},{5... | collective-permute-start | bytes 786440 | tf_op jit(solution)/shard_map/ppermute | solution.py:444
  63.5 0.5 collective-permute-done.15.refs_2_
  63.9 0.0 collective-permute-start.16
  63.9 0.0 collective-permute-done.20.refs_1_
  63.9 0.1 shard_map.102
  64.0 2.6 %collective-permute-start.21 = (bf16[8,64,256]{2,1,0:T(8,128)(2,1)S(1)}, bf16[8,64,256]{2,1,0:T(8,128)(2,1)S(1)}, u32[]{:S(2)}, u32[]{:S(2)}) collective-permute-start(bf16[8,64,256]{2,1,0:T(8,128)(2,1)S(1)} %shard_map.102), channel_id=1, source_target_pairs={{0,24},{4,28},{8,0},{12,4},{16,8},{20,12},{24,16},{28,20},{1,25},{... | collective-permute-start | bytes 786440 | tf_op jit(solution)/shard_map/ppermute | solution.py:447
  66.6 0.3 collective-permute-start.18
  66.9 0.9 %collective-permute-done.19.refs_2_ = bf16[8,64,256]{2,1,0:T(8,128)(2,1)S(1)} collective-permute-done((bf16[8,64,256]{2,1,0:T(8,128)(2,1)S(1)}, bf16[8,64,256]{2,1,0:T(8,128)(2,1)S(1)}, u32[]{:S(2)}, u32[]{:S(2)}) %collective-permute-start.19) | collective-permute-done | bytes 262176 | tf_op jit(solution)/shard_map/ppermute | solution.py:444
  67.8 0.1 shard_map.101.refs_0_
  67.9 5.6 %collective-permute-done.21.refs_1_ = bf16[8,64,256]{2,1,0:T(8,128)(2,1)S(1)} collective-permute-done((bf16[8,64,256]{2,1,0:T(8,128)(2,1)S(1)}, bf16[8,64,256]{2,1,0:T(8,128)(2,1)S(1)}, u32[]{:S(2)}, u32[]{:S(2)}) %collective-permute-start.21) | collective-permute-done | bytes 262176 | tf_op jit(solution)/shard_map/ppermute | solution.py:447
  73.5 0.1 collective-permute-start.22
  73.6 1.0 %collective-permute-start.23 = (bf16[2,64,256]{2,1,0:T(8,128)(2,1)S(1)}, bf16[2,64,256]{2,1,0:T(8,128)(2,1)S(1)}, u32[]{:S(2)}, u32[]{:S(2)}) collective-permute-start(bf16[2,64,256]{2,1,0:T(8,128)(2,1)S(1)} %get-tuple-element.99), channel_id=1, source_target_pairs={{0,2},{1,3},{2,0},{3,1},{4,6},{5,7},{6,4},{7,5},{8,10},{9,11},{10,... | collective-permute-start | bytes 196616 | tf_op jit(solution)/shard_map/ppermute | solution.py:348
  74.6 0.8 %collective-permute-start.24 = (bf16[2,64,256]{2,1,0:T(8,128)(2,1)S(1)}, bf16[2,64,256]{2,1,0:T(8,128)(2,1)S(1)}, u32[]{:S(2)}, u32[]{:S(2)}) collective-permute-start(bf16[2,64,256]{2,1,0:T(8,128)(2,1)S(1)} %get-tuple-element.100), channel_id=1, source_target_pairs={{0,3},{1,2},{2,1},{3,0},{4,7},{5,6},{6,5},{7,4},{8,11},{9,10},{10,... | collective-permute-start | bytes 196616 | tf_op jit(solution)/shard_map/ppermute | solution.py:348
  75.5 0.0 collective-permute-done.16.refs_1_
  75.5 0.0 collective-permute-done.18.refs_3_
  75.5 0.8 %shard_map.100 = bf16[64,4096]{1,0:T(8,128)(2,1)} custom-call(s32[1]{0:T(128)} %bitcast.me_ref, bf16[64,1024]{1,0:T(8,128)(2,1)S(1)} %get-tuple-element.84.refs_0_, bf16[64,1024]{1,0:T(8,128)(2,1)S(1)} %collective-permute-done.16.refs_1_, bf16[64,1024]{1,0:T(8,128)(2,1)S(1)} %get-tuple-element.106.refs_2_, bf16[64,1024]{1,0:T(8,128)(2,1)S(1)} %collective-permute-done.18.refs_3_), custom_call_target="tpu_custom_call" | custom-call | tf_op jit(solution)/shard_map/pallas_call | solution.py:327
  76.3 2.3 %collective-permute-done.23.refs_2_ = bf16[2,64,256]{2,1,0:T(8,128)(2,1)S(1)} collective-permute-done((bf16[2,64,256]{2,1,0:T(8,128)(2,1)S(1)}, bf16[2,64,256]{2,1,0:T(8,128)(2,1)S(1)}, u32[]{:S(2)}, u32[]{:S(2)}) %collective-permute-start.23) | collective-permute-done | bytes 65568 | tf_op jit(solution)/shard_map/ppermute | solution.py:348
  78.6 0.5 collective-permute-done.24.refs_3_
  79.1 0.8 shard_map.104
  (23 shorter events, 0.3 us)
Async XLA Ops:
  0.6 17.6 %copy-start.2 = (s32[16,8,4]{0,2,1:T(4,128)S(1)}, s32[16,8,4]{0,2,1:T(4,128)}, u32[]{:S(2)}) copy-start(s32[16,8,4]{0,2,1:T(4,128)} %param.13) | copy-start | bytes 6148
  2.4 4.0 %collective-permute-start = (bf16[2,64,256]{2,1,0:T(8,128)(2,1)}, bf16[2,64,256]{2,1,0:T(8,128)(2,1)S(1)}, u32[]{:S(2)}, u32[]{:S(2)}) collective-permute-start(bf16[2,64,256]{2,1,0:T(8,128)(2,1)} %get-tuple-element.54), channel_id=1, source_target_pairs={{0,1},{1,0},{2,3},{3,2},{4,5},{5,4},{6,7},{7,6},{8,9},{9,8},{10,11... | collective-permute-start | bytes 196616 | tf_op jit(solution)/shard_map/ppermute | solution.py:348
  2.9 5.5 %collective-permute-start.1 = (bf16[2,64,256]{2,1,0:T(8,128)(2,1)}, bf16[2,64,256]{2,1,0:T(8,128)(2,1)S(1)}, u32[]{:S(2)}, u32[]{:S(2)}) collective-permute-start(bf16[2,64,256]{2,1,0:T(8,128)(2,1)} %get-tuple-element.55), channel_id=1, source_target_pairs={{0,2},{1,3},{2,0},{3,1},{4,6},{5,7},{6,4},{7,5},{8,10},{9,11},{10,... | collective-permute-start | bytes 196616 | tf_op jit(solution)/shard_map/ppermute | solution.py:348
  5.5 4.3 %collective-permute-start.2 = (bf16[2,64,256]{2,1,0:T(8,128)(2,1)}, bf16[2,64,256]{2,1,0:T(8,128)(2,1)S(1)}, u32[]{:S(2)}, u32[]{:S(2)}) collective-permute-start(bf16[2,64,256]{2,1,0:T(8,128)(2,1)} %get-tuple-element.56), channel_id=1, source_target_pairs={{0,3},{1,2},{2,1},{3,0},{4,7},{5,6},{6,5},{7,4},{8,11},{9,10},{10,... | collective-permute-start | bytes 196616 | tf_op jit(solution)/shard_map/ppermute | solution.py:348
  9.8 10.3 %collective-permute-start.3 = (bf16[8,64,256]{2,1,0:T(8,128)(2,1)S(1)}, bf16[8,64,256]{2,1,0:T(8,128)(2,1)S(1)}, u32[]{:S(2)}, u32[]{:S(2)}) collective-permute-start(bf16[8,64,256]{2,1,0:T(8,128)(2,1)S(1)} %constant_dynamic-update-slice_fusion.own_kv_ref), channel_id=1, source_target_pairs={{0,8},{4,12},{8,16},{12,20},{16,24},{20,28},{24,0},{28,4},{1,9},{5... | collective-permute-start | bytes 786440 | tf_op jit(solution)/shard_map/ppermute | solution.py:390
  11.4 11.3 %collective-permute-start.4 = (bf16[8,64,256]{2,1,0:T(8,128)(2,1)S(1)}, bf16[8,64,256]{2,1,0:T(8,128)(2,1)S(1)}, u32[]{:S(2)}, u32[]{:S(2)}) collective-permute-start(bf16[8,64,256]{2,1,0:T(8,128)(2,1)S(1)} %constant_dynamic-update-slice_fusion.own_kv_ref), channel_id=1, source_target_pairs={{0,4},{4,0},{8,12},{12,8},{16,20},{20,16},{24,28},{28,24},{1,5},{5... | collective-permute-start | bytes 786440 | tf_op jit(solution)/shard_map/ppermute | solution.py:391
  15.9 6.8 %copy-start.3 = (bf16[528,256]{1,0:T(8,128)(2,1)S(1)}, bf16[528,256]{1,0:T(8,128)(2,1)}, u32[]{:S(2)}) copy-start(bf16[528,256]{1,0:T(8,128)(2,1)} %get-tuple-element.68) | copy-start | bytes 811012
  15.9 10.3 %collective-permute-start.7 = (bf16[8,64,256]{2,1,0:T(8,128)(2,1)S(1)}, bf16[8,64,256]{2,1,0:T(8,128)(2,1)S(1)}, u32[]{:S(2)}, u32[]{:S(2)}) collective-permute-start(bf16[8,64,256]{2,1,0:T(8,128)(2,1)S(1)} %constant_dynamic-update-slice_fusion.own_kv_ref), channel_id=1, source_target_pairs={{0,24},{4,28},{8,0},{12,4},{16,8},{20,12},{24,16},{28,20},{1,25},{... | collective-permute-start | bytes 786440 | tf_op jit(solution)/shard_map/ppermute | solution.py:395
  18.4 14.4 %collective-permute-start.11 = (bf16[1056,256]{1,0:T(8,128)(2,1)}, bf16[1056,256]{1,0:T(8,128)(2,1)S(1)}, u32[]{:S(2)}, u32[]{:S(2)}) collective-permute-start(bf16[1056,256]{1,0:T(8,128)(2,1)} %get-tuple-element.69), channel_id=1, source_target_pairs={{0,2},{1,3},{2,0},{3,1},{4,6},{5,7},{6,4},{7,5},{8,10},{9,11},{10,... | collective-permute-start | bytes 1622024 | tf_op jit(solution)/shard_map/ppermute | solution.py:358
  20.2 7.8 %collective-permute-start.6 = (bf16[8,64,256]{2,1,0:T(8,128)(2,1)S(1)}, bf16[8,64,256]{2,1,0:T(8,128)(2,1)S(1)}, u32[]{:S(2)}, u32[]{:S(2)}) collective-permute-start(bf16[8,64,256]{2,1,0:T(8,128)(2,1)S(1)} %collective-permute-done.3), channel_id=1, source_target_pairs={{0,4},{4,0},{8,12},{12,8},{16,20},{20,16},{24,28},{28,24},{1,5},{5... | collective-permute-start | bytes 786440 | tf_op jit(solution)/shard_map/ppermute | solution.py:406
  22.3 10.1 %collective-permute-start.5 = (bf16[8,64,256]{2,1,0:T(8,128)(2,1)S(1)}, bf16[8,64,256]{2,1,0:T(8,128)(2,1)S(1)}, u32[]{:S(2)}, u32[]{:S(2)}) collective-permute-start(bf16[8,64,256]{2,1,0:T(8,128)(2,1)S(1)} %collective-permute-done.3), channel_id=1, source_target_pairs={{0,8},{4,12},{8,16},{12,20},{16,24},{20,28},{24,0},{28,4},{1,9},{5... | collective-permute-start | bytes 786440 | tf_op jit(solution)/shard_map/ppermute | solution.py:405
  22.7 17.3 %collective-permute-start.10 = (bf16[528,256]{1,0:T(8,128)(2,1)S(1)}, bf16[528,256]{1,0:T(8,128)(2,1)S(1)}, u32[]{:S(2)}, u32[]{:S(2)}) collective-permute-start(bf16[528,256]{1,0:T(8,128)(2,1)S(1)} %copy-done.3), channel_id=1, source_target_pairs={{0,1},{1,0},{2,3},{3,2},{4,5},{5,4},{6,7},{7,6},{8,9},{9,8},{10,11... | collective-permute-start | bytes 811016 | tf_op jit(solution)/shard_map/ppermute | solution.py:359
  26.2 13.8 %collective-permute-start.9 = (bf16[8,64,256]{2,1,0:T(8,128)(2,1)S(1)}, bf16[8,64,256]{2,1,0:T(8,128)(2,1)S(1)}, u32[]{:S(2)}, u32[]{:S(2)}) collective-permute-start(bf16[8,64,256]{2,1,0:T(8,128)(2,1)S(1)} %collective-permute-done.7), channel_id=1, source_target_pairs={{0,4},{4,0},{8,12},{12,8},{16,20},{20,16},{24,28},{28,24},{1,5},{5... | collective-permute-start | bytes 786440 | tf_op jit(solution)/shard_map/ppermute | solution.py:407
  27.9 12.1 %copy-start = (bf16[528,256]{1,0:T(8,128)(2,1)S(1)}, bf16[528,256]{1,0:T(8,128)(2,1)}, u32[]{:S(2)}) copy-start(bf16[528,256]{1,0:T(8,128)(2,1)} %get-tuple-element.67.refs_0_) | copy-start | bytes 811012
  27.9 12.1 %copy-start.1 = (f32[256,8]{0,1:T(8,128)S(1)}, f32[256,8]{0,1:T(8,128)}, u32[]{:S(2)}) copy-start(f32[256,8]{0,1:T(8,128)} %param.12) | copy-start | bytes 24580
  32.4 7.6 %collective-permute-start.8 = (bf16[8,64,256]{2,1,0:T(8,128)(2,1)S(1)}, bf16[8,64,256]{2,1,0:T(8,128)(2,1)S(1)}, u32[]{:S(2)}, u32[]{:S(2)}) collective-permute-start(bf16[8,64,256]{2,1,0:T(8,128)(2,1)S(1)} %collective-permute-done.5), channel_id=1, source_target_pairs={{0,4},{4,0},{8,12},{12,8},{16,20},{20,16},{24,28},{28,24},{1,5},{5... | collective-permute-start | bytes 786440 | tf_op jit(solution)/shard_map/ppermute | solution.py:409
  32.9 7.1 %collective-permute-start.12 = (bf16[528,256]{1,0:T(8,128)(2,1)S(1)}, bf16[528,256]{1,0:T(8,128)(2,1)S(1)}, u32[]{:S(2)}, u32[]{:S(2)}) collective-permute-start(bf16[528,256]{1,0:T(8,128)(2,1)S(1)} %get-tuple-element.103), channel_id=1, source_target_pairs={{0,1},{1,0},{2,3},{3,2},{4,5},{5,4},{6,7},{7,6},{8,9},{9,8},{10,11... | collective-permute-start | bytes 811016 | tf_op jit(solution)/shard_map/ppermute | solution.py:360
  43.1 16.7 %collective-permute-start.13 = (bf16[16,64,256]{2,1,0:T(8,128)(2,1)S(1)}, bf16[16,64,256]{2,1,0:T(8,128)(2,1)S(1)}, u32[]{:S(2)}, u32[]{:S(2)}) collective-permute-start(bf16[16,64,256]{2,1,0:T(8,128)(2,1)S(1)} %get-tuple-element.71), channel_id=1, source_target_pairs={{0,8},{4,12},{8,16},{12,20},{16,24},{20,28},{24,0},{28,4},{1,9},{5... | collective-permute-start | bytes 1572872 | tf_op jit(solution)/shard_map/ppermute | solution.py:438
  45.5 7.6 %collective-permute-start.14 = (bf16[8,64,256]{2,1,0:T(8,128)(2,1)S(1)}, bf16[8,64,256]{2,1,0:T(8,128)(2,1)S(1)}, u32[]{:S(2)}, u32[]{:S(2)}) collective-permute-start(bf16[8,64,256]{2,1,0:T(8,128)(2,1)S(1)} %get-tuple-element.72), channel_id=1, source_target_pairs={{0,4},{4,0},{8,12},{12,8},{16,20},{20,16},{24,28},{28,24},{1,5},{5... | collective-permute-start | bytes 786440 | tf_op jit(solution)/shard_map/ppermute | solution.py:437
  53.1 10.8 %collective-permute-start.15 = (bf16[8,64,256]{2,1,0:T(8,128)(2,1)S(1)}, bf16[8,64,256]{2,1,0:T(8,128)(2,1)S(1)}, u32[]{:S(2)}, u32[]{:S(2)}) collective-permute-start(bf16[8,64,256]{2,1,0:T(8,128)(2,1)S(1)} %shard_map.99), channel_id=1, source_target_pairs={{0,24},{4,28},{8,0},{12,4},{16,8},{20,12},{24,16},{28,20},{1,25},{... | collective-permute-start | bytes 786440 | tf_op jit(solution)/shard_map/ppermute | solution.py:441
  54.6 9.3 %collective-permute-start.20 = (bf16[8,64,256]{2,1,0:T(8,128)(2,1)S(1)}, bf16[8,64,256]{2,1,0:T(8,128)(2,1)S(1)}, u32[]{:S(2)}, u32[]{:S(2)}) collective-permute-start(bf16[8,64,256]{2,1,0:T(8,128)(2,1)S(1)} %get-tuple-element.93), channel_id=1, source_target_pairs={{0,4},{4,0},{8,12},{12,8},{16,20},{20,16},{24,28},{28,24},{1,5},{5... | collective-permute-start | bytes 786440 | tf_op jit(solution)/shard_map/ppermute | solution.py:439
  59.9 6.7 %collective-permute-start.17 = (bf16[128,1024]{1,0:T(8,128)(2,1)S(1)}, bf16[128,1024]{1,0:T(8,128)(2,1)S(1)}, u32[]{:S(2)}, u32[]{:S(2)}) collective-permute-start(bf16[128,1024]{1,0:T(8,128)(2,1)S(1)} %get-tuple-element.89), channel_id=1, source_target_pairs={{0,2},{1,3},{2,0},{3,1},{4,6},{5,7},{6,4},{7,5},{8,10},{9,11},{10,... | collective-permute-start | bytes 786440 | tf_op jit(solution)/shard_map/ppermute | solution.py:358
  61.4 6.4 %collective-permute-start.19 = (bf16[8,64,256]{2,1,0:T(8,128)(2,1)S(1)}, bf16[8,64,256]{2,1,0:T(8,128)(2,1)S(1)}, u32[]{:S(2)}, u32[]{:S(2)}) collective-permute-start(bf16[8,64,256]{2,1,0:T(8,128)(2,1)S(1)} %shard_map.97), channel_id=1, source_target_pairs={{0,4},{4,0},{8,12},{12,8},{16,20},{20,16},{24,28},{28,24},{1,5},{5... | collective-permute-start | bytes 786440 | tf_op jit(solution)/shard_map/ppermute | solution.py:444
  63.9 11.6 %collective-permute-start.16 = (bf16[64,1024]{1,0:T(8,128)(2,1)S(1)}, bf16[64,1024]{1,0:T(8,128)(2,1)S(1)}, u32[]{:S(2)}, u32[]{:S(2)}) collective-permute-start(bf16[64,1024]{1,0:T(8,128)(2,1)S(1)} %get-tuple-element.88), channel_id=1, source_target_pairs={{0,1},{1,0},{2,3},{3,2},{4,5},{5,4},{6,7},{7,6},{8,9},{9,8},{10,11... | collective-permute-start | bytes 393224 | tf_op jit(solution)/shard_map/ppermute | solution.py:359
  64.0 9.5 %collective-permute-start.21 = (bf16[8,64,256]{2,1,0:T(8,128)(2,1)S(1)}, bf16[8,64,256]{2,1,0:T(8,128)(2,1)S(1)}, u32[]{:S(2)}, u32[]{:S(2)}) collective-permute-start(bf16[8,64,256]{2,1,0:T(8,128)(2,1)S(1)} %shard_map.102), channel_id=1, source_target_pairs={{0,24},{4,28},{8,0},{12,4},{16,8},{20,12},{24,16},{28,20},{1,25},{... | collective-permute-start | bytes 786440 | tf_op jit(solution)/shard_map/ppermute | solution.py:447
  66.6 8.8 %collective-permute-start.18 = (bf16[64,1024]{1,0:T(8,128)(2,1)S(1)}, bf16[64,1024]{1,0:T(8,128)(2,1)S(1)}, u32[]{:S(2)}, u32[]{:S(2)}) collective-permute-start(bf16[64,1024]{1,0:T(8,128)(2,1)S(1)} %get-tuple-element.105), channel_id=1, source_target_pairs={{0,1},{1,0},{2,3},{3,2},{4,5},{5,4},{6,7},{7,6},{8,9},{9,8},{10,11... | collective-permute-start | bytes 393224 | tf_op jit(solution)/shard_map/ppermute | solution.py:360
  73.5 2.8 %collective-permute-start.22 = (bf16[2,64,256]{2,1,0:T(8,128)(2,1)S(1)}, bf16[2,64,256]{2,1,0:T(8,128)(2,1)S(1)}, u32[]{:S(2)}, u32[]{:S(2)}) collective-permute-start(bf16[2,64,256]{2,1,0:T(8,128)(2,1)S(1)} %get-tuple-element.98), channel_id=1, source_target_pairs={{0,1},{1,0},{2,3},{3,2},{4,5},{5,4},{6,7},{7,6},{8,9},{9,8},{10,11... | collective-permute-start | bytes 196616 | tf_op jit(solution)/shard_map/ppermute | solution.py:348
  73.6 5.0 %collective-permute-start.23 = (bf16[2,64,256]{2,1,0:T(8,128)(2,1)S(1)}, bf16[2,64,256]{2,1,0:T(8,128)(2,1)S(1)}, u32[]{:S(2)}, u32[]{:S(2)}) collective-permute-start(bf16[2,64,256]{2,1,0:T(8,128)(2,1)S(1)} %get-tuple-element.99), channel_id=1, source_target_pairs={{0,2},{1,3},{2,0},{3,1},{4,6},{5,7},{6,4},{7,5},{8,10},{9,11},{10,... | collective-permute-start | bytes 196616 | tf_op jit(solution)/shard_map/ppermute | solution.py:348
  74.6 4.4 %collective-permute-start.24 = (bf16[2,64,256]{2,1,0:T(8,128)(2,1)S(1)}, bf16[2,64,256]{2,1,0:T(8,128)(2,1)S(1)}, u32[]{:S(2)}, u32[]{:S(2)}) collective-permute-start(bf16[2,64,256]{2,1,0:T(8,128)(2,1)S(1)} %get-tuple-element.100), channel_id=1, source_target_pairs={{0,3},{1,2},{2,1},{3,0},{4,7},{5,6},{6,5},{7,4},{8,11},{9,10},{10,... | collective-permute-start | bytes 196616 | tf_op jit(solution)/shard_map/ppermute | solution.py:348

commit v6 on v5

--- a/solution.py
+++ b/solution.py
@@ -285,21 +285,24 @@
         done += size
 
 
-def add_rounded(units, *terms, cuts=1, kind=jnp.bfloat16, bytes_moved=2_000_000):
+def add_parts(outs, *terms, bytes_moved=2_000_000):
     terms = [term if isinstance(term, tuple) else (term, 0) for term in terms]
     arrays = [array for array, _ in terms]
-    piece = jax.ShapeDtypeStruct((units // cuts,) + arrays[0].shape[1:], kind)
-    outs = pl.pallas_call(
+    tail = arrays[0].shape[1:]
+    return pl.pallas_call(
         functools.partial(add_kernel, [first for _, first in terms]),
-        out_shape=(piece,) * cuts,
+        out_shape=[jax.ShapeDtypeStruct((size,) + tail, kind) for size, kind in outs],
         in_specs=[VMEM] * len(arrays),
-        out_specs=(VMEM,) * cuts,
+        out_specs=[VMEM] * len(outs),
         compiler_params=PARAMS,
         cost_estimate=pl.CostEstimate(
             flops=2_000_000, bytes_accessed=bytes_moved, transcendentals=0
         ),
     )(*arrays)
-    return outs if cuts > 1 else outs[0]
+
+
+def add_rounded(units, *terms):
+    return add_parts([(units, jnp.bfloat16)], *terms)[0]
 
 
 def unpack_q_kernel(peers, me_ref, *refs):
@@ -309,36 +312,42 @@
         gq_ref[:, lanes(me_ref[0] ^ c, width)] = refs[c][...]
 
 
-def unpack_kv_kernel(peers, me_ref, *refs):
-    gk_ref, gv_ref = refs[peers:]
+def unpack_kv_kernel(counts, me_ref, *refs):
+    *term_refs, gk_ref, gv_ref = refs
     kv_heads = refs[0].shape[0]
-    for c in range(peers):
+    at = 0
+    for c, count in enumerate(counts):
+        terms = term_refs[at : at + count]
+        at += count
         for g in range(kv_heads):
             cols = lanes((me_ref[0] ^ c) * kv_heads + g, HD)
-            gk_ref[:, cols] = refs[c][g, :, :HD]
-            gv_ref[:, cols] = refs[c][g, :, HD:]
+            total = terms[0][g]
+            if count > 1:
+                total = sum(term[g].astype(jnp.float32) for term in terms).astype(jnp.bfloat16)
+            gk_ref[:, cols] = total[:, :HD]
+            gv_ref[:, cols] = total[:, HD:]
 
 
 def unpack(me, dq, dkv):
     peers = len(dq)
     tokens, width = dq[0].shape
-    kv_width = dkv[0].shape[0] * peers * HD
-    spec = [SMEM] + [VMEM] * peers
+    kv_width = dkv[0][0].shape[0] * peers * HD
     grad_q = pl.pallas_call(
         functools.partial(unpack_q_kernel, peers),
         out_shape=jax.ShapeDtypeStruct((tokens, peers * width), jnp.bfloat16),
-        in_specs=spec,
+        in_specs=[SMEM] + [VMEM] * peers,
         out_specs=VMEM,
         compiler_params=PARAMS,
     )(me, *dq)
-    grad_q, dkv[0] = lax.optimization_barrier((grad_q, dkv[0]))
+    flat = [term for terms in dkv for term in terms]
+    grad_q, flat[0] = lax.optimization_barrier((grad_q, flat[0]))
     grad_k, grad_v = pl.pallas_call(
-        functools.partial(unpack_kv_kernel, peers),
+        functools.partial(unpack_kv_kernel, [len(terms) for terms in dkv]),
         out_shape=(jax.ShapeDtypeStruct((tokens, kv_width), jnp.bfloat16),) * 2,
-        in_specs=spec,
+        in_specs=[SMEM] + [VMEM] * len(flat),
         out_specs=(VMEM, VMEM),
         compiler_params=PARAMS,
-    )(me, *dkv)
+    )(me, *flat)
     return grad_q, grad_k, grad_v
 
 
@@ -358,6 +367,15 @@
     far = lax.ppermute(far, "head", across)
     near = lax.ppermute(near, "head", flip)
     return [here, near, far[:rows], lax.ppermute(far[rows:], "head", flip)]
+
+
+def send_back(piece, c, shards, peers):
+    pairs = [
+        (s * peers + h, (s - 2) % shards * peers + (h ^ c))
+        for s in range(shards)
+        for h in range(peers)
+    ]
+    return lax.ppermute(piece, ("seq", "head"), pairs)
 
 
 def body(queries, keys, values, outputs_saved, grad_out, lse, block_lists):
@@ -391,10 +409,8 @@
         cross0 = lax.ppermute(own_kv, "seq", swap)
         later_me, held = lax.optimization_barrier((me_ref, own_kv))
         q_pieces = pack_q(later_me, queries, grad_out, outputs_saved, peers)
-        held, q_pieces = lax.optimization_barrier((held, q_pieces))
-        same3 = lax.ppermute(held, "seq", back)
+        per_peer, q_pieces = lax.optimization_barrier((per_peer, q_pieces))
         qdo = exchange_rows(*q_pieces)
-        per_peer, same1 = lax.optimization_barrier((per_peer, same1))
         mine = lax.dynamic_index_in_dim(per_peer, me, 0, keepdims=False)
         owner = mine // key_count
         apart = (me // 2 - owner // 2) % far
@@ -402,6 +418,8 @@
         piece = jnp.where(crossed == 1, far - 1 + (apart + 1) % far, apart - 1)
         slots = piece * units + (mine % key_count ^ head_me) * kv_heads + group_of
         slots = jnp.roll(slots, block_turn)
+        held, slots = lax.optimization_barrier((held, slots))
+        same3 = lax.ppermute(held, "seq", back)
         same2 = lax.ppermute(same1, "seq", ahead)
         cross1 = lax.ppermute(same1, "seq", swap)
         cross3 = lax.ppermute(same3, "seq", swap)
@@ -442,11 +460,23 @@
         near = add_rounded(units, leave0, (came3, units))
         near, dq = lax.optimization_barrier((near, dq))
         came0 = lax.ppermute(near, "seq", swap)
-        base = add_rounded(units, own, came3, came0, kind=jnp.float32, bytes_moved=16_000_000)
-        hop, dq[1:2] = lax.optimization_barrier((hop, dq[1:2]))
-        side = lax.ppermute(add_rounded(units, stay1, came1, hop), "seq", back)
+        half, pair = units // 2, units // peers
+        outs = [(half, wide), (pair, low), (pair, low)]
+        base, *base_far = add_parts(outs, own, came3, came0, bytes_moved=16_000_000)
+        base, dq[1:2] = lax.optimization_barrier((base, dq[1:2]))
+        outs = [(half, low), (pair, low), (pair, low)]
+        side, *side_far = add_parts(outs, stay1, came1, hop)
+        side_far = [send_back(piece, c, shards, peers) for c, piece in zip((2, 3), side_far)]
+        side = lax.ppermute(side, "seq", back)
         dq = exchange_rows(*dq)
-        dkv = exchange(add_rounded(units, base, side, cuts=peers))
+        base_far = [
+            lax.ppermute(piece, "head", [(h, h ^ c) for h in range(peers)])
+            for c, piece in zip((2, 3), base_far)
+        ]
+        side, base_far, side_far = lax.optimization_barrier((side, base_far, side_far))
+        here, near = add_parts([(pair, low)] * 2, base, side)
+        near = lax.ppermute(near, "head", [(h, h ^ 1) for h in range(peers)])
+        dkv = [[here], [near]] + [list(terms) for terms in zip(base_far, side_far)]
     else:
         parts = lax.all_to_all(parts[0], "seq", 0, 0, tiled=True)
         chosen = (jnp.arange(units)[:, None] == wanted[None, :]) & (used[None, :] > 0)
@@ -456,7 +486,9 @@
             preferred_element_type=jnp.float32,
         )
         dq = exchange_rows(*dq)
-        dkv = exchange(add_rounded(units, own, total.reshape(own.shape), cuts=peers))
+        outs = [(kv_heads, jnp.bfloat16)] * peers
+        dkv = exchange(add_parts(outs, own, total.reshape(own.shape)))
+        dkv = [[piece] for piece in dkv]
     return unpack(me_ref, dq, dkv)
 
 

time: 80.1 us -> 79.6 us (level)
  waiting for transfers between devices: 35.8 us -> 33.1 us
  starting transfers between devices: 27.9 us -> 29.3 us
    ppermute x1 -> x6, starting transfers between devices: 2.6 us -> 8.08 us  [the longest x1 2.89 us: body(): side = lax.ppermute(side, 'seq', back)]
    ppermute x6 -> x3, waiting for transfers between devices: 6.17 us -> 2.46 us  [exchange(): lax.ppermute(pieces[c], 'head', [(h, h ^ c) for h in range(peers)])]
    ppermute x1, waiting for transfers between devices: 0.39 us -> 2.54 us  [body(): same1 = lax.ppermute(own_kv, 'seq', ahead)]
    ppermute x6 -> x3, starting transfers between devices: 5.08 us -> 3.15 us  [exchange(): lax.ppermute(pieces[c], 'head', [(h, h ^ c) for h in range(peers)])]
    ppermute x1 -> x6, waiting for transfers between devices: 5.6 us -> 3.73 us  [the longest x2 3.06 us: body(): lax.ppermute(piece, 'head', [(h, h ^ c) for h in range(peers)])]
    ppermute x1, starting transfers between devices: 1.51 us -> 3.18 us  [body(): hop = lax.ppermute(add_rounded(units, stay2, came2), 'seq', back)]
    ppermute x1, starting transfers between devices: 2.12 us -> 0.51 us  [body(): cross1 = lax.ppermute(same1, 'seq', swap)]
    ppermute x1, starting transfers between devices: 2.03 us -> 0.5 us  [body(): came0 = lax.ppermute(near, 'seq', swap)]
  transfers between devices with their start and end apart: 25 -> 27, of which waited for: 13 -> 14; matrix products, arithmetic and copies ran while one was open for 2% -> 3% of each run, Pallas kernels for 10% -> 10%
where the time goes in v6:
time: 79.6 us; the launch traced here: 79.3 us
  waiting for transfers between devices  33.1 us (42%)
  starting transfers between devices  29.3 us (37%)
  Pallas kernels  13.5 us (17%)
  local copies, waits for them, and re-layouts  2.26 us (3%)
  between operations  0.92 us (1%)
    ppermute x1, waiting for transfers between devices, body(): cross2 = lax.ppermute(held, 'seq', swap)  7.13 us
    ppermute x1, waiting for transfers between devices, body(): same3 = lax.ppermute(held, 'seq', back)  4.8 us
    ppermute x1, waiting for transfers between devices, body(): same2 = lax.ppermute(same1, 'seq', ahead)  4.13 us
    pallas_call x1, Pallas kernels, own_terms(): pl.pallas_call(functools.partial(own_kernel, peers), out_shape=(piece,) *...  3.84 us
    ppermute x1, waiting for transfers between devices, body(): came3 = lax.ppermute(away3, 'seq', ahead)  3.43 us
    ppermute x1, waiting for transfers between devices, body(): came2 = lax.ppermute(leave2, 'seq', swap)  3.37 us
    ppermute x1, starting transfers between devices, body(): hop = lax.ppermute(add_rounded(units, stay2, came2), 'seq', back)  3.18 us
    ppermute x3, starting transfers between devices, exchange(): lax.ppermute(pieces[c], 'head', [(h, h ^ c) for h in range(peers)])  3.15 us
  transfers between devices with their start and end apart: 27, of which 14 were waited for; matrix products, arithmetic and copies ran while one was open for 3% of the time, Pallas kernels for 10%

profile of v6, /device:TPU:0, one launch (start us, length us, event | category | flops | bytes accessed | tf_op | source)
XLA Modules:
  0.0 79.3 jit_solution(14973674948208170817)
XLA Ops:
  0.6 1.7 %shard_map.94 = (bf16[2,64,256]{2,1,0:T(8,128)(2,1)}, bf16[2,64,256]{2,1,0:T(8,128)(2,1)}, bf16[2,64,256]{2,1,0:T(8,128)(2,1)}, bf16[2,64,256]{2,1,0:T(8,128)(2,1)}) custom-call(s32[1]{0:T(128)} %bitcast.me_ref, bf16[64,1024]{1,0:T(8,128)(2,1)} %k_ref.1, bf16[64,1024]{1,0:T(8,128)(2,1)} %v_ref.1), custom_call_target="tpu_custom_call" | custom-call | tf_op jit(solution)/shard_map/pallas_call | solution.py:63
  2.4 0.5 collective-permute-start
  2.9 2.6 %collective-permute-start.1 = (bf16[2,64,256]{2,1,0:T(8,128)(2,1)}, bf16[2,64,256]{2,1,0:T(8,128)(2,1)S(1)}, u32[]{:S(2)}, u32[]{:S(2)}) collective-permute-start(bf16[2,64,256]{2,1,0:T(8,128)(2,1)} %get-tuple-element.64), channel_id=1, source_target_pairs={{0,2},{1,3},{2,0},{3,1},{4,6},{5,7},{6,4},{7,5},{8,10},{9,11},{10,... | collective-permute-start | bytes 196616 | tf_op jit(solution)/shard_map/ppermute | solution.py:357
  5.4 0.1 collective-permute-start.2
  5.5 0.8 %copy.10 = s32[16,8,4]{2,1,0:T(8,128)S(1)} copy(s32[16,8,4]{0,2,1:T(4,128)} %param.13) | data formatting | bytes 4096 | tf_op args[6]
  6.4 0.1 reshape.13
  6.5 0.8 %constant_dynamic-update-slice_fusion.3 = bf16[8,64,256]{2,1,0:T(8,128)(2,1)S(1)} fusion(bf16[2,64,256]{2,1,0:T(8,128)(2,1)} %get-tuple-element.62), kind=kLoop, calls=%fused_computation.3 | loop fusion | bytes 131072
  7.3 1.0 %collective-permute-done.1 = bf16[2,64,256]{2,1,0:T(8,128)(2,1)S(1)} collective-permute-done((bf16[2,64,256]{2,1,0:T(8,128)(2,1)}, bf16[2,64,256]{2,1,0:T(8,128)(2,1)S(1)}, u32[]{:S(2)}, u32[]{:S(2)}) %collective-permute-start.1) | collective-permute-done | bytes 65568 | tf_op jit(solution)/shard_map/ppermute | solution.py:357
  8.4 1.4 %collective-permute-done.2 = bf16[2,64,256]{2,1,0:T(8,128)(2,1)S(1)} collective-permute-done((bf16[2,64,256]{2,1,0:T(8,128)(2,1)}, bf16[2,64,256]{2,1,0:T(8,128)(2,1)S(1)}, u32[]{:S(2)}, u32[]{:S(2)}) %collective-permute-start.2) | collective-permute-done | bytes 65568 | tf_op jit(solution)/shard_map/ppermute | solution.py:357
  9.8 1.5 %collective-permute-start.4 = (bf16[8,64,256]{2,1,0:T(8,128)(2,1)S(1)}, bf16[8,64,256]{2,1,0:T(8,128)(2,1)S(1)}, u32[]{:S(2)}, u32[]{:S(2)}) collective-permute-start(bf16[8,64,256]{2,1,0:T(8,128)(2,1)S(1)} %constant_dynamic-update-slice_fusion.own_kv_ref), channel_id=1, source_target_pairs={{0,4},{4,0},{8,12},{12,8},{16,20},{20,16},{24,28},{28,24},{1,5},{5... | collective-permute-start | bytes 786440 | tf_op jit(solution)/shard_map/ppermute | solution.py:409
  11.3 1.6 %collective-permute-start.3 = (bf16[8,64,256]{2,1,0:T(8,128)(2,1)S(1)}, bf16[8,64,256]{2,1,0:T(8,128)(2,1)S(1)}, u32[]{:S(2)}, u32[]{:S(2)}) collective-permute-start(bf16[8,64,256]{2,1,0:T(8,128)(2,1)S(1)} %constant_dynamic-update-slice_fusion.own_kv_ref), channel_id=1, source_target_pairs={{0,8},{4,12},{8,16},{12,20},{16,24},{20,28},{24,0},{28,4},{1,9},{5... | collective-permute-start | bytes 786440 | tf_op jit(solution)/shard_map/ppermute | solution.py:408
  12.9 3.0 %shard_map.95 = (bf16[528,256]{1,0:T(8,128)(2,1)}, bf16[528,256]{1,0:T(8,128)(2,1)}, bf16[1056,256]{1,0:T(8,128)(2,1)}) custom-call(s32[1]{0:T(128)} %bitcast.me_ref, bf16[64,4096]{1,0:T(8,128)(2,1)} %q_any.1, bf16[64,4096]{1,0:T(8,128)(2,1)} %do_any.1, bf16[64,4096]{1,0:T(8,128)(2,1)} %o_any.1), custom_call_target="tpu_custom_call" | custom-call | tf_op jit(solution)/shard_map/pallas_call | solution.py:117
  15.9 0.1 pad_add_fusion
  16.0 0.1 dynamic_slice.9.slot_ref
  16.1 2.2 %collective-permute-start.7 = (bf16[8,64,256]{2,1,0:T(8,128)(2,1)S(1)}, bf16[8,64,256]{2,1,0:T(8,128)(2,1)S(1)}, u32[]{:S(2)}, u32[]{:S(2)}) collective-permute-start(bf16[8,64,256]{2,1,0:T(8,128)(2,1)S(1)} %constant_dynamic-update-slice_fusion.own_kv_ref), channel_id=1, source_target_pairs={{0,24},{4,28},{8,0},{12,4},{16,8},{20,12},{24,16},{28,20},{1,25},{... | collective-permute-start | bytes 786440 | tf_op jit(solution)/shard_map/ppermute | solution.py:422
  18.3 1.3 %collective-permute-start.11 = (bf16[1056,256]{1,0:T(8,128)(2,1)}, bf16[1056,256]{1,0:T(8,128)(2,1)S(1)}, u32[]{:S(2)}, u32[]{:S(2)}) collective-permute-start(bf16[1056,256]{1,0:T(8,128)(2,1)} %get-tuple-element.78), channel_id=1, source_target_pairs={{0,2},{1,3},{2,0},{3,1},{4,6},{5,7},{6,4},{7,5},{8,10},{9,11},{10,... | collective-permute-start | bytes 1622024 | tf_op jit(solution)/shard_map/ppermute | solution.py:367
  19.6 2.5 %collective-permute-done.3 = bf16[8,64,256]{2,1,0:T(8,128)(2,1)S(1)} collective-permute-done((bf16[8,64,256]{2,1,0:T(8,128)(2,1)S(1)}, bf16[8,64,256]{2,1,0:T(8,128)(2,1)S(1)}, u32[]{:S(2)}, u32[]{:S(2)}) %collective-permute-start.3) | collective-permute-done | bytes 262176 | tf_op jit(solution)/shard_map/ppermute | solution.py:408
  22.1 0.5 collective-permute-start.6
  22.6 0.0 collective-permute-start.5
  22.6 0.2 dynamic_update_slice.21
  22.8 0.0 collective-permute-done.4
  22.9 0.1 collective-permute-start.10
  22.9 4.8 %collective-permute-done.7 = bf16[8,64,256]{2,1,0:T(8,128)(2,1)S(1)} collective-permute-done((bf16[8,64,256]{2,1,0:T(8,128)(2,1)S(1)}, bf16[8,64,256]{2,1,0:T(8,128)(2,1)S(1)}, u32[]{:S(2)}, u32[]{:S(2)}) %collective-permute-start.7) | collective-permute-done | bytes 262176 | tf_op jit(solution)/shard_map/ppermute | solution.py:422
  27.7 0.5 collective-permute-start.9
  28.3 0.0 copy-start
  28.3 0.0 copy-start.1
  28.3 0.2 collective-permute-done.6
  28.5 4.1 %collective-permute-done.5 = bf16[8,64,256]{2,1,0:T(8,128)(2,1)S(1)} collective-permute-done((bf16[8,64,256]{2,1,0:T(8,128)(2,1)S(1)}, bf16[8,64,256]{2,1,0:T(8,128)(2,1)S(1)}, u32[]{:S(2)}, u32[]{:S(2)}) %collective-permute-start.5) | collective-permute-done | bytes 262176 | tf_op jit(solution)/shard_map/ppermute | solution.py:423
  32.6 1.5 %collective-permute-start.8 = (bf16[8,64,256]{2,1,0:T(8,128)(2,1)S(1)}, bf16[8,64,256]{2,1,0:T(8,128)(2,1)S(1)}, u32[]{:S(2)}, u32[]{:S(2)}) collective-permute-start(bf16[8,64,256]{2,1,0:T(8,128)(2,1)S(1)} %collective-permute-done.5), channel_id=1, source_target_pairs={{0,4},{4,0},{8,12},{12,8},{16,20},{20,16},{24,28},{28,24},{1,5},{5... | collective-permute-start | bytes 786440 | tf_op jit(solution)/shard_map/ppermute | solution.py:427
  34.2 0.0 collective-permute-done.11
  34.3 0.1 collective-permute-start.12
  34.4 7.1 %collective-permute-done.8 = bf16[8,64,256]{2,1,0:T(8,128)(2,1)S(1)} collective-permute-done((bf16[8,64,256]{2,1,0:T(8,128)(2,1)S(1)}, bf16[8,64,256]{2,1,0:T(8,128)(2,1)S(1)}, u32[]{:S(2)}, u32[]{:S(2)}) %collective-permute-start.8) | collective-permute-done | bytes 262176 | tf_op jit(solution)/shard_map/ppermute | solution.py:427
  41.5 0.0 collective-permute-done.9
  41.6 0.0 collective-permute-done.10.refs_1_
  41.6 0.0 collective-permute-done.12.refs_3_
  41.6 3.1 %shard_map.96 = (f32[2,8,256]{2,1,0:T(8,128)S(1)}, f32[64,1024]{1,0:T(8,128)S(1)}, f32[64,1024]{1,0:T(8,128)S(1)}, f32[64,1024]{1,0:T(8,128)S(1)}, f32[64,1024]{...) custom-call(s32[1]{0:T(128)} %bitcast.me_ref, ...), custom_call_target="tpu_custom_call" | custom-call | flops 671000000 | bytes 8000000 | tf_op jit(solution)/shard_map/pallas_call | solution.py:257
  44.7 0.9 %collective-permute-start.13 = (bf16[16,64,256]{2,1,0:T(8,128)(2,1)S(1)}, bf16[16,64,256]{2,1,0:T(8,128)(2,1)S(1)}, u32[]{:S(2)}, u32[]{:S(2)}) collective-permute-start(bf16[16,64,256]{2,1,0:T(8,128)(2,1)S(1)} %get-tuple-element.80), channel_id=1, source_target_pairs={{0,8},{4,12},{8,16},{12,20},{16,24},{20,28},{24,0},{28,4},{1,9},{5... | collective-permute-start | bytes 1572872 | tf_op jit(solution)/shard_map/ppermute | solution.py:456
  45.6 1.5 %collective-permute-start.14 = (bf16[8,64,256]{2,1,0:T(8,128)(2,1)S(1)}, bf16[8,64,256]{2,1,0:T(8,128)(2,1)S(1)}, u32[]{:S(2)}, u32[]{:S(2)}) collective-permute-start(bf16[8,64,256]{2,1,0:T(8,128)(2,1)S(1)} %get-tuple-element.81), channel_id=1, source_target_pairs={{0,4},{4,0},{8,12},{12,8},{16,20},{20,16},{24,28},{28,24},{1,5},{5... | collective-permute-start | bytes 786440 | tf_op jit(solution)/shard_map/ppermute | solution.py:455
  47.1 0.5 collective-permute-start.19
  47.6 3.8 %shard_map.98 = (bf16[64,1024]{1,0:T(8,128)(2,1)S(1)}, bf16[64,1024]{1,0:T(8,128)(2,1)S(1)}, bf16[128,1024]{1,0:T(8,128)(2,1)S(1)}, f32[8,64,256]{2,1,0:T(8,128)S(1)}) custom-call(s32[1]{0:T(128)} %bitcast.me_ref, bf16[8,64,256]{2,1,0:T(8,128)(2,1)S(1)} %constant_dynamic-update-slice_fusion.own_kv_ref, f32[2,8,256]{2,1,0:T(8,128)S(1)} %get-tuple-element.82.stats_ref, ...), custom_call_target="tpu_custom_call" | custom-call | flops 335000000 | bytes 4000000 | tf_op jit(solution)/shard_map/pallas_call | solution.py:180
  51.5 3.4 %collective-permute-done.14.refs_1_ = bf16[8,64,256]{2,1,0:T(8,128)(2,1)S(1)} collective-permute-done((bf16[8,64,256]{2,1,0:T(8,128)(2,1)S(1)}, bf16[8,64,256]{2,1,0:T(8,128)(2,1)S(1)}, u32[]{:S(2)}, u32[]{:S(2)}) %collective-permute-start.14) | collective-permute-done | bytes 262176 | tf_op jit(solution)/shard_map/ppermute | solution.py:455
  54.9 3.2 %collective-permute-start.20 = (bf16[8,64,256]{2,1,0:T(8,128)(2,1)S(1)}, bf16[8,64,256]{2,1,0:T(8,128)(2,1)S(1)}, u32[]{:S(2)}, u32[]{:S(2)}) collective-permute-start(bf16[8,64,256]{2,1,0:T(8,128)(2,1)S(1)} %shard_map.101), channel_id=1, source_target_pairs={{0,24},{4,28},{8,0},{12,4},{16,8},{20,12},{24,16},{28,20},{1,25},{... | collective-permute-start | bytes 786440 | tf_op jit(solution)/shard_map/ppermute | solution.py:459
  58.1 3.4 %collective-permute-done.13.refs_1_ = bf16[16,64,256]{2,1,0:T(8,128)(2,1)S(1)} collective-permute-done((bf16[16,64,256]{2,1,0:T(8,128)(2,1)S(1)}, bf16[16,64,256]{2,1,0:T(8,128)(2,1)S(1)}, u32[]{:S(2)}, u32[]{:S(2)}) %collective-permute-start.13) | collective-permute-done | bytes 524320 | tf_op jit(solution)/shard_map/ppermute | solution.py:456
  61.5 0.1 shard_map.97
  61.6 1.7 %collective-permute-start.17 = (bf16[128,1024]{1,0:T(8,128)(2,1)S(1)}, bf16[128,1024]{1,0:T(8,128)(2,1)S(1)}, u32[]{:S(2)}, u32[]{:S(2)}) collective-permute-start(bf16[128,1024]{1,0:T(8,128)(2,1)S(1)} %get-tuple-element.99), channel_id=1, source_target_pairs={{0,2},{1,3},{2,0},{3,1},{4,6},{5,7},{6,4},{7,5},{8,10},{9,11},{10,... | collective-permute-start | bytes 786440 | tf_op jit(solution)/shard_map/ppermute | solution.py:367
  63.2 0.5 collective-permute-start.15
  63.7 0.0 collective-permute-done.19.refs_1_
  63.7 1.3 %collective-permute-done.20.refs_2_ = bf16[8,64,256]{2,1,0:T(8,128)(2,1)S(1)} collective-permute-done((bf16[8,64,256]{2,1,0:T(8,128)(2,1)S(1)}, bf16[8,64,256]{2,1,0:T(8,128)(2,1)S(1)}, u32[]{:S(2)}, u32[]{:S(2)}) %collective-permute-start.20) | collective-permute-done | bytes 262176 | tf_op jit(solution)/shard_map/ppermute | solution.py:459
  65.1 0.1 shard_map.102
  65.1 2.5 %collective-permute-start.24 = (bf16[2,64,256]{2,1,0:T(8,128)(2,1)S(1)}, bf16[2,64,256]{2,1,0:T(8,128)(2,1)S(1)}, u32[]{:S(2)}, u32[]{:S(2)}) collective-permute-start(bf16[2,64,256]{2,1,0:T(8,128)(2,1)S(1)} %get-tuple-element.108), channel_id=1, source_target_pairs={{0,26},{1,27},{2,24},{3,25},{4,30},{5,31},{6,28},{7,29},{8,2},{9,3... | collective-permute-start | bytes 196616 | tf_op jit(solution)/shard_map/ppermute | solution.py:378
  67.7 2.9 %collective-permute-start.21 = (bf16[4,64,256]{2,1,0:T(8,128)(2,1)S(1)}, bf16[4,64,256]{2,1,0:T(8,128)(2,1)S(1)}, u32[]{:S(2)}, u32[]{:S(2)}) collective-permute-start(bf16[4,64,256]{2,1,0:T(8,128)(2,1)S(1)} %get-tuple-element.105), channel_id=1, source_target_pairs={{0,24},{4,28},{8,0},{12,4},{16,8},{20,12},{24,16},{28,20},{1,25},{... | collective-permute-start | bytes 393224 | tf_op jit(solution)/shard_map/ppermute | solution.py:470
  70.6 0.1 shard_map.99
  70.7 1.7 %collective-permute-start.22 = (bf16[2,64,256]{2,1,0:T(8,128)(2,1)S(1)}, bf16[2,64,256]{2,1,0:T(8,128)(2,1)S(1)}, u32[]{:S(2)}, u32[]{:S(2)}) collective-permute-start(bf16[2,64,256]{2,1,0:T(8,128)(2,1)S(1)} %get-tuple-element.106), channel_id=1, source_target_pairs={{0,2},{1,3},{2,0},{3,1},{4,6},{5,7},{6,4},{7,5},{8,10},{9,11},{10,... | collective-permute-start | bytes 196616 | tf_op jit(solution)/shard_map/ppermute | solution.py:473
  72.4 0.9 %collective-permute-start.23 = (bf16[2,64,256]{2,1,0:T(8,128)(2,1)S(1)}, bf16[2,64,256]{2,1,0:T(8,128)(2,1)S(1)}, u32[]{:S(2)}, u32[]{:S(2)}) collective-permute-start(bf16[2,64,256]{2,1,0:T(8,128)(2,1)S(1)} %get-tuple-element.107), channel_id=1, source_target_pairs={{0,3},{1,2},{2,1},{3,0},{4,7},{5,6},{6,5},{7,4},{8,11},{9,10},{10,... | collective-permute-start | bytes 196616 | tf_op jit(solution)/shard_map/ppermute | solution.py:473
  73.3 0.0 collective-permute-done.25.refs_5_
  73.3 0.5 collective-permute-start.18
  73.8 0.3 collective-permute-done.21.refs_1_
  74.1 1.5 %collective-permute-done.22.refs_2_ = bf16[2,64,256]{2,1,0:T(8,128)(2,1)S(1)} collective-permute-done((bf16[2,64,256]{2,1,0:T(8,128)(2,1)S(1)}, bf16[2,64,256]{2,1,0:T(8,128)(2,1)S(1)}, u32[]{:S(2)}, u32[]{:S(2)}) %collective-permute-start.22) | collective-permute-done | bytes 65568 | tf_op jit(solution)/shard_map/ppermute | solution.py:473
  75.6 1.6 %collective-permute-done.23.refs_4_ = bf16[2,64,256]{2,1,0:T(8,128)(2,1)S(1)} collective-permute-done((bf16[2,64,256]{2,1,0:T(8,128)(2,1)S(1)}, bf16[2,64,256]{2,1,0:T(8,128)(2,1)S(1)}, u32[]{:S(2)}, u32[]{:S(2)}) %collective-permute-start.23) | collective-permute-done | bytes 65568 | tf_op jit(solution)/shard_map/ppermute | solution.py:473
  77.2 0.1 collective-permute-start.26
  77.3 0.0 collective-permute-done.18.refs_3_
  77.3 0.8 %shard_map.100 = bf16[64,4096]{1,0:T(8,128)(2,1)} custom-call(s32[1]{0:T(128)} %bitcast.me_ref, bf16[64,1024]{1,0:T(8,128)(2,1)S(1)} %get-tuple-element.93.refs_0_, bf16[64,1024]{1,0:T(8,128)(2,1)S(1)} %collective-permute-done.16.refs_1_, bf16[64,1024]{1,0:T(8,128)(2,1)S(1)} %get-tuple-element.124.refs_2_, bf16[64,1024]{1,0:T(8,128)(2,1)S(1)} %collective-permute-done.18.refs_3_), custom_call_target="tpu_custom_call" | custom-call | tf_op jit(solution)/shard_map/pallas_call | solution.py:335
  78.1 0.4 collective-permute-done.26.refs_1_
  78.5 0.8 shard_map.104
  (25 shorter events, 0.3 us)
Async XLA Ops:
  2.4 5.0 %collective-permute-start = (bf16[2,64,256]{2,1,0:T(8,128)(2,1)}, bf16[2,64,256]{2,1,0:T(8,128)(2,1)S(1)}, u32[]{:S(2)}, u32[]{:S(2)}) collective-permute-start(bf16[2,64,256]{2,1,0:T(8,128)(2,1)} %get-tuple-element.63), channel_id=1, source_target_pairs={{0,1},{1,0},{2,3},{3,2},{4,5},{5,4},{6,7},{7,6},{8,9},{9,8},{10,11... | collective-permute-start | bytes 196616 | tf_op jit(solution)/shard_map/ppermute | solution.py:357
  2.9 5.5 %collective-permute-start.1 = (bf16[2,64,256]{2,1,0:T(8,128)(2,1)}, bf16[2,64,256]{2,1,0:T(8,128)(2,1)S(1)}, u32[]{:S(2)}, u32[]{:S(2)}) collective-permute-start(bf16[2,64,256]{2,1,0:T(8,128)(2,1)} %get-tuple-element.64), channel_id=1, source_target_pairs={{0,2},{1,3},{2,0},{3,1},{4,6},{5,7},{6,4},{7,5},{8,10},{9,11},{10,... | collective-permute-start | bytes 196616 | tf_op jit(solution)/shard_map/ppermute | solution.py:357
  5.4 4.3 %collective-permute-start.2 = (bf16[2,64,256]{2,1,0:T(8,128)(2,1)}, bf16[2,64,256]{2,1,0:T(8,128)(2,1)S(1)}, u32[]{:S(2)}, u32[]{:S(2)}) collective-permute-start(bf16[2,64,256]{2,1,0:T(8,128)(2,1)} %get-tuple-element.65), channel_id=1, source_target_pairs={{0,3},{1,2},{2,1},{3,0},{4,7},{5,6},{6,5},{7,4},{8,11},{9,10},{10,... | collective-permute-start | bytes 196616 | tf_op jit(solution)/shard_map/ppermute | solution.py:357
  9.8 13.0 %collective-permute-start.4 = (bf16[8,64,256]{2,1,0:T(8,128)(2,1)S(1)}, bf16[8,64,256]{2,1,0:T(8,128)(2,1)S(1)}, u32[]{:S(2)}, u32[]{:S(2)}) collective-permute-start(bf16[8,64,256]{2,1,0:T(8,128)(2,1)S(1)} %constant_dynamic-update-slice_fusion.own_kv_ref), channel_id=1, source_target_pairs={{0,4},{4,0},{8,12},{12,8},{16,20},{20,16},{24,28},{28,24},{1,5},{5... | collective-permute-start | bytes 786440 | tf_op jit(solution)/shard_map/ppermute | solution.py:409
  11.3 10.8 %collective-permute-start.3 = (bf16[8,64,256]{2,1,0:T(8,128)(2,1)S(1)}, bf16[8,64,256]{2,1,0:T(8,128)(2,1)S(1)}, u32[]{:S(2)}, u32[]{:S(2)}) collective-permute-start(bf16[8,64,256]{2,1,0:T(8,128)(2,1)S(1)} %constant_dynamic-update-slice_fusion.own_kv_ref), channel_id=1, source_target_pairs={{0,8},{4,12},{8,16},{12,20},{16,24},{20,28},{24,0},{28,4},{1,9},{5... | collective-permute-start | bytes 786440 | tf_op jit(solution)/shard_map/ppermute | solution.py:408
  15.9 7.0 %copy-start.2 = (bf16[528,256]{1,0:T(8,128)(2,1)S(1)}, bf16[528,256]{1,0:T(8,128)(2,1)}, u32[]{:S(2)}) copy-start(bf16[528,256]{1,0:T(8,128)(2,1)} %get-tuple-element.77) | copy-start | bytes 811012
  16.1 11.7 %collective-permute-start.7 = (bf16[8,64,256]{2,1,0:T(8,128)(2,1)S(1)}, bf16[8,64,256]{2,1,0:T(8,128)(2,1)S(1)}, u32[]{:S(2)}, u32[]{:S(2)}) collective-permute-start(bf16[8,64,256]{2,1,0:T(8,128)(2,1)S(1)} %constant_dynamic-update-slice_fusion.own_kv_ref), channel_id=1, source_target_pairs={{0,24},{4,28},{8,0},{12,4},{16,8},{20,12},{24,16},{28,20},{1,25},{... | collective-permute-start | bytes 786440 | tf_op jit(solution)/shard_map/ppermute | solution.py:422
  18.3 15.9 %collective-permute-start.11 = (bf16[1056,256]{1,0:T(8,128)(2,1)}, bf16[1056,256]{1,0:T(8,128)(2,1)S(1)}, u32[]{:S(2)}, u32[]{:S(2)}) collective-permute-start(bf16[1056,256]{1,0:T(8,128)(2,1)} %get-tuple-element.78), channel_id=1, source_target_pairs={{0,2},{1,3},{2,0},{3,1},{4,6},{5,7},{6,4},{7,5},{8,10},{9,11},{10,... | collective-permute-start | bytes 1622024 | tf_op jit(solution)/shard_map/ppermute | solution.py:367
  22.1 6.4 %collective-permute-start.6 = (bf16[8,64,256]{2,1,0:T(8,128)(2,1)S(1)}, bf16[8,64,256]{2,1,0:T(8,128)(2,1)S(1)}, u32[]{:S(2)}, u32[]{:S(2)}) collective-permute-start(bf16[8,64,256]{2,1,0:T(8,128)(2,1)S(1)} %collective-permute-done.3), channel_id=1, source_target_pairs={{0,4},{4,0},{8,12},{12,8},{16,20},{20,16},{24,28},{28,24},{1,5},{5... | collective-permute-start | bytes 786440 | tf_op jit(solution)/shard_map/ppermute | solution.py:424
  22.6 10.0 %collective-permute-start.5 = (bf16[8,64,256]{2,1,0:T(8,128)(2,1)S(1)}, bf16[8,64,256]{2,1,0:T(8,128)(2,1)S(1)}, u32[]{:S(2)}, u32[]{:S(2)}) collective-permute-start(bf16[8,64,256]{2,1,0:T(8,128)(2,1)S(1)} %collective-permute-done.3), channel_id=1, source_target_pairs={{0,8},{4,12},{8,16},{12,20},{16,24},{20,28},{24,0},{28,4},{1,9},{5... | collective-permute-start | bytes 786440 | tf_op jit(solution)/shard_map/ppermute | solution.py:423
  22.9 18.7 %collective-permute-start.10 = (bf16[528,256]{1,0:T(8,128)(2,1)S(1)}, bf16[528,256]{1,0:T(8,128)(2,1)S(1)}, u32[]{:S(2)}, u32[]{:S(2)}) collective-permute-start(bf16[528,256]{1,0:T(8,128)(2,1)S(1)} %copy-done.2), channel_id=1, source_target_pairs={{0,1},{1,0},{2,3},{3,2},{4,5},{5,4},{6,7},{7,6},{8,9},{9,8},{10,11... | collective-permute-start | bytes 811016 | tf_op jit(solution)/shard_map/ppermute | solution.py:368
  27.7 13.8 %collective-permute-start.9 = (bf16[8,64,256]{2,1,0:T(8,128)(2,1)S(1)}, bf16[8,64,256]{2,1,0:T(8,128)(2,1)S(1)}, u32[]{:S(2)}, u32[]{:S(2)}) collective-permute-start(bf16[8,64,256]{2,1,0:T(8,128)(2,1)S(1)} %collective-permute-done.7), channel_id=1, source_target_pairs={{0,4},{4,0},{8,12},{12,8},{16,20},{20,16},{24,28},{28,24},{1,5},{5... | collective-permute-start | bytes 786440 | tf_op jit(solution)/shard_map/ppermute | solution.py:425
  28.3 13.3 %copy-start = (bf16[528,256]{1,0:T(8,128)(2,1)S(1)}, bf16[528,256]{1,0:T(8,128)(2,1)}, u32[]{:S(2)}) copy-start(bf16[528,256]{1,0:T(8,128)(2,1)} %get-tuple-element.76.refs_0_) | copy-start | bytes 811012
  28.3 13.3 %copy-start.1 = (f32[256,8]{0,1:T(8,128)S(1)}, f32[256,8]{0,1:T(8,128)}, u32[]{:S(2)}) copy-start(f32[256,8]{0,1:T(8,128)} %param.12) | copy-start | bytes 24580
  32.6 8.9 %collective-permute-start.8 = (bf16[8,64,256]{2,1,0:T(8,128)(2,1)S(1)}, bf16[8,64,256]{2,1,0:T(8,128)(2,1)S(1)}, u32[]{:S(2)}, u32[]{:S(2)}) collective-permute-start(bf16[8,64,256]{2,1,0:T(8,128)(2,1)S(1)} %collective-permute-done.5), channel_id=1, source_target_pairs={{0,4},{4,0},{8,12},{12,8},{16,20},{20,16},{24,28},{28,24},{1,5},{5... | collective-permute-start | bytes 786440 | tf_op jit(solution)/shard_map/ppermute | solution.py:427
  34.3 7.3 %collective-permute-start.12 = (bf16[528,256]{1,0:T(8,128)(2,1)S(1)}, bf16[528,256]{1,0:T(8,128)(2,1)S(1)}, u32[]{:S(2)}, u32[]{:S(2)}) collective-permute-start(bf16[528,256]{1,0:T(8,128)(2,1)S(1)} %get-tuple-element.121), channel_id=1, source_target_pairs={{0,1},{1,0},{2,3},{3,2},{4,5},{5,4},{6,7},{7,6},{8,9},{9,8},{10,11... | collective-permute-start | bytes 811016 | tf_op jit(solution)/shard_map/ppermute | solution.py:369
  44.7 16.8 %collective-permute-start.13 = (bf16[16,64,256]{2,1,0:T(8,128)(2,1)S(1)}, bf16[16,64,256]{2,1,0:T(8,128)(2,1)S(1)}, u32[]{:S(2)}, u32[]{:S(2)}) collective-permute-start(bf16[16,64,256]{2,1,0:T(8,128)(2,1)S(1)} %get-tuple-element.80), channel_id=1, source_target_pairs={{0,8},{4,12},{8,16},{12,20},{16,24},{20,28},{24,0},{28,4},{1,9},{5... | collective-permute-start | bytes 1572872 | tf_op jit(solution)/shard_map/ppermute | solution.py:456
  45.6 9.2 %collective-permute-start.14 = (bf16[8,64,256]{2,1,0:T(8,128)(2,1)S(1)}, bf16[8,64,256]{2,1,0:T(8,128)(2,1)S(1)}, u32[]{:S(2)}, u32[]{:S(2)}) collective-permute-start(bf16[8,64,256]{2,1,0:T(8,128)(2,1)S(1)} %get-tuple-element.81), channel_id=1, source_target_pairs={{0,4},{4,0},{8,12},{12,8},{16,20},{20,16},{24,28},{28,24},{1,5},{5... | collective-permute-start | bytes 786440 | tf_op jit(solution)/shard_map/ppermute | solution.py:455
  47.1 16.6 %collective-permute-start.19 = (bf16[8,64,256]{2,1,0:T(8,128)(2,1)S(1)}, bf16[8,64,256]{2,1,0:T(8,128)(2,1)S(1)}, u32[]{:S(2)}, u32[]{:S(2)}) collective-permute-start(bf16[8,64,256]{2,1,0:T(8,128)(2,1)S(1)} %get-tuple-element.102), channel_id=1, source_target_pairs={{0,4},{4,0},{8,12},{12,8},{16,20},{20,16},{24,28},{28,24},{1,5},{5... | collective-permute-start | bytes 786440 | tf_op jit(solution)/shard_map/ppermute | solution.py:457
  54.9 10.2 %collective-permute-start.20 = (bf16[8,64,256]{2,1,0:T(8,128)(2,1)S(1)}, bf16[8,64,256]{2,1,0:T(8,128)(2,1)S(1)}, u32[]{:S(2)}, u32[]{:S(2)}) collective-permute-start(bf16[8,64,256]{2,1,0:T(8,128)(2,1)S(1)} %shard_map.101), channel_id=1, source_target_pairs={{0,24},{4,28},{8,0},{12,4},{16,8},{20,12},{24,16},{28,20},{1,25},{... | collective-permute-start | bytes 786440 | tf_op jit(solution)/shard_map/ppermute | solution.py:459
  61.6 9.0 %collective-permute-start.17 = (bf16[128,1024]{1,0:T(8,128)(2,1)S(1)}, bf16[128,1024]{1,0:T(8,128)(2,1)S(1)}, u32[]{:S(2)}, u32[]{:S(2)}) collective-permute-start(bf16[128,1024]{1,0:T(8,128)(2,1)S(1)} %get-tuple-element.99), channel_id=1, source_target_pairs={{0,2},{1,3},{2,0},{3,1},{4,6},{5,7},{6,4},{7,5},{8,10},{9,11},{10,... | collective-permute-start | bytes 786440 | tf_op jit(solution)/shard_map/ppermute | solution.py:367
  63.2 7.4 %collective-permute-start.15 = (bf16[8,64,256]{2,1,0:T(8,128)(2,1)S(1)}, bf16[8,64,256]{2,1,0:T(8,128)(2,1)S(1)}, u32[]{:S(2)}, u32[]{:S(2)}) collective-permute-start(bf16[8,64,256]{2,1,0:T(8,128)(2,1)S(1)} %shard_map.97), channel_id=1, source_target_pairs={{0,4},{4,0},{8,12},{12,8},{16,20},{20,16},{24,28},{28,24},{1,5},{5... | collective-permute-start | bytes 786440 | tf_op jit(solution)/shard_map/ppermute | solution.py:462
  65.1 8.1 %collective-permute-start.24 = (bf16[2,64,256]{2,1,0:T(8,128)(2,1)S(1)}, bf16[2,64,256]{2,1,0:T(8,128)(2,1)S(1)}, u32[]{:S(2)}, u32[]{:S(2)}) collective-permute-start(bf16[2,64,256]{2,1,0:T(8,128)(2,1)S(1)} %get-tuple-element.108), channel_id=1, source_target_pairs={{0,26},{1,27},{2,24},{3,25},{4,30},{5,31},{6,28},{7,29},{8,2},{9,3... | collective-permute-start | bytes 196616 | tf_op jit(solution)/shard_map/ppermute | solution.py:378
  67.7 5.6 %collective-permute-start.25 = (bf16[2,64,256]{2,1,0:T(8,128)(2,1)S(1)}, bf16[2,64,256]{2,1,0:T(8,128)(2,1)S(1)}, u32[]{:S(2)}, u32[]{:S(2)}) collective-permute-start(bf16[2,64,256]{2,1,0:T(8,128)(2,1)S(1)} %get-tuple-element.109), channel_id=1, source_target_pairs={{0,27},{1,26},{2,25},{3,24},{4,31},{5,30},{6,29},{7,28},{8,3},{9,2... | collective-permute-start | bytes 196616 | tf_op jit(solution)/shard_map/ppermute | solution.py:378
  67.7 6.4 %collective-permute-start.21 = (bf16[4,64,256]{2,1,0:T(8,128)(2,1)S(1)}, bf16[4,64,256]{2,1,0:T(8,128)(2,1)S(1)}, u32[]{:S(2)}, u32[]{:S(2)}) collective-permute-start(bf16[4,64,256]{2,1,0:T(8,128)(2,1)S(1)} %get-tuple-element.105), channel_id=1, source_target_pairs={{0,24},{4,28},{8,0},{12,4},{16,8},{20,12},{24,16},{28,20},{1,25},{... | collective-permute-start | bytes 393224 | tf_op jit(solution)/shard_map/ppermute | solution.py:470
  70.7 4.8 %collective-permute-start.22 = (bf16[2,64,256]{2,1,0:T(8,128)(2,1)S(1)}, bf16[2,64,256]{2,1,0:T(8,128)(2,1)S(1)}, u32[]{:S(2)}, u32[]{:S(2)}) collective-permute-start(bf16[2,64,256]{2,1,0:T(8,128)(2,1)S(1)} %get-tuple-element.106), channel_id=1, source_target_pairs={{0,2},{1,3},{2,0},{3,1},{4,6},{5,7},{6,4},{7,5},{8,10},{9,11},{10,... | collective-permute-start | bytes 196616 | tf_op jit(solution)/shard_map/ppermute | solution.py:473
  72.4 4.8 %collective-permute-start.23 = (bf16[2,64,256]{2,1,0:T(8,128)(2,1)S(1)}, bf16[2,64,256]{2,1,0:T(8,128)(2,1)S(1)}, u32[]{:S(2)}, u32[]{:S(2)}) collective-permute-start(bf16[2,64,256]{2,1,0:T(8,128)(2,1)S(1)} %get-tuple-element.107), channel_id=1, source_target_pairs={{0,3},{1,2},{2,1},{3,0},{4,7},{5,6},{6,5},{7,4},{8,11},{9,10},{10,... | collective-permute-start | bytes 196616 | tf_op jit(solution)/shard_map/ppermute | solution.py:473
  73.3 4.0 %collective-permute-start.16 = (bf16[64,1024]{1,0:T(8,128)(2,1)S(1)}, bf16[64,1024]{1,0:T(8,128)(2,1)S(1)}, u32[]{:S(2)}, u32[]{:S(2)}) collective-permute-start(bf16[64,1024]{1,0:T(8,128)(2,1)S(1)} %get-tuple-element.98), channel_id=1, source_target_pairs={{0,1},{1,0},{2,3},{3,2},{4,5},{5,4},{6,7},{7,6},{8,9},{9,8},{10,11... | collective-permute-start | bytes 393224 | tf_op jit(solution)/shard_map/ppermute | solution.py:368
  73.3 4.0 %collective-permute-start.18 = (bf16[64,1024]{1,0:T(8,128)(2,1)S(1)}, bf16[64,1024]{1,0:T(8,128)(2,1)S(1)}, u32[]{:S(2)}, u32[]{:S(2)}) collective-permute-start(bf16[64,1024]{1,0:T(8,128)(2,1)S(1)} %get-tuple-element.123), channel_id=1, source_target_pairs={{0,1},{1,0},{2,3},{3,2},{4,5},{5,4},{6,7},{7,6},{8,9},{9,8},{10,11... | collective-permute-start | bytes 393224 | tf_op jit(solution)/shard_map/ppermute | solution.py:369
  77.2 1.3 %collective-permute-start.26 = (bf16[2,64,256]{2,1,0:T(8,128)(2,1)S(1)}, bf16[2,64,256]{2,1,0:T(8,128)(2,1)S(1)}, u32[]{:S(2)}, u32[]{:S(2)}) collective-permute-start(bf16[2,64,256]{2,1,0:T(8,128)(2,1)S(1)} %get-tuple-element.114), channel_id=1, source_target_pairs={{0,1},{1,0},{2,3},{3,2},{4,5},{5,4},{6,7},{7,6},{8,9},{9,8},{10,11... | collective-permute-start | bytes 196616 | tf_op jit(solution)/shard_map/ppermute | solution.py:478

commit v7 on v6

--- a/solution.py
+++ b/solution.py
@@ -360,13 +360,16 @@
     return [pieces[0]] + moved
 
 
-def exchange_rows(here, near, far):
+def exchange_cores(here, near, far):
     rows = here.shape[0]
     flip = [(h, h ^ 1) for h in range(4)]
-    across = [(h, h ^ 2) for h in range(4)]
-    far = lax.ppermute(far, "head", across)
     near = lax.ppermute(near, "head", flip)
     return [here, near, far[:rows], lax.ppermute(far[rows:], "head", flip)]
+
+
+def exchange_rows(here, near, far):
+    across = [(h, h ^ 2) for h in range(4)]
+    return exchange_cores(here, near, lax.ppermute(far, "head", across))
 
 
 def send_back(piece, c, shards, peers):
@@ -455,20 +458,21 @@
         came2 = lax.ppermute(leave2, "seq", swap)
         came3 = lax.ppermute(away3, "seq", ahead)
         came1 = lax.ppermute(leave1, "seq", swap)
-        came2, dq = lax.optimization_barrier((came2, dq))
         hop = lax.ppermute(add_rounded(units, stay2, came2), "seq", back)
+        across = [(h, h ^ 2) for h in range(peers)]
+        dq[2] = lax.ppermute(dq[2], "head", across)
+        came3, dq[2] = lax.optimization_barrier((came3, dq[2]))
         near = add_rounded(units, leave0, (came3, units))
-        near, dq = lax.optimization_barrier((near, dq))
         came0 = lax.ppermute(near, "seq", swap)
         half, pair = units // 2, units // peers
         outs = [(half, wide), (pair, low), (pair, low)]
         base, *base_far = add_parts(outs, own, came3, came0, bytes_moved=16_000_000)
-        base, dq[1:2] = lax.optimization_barrier((base, dq[1:2]))
+        base, dq = lax.optimization_barrier((base, dq))
         outs = [(half, low), (pair, low), (pair, low)]
         side, *side_far = add_parts(outs, stay1, came1, hop)
         side_far = [send_back(piece, c, shards, peers) for c, piece in zip((2, 3), side_far)]
         side = lax.ppermute(side, "seq", back)
-        dq = exchange_rows(*dq)
+        dq = exchange_cores(*dq)
         base_far = [
             lax.ppermute(piece, "head", [(h, h ^ c) for h in range(peers)])
             for c, piece in zip((2, 3), base_far)

time: 79.6 us -> 77.7 us (0.976)
  waiting for transfers between devices: 33.1 us -> 32 us
    ppermute x1, waiting for transfers between devices: 3.37 us -> 0.01 us  [body(): came2 = lax.ppermute(leave2, 'seq', swap)]
    ppermute x6, waiting for transfers between devices: 0.02 us -> 1.97 us  [the longest x1 1.96 us: body(): dq[2] = lax.ppermute(dq[2], 'head', across)]
    ppermute x2, waiting for transfers between devices: 3.06 us -> 1.13 us  [body(): lax.ppermute(piece, 'head', [(h, h ^ c) for h in range(peers)])]
    ppermute x1, waiting for transfers between devices: 1.33 us -> 2.93 us  [body(): hop = lax.ppermute(add_rounded(units, stay2, came2), 'seq', back)]
    ppermute x2, starting transfers between devices: 2.57 us -> 1.39 us  [body(): lax.ppermute(piece, 'head', [(h, h ^ c) for h in range(peers)])]
where the time goes in v7:
time: 77.7 us; the launch traced here: 77.4 us
  waiting for transfers between devices  32 us (41%)
  starting transfers between devices  28.6 us (37%)
  Pallas kernels  13.5 us (17%)
  local copies, waits for them, and re-layouts  2.26 us (3%)
  between operations  0.89 us (1%)
    ppermute x1, waiting for transfers between devices, body(): cross2 = lax.ppermute(held, 'seq', swap)  7.13 us
    ppermute x1, waiting for transfers between devices, body(): same3 = lax.ppermute(held, 'seq', back)  4.8 us
    ppermute x1, waiting for transfers between devices, body(): same2 = lax.ppermute(same1, 'seq', ahead)  4.13 us
    pallas_call x1, Pallas kernels, own_terms(): pl.pallas_call(functools.partial(own_kernel, peers), out_shape=(piece,) *...  3.85 us
    ppermute x1, starting transfers between devices, body(): hop = lax.ppermute(add_rounded(units, stay2, came2), 'seq', back)  3.18 us
    ppermute x3, starting transfers between devices, exchange(): lax.ppermute(pieces[c], 'head', [(h, h ^ c) for h in range(peers)])  3.15 us
    ppermute x1, waiting for transfers between devices, body(): came3 = lax.ppermute(away3, 'seq', ahead)  3.14 us
    pallas_call x1, Pallas kernels, listed_terms(): pl.pallas_call(functools.partial(listed_kernel, peers), out_shape=(jax.Sh...  3.1 us
  transfers between devices with their start and end apart: 27, of which 14 were waited for; matrix products, arithmetic and copies ran while one was open for 3% of the time, Pallas kernels for 10%

profile of v7, /device:TPU:0, one launch (start us, length us, event | category | flops | bytes accessed | tf_op | source)
XLA Modules:
  0.0 77.4 jit_solution(15761010056790539377)
XLA Ops:
  0.6 1.7 %shard_map.94 = (bf16[2,64,256]{2,1,0:T(8,128)(2,1)}, bf16[2,64,256]{2,1,0:T(8,128)(2,1)}, bf16[2,64,256]{2,1,0:T(8,128)(2,1)}, bf16[2,64,256]{2,1,0:T(8,128)(2,1)}) custom-call(s32[1]{0:T(128)} %bitcast.me_ref, bf16[64,1024]{1,0:T(8,128)(2,1)} %k_ref.1, bf16[64,1024]{1,0:T(8,128)(2,1)} %v_ref.1), custom_call_target="tpu_custom_call" | custom-call | tf_op jit(solution)/shard_map/pallas_call | solution.py:63
  2.4 0.5 collective-permute-start
  2.9 2.6 %collective-permute-start.1 = (bf16[2,64,256]{2,1,0:T(8,128)(2,1)}, bf16[2,64,256]{2,1,0:T(8,128)(2,1)S(1)}, u32[]{:S(2)}, u32[]{:S(2)}) collective-permute-start(bf16[2,64,256]{2,1,0:T(8,128)(2,1)} %get-tuple-element.60), channel_id=1, source_target_pairs={{0,2},{1,3},{2,0},{3,1},{4,6},{5,7},{6,4},{7,5},{8,10},{9,11},{10,... | collective-permute-start | bytes 196616 | tf_op jit(solution)/shard_map/ppermute | solution.py:357
  5.4 0.1 collective-permute-start.2
  5.5 0.8 %copy.10 = s32[16,8,4]{2,1,0:T(8,128)S(1)} copy(s32[16,8,4]{0,2,1:T(4,128)} %param.13) | data formatting | bytes 4096 | tf_op args[6]
  6.4 0.1 reshape.13
  6.5 0.8 %constant_dynamic-update-slice_fusion.3 = bf16[8,64,256]{2,1,0:T(8,128)(2,1)S(1)} fusion(bf16[2,64,256]{2,1,0:T(8,128)(2,1)} %get-tuple-element.58), kind=kLoop, calls=%fused_computation.3 | loop fusion | bytes 131072
  7.3 1.0 %collective-permute-done.1 = bf16[2,64,256]{2,1,0:T(8,128)(2,1)S(1)} collective-permute-done((bf16[2,64,256]{2,1,0:T(8,128)(2,1)}, bf16[2,64,256]{2,1,0:T(8,128)(2,1)S(1)}, u32[]{:S(2)}, u32[]{:S(2)}) %collective-permute-start.1) | collective-permute-done | bytes 65568 | tf_op jit(solution)/shard_map/ppermute | solution.py:357
  8.4 1.4 %collective-permute-done.2 = bf16[2,64,256]{2,1,0:T(8,128)(2,1)S(1)} collective-permute-done((bf16[2,64,256]{2,1,0:T(8,128)(2,1)}, bf16[2,64,256]{2,1,0:T(8,128)(2,1)S(1)}, u32[]{:S(2)}, u32[]{:S(2)}) %collective-permute-start.2) | collective-permute-done | bytes 65568 | tf_op jit(solution)/shard_map/ppermute | solution.py:357
  9.8 1.5 %collective-permute-start.4 = (bf16[8,64,256]{2,1,0:T(8,128)(2,1)S(1)}, bf16[8,64,256]{2,1,0:T(8,128)(2,1)S(1)}, u32[]{:S(2)}, u32[]{:S(2)}) collective-permute-start(bf16[8,64,256]{2,1,0:T(8,128)(2,1)S(1)} %constant_dynamic-update-slice_fusion.own_kv_ref), channel_id=1, source_target_pairs={{0,4},{4,0},{8,12},{12,8},{16,20},{20,16},{24,28},{28,24},{1,5},{5... | collective-permute-start | bytes 786440 | tf_op jit(solution)/shard_map/ppermute | solution.py:412
  11.3 1.6 %collective-permute-start.3 = (bf16[8,64,256]{2,1,0:T(8,128)(2,1)S(1)}, bf16[8,64,256]{2,1,0:T(8,128)(2,1)S(1)}, u32[]{:S(2)}, u32[]{:S(2)}) collective-permute-start(bf16[8,64,256]{2,1,0:T(8,128)(2,1)S(1)} %constant_dynamic-update-slice_fusion.own_kv_ref), channel_id=1, source_target_pairs={{0,8},{4,12},{8,16},{12,20},{16,24},{20,28},{24,0},{28,4},{1,9},{5... | collective-permute-start | bytes 786440 | tf_op jit(solution)/shard_map/ppermute | solution.py:411
  12.9 3.0 %shard_map.95 = (bf16[528,256]{1,0:T(8,128)(2,1)}, bf16[528,256]{1,0:T(8,128)(2,1)}, bf16[1056,256]{1,0:T(8,128)(2,1)}) custom-call(s32[1]{0:T(128)} %bitcast.me_ref, bf16[64,4096]{1,0:T(8,128)(2,1)} %q_any.1, bf16[64,4096]{1,0:T(8,128)(2,1)} %do_any.1, bf16[64,4096]{1,0:T(8,128)(2,1)} %o_any.1), custom_call_target="tpu_custom_call" | custom-call | tf_op jit(solution)/shard_map/pallas_call | solution.py:117
  15.9 0.1 pad_add_fusion
  16.0 0.1 dynamic_slice.9.slot_ref
  16.1 2.2 %collective-permute-start.7 = (bf16[8,64,256]{2,1,0:T(8,128)(2,1)S(1)}, bf16[8,64,256]{2,1,0:T(8,128)(2,1)S(1)}, u32[]{:S(2)}, u32[]{:S(2)}) collective-permute-start(bf16[8,64,256]{2,1,0:T(8,128)(2,1)S(1)} %constant_dynamic-update-slice_fusion.own_kv_ref), channel_id=1, source_target_pairs={{0,24},{4,28},{8,0},{12,4},{16,8},{20,12},{24,16},{28,20},{1,25},{... | collective-permute-start | bytes 786440 | tf_op jit(solution)/shard_map/ppermute | solution.py:425
  18.3 1.3 %collective-permute-start.11 = (bf16[1056,256]{1,0:T(8,128)(2,1)}, bf16[1056,256]{1,0:T(8,128)(2,1)S(1)}, u32[]{:S(2)}, u32[]{:S(2)}) collective-permute-start(bf16[1056,256]{1,0:T(8,128)(2,1)} %get-tuple-element.74), channel_id=1, source_target_pairs={{0,2},{1,3},{2,0},{3,1},{4,6},{5,7},{6,4},{7,5},{8,10},{9,11},{10,... | collective-permute-start | bytes 1622024 | tf_op jit(solution)/shard_map/ppermute | solution.py:372
  19.6 2.5 %collective-permute-done.3 = bf16[8,64,256]{2,1,0:T(8,128)(2,1)S(1)} collective-permute-done((bf16[8,64,256]{2,1,0:T(8,128)(2,1)S(1)}, bf16[8,64,256]{2,1,0:T(8,128)(2,1)S(1)}, u32[]{:S(2)}, u32[]{:S(2)}) %collective-permute-start.3) | collective-permute-done | bytes 262176 | tf_op jit(solution)/shard_map/ppermute | solution.py:411
  22.1 0.5 collective-permute-start.6
  22.6 0.0 collective-permute-start.5
  22.6 0.2 dynamic_update_slice.21
  22.9 0.1 collective-permute-start.10
  22.9 4.8 %collective-permute-done.7 = bf16[8,64,256]{2,1,0:T(8,128)(2,1)S(1)} collective-permute-done((bf16[8,64,256]{2,1,0:T(8,128)(2,1)S(1)}, bf16[8,64,256]{2,1,0:T(8,128)(2,1)S(1)}, u32[]{:S(2)}, u32[]{:S(2)}) %collective-permute-start.7) | collective-permute-done | bytes 262176 | tf_op jit(solution)/shard_map/ppermute | solution.py:425
  27.7 0.5 collective-permute-start.9
  28.3 0.0 copy-start
  28.3 0.0 copy-start.1
  28.3 0.2 collective-permute-done.6
  28.5 4.1 %collective-permute-done.5 = bf16[8,64,256]{2,1,0:T(8,128)(2,1)S(1)} collective-permute-done((bf16[8,64,256]{2,1,0:T(8,128)(2,1)S(1)}, bf16[8,64,256]{2,1,0:T(8,128)(2,1)S(1)}, u32[]{:S(2)}, u32[]{:S(2)}) %collective-permute-start.5) | collective-permute-done | bytes 262176 | tf_op jit(solution)/shard_map/ppermute | solution.py:426
  32.6 1.5 %collective-permute-start.8 = (bf16[8,64,256]{2,1,0:T(8,128)(2,1)S(1)}, bf16[8,64,256]{2,1,0:T(8,128)(2,1)S(1)}, u32[]{:S(2)}, u32[]{:S(2)}) collective-permute-start(bf16[8,64,256]{2,1,0:T(8,128)(2,1)S(1)} %collective-permute-done.5), channel_id=1, source_target_pairs={{0,4},{4,0},{8,12},{12,8},{16,20},{20,16},{24,28},{28,24},{1,5},{5... | collective-permute-start | bytes 786440 | tf_op jit(solution)/shard_map/ppermute | solution.py:430
  34.2 0.0 collective-permute-done.11
  34.3 0.1 collective-permute-start.12
  34.4 7.1 %collective-permute-done.8 = bf16[8,64,256]{2,1,0:T(8,128)(2,1)S(1)} collective-permute-done((bf16[8,64,256]{2,1,0:T(8,128)(2,1)S(1)}, bf16[8,64,256]{2,1,0:T(8,128)(2,1)S(1)}, u32[]{:S(2)}, u32[]{:S(2)}) %collective-permute-start.8) | collective-permute-done | bytes 262176 | tf_op jit(solution)/shard_map/ppermute | solution.py:430
  41.5 0.0 collective-permute-done.9
  41.6 0.0 collective-permute-done.12.refs_3_
  41.6 3.1 %shard_map.96 = (f32[2,8,256]{2,1,0:T(8,128)S(1)}, f32[64,1024]{1,0:T(8,128)S(1)}, f32[64,1024]{1,0:T(8,128)S(1)}, f32[64,1024]{1,0:T(8,128)S(1)}, f32[64,1024]{...) custom-call(s32[1]{0:T(128)} %bitcast.me_ref, ...), custom_call_target="tpu_custom_call" | custom-call | flops 671000000 | bytes 8000000 | tf_op jit(solution)/shard_map/pallas_call | solution.py:257
  44.7 0.9 %collective-permute-start.13 = (bf16[16,64,256]{2,1,0:T(8,128)(2,1)S(1)}, bf16[16,64,256]{2,1,0:T(8,128)(2,1)S(1)}, u32[]{:S(2)}, u32[]{:S(2)}) collective-permute-start(bf16[16,64,256]{2,1,0:T(8,128)(2,1)S(1)} %get-tuple-element.81), channel_id=1, source_target_pairs={{0,8},{4,12},{8,16},{12,20},{16,24},{20,28},{24,0},{28,4},{1,9},{5... | collective-permute-start | bytes 1572872 | tf_op jit(solution)/shard_map/ppermute | solution.py:459
  45.6 1.5 %collective-permute-start.19 = (bf16[8,64,256]{2,1,0:T(8,128)(2,1)S(1)}, bf16[8,64,256]{2,1,0:T(8,128)(2,1)S(1)}, u32[]{:S(2)}, u32[]{:S(2)}) collective-permute-start(bf16[8,64,256]{2,1,0:T(8,128)(2,1)S(1)} %get-tuple-element.96), channel_id=1, source_target_pairs={{0,4},{4,0},{8,12},{12,8},{16,20},{20,16},{24,28},{28,24},{1,5},{5... | collective-permute-start | bytes 786440 | tf_op jit(solution)/shard_map/ppermute | solution.py:458
  47.1 3.8 %shard_map.97 = (bf16[64,1024]{1,0:T(8,128)(2,1)S(1)}, bf16[64,1024]{1,0:T(8,128)(2,1)S(1)}, bf16[128,1024]{1,0:T(8,128)(2,1)S(1)}, f32[8,64,256]{2,1,0:T(8,128)S(1)}) custom-call(s32[1]{0:T(128)} %bitcast.me_ref, bf16[8,64,256]{2,1,0:T(8,128)(2,1)S(1)} %constant_dynamic-update-slice_fusion.own_kv_ref, f32[2,8,256]{2,1,0:T(8,128)S(1)} %get-tuple-element.75.stats_ref, ...), custom_call_target="tpu_custom_call" | custom-call | flops 335000000 | bytes 4000000 | tf_op jit(solution)/shard_map/pallas_call | solution.py:180
  51.0 1.7 %collective-permute-start.14 = (bf16[128,1024]{1,0:T(8,128)(2,1)S(1)}, bf16[128,1024]{1,0:T(8,128)(2,1)S(1)}, u32[]{:S(2)}, u32[]{:S(2)}) collective-permute-start(bf16[128,1024]{1,0:T(8,128)(2,1)S(1)} %get-tuple-element.82), channel_id=1, source_target_pairs={{0,2},{1,3},{2,0},{3,1},{4,6},{5,7},{6,4},{7,5},{8,10},{9,11},{10,... | collective-permute-start | bytes 786440 | tf_op jit(solution)/shard_map/ppermute | solution.py:463
  52.6 0.5 collective-permute-start.18
  53.1 0.0 collective-permute-done.19.refs_1_
  53.1 0.1 shard_map.101
  53.2 3.2 %collective-permute-start.20 = (bf16[8,64,256]{2,1,0:T(8,128)(2,1)S(1)}, bf16[8,64,256]{2,1,0:T(8,128)(2,1)S(1)}, u32[]{:S(2)}, u32[]{:S(2)}) collective-permute-start(bf16[8,64,256]{2,1,0:T(8,128)(2,1)S(1)} %shard_map.101), channel_id=1, source_target_pairs={{0,24},{4,28},{8,0},{12,4},{16,8},{20,12},{24,16},{28,20},{1,25},{... | collective-permute-start | bytes 786440 | tf_op jit(solution)/shard_map/ppermute | solution.py:461
  56.4 2.0 %collective-permute-done.14 = bf16[128,1024]{1,0:T(8,128)(2,1)S(1)} collective-permute-done((bf16[128,1024]{1,0:T(8,128)(2,1)S(1)}, bf16[128,1024]{1,0:T(8,128)(2,1)S(1)}, u32[]{:S(2)}, u32[]{:S(2)}) %collective-permute-start.14) | collective-permute-done | bytes 262176 | tf_op jit(solution)/shard_map/ppermute | solution.py:463
  58.3 3.1 %collective-permute-done.13.refs_1_ = bf16[16,64,256]{2,1,0:T(8,128)(2,1)S(1)} collective-permute-done((bf16[16,64,256]{2,1,0:T(8,128)(2,1)S(1)}, bf16[16,64,256]{2,1,0:T(8,128)(2,1)S(1)}, u32[]{:S(2)}, u32[]{:S(2)}) %collective-permute-start.13) | collective-permute-done | bytes 524320 | tf_op jit(solution)/shard_map/ppermute | solution.py:459
  61.5 0.1 shard_map.98
  61.6 0.6 collective-permute-start.15
  62.1 2.9 %collective-permute-done.20.refs_2_ = bf16[8,64,256]{2,1,0:T(8,128)(2,1)S(1)} collective-permute-done((bf16[8,64,256]{2,1,0:T(8,128)(2,1)S(1)}, bf16[8,64,256]{2,1,0:T(8,128)(2,1)S(1)}, u32[]{:S(2)}, u32[]{:S(2)}) %collective-permute-start.20) | collective-permute-done | bytes 262176 | tf_op jit(solution)/shard_map/ppermute | solution.py:461
  65.1 0.1 shard_map.102
  65.1 2.5 %collective-permute-start.24 = (bf16[2,64,256]{2,1,0:T(8,128)(2,1)S(1)}, bf16[2,64,256]{2,1,0:T(8,128)(2,1)S(1)}, u32[]{:S(2)}, u32[]{:S(2)}) collective-permute-start(bf16[2,64,256]{2,1,0:T(8,128)(2,1)S(1)} %get-tuple-element.100), channel_id=1, source_target_pairs={{0,26},{1,27},{2,24},{3,25},{4,30},{5,31},{6,28},{7,29},{8,2},{9,3... | collective-permute-start | bytes 196616 | tf_op jit(solution)/shard_map/ppermute | solution.py:381
  67.7 0.0 collective-permute-start.25
  67.7 2.5 %collective-permute-start.21 = (bf16[4,64,256]{2,1,0:T(8,128)(2,1)S(1)}, bf16[4,64,256]{2,1,0:T(8,128)(2,1)S(1)}, u32[]{:S(2)}, u32[]{:S(2)}) collective-permute-start(bf16[4,64,256]{2,1,0:T(8,128)(2,1)S(1)} %get-tuple-element.97), channel_id=1, source_target_pairs={{0,24},{4,28},{8,0},{12,4},{16,8},{20,12},{24,16},{28,20},{1,25},{... | collective-permute-start | bytes 393224 | tf_op jit(solution)/shard_map/ppermute | solution.py:474
  70.2 0.0 collective-permute-done.15.refs_2_
  70.2 0.1 shard_map.99
  70.2 0.5 collective-permute-start.22
  70.7 0.9 %collective-permute-start.23 = (bf16[2,64,256]{2,1,0:T(8,128)(2,1)S(1)}, bf16[2,64,256]{2,1,0:T(8,128)(2,1)S(1)}, u32[]{:S(2)}, u32[]{:S(2)}) collective-permute-start(bf16[2,64,256]{2,1,0:T(8,128)(2,1)S(1)} %get-tuple-element.99), channel_id=1, source_target_pairs={{0,3},{1,2},{2,1},{3,0},{4,7},{5,6},{6,5},{7,4},{8,11},{9,10},{10,... | collective-permute-start | bytes 196616 | tf_op jit(solution)/shard_map/ppermute | solution.py:477
  71.7 0.0 collective-permute-done.24.refs_3_
  71.7 0.9 %collective-permute-start.16 = (bf16[64,1024]{1,0:T(8,128)(2,1)S(1)}, bf16[64,1024]{1,0:T(8,128)(2,1)S(1)}, u32[]{:S(2)}, u32[]{:S(2)}) collective-permute-start(bf16[64,1024]{1,0:T(8,128)(2,1)S(1)} %get-tuple-element.90), channel_id=1, source_target_pairs={{0,1},{1,0},{2,3},{3,2},{4,5},{5,4},{6,7},{7,6},{8,9},{9,8},{10,11... | collective-permute-start | bytes 393224 | tf_op jit(solution)/shard_map/ppermute | solution.py:366
  72.6 0.5 collective-permute-done.25.refs_5_
  73.0 1.0 %collective-permute-done.21.refs_1_ = bf16[4,64,256]{2,1,0:T(8,128)(2,1)S(1)} collective-permute-done((bf16[4,64,256]{2,1,0:T(8,128)(2,1)S(1)}, bf16[4,64,256]{2,1,0:T(8,128)(2,1)S(1)}, u32[]{:S(2)}, u32[]{:S(2)}) %collective-permute-start.21) | collective-permute-done | bytes 131104 | tf_op jit(solution)/shard_map/ppermute | solution.py:474
  74.0 1.1 %collective-permute-done.22.refs_2_ = bf16[2,64,256]{2,1,0:T(8,128)(2,1)S(1)} collective-permute-done((bf16[2,64,256]{2,1,0:T(8,128)(2,1)S(1)}, bf16[2,64,256]{2,1,0:T(8,128)(2,1)S(1)}, u32[]{:S(2)}, u32[]{:S(2)}) %collective-permute-start.22) | collective-permute-done | bytes 65568 | tf_op jit(solution)/shard_map/ppermute | solution.py:477
  75.2 0.6 collective-permute-start.26
  75.8 0.8 %shard_map.100 = bf16[64,4096]{1,0:T(8,128)(2,1)} custom-call(s32[1]{0:T(128)} %bitcast.me_ref, bf16[64,1024]{1,0:T(8,128)(2,1)S(1)} %get-tuple-element.89.refs_0_, bf16[64,1024]{1,0:T(8,128)(2,1)S(1)} %collective-permute-done.16.refs_1_, bf16[64,1024]{1,0:T(8,128)(2,1)S(1)} %get-tuple-element.116.refs_2_, bf16[64,1024]{1,0:T(8,128)(2,1)S(1)} %collective-permute-done.17.refs_3_), custom_call_target="tpu_custom_call" | custom-call | tf_op jit(solution)/shard_map/pallas_call | solution.py:335
  76.6 0.1 collective-permute-done.26.refs_1_
  76.6 0.8 shard_map.104
  (25 shorter events, 0.3 us)
Async XLA Ops:
  2.4 5.0 %collective-permute-start = (bf16[2,64,256]{2,1,0:T(8,128)(2,1)}, bf16[2,64,256]{2,1,0:T(8,128)(2,1)S(1)}, u32[]{:S(2)}, u32[]{:S(2)}) collective-permute-start(bf16[2,64,256]{2,1,0:T(8,128)(2,1)} %get-tuple-element.59), channel_id=1, source_target_pairs={{0,1},{1,0},{2,3},{3,2},{4,5},{5,4},{6,7},{7,6},{8,9},{9,8},{10,11... | collective-permute-start | bytes 196616 | tf_op jit(solution)/shard_map/ppermute | solution.py:357
  2.9 5.5 %collective-permute-start.1 = (bf16[2,64,256]{2,1,0:T(8,128)(2,1)}, bf16[2,64,256]{2,1,0:T(8,128)(2,1)S(1)}, u32[]{:S(2)}, u32[]{:S(2)}) collective-permute-start(bf16[2,64,256]{2,1,0:T(8,128)(2,1)} %get-tuple-element.60), channel_id=1, source_target_pairs={{0,2},{1,3},{2,0},{3,1},{4,6},{5,7},{6,4},{7,5},{8,10},{9,11},{10,... | collective-permute-start | bytes 196616 | tf_op jit(solution)/shard_map/ppermute | solution.py:357
  5.4 4.3 %collective-permute-start.2 = (bf16[2,64,256]{2,1,0:T(8,128)(2,1)}, bf16[2,64,256]{2,1,0:T(8,128)(2,1)S(1)}, u32[]{:S(2)}, u32[]{:S(2)}) collective-permute-start(bf16[2,64,256]{2,1,0:T(8,128)(2,1)} %get-tuple-element.61), channel_id=1, source_target_pairs={{0,3},{1,2},{2,1},{3,0},{4,7},{5,6},{6,5},{7,4},{8,11},{9,10},{10,... | collective-permute-start | bytes 196616 | tf_op jit(solution)/shard_map/ppermute | solution.py:357
  9.8 13.0 %collective-permute-start.4 = (bf16[8,64,256]{2,1,0:T(8,128)(2,1)S(1)}, bf16[8,64,256]{2,1,0:T(8,128)(2,1)S(1)}, u32[]{:S(2)}, u32[]{:S(2)}) collective-permute-start(bf16[8,64,256]{2,1,0:T(8,128)(2,1)S(1)} %constant_dynamic-update-slice_fusion.own_kv_ref), channel_id=1, source_target_pairs={{0,4},{4,0},{8,12},{12,8},{16,20},{20,16},{24,28},{28,24},{1,5},{5... | collective-permute-start | bytes 786440 | tf_op jit(solution)/shard_map/ppermute | solution.py:412
  11.3 10.8 %collective-permute-start.3 = (bf16[8,64,256]{2,1,0:T(8,128)(2,1)S(1)}, bf16[8,64,256]{2,1,0:T(8,128)(2,1)S(1)}, u32[]{:S(2)}, u32[]{:S(2)}) collective-permute-start(bf16[8,64,256]{2,1,0:T(8,128)(2,1)S(1)} %constant_dynamic-update-slice_fusion.own_kv_ref), channel_id=1, source_target_pairs={{0,8},{4,12},{8,16},{12,20},{16,24},{20,28},{24,0},{28,4},{1,9},{5... | collective-permute-start | bytes 786440 | tf_op jit(solution)/shard_map/ppermute | solution.py:411
  15.9 7.0 %copy-start.2 = (bf16[528,256]{1,0:T(8,128)(2,1)S(1)}, bf16[528,256]{1,0:T(8,128)(2,1)}, u32[]{:S(2)}) copy-start(bf16[528,256]{1,0:T(8,128)(2,1)} %get-tuple-element.73) | copy-start | bytes 811012
  16.1 11.7 %collective-permute-start.7 = (bf16[8,64,256]{2,1,0:T(8,128)(2,1)S(1)}, bf16[8,64,256]{2,1,0:T(8,128)(2,1)S(1)}, u32[]{:S(2)}, u32[]{:S(2)}) collective-permute-start(bf16[8,64,256]{2,1,0:T(8,128)(2,1)S(1)} %constant_dynamic-update-slice_fusion.own_kv_ref), channel_id=1, source_target_pairs={{0,24},{4,28},{8,0},{12,4},{16,8},{20,12},{24,16},{28,20},{1,25},{... | collective-permute-start | bytes 786440 | tf_op jit(solution)/shard_map/ppermute | solution.py:425
  18.3 15.9 %collective-permute-start.11 = (bf16[1056,256]{1,0:T(8,128)(2,1)}, bf16[1056,256]{1,0:T(8,128)(2,1)S(1)}, u32[]{:S(2)}, u32[]{:S(2)}) collective-permute-start(bf16[1056,256]{1,0:T(8,128)(2,1)} %get-tuple-element.74), channel_id=1, source_target_pairs={{0,2},{1,3},{2,0},{3,1},{4,6},{5,7},{6,4},{7,5},{8,10},{9,11},{10,... | collective-permute-start | bytes 1622024 | tf_op jit(solution)/shard_map/ppermute | solution.py:372
  22.1 6.4 %collective-permute-start.6 = (bf16[8,64,256]{2,1,0:T(8,128)(2,1)S(1)}, bf16[8,64,256]{2,1,0:T(8,128)(2,1)S(1)}, u32[]{:S(2)}, u32[]{:S(2)}) collective-permute-start(bf16[8,64,256]{2,1,0:T(8,128)(2,1)S(1)} %collective-permute-done.3), channel_id=1, source_target_pairs={{0,4},{4,0},{8,12},{12,8},{16,20},{20,16},{24,28},{28,24},{1,5},{5... | collective-permute-start | bytes 786440 | tf_op jit(solution)/shard_map/ppermute | solution.py:427
  22.6 10.0 %collective-permute-start.5 = (bf16[8,64,256]{2,1,0:T(8,128)(2,1)S(1)}, bf16[8,64,256]{2,1,0:T(8,128)(2,1)S(1)}, u32[]{:S(2)}, u32[]{:S(2)}) collective-permute-start(bf16[8,64,256]{2,1,0:T(8,128)(2,1)S(1)} %collective-permute-done.3), channel_id=1, source_target_pairs={{0,8},{4,12},{8,16},{12,20},{16,24},{20,28},{24,0},{28,4},{1,9},{5... | collective-permute-start | bytes 786440 | tf_op jit(solution)/shard_map/ppermute | solution.py:426
  22.9 18.7 %collective-permute-start.10 = (bf16[528,256]{1,0:T(8,128)(2,1)S(1)}, bf16[528,256]{1,0:T(8,128)(2,1)S(1)}, u32[]{:S(2)}, u32[]{:S(2)}) collective-permute-start(bf16[528,256]{1,0:T(8,128)(2,1)S(1)} %copy-done.2), channel_id=1, source_target_pairs={{0,1},{1,0},{2,3},{3,2},{4,5},{5,4},{6,7},{7,6},{8,9},{9,8},{10,11... | collective-permute-start | bytes 811016 | tf_op jit(solution)/shard_map/ppermute | solution.py:366
  27.7 13.8 %collective-permute-start.9 = (bf16[8,64,256]{2,1,0:T(8,128)(2,1)S(1)}, bf16[8,64,256]{2,1,0:T(8,128)(2,1)S(1)}, u32[]{:S(2)}, u32[]{:S(2)}) collective-permute-start(bf16[8,64,256]{2,1,0:T(8,128)(2,1)S(1)} %collective-permute-done.7), channel_id=1, source_target_pairs={{0,4},{4,0},{8,12},{12,8},{16,20},{20,16},{24,28},{28,24},{1,5},{5... | collective-permute-start | bytes 786440 | tf_op jit(solution)/shard_map/ppermute | solution.py:428
  28.3 13.3 %copy-start = (bf16[528,256]{1,0:T(8,128)(2,1)S(1)}, bf16[528,256]{1,0:T(8,128)(2,1)}, u32[]{:S(2)}) copy-start(bf16[528,256]{1,0:T(8,128)(2,1)} %get-tuple-element.72.refs_0_) | copy-start | bytes 811012
  28.3 13.3 %copy-start.1 = (f32[256,8]{0,1:T(8,128)S(1)}, f32[256,8]{0,1:T(8,128)}, u32[]{:S(2)}) copy-start(f32[256,8]{0,1:T(8,128)} %param.12) | copy-start | bytes 24580
  32.6 8.9 %collective-permute-start.8 = (bf16[8,64,256]{2,1,0:T(8,128)(2,1)S(1)}, bf16[8,64,256]{2,1,0:T(8,128)(2,1)S(1)}, u32[]{:S(2)}, u32[]{:S(2)}) collective-permute-start(bf16[8,64,256]{2,1,0:T(8,128)(2,1)S(1)} %collective-permute-done.5), channel_id=1, source_target_pairs={{0,4},{4,0},{8,12},{12,8},{16,20},{20,16},{24,28},{28,24},{1,5},{5... | collective-permute-start | bytes 786440 | tf_op jit(solution)/shard_map/ppermute | solution.py:430
  34.3 7.3 %collective-permute-start.12 = (bf16[528,256]{1,0:T(8,128)(2,1)S(1)}, bf16[528,256]{1,0:T(8,128)(2,1)S(1)}, u32[]{:S(2)}, u32[]{:S(2)}) collective-permute-start(bf16[528,256]{1,0:T(8,128)(2,1)S(1)} %get-tuple-element.113), channel_id=1, source_target_pairs={{0,1},{1,0},{2,3},{3,2},{4,5},{5,4},{6,7},{7,6},{8,9},{9,8},{10,11... | collective-permute-start | bytes 811016 | tf_op jit(solution)/shard_map/ppermute | solution.py:367
  44.7 16.8 %collective-permute-start.13 = (bf16[16,64,256]{2,1,0:T(8,128)(2,1)S(1)}, bf16[16,64,256]{2,1,0:T(8,128)(2,1)S(1)}, u32[]{:S(2)}, u32[]{:S(2)}) collective-permute-start(bf16[16,64,256]{2,1,0:T(8,128)(2,1)S(1)} %get-tuple-element.81), channel_id=1, source_target_pairs={{0,8},{4,12},{8,16},{12,20},{16,24},{20,28},{24,0},{28,4},{1,9},{5... | collective-permute-start | bytes 1572872 | tf_op jit(solution)/shard_map/ppermute | solution.py:459
  45.6 7.5 %collective-permute-start.19 = (bf16[8,64,256]{2,1,0:T(8,128)(2,1)S(1)}, bf16[8,64,256]{2,1,0:T(8,128)(2,1)S(1)}, u32[]{:S(2)}, u32[]{:S(2)}) collective-permute-start(bf16[8,64,256]{2,1,0:T(8,128)(2,1)S(1)} %get-tuple-element.96), channel_id=1, source_target_pairs={{0,4},{4,0},{8,12},{12,8},{16,20},{20,16},{24,28},{28,24},{1,5},{5... | collective-permute-start | bytes 786440 | tf_op jit(solution)/shard_map/ppermute | solution.py:458
  51.0 7.4 %collective-permute-start.14 = (bf16[128,1024]{1,0:T(8,128)(2,1)S(1)}, bf16[128,1024]{1,0:T(8,128)(2,1)S(1)}, u32[]{:S(2)}, u32[]{:S(2)}) collective-permute-start(bf16[128,1024]{1,0:T(8,128)(2,1)S(1)} %get-tuple-element.82), channel_id=1, source_target_pairs={{0,2},{1,3},{2,0},{3,1},{4,6},{5,7},{6,4},{7,5},{8,10},{9,11},{10,... | collective-permute-start | bytes 786440 | tf_op jit(solution)/shard_map/ppermute | solution.py:463
  52.6 9.5 %collective-permute-start.18 = (bf16[8,64,256]{2,1,0:T(8,128)(2,1)S(1)}, bf16[8,64,256]{2,1,0:T(8,128)(2,1)S(1)}, u32[]{:S(2)}, u32[]{:S(2)}) collective-permute-start(bf16[8,64,256]{2,1,0:T(8,128)(2,1)S(1)} %get-tuple-element.94), channel_id=1, source_target_pairs={{0,4},{4,0},{8,12},{12,8},{16,20},{20,16},{24,28},{28,24},{1,5},{5... | collective-permute-start | bytes 786440 | tf_op jit(solution)/shard_map/ppermute | solution.py:460
  53.2 11.8 %collective-permute-start.20 = (bf16[8,64,256]{2,1,0:T(8,128)(2,1)S(1)}, bf16[8,64,256]{2,1,0:T(8,128)(2,1)S(1)}, u32[]{:S(2)}, u32[]{:S(2)}) collective-permute-start(bf16[8,64,256]{2,1,0:T(8,128)(2,1)S(1)} %shard_map.101), channel_id=1, source_target_pairs={{0,24},{4,28},{8,0},{12,4},{16,8},{20,12},{24,16},{28,20},{1,25},{... | collective-permute-start | bytes 786440 | tf_op jit(solution)/shard_map/ppermute | solution.py:461
  61.6 8.6 %collective-permute-start.15 = (bf16[8,64,256]{2,1,0:T(8,128)(2,1)S(1)}, bf16[8,64,256]{2,1,0:T(8,128)(2,1)S(1)}, u32[]{:S(2)}, u32[]{:S(2)}) collective-permute-start(bf16[8,64,256]{2,1,0:T(8,128)(2,1)S(1)} %shard_map.98), channel_id=1, source_target_pairs={{0,4},{4,0},{8,12},{12,8},{16,20},{20,16},{24,28},{28,24},{1,5},{5... | collective-permute-start | bytes 786440 | tf_op jit(solution)/shard_map/ppermute | solution.py:466
  65.1 6.5 %collective-permute-start.24 = (bf16[2,64,256]{2,1,0:T(8,128)(2,1)S(1)}, bf16[2,64,256]{2,1,0:T(8,128)(2,1)S(1)}, u32[]{:S(2)}, u32[]{:S(2)}) collective-permute-start(bf16[2,64,256]{2,1,0:T(8,128)(2,1)S(1)} %get-tuple-element.100), channel_id=1, source_target_pairs={{0,26},{1,27},{2,24},{3,25},{4,30},{5,31},{6,28},{7,29},{8,2},{9,3... | collective-permute-start | bytes 196616 | tf_op jit(solution)/shard_map/ppermute | solution.py:381
  67.7 5.4 %collective-permute-start.25 = (bf16[2,64,256]{2,1,0:T(8,128)(2,1)S(1)}, bf16[2,64,256]{2,1,0:T(8,128)(2,1)S(1)}, u32[]{:S(2)}, u32[]{:S(2)}) collective-permute-start(bf16[2,64,256]{2,1,0:T(8,128)(2,1)S(1)} %get-tuple-element.101), channel_id=1, source_target_pairs={{0,27},{1,26},{2,25},{3,24},{4,31},{5,30},{6,29},{7,28},{8,3},{9,2... | collective-permute-start | bytes 196616 | tf_op jit(solution)/shard_map/ppermute | solution.py:381
  67.7 6.3 %collective-permute-start.21 = (bf16[4,64,256]{2,1,0:T(8,128)(2,1)S(1)}, bf16[4,64,256]{2,1,0:T(8,128)(2,1)S(1)}, u32[]{:S(2)}, u32[]{:S(2)}) collective-permute-start(bf16[4,64,256]{2,1,0:T(8,128)(2,1)S(1)} %get-tuple-element.97), channel_id=1, source_target_pairs={{0,24},{4,28},{8,0},{12,4},{16,8},{20,12},{24,16},{28,20},{1,25},{... | collective-permute-start | bytes 393224 | tf_op jit(solution)/shard_map/ppermute | solution.py:474
  70.2 4.9 %collective-permute-start.22 = (bf16[2,64,256]{2,1,0:T(8,128)(2,1)S(1)}, bf16[2,64,256]{2,1,0:T(8,128)(2,1)S(1)}, u32[]{:S(2)}, u32[]{:S(2)}) collective-permute-start(bf16[2,64,256]{2,1,0:T(8,128)(2,1)S(1)} %get-tuple-element.98), channel_id=1, source_target_pairs={{0,2},{1,3},{2,0},{3,1},{4,6},{5,7},{6,4},{7,5},{8,10},{9,11},{10,... | collective-permute-start | bytes 196616 | tf_op jit(solution)/shard_map/ppermute | solution.py:477
  70.7 4.4 %collective-permute-start.23 = (bf16[2,64,256]{2,1,0:T(8,128)(2,1)S(1)}, bf16[2,64,256]{2,1,0:T(8,128)(2,1)S(1)}, u32[]{:S(2)}, u32[]{:S(2)}) collective-permute-start(bf16[2,64,256]{2,1,0:T(8,128)(2,1)S(1)} %get-tuple-element.99), channel_id=1, source_target_pairs={{0,3},{1,2},{2,1},{3,0},{4,7},{5,6},{6,5},{7,4},{8,11},{9,10},{10,... | collective-permute-start | bytes 196616 | tf_op jit(solution)/shard_map/ppermute | solution.py:477
  71.7 4.1 %collective-permute-start.16 = (bf16[64,1024]{1,0:T(8,128)(2,1)S(1)}, bf16[64,1024]{1,0:T(8,128)(2,1)S(1)}, u32[]{:S(2)}, u32[]{:S(2)}) collective-permute-start(bf16[64,1024]{1,0:T(8,128)(2,1)S(1)} %get-tuple-element.90), channel_id=1, source_target_pairs={{0,1},{1,0},{2,3},{3,2},{4,5},{5,4},{6,7},{7,6},{8,9},{9,8},{10,11... | collective-permute-start | bytes 393224 | tf_op jit(solution)/shard_map/ppermute | solution.py:366
  73.0 2.7 %collective-permute-start.17 = (bf16[64,1024]{1,0:T(8,128)(2,1)S(1)}, bf16[64,1024]{1,0:T(8,128)(2,1)S(1)}, u32[]{:S(2)}, u32[]{:S(2)}) collective-permute-start(bf16[64,1024]{1,0:T(8,128)(2,1)S(1)} %get-tuple-element.115), channel_id=1, source_target_pairs={{0,1},{1,0},{2,3},{3,2},{4,5},{5,4},{6,7},{7,6},{8,9},{9,8},{10,11... | collective-permute-start | bytes 393224 | tf_op jit(solution)/shard_map/ppermute | solution.py:367
  75.2 1.5 %collective-permute-start.26 = (bf16[2,64,256]{2,1,0:T(8,128)(2,1)S(1)}, bf16[2,64,256]{2,1,0:T(8,128)(2,1)S(1)}, u32[]{:S(2)}, u32[]{:S(2)}) collective-permute-start(bf16[2,64,256]{2,1,0:T(8,128)(2,1)S(1)} %get-tuple-element.106), channel_id=1, source_target_pairs={{0,1},{1,0},{2,3},{3,2},{4,5},{5,4},{6,7},{7,6},{8,9},{9,8},{10,11... | collective-permute-start | bytes 196616 | tf_op jit(solution)/shard_map/ppermute | solution.py:482

commit v8 on v7

--- a/solution.py
+++ b/solution.py
@@ -412,8 +412,10 @@
         cross0 = lax.ppermute(own_kv, "seq", swap)
         later_me, held = lax.optimization_barrier((me_ref, own_kv))
         q_pieces = pack_q(later_me, queries, grad_out, outputs_saved, peers)
-        per_peer, q_pieces = lax.optimization_barrier((per_peer, q_pieces))
+        held, q_pieces = lax.optimization_barrier((held, q_pieces))
+        same3 = lax.ppermute(held, "seq", back)
         qdo = exchange_rows(*q_pieces)
+        per_peer, same1 = lax.optimization_barrier((per_peer, same1))
         mine = lax.dynamic_index_in_dim(per_peer, me, 0, keepdims=False)
         owner = mine // key_count
         apart = (me // 2 - owner // 2) % far
@@ -421,8 +423,6 @@
         piece = jnp.where(crossed == 1, far - 1 + (apart + 1) % far, apart - 1)
         slots = piece * units + (mine % key_count ^ head_me) * kv_heads + group_of
         slots = jnp.roll(slots, block_turn)
-        held, slots = lax.optimization_barrier((held, slots))
-        same3 = lax.ppermute(held, "seq", back)
         same2 = lax.ppermute(same1, "seq", ahead)
         cross1 = lax.ppermute(same1, "seq", swap)
         cross3 = lax.ppermute(same3, "seq", swap)

time: 77.7 us -> 77.1 us (level)
  starting transfers between devices: 28.6 us -> 31.5 us
  waiting for transfers between devices: 32 us -> 29.2 us
    ppermute x1, waiting for transfers between devices: 2.54 us -> 0.39 us  [body(): same1 = lax.ppermute(own_kv, 'seq', ahead)]
    ppermute x1, starting transfers between devices: 3.18 us -> 1.3 us  [body(): hop = lax.ppermute(add_rounded(units, stay2, came2), 'seq', back)]
    ppermute x1, starting transfers between devices: 0.51 us -> 2.13 us  [body(): cross1 = lax.ppermute(same1, 'seq', swap)]
    ppermute x1, starting transfers between devices: 0.9 us -> 2.32 us  [body(): came3 = lax.ppermute(away3, 'seq', ahead)]
    ppermute x1, starting transfers between devices: 0.57 us -> 1.93 us  [body(): came0 = lax.ppermute(near, 'seq', swap)]
    ppermute x1, waiting for transfers between devices: 4.8 us -> 3.47 us  [body(): same3 = lax.ppermute(held, 'seq', back)]
    ppermute x1, starting transfers between devices: 0.49 us -> 1.76 us  [body(): came1 = lax.ppermute(leave1, 'seq', swap)]
    ppermute x1, starting transfers between devices: 1.53 us -> 0.27 us  [body(): came2 = lax.ppermute(leave2, 'seq', swap)]
  transfers between devices with their start and end apart: 27 -> 27, of which waited for: 14 -> 15; matrix products, arithmetic and copies ran while one was open for 3% -> 2% of each run, Pallas kernels for 10% -> 10%
where the time goes in v8:
time: 77.1 us; the launch traced here: 76.8 us
  starting transfers between devices  31.5 us (41%)
  waiting for transfers between devices  29.2 us (38%)
  Pallas kernels  13.5 us (18%)
  local copies, waits for them, and re-layouts  1.55 us (2%)
  between operations  0.9 us (1%)
    ppermute x1, waiting for transfers between devices, body(): cross2 = lax.ppermute(held, 'seq', swap)  6.96 us
    ppermute x1, waiting for transfers between devices, body(): same2 = lax.ppermute(same1, 'seq', ahead)  4.4 us
    pallas_call x1, Pallas kernels, own_terms(): pl.pallas_call(functools.partial(own_kernel, peers), out_shape=(piece,) *...  3.84 us
    ppermute x2, starting transfers between devices, send_back(): return lax.ppermute(piece, ('seq', 'head'), pairs)  3.63 us
    ppermute x1, waiting for transfers between devices, body(): same3 = lax.ppermute(held, 'seq', back)  3.47 us
    ppermute x3, waiting for transfers between devices, exchange(): lax.ppermute(pieces[c], 'head', [(h, h ^ c) for h in range(peers)])  3.42 us
    ppermute x3, starting transfers between devices, exchange(): lax.ppermute(pieces[c], 'head', [(h, h ^ c) for h in range(peers)])  3.15 us
    pallas_call x1, Pallas kernels, listed_terms(): pl.pallas_call(functools.partial(listed_kernel, peers), out_shape=(jax.Sh...  3.1 us
  transfers between devices with their start and end apart: 27, of which 15 were waited for; matrix products, arithmetic and copies ran while one was open for 2% of the time, Pallas kernels for 10%

profile of v8, /device:TPU:0, one launch (start us, length us, event | category | flops | bytes accessed | tf_op | source)
XLA Modules:
  0.0 76.8 jit_solution(9382963928455029632)
XLA Ops:
  0.6 1.7 %shard_map.94 = (bf16[2,64,256]{2,1,0:T(8,128)(2,1)}, bf16[2,64,256]{2,1,0:T(8,128)(2,1)}, bf16[2,64,256]{2,1,0:T(8,128)(2,1)}, bf16[2,64,256]{2,1,0:T(8,128)(2,1)}) custom-call(s32[1]{0:T(128)} %bitcast.me_ref, bf16[64,1024]{1,0:T(8,128)(2,1)} %k_ref.1, bf16[64,1024]{1,0:T(8,128)(2,1)} %v_ref.1), custom_call_target="tpu_custom_call" | custom-call | tf_op jit(solution)/shard_map/pallas_call | solution.py:63
  2.4 0.5 collective-permute-start
  2.9 2.6 %collective-permute-start.1 = (bf16[2,64,256]{2,1,0:T(8,128)(2,1)}, bf16[2,64,256]{2,1,0:T(8,128)(2,1)S(1)}, u32[]{:S(2)}, u32[]{:S(2)}) collective-permute-start(bf16[2,64,256]{2,1,0:T(8,128)(2,1)} %get-tuple-element.60), channel_id=1, source_target_pairs={{0,2},{1,3},{2,0},{3,1},{4,6},{5,7},{6,4},{7,5},{8,10},{9,11},{10,... | collective-permute-start | bytes 196616 | tf_op jit(solution)/shard_map/ppermute | solution.py:357
  5.5 0.1 collective-permute-start.2
  5.5 0.8 %constant_dynamic-update-slice_fusion.3 = bf16[8,64,256]{2,1,0:T(8,128)(2,1)S(1)} fusion(bf16[2,64,256]{2,1,0:T(8,128)(2,1)} %get-tuple-element.58), kind=kLoop, calls=%fused_computation.3 | loop fusion | bytes 131072
  6.4 0.0 collective-permute-done
  6.4 2.0 %collective-permute-done.1 = bf16[2,64,256]{2,1,0:T(8,128)(2,1)S(1)} collective-permute-done((bf16[2,64,256]{2,1,0:T(8,128)(2,1)}, bf16[2,64,256]{2,1,0:T(8,128)(2,1)S(1)}, u32[]{:S(2)}, u32[]{:S(2)}) %collective-permute-start.1) | collective-permute-done | bytes 65568 | tf_op jit(solution)/shard_map/ppermute | solution.py:357
  8.4 1.4 %collective-permute-done.2 = bf16[2,64,256]{2,1,0:T(8,128)(2,1)S(1)} collective-permute-done((bf16[2,64,256]{2,1,0:T(8,128)(2,1)}, bf16[2,64,256]{2,1,0:T(8,128)(2,1)S(1)}, u32[]{:S(2)}, u32[]{:S(2)}) %collective-permute-start.2) | collective-permute-done | bytes 65568 | tf_op jit(solution)/shard_map/ppermute | solution.py:357
  9.8 1.6 %collective-permute-start.3 = (bf16[8,64,256]{2,1,0:T(8,128)(2,1)S(1)}, bf16[8,64,256]{2,1,0:T(8,128)(2,1)S(1)}, u32[]{:S(2)}, u32[]{:S(2)}) collective-permute-start(bf16[8,64,256]{2,1,0:T(8,128)(2,1)S(1)} %constant_dynamic-update-slice_fusion.own_kv_ref), channel_id=1, source_target_pairs={{0,8},{4,12},{8,16},{12,20},{16,24},{20,28},{24,0},{28,4},{1,9},{5... | collective-permute-start | bytes 786440 | tf_op jit(solution)/shard_map/ppermute | solution.py:411
  11.4 1.5 %collective-permute-start.4 = (bf16[8,64,256]{2,1,0:T(8,128)(2,1)S(1)}, bf16[8,64,256]{2,1,0:T(8,128)(2,1)S(1)}, u32[]{:S(2)}, u32[]{:S(2)}) collective-permute-start(bf16[8,64,256]{2,1,0:T(8,128)(2,1)S(1)} %constant_dynamic-update-slice_fusion.own_kv_ref), channel_id=1, source_target_pairs={{0,4},{4,0},{8,12},{12,8},{16,20},{20,16},{24,28},{28,24},{1,5},{5... | collective-permute-start | bytes 786440 | tf_op jit(solution)/shard_map/ppermute | solution.py:412
  12.9 3.0 %shard_map.95 = (bf16[528,256]{1,0:T(8,128)(2,1)}, bf16[528,256]{1,0:T(8,128)(2,1)}, bf16[1056,256]{1,0:T(8,128)(2,1)}) custom-call(s32[1]{0:T(128)} %bitcast.me_ref, bf16[64,4096]{1,0:T(8,128)(2,1)} %q_any.1, bf16[64,4096]{1,0:T(8,128)(2,1)} %do_any.1, bf16[64,4096]{1,0:T(8,128)(2,1)} %o_any.1), custom_call_target="tpu_custom_call" | custom-call | tf_op jit(solution)/shard_map/pallas_call | solution.py:117
  15.9 2.3 %collective-permute-start.7 = (bf16[8,64,256]{2,1,0:T(8,128)(2,1)S(1)}, bf16[8,64,256]{2,1,0:T(8,128)(2,1)S(1)}, u32[]{:S(2)}, u32[]{:S(2)}) collective-permute-start(bf16[8,64,256]{2,1,0:T(8,128)(2,1)S(1)} %constant_dynamic-update-slice_fusion.own_kv_ref), channel_id=1, source_target_pairs={{0,24},{4,28},{8,0},{12,4},{16,8},{20,12},{24,16},{28,20},{1,25},{... | collective-permute-start | bytes 786440 | tf_op jit(solution)/shard_map/ppermute | solution.py:416
  18.2 0.1 copy.10
  18.3 0.1 reshape.13
  18.4 1.3 %collective-permute-start.11 = (bf16[1056,256]{1,0:T(8,128)(2,1)}, bf16[1056,256]{1,0:T(8,128)(2,1)S(1)}, u32[]{:S(2)}, u32[]{:S(2)}) collective-permute-start(bf16[1056,256]{1,0:T(8,128)(2,1)} %get-tuple-element.74), channel_id=1, source_target_pairs={{0,2},{1,3},{2,0},{3,1},{4,6},{5,7},{6,4},{7,5},{8,10},{9,11},{10,... | collective-permute-start | bytes 1622024 | tf_op jit(solution)/shard_map/ppermute | solution.py:372
  19.8 0.4 collective-permute-done.3
  20.1 2.1 %collective-permute-start.6 = (bf16[8,64,256]{2,1,0:T(8,128)(2,1)S(1)}, bf16[8,64,256]{2,1,0:T(8,128)(2,1)S(1)}, u32[]{:S(2)}, u32[]{:S(2)}) collective-permute-start(bf16[8,64,256]{2,1,0:T(8,128)(2,1)S(1)} %collective-permute-done.3), channel_id=1, source_target_pairs={{0,4},{4,0},{8,12},{12,8},{16,20},{20,16},{24,28},{28,24},{1,5},{5... | collective-permute-start | bytes 786440 | tf_op jit(solution)/shard_map/ppermute | solution.py:427
  22.3 0.2 dynamic_update_slice.21
  22.5 0.1 pad_add_fusion
  22.6 0.1 dynamic_slice.9.slot_ref
  22.7 0.0 collective-permute-start.10
  22.7 3.5 %collective-permute-done.7 = bf16[8,64,256]{2,1,0:T(8,128)(2,1)S(1)} collective-permute-done((bf16[8,64,256]{2,1,0:T(8,128)(2,1)S(1)}, bf16[8,64,256]{2,1,0:T(8,128)(2,1)S(1)}, u32[]{:S(2)}, u32[]{:S(2)}) %collective-permute-start.7) | collective-permute-done | bytes 262176 | tf_op jit(solution)/shard_map/ppermute | solution.py:416
  26.2 1.7 %collective-permute-start.9 = (bf16[8,64,256]{2,1,0:T(8,128)(2,1)S(1)}, bf16[8,64,256]{2,1,0:T(8,128)(2,1)S(1)}, u32[]{:S(2)}, u32[]{:S(2)}) collective-permute-start(bf16[8,64,256]{2,1,0:T(8,128)(2,1)S(1)} %collective-permute-done.7), channel_id=1, source_target_pairs={{0,4},{4,0},{8,12},{12,8},{16,20},{20,16},{24,28},{28,24},{1,5},{5... | collective-permute-start | bytes 786440 | tf_op jit(solution)/shard_map/ppermute | solution.py:428
  27.9 0.0 copy-start
  27.9 0.0 copy-start.1
  27.9 0.0 collective-permute-done.6
  27.9 4.4 %collective-permute-done.5 = bf16[8,64,256]{2,1,0:T(8,128)(2,1)S(1)} collective-permute-done((bf16[8,64,256]{2,1,0:T(8,128)(2,1)S(1)}, bf16[8,64,256]{2,1,0:T(8,128)(2,1)S(1)}, u32[]{:S(2)}, u32[]{:S(2)}) %collective-permute-start.5) | collective-permute-done | bytes 262176 | tf_op jit(solution)/shard_map/ppermute | solution.py:426
  32.3 0.4 collective-permute-start.8
  32.8 0.0 collective-permute-done.11
  32.9 0.1 collective-permute-start.12
  33.0 7.0 %collective-permute-done.8 = bf16[8,64,256]{2,1,0:T(8,128)(2,1)S(1)} collective-permute-done((bf16[8,64,256]{2,1,0:T(8,128)(2,1)S(1)}, bf16[8,64,256]{2,1,0:T(8,128)(2,1)S(1)}, u32[]{:S(2)}, u32[]{:S(2)}) %collective-permute-start.8) | collective-permute-done | bytes 262176 | tf_op jit(solution)/shard_map/ppermute | solution.py:430
  39.9 0.0 collective-permute-done.9
  40.0 0.0 collective-permute-done.12.refs_3_
  40.0 3.1 %shard_map.96 = (f32[2,8,256]{2,1,0:T(8,128)S(1)}, f32[64,1024]{1,0:T(8,128)S(1)}, f32[64,1024]{1,0:T(8,128)S(1)}, f32[64,1024]{1,0:T(8,128)S(1)}, f32[64,1024]{...) custom-call(s32[1]{0:T(128)} %bitcast.me_ref, ...), custom_call_target="tpu_custom_call" | custom-call | flops 671000000 | bytes 8000000 | tf_op jit(solution)/shard_map/pallas_call | solution.py:257
  43.1 2.3 %collective-permute-start.13 = (bf16[16,64,256]{2,1,0:T(8,128)(2,1)S(1)}, bf16[16,64,256]{2,1,0:T(8,128)(2,1)S(1)}, u32[]{:S(2)}, u32[]{:S(2)}) collective-permute-start(bf16[16,64,256]{2,1,0:T(8,128)(2,1)S(1)} %get-tuple-element.81), channel_id=1, source_target_pairs={{0,8},{4,12},{8,16},{12,20},{16,24},{20,28},{24,0},{28,4},{1,9},{5... | collective-permute-start | bytes 1572872 | tf_op jit(solution)/shard_map/ppermute | solution.py:459
  45.5 0.3 collective-permute-start.19
  45.7 3.8 %shard_map.97 = (bf16[64,1024]{1,0:T(8,128)(2,1)S(1)}, bf16[64,1024]{1,0:T(8,128)(2,1)S(1)}, bf16[128,1024]{1,0:T(8,128)(2,1)S(1)}, f32[8,64,256]{2,1,0:T(8,128)S(1)}) custom-call(s32[1]{0:T(128)} %bitcast.me_ref, bf16[8,64,256]{2,1,0:T(8,128)(2,1)S(1)} %constant_dynamic-update-slice_fusion.own_kv_ref, f32[2,8,256]{2,1,0:T(8,128)S(1)} %get-tuple-element.75.stats_ref, ...), custom_call_target="tpu_custom_call" | custom-call | flops 335000000 | bytes 4000000 | tf_op jit(solution)/shard_map/pallas_call | solution.py:180
  49.6 1.7 %collective-permute-start.14 = (bf16[128,1024]{1,0:T(8,128)(2,1)S(1)}, bf16[128,1024]{1,0:T(8,128)(2,1)S(1)}, u32[]{:S(2)}, u32[]{:S(2)}) collective-permute-start(bf16[128,1024]{1,0:T(8,128)(2,1)S(1)} %get-tuple-element.82), channel_id=1, source_target_pairs={{0,2},{1,3},{2,0},{3,1},{4,6},{5,7},{6,4},{7,5},{8,10},{9,11},{10,... | collective-permute-start | bytes 786440 | tf_op jit(solution)/shard_map/ppermute | solution.py:463
  51.2 1.8 %collective-permute-start.18 = (bf16[8,64,256]{2,1,0:T(8,128)(2,1)S(1)}, bf16[8,64,256]{2,1,0:T(8,128)(2,1)S(1)}, u32[]{:S(2)}, u32[]{:S(2)}) collective-permute-start(bf16[8,64,256]{2,1,0:T(8,128)(2,1)S(1)} %get-tuple-element.94), channel_id=1, source_target_pairs={{0,4},{4,0},{8,12},{12,8},{16,20},{20,16},{24,28},{28,24},{1,5},{5... | collective-permute-start | bytes 786440 | tf_op jit(solution)/shard_map/ppermute | solution.py:460
  53.0 0.2 collective-permute-done.19.refs_1_
  53.2 0.1 shard_map.101
  53.3 1.3 %collective-permute-start.20 = (bf16[8,64,256]{2,1,0:T(8,128)(2,1)S(1)}, bf16[8,64,256]{2,1,0:T(8,128)(2,1)S(1)}, u32[]{:S(2)}, u32[]{:S(2)}) collective-permute-start(bf16[8,64,256]{2,1,0:T(8,128)(2,1)S(1)} %shard_map.101), channel_id=1, source_target_pairs={{0,24},{4,28},{8,0},{12,4},{16,8},{20,12},{24,16},{28,20},{1,25},{... | collective-permute-start | bytes 786440 | tf_op jit(solution)/shard_map/ppermute | solution.py:461
  54.6 2.3 %collective-permute-done.14 = bf16[128,1024]{1,0:T(8,128)(2,1)S(1)} collective-permute-done((bf16[128,1024]{1,0:T(8,128)(2,1)S(1)}, bf16[128,1024]{1,0:T(8,128)(2,1)S(1)}, u32[]{:S(2)}, u32[]{:S(2)}) %collective-permute-start.14) | collective-permute-done | bytes 262176 | tf_op jit(solution)/shard_map/ppermute | solution.py:463
  57.0 2.9 %collective-permute-done.13.refs_1_ = bf16[16,64,256]{2,1,0:T(8,128)(2,1)S(1)} collective-permute-done((bf16[16,64,256]{2,1,0:T(8,128)(2,1)S(1)}, bf16[16,64,256]{2,1,0:T(8,128)(2,1)S(1)}, u32[]{:S(2)}, u32[]{:S(2)}) %collective-permute-start.13) | collective-permute-done | bytes 524320 | tf_op jit(solution)/shard_map/ppermute | solution.py:459
  59.8 0.1 shard_map.98
  59.9 1.9 %collective-permute-start.15 = (bf16[8,64,256]{2,1,0:T(8,128)(2,1)S(1)}, bf16[8,64,256]{2,1,0:T(8,128)(2,1)S(1)}, u32[]{:S(2)}, u32[]{:S(2)}) collective-permute-start(bf16[8,64,256]{2,1,0:T(8,128)(2,1)S(1)} %shard_map.98), channel_id=1, source_target_pairs={{0,4},{4,0},{8,12},{12,8},{16,20},{20,16},{24,28},{28,24},{1,5},{5... | collective-permute-start | bytes 786440 | tf_op jit(solution)/shard_map/ppermute | solution.py:466
  61.8 0.0 collective-permute-done.18.refs_1_
  61.8 2.1 %collective-permute-done.20.refs_2_ = bf16[8,64,256]{2,1,0:T(8,128)(2,1)S(1)} collective-permute-done((bf16[8,64,256]{2,1,0:T(8,128)(2,1)S(1)}, bf16[8,64,256]{2,1,0:T(8,128)(2,1)S(1)}, u32[]{:S(2)}, u32[]{:S(2)}) %collective-permute-start.20) | collective-permute-done | bytes 262176 | tf_op jit(solution)/shard_map/ppermute | solution.py:461
  63.9 0.1 shard_map.102
  64.0 3.6 %collective-permute-start.24 = (bf16[2,64,256]{2,1,0:T(8,128)(2,1)S(1)}, bf16[2,64,256]{2,1,0:T(8,128)(2,1)S(1)}, u32[]{:S(2)}, u32[]{:S(2)}) collective-permute-start(bf16[2,64,256]{2,1,0:T(8,128)(2,1)S(1)} %get-tuple-element.100), channel_id=1, source_target_pairs={{0,26},{1,27},{2,24},{3,25},{4,30},{5,31},{6,28},{7,29},{8,2},{9,3... | collective-permute-start | bytes 196616 | tf_op jit(solution)/shard_map/ppermute | solution.py:381
  67.6 1.6 %collective-permute-start.21 = (bf16[4,64,256]{2,1,0:T(8,128)(2,1)S(1)}, bf16[4,64,256]{2,1,0:T(8,128)(2,1)S(1)}, u32[]{:S(2)}, u32[]{:S(2)}) collective-permute-start(bf16[4,64,256]{2,1,0:T(8,128)(2,1)S(1)} %get-tuple-element.97), channel_id=1, source_target_pairs={{0,24},{4,28},{8,0},{12,4},{16,8},{20,12},{24,16},{28,20},{1,25},{... | collective-permute-start | bytes 393224 | tf_op jit(solution)/shard_map/ppermute | solution.py:474
  69.3 0.0 collective-permute-done.15.refs_2_
  69.3 0.1 shard_map.99
  69.4 0.5 collective-permute-start.22
  69.9 0.9 %collective-permute-start.23 = (bf16[2,64,256]{2,1,0:T(8,128)(2,1)S(1)}, bf16[2,64,256]{2,1,0:T(8,128)(2,1)S(1)}, u32[]{:S(2)}, u32[]{:S(2)}) collective-permute-start(bf16[2,64,256]{2,1,0:T(8,128)(2,1)S(1)} %get-tuple-element.99), channel_id=1, source_target_pairs={{0,3},{1,2},{2,1},{3,0},{4,7},{5,6},{6,5},{7,4},{8,11},{9,10},{10,... | collective-permute-start | bytes 196616 | tf_op jit(solution)/shard_map/ppermute | solution.py:477
  70.8 0.9 %collective-permute-start.16 = (bf16[64,1024]{1,0:T(8,128)(2,1)S(1)}, bf16[64,1024]{1,0:T(8,128)(2,1)S(1)}, u32[]{:S(2)}, u32[]{:S(2)}) collective-permute-start(bf16[64,1024]{1,0:T(8,128)(2,1)S(1)} %get-tuple-element.90), channel_id=1, source_target_pairs={{0,1},{1,0},{2,3},{3,2},{4,5},{5,4},{6,7},{7,6},{8,9},{9,8},{10,11... | collective-permute-start | bytes 393224 | tf_op jit(solution)/shard_map/ppermute | solution.py:366
  71.7 1.2 %collective-permute-done.25.refs_5_ = bf16[2,64,256]{2,1,0:T(8,128)(2,1)S(1)} collective-permute-done((bf16[2,64,256]{2,1,0:T(8,128)(2,1)S(1)}, bf16[2,64,256]{2,1,0:T(8,128)(2,1)S(1)}, u32[]{:S(2)}, u32[]{:S(2)}) %collective-permute-start.25) | collective-permute-done | bytes 65568 | tf_op jit(solution)/shard_map/ppermute | solution.py:381
  72.8 0.6 collective-permute-done.21.refs_1_
  73.4 1.0 %collective-permute-done.22.refs_2_ = bf16[2,64,256]{2,1,0:T(8,128)(2,1)S(1)} collective-permute-done((bf16[2,64,256]{2,1,0:T(8,128)(2,1)S(1)}, bf16[2,64,256]{2,1,0:T(8,128)(2,1)S(1)}, u32[]{:S(2)}, u32[]{:S(2)}) %collective-permute-start.22) | collective-permute-done | bytes 65568 | tf_op jit(solution)/shard_map/ppermute | solution.py:477
  74.4 0.3 collective-permute-done.23.refs_4_
  74.7 0.5 collective-permute-start.26
  75.2 0.8 %shard_map.100 = bf16[64,4096]{1,0:T(8,128)(2,1)} custom-call(s32[1]{0:T(128)} %bitcast.me_ref, bf16[64,1024]{1,0:T(8,128)(2,1)S(1)} %get-tuple-element.89.refs_0_, bf16[64,1024]{1,0:T(8,128)(2,1)S(1)} %collective-permute-done.16.refs_1_, bf16[64,1024]{1,0:T(8,128)(2,1)S(1)} %get-tuple-element.116.refs_2_, bf16[64,1024]{1,0:T(8,128)(2,1)S(1)} %collective-permute-done.17.refs_3_), custom_call_target="tpu_custom_call" | custom-call | tf_op jit(solution)/shard_map/pallas_call | solution.py:335
  76.0 0.1 collective-permute-done.26.refs_1_
  76.0 0.8 shard_map.104
  (27 shorter events, 0.3 us)
Async XLA Ops:
  0.6 17.6 %copy-start.2 = (s32[16,8,4]{0,2,1:T(4,128)S(1)}, s32[16,8,4]{0,2,1:T(4,128)}, u32[]{:S(2)}) copy-start(s32[16,8,4]{0,2,1:T(4,128)} %param.13) | copy-start | bytes 6148
  2.4 4.0 %collective-permute-start = (bf16[2,64,256]{2,1,0:T(8,128)(2,1)}, bf16[2,64,256]{2,1,0:T(8,128)(2,1)S(1)}, u32[]{:S(2)}, u32[]{:S(2)}) collective-permute-start(bf16[2,64,256]{2,1,0:T(8,128)(2,1)} %get-tuple-element.59), channel_id=1, source_target_pairs={{0,1},{1,0},{2,3},{3,2},{4,5},{5,4},{6,7},{7,6},{8,9},{9,8},{10,11... | collective-permute-start | bytes 196616 | tf_op jit(solution)/shard_map/ppermute | solution.py:357
  2.9 5.5 %collective-permute-start.1 = (bf16[2,64,256]{2,1,0:T(8,128)(2,1)}, bf16[2,64,256]{2,1,0:T(8,128)(2,1)S(1)}, u32[]{:S(2)}, u32[]{:S(2)}) collective-permute-start(bf16[2,64,256]{2,1,0:T(8,128)(2,1)} %get-tuple-element.60), channel_id=1, source_target_pairs={{0,2},{1,3},{2,0},{3,1},{4,6},{5,7},{6,4},{7,5},{8,10},{9,11},{10,... | collective-permute-start | bytes 196616 | tf_op jit(solution)/shard_map/ppermute | solution.py:357
  5.5 4.3 %collective-permute-start.2 = (bf16[2,64,256]{2,1,0:T(8,128)(2,1)}, bf16[2,64,256]{2,1,0:T(8,128)(2,1)S(1)}, u32[]{:S(2)}, u32[]{:S(2)}) collective-permute-start(bf16[2,64,256]{2,1,0:T(8,128)(2,1)} %get-tuple-element.61), channel_id=1, source_target_pairs={{0,3},{1,2},{2,1},{3,0},{4,7},{5,6},{6,5},{7,4},{8,11},{9,10},{10,... | collective-permute-start | bytes 196616 | tf_op jit(solution)/shard_map/ppermute | solution.py:357
  9.8 10.3 %collective-permute-start.3 = (bf16[8,64,256]{2,1,0:T(8,128)(2,1)S(1)}, bf16[8,64,256]{2,1,0:T(8,128)(2,1)S(1)}, u32[]{:S(2)}, u32[]{:S(2)}) collective-permute-start(bf16[8,64,256]{2,1,0:T(8,128)(2,1)S(1)} %constant_dynamic-update-slice_fusion.own_kv_ref), channel_id=1, source_target_pairs={{0,8},{4,12},{8,16},{12,20},{16,24},{20,28},{24,0},{28,4},{1,9},{5... | collective-permute-start | bytes 786440 | tf_op jit(solution)/shard_map/ppermute | solution.py:411
  11.4 11.3 %collective-permute-start.4 = (bf16[8,64,256]{2,1,0:T(8,128)(2,1)S(1)}, bf16[8,64,256]{2,1,0:T(8,128)(2,1)S(1)}, u32[]{:S(2)}, u32[]{:S(2)}) collective-permute-start(bf16[8,64,256]{2,1,0:T(8,128)(2,1)S(1)} %constant_dynamic-update-slice_fusion.own_kv_ref), channel_id=1, source_target_pairs={{0,4},{4,0},{8,12},{12,8},{16,20},{20,16},{24,28},{28,24},{1,5},{5... | collective-permute-start | bytes 786440 | tf_op jit(solution)/shard_map/ppermute | solution.py:412
  15.9 6.8 %copy-start.3 = (bf16[528,256]{1,0:T(8,128)(2,1)S(1)}, bf16[528,256]{1,0:T(8,128)(2,1)}, u32[]{:S(2)}) copy-start(bf16[528,256]{1,0:T(8,128)(2,1)} %get-tuple-element.73) | copy-start | bytes 811012
  15.9 10.3 %collective-permute-start.7 = (bf16[8,64,256]{2,1,0:T(8,128)(2,1)S(1)}, bf16[8,64,256]{2,1,0:T(8,128)(2,1)S(1)}, u32[]{:S(2)}, u32[]{:S(2)}) collective-permute-start(bf16[8,64,256]{2,1,0:T(8,128)(2,1)S(1)} %constant_dynamic-update-slice_fusion.own_kv_ref), channel_id=1, source_target_pairs={{0,24},{4,28},{8,0},{12,4},{16,8},{20,12},{24,16},{28,20},{1,25},{... | collective-permute-start | bytes 786440 | tf_op jit(solution)/shard_map/ppermute | solution.py:416
  18.4 14.4 %collective-permute-start.11 = (bf16[1056,256]{1,0:T(8,128)(2,1)}, bf16[1056,256]{1,0:T(8,128)(2,1)S(1)}, u32[]{:S(2)}, u32[]{:S(2)}) collective-permute-start(bf16[1056,256]{1,0:T(8,128)(2,1)} %get-tuple-element.74), channel_id=1, source_target_pairs={{0,2},{1,3},{2,0},{3,1},{4,6},{5,7},{6,4},{7,5},{8,10},{9,11},{10,... | collective-permute-start | bytes 1622024 | tf_op jit(solution)/shard_map/ppermute | solution.py:372
  20.1 7.8 %collective-permute-start.6 = (bf16[8,64,256]{2,1,0:T(8,128)(2,1)S(1)}, bf16[8,64,256]{2,1,0:T(8,128)(2,1)S(1)}, u32[]{:S(2)}, u32[]{:S(2)}) collective-permute-start(bf16[8,64,256]{2,1,0:T(8,128)(2,1)S(1)} %collective-permute-done.3), channel_id=1, source_target_pairs={{0,4},{4,0},{8,12},{12,8},{16,20},{20,16},{24,28},{28,24},{1,5},{5... | collective-permute-start | bytes 786440 | tf_op jit(solution)/shard_map/ppermute | solution.py:427
  22.3 10.1 %collective-permute-start.5 = (bf16[8,64,256]{2,1,0:T(8,128)(2,1)S(1)}, bf16[8,64,256]{2,1,0:T(8,128)(2,1)S(1)}, u32[]{:S(2)}, u32[]{:S(2)}) collective-permute-start(bf16[8,64,256]{2,1,0:T(8,128)(2,1)S(1)} %collective-permute-done.3), channel_id=1, source_target_pairs={{0,8},{4,12},{8,16},{12,20},{16,24},{20,28},{24,0},{28,4},{1,9},{5... | collective-permute-start | bytes 786440 | tf_op jit(solution)/shard_map/ppermute | solution.py:426
  22.7 17.3 %collective-permute-start.10 = (bf16[528,256]{1,0:T(8,128)(2,1)S(1)}, bf16[528,256]{1,0:T(8,128)(2,1)S(1)}, u32[]{:S(2)}, u32[]{:S(2)}) collective-permute-start(bf16[528,256]{1,0:T(8,128)(2,1)S(1)} %copy-done.3), channel_id=1, source_target_pairs={{0,1},{1,0},{2,3},{3,2},{4,5},{5,4},{6,7},{7,6},{8,9},{9,8},{10,11... | collective-permute-start | bytes 811016 | tf_op jit(solution)/shard_map/ppermute | solution.py:366
  26.2 13.8 %collective-permute-start.9 = (bf16[8,64,256]{2,1,0:T(8,128)(2,1)S(1)}, bf16[8,64,256]{2,1,0:T(8,128)(2,1)S(1)}, u32[]{:S(2)}, u32[]{:S(2)}) collective-permute-start(bf16[8,64,256]{2,1,0:T(8,128)(2,1)S(1)} %collective-permute-done.7), channel_id=1, source_target_pairs={{0,4},{4,0},{8,12},{12,8},{16,20},{20,16},{24,28},{28,24},{1,5},{5... | collective-permute-start | bytes 786440 | tf_op jit(solution)/shard_map/ppermute | solution.py:428
  27.9 12.1 %copy-start = (bf16[528,256]{1,0:T(8,128)(2,1)S(1)}, bf16[528,256]{1,0:T(8,128)(2,1)}, u32[]{:S(2)}) copy-start(bf16[528,256]{1,0:T(8,128)(2,1)} %get-tuple-element.72.refs_0_) | copy-start | bytes 811012
  27.9 12.1 %copy-start.1 = (f32[256,8]{0,1:T(8,128)S(1)}, f32[256,8]{0,1:T(8,128)}, u32[]{:S(2)}) copy-start(f32[256,8]{0,1:T(8,128)} %param.12) | copy-start | bytes 24580
  32.3 7.6 %collective-permute-start.8 = (bf16[8,64,256]{2,1,0:T(8,128)(2,1)S(1)}, bf16[8,64,256]{2,1,0:T(8,128)(2,1)S(1)}, u32[]{:S(2)}, u32[]{:S(2)}) collective-permute-start(bf16[8,64,256]{2,1,0:T(8,128)(2,1)S(1)} %collective-permute-done.5), channel_id=1, source_target_pairs={{0,4},{4,0},{8,12},{12,8},{16,20},{20,16},{24,28},{28,24},{1,5},{5... | collective-permute-start | bytes 786440 | tf_op jit(solution)/shard_map/ppermute | solution.py:430
  32.9 7.1 %collective-permute-start.12 = (bf16[528,256]{1,0:T(8,128)(2,1)S(1)}, bf16[528,256]{1,0:T(8,128)(2,1)S(1)}, u32[]{:S(2)}, u32[]{:S(2)}) collective-permute-start(bf16[528,256]{1,0:T(8,128)(2,1)S(1)} %get-tuple-element.113), channel_id=1, source_target_pairs={{0,1},{1,0},{2,3},{3,2},{4,5},{5,4},{6,7},{7,6},{8,9},{9,8},{10,11... | collective-permute-start | bytes 811016 | tf_op jit(solution)/shard_map/ppermute | solution.py:367
  43.1 16.7 %collective-permute-start.13 = (bf16[16,64,256]{2,1,0:T(8,128)(2,1)S(1)}, bf16[16,64,256]{2,1,0:T(8,128)(2,1)S(1)}, u32[]{:S(2)}, u32[]{:S(2)}) collective-permute-start(bf16[16,64,256]{2,1,0:T(8,128)(2,1)S(1)} %get-tuple-element.81), channel_id=1, source_target_pairs={{0,8},{4,12},{8,16},{12,20},{16,24},{20,28},{24,0},{28,4},{1,9},{5... | collective-permute-start | bytes 1572872 | tf_op jit(solution)/shard_map/ppermute | solution.py:459
  45.5 7.8 %collective-permute-start.19 = (bf16[8,64,256]{2,1,0:T(8,128)(2,1)S(1)}, bf16[8,64,256]{2,1,0:T(8,128)(2,1)S(1)}, u32[]{:S(2)}, u32[]{:S(2)}) collective-permute-start(bf16[8,64,256]{2,1,0:T(8,128)(2,1)S(1)} %get-tuple-element.96), channel_id=1, source_target_pairs={{0,4},{4,0},{8,12},{12,8},{16,20},{20,16},{24,28},{28,24},{1,5},{5... | collective-permute-start | bytes 786440 | tf_op jit(solution)/shard_map/ppermute | solution.py:458
  49.6 7.4 %collective-permute-start.14 = (bf16[128,1024]{1,0:T(8,128)(2,1)S(1)}, bf16[128,1024]{1,0:T(8,128)(2,1)S(1)}, u32[]{:S(2)}, u32[]{:S(2)}) collective-permute-start(bf16[128,1024]{1,0:T(8,128)(2,1)S(1)} %get-tuple-element.82), channel_id=1, source_target_pairs={{0,2},{1,3},{2,0},{3,1},{4,6},{5,7},{6,4},{7,5},{8,10},{9,11},{10,... | collective-permute-start | bytes 786440 | tf_op jit(solution)/shard_map/ppermute | solution.py:463
  51.2 10.6 %collective-permute-start.18 = (bf16[8,64,256]{2,1,0:T(8,128)(2,1)S(1)}, bf16[8,64,256]{2,1,0:T(8,128)(2,1)S(1)}, u32[]{:S(2)}, u32[]{:S(2)}) collective-permute-start(bf16[8,64,256]{2,1,0:T(8,128)(2,1)S(1)} %get-tuple-element.94), channel_id=1, source_target_pairs={{0,4},{4,0},{8,12},{12,8},{16,20},{20,16},{24,28},{28,24},{1,5},{5... | collective-permute-start | bytes 786440 | tf_op jit(solution)/shard_map/ppermute | solution.py:460
  53.3 10.6 %collective-permute-start.20 = (bf16[8,64,256]{2,1,0:T(8,128)(2,1)S(1)}, bf16[8,64,256]{2,1,0:T(8,128)(2,1)S(1)}, u32[]{:S(2)}, u32[]{:S(2)}) collective-permute-start(bf16[8,64,256]{2,1,0:T(8,128)(2,1)S(1)} %shard_map.101), channel_id=1, source_target_pairs={{0,24},{4,28},{8,0},{12,4},{16,8},{20,12},{24,16},{28,20},{1,25},{... | collective-permute-start | bytes 786440 | tf_op jit(solution)/shard_map/ppermute | solution.py:461
  59.9 9.4 %collective-permute-start.15 = (bf16[8,64,256]{2,1,0:T(8,128)(2,1)S(1)}, bf16[8,64,256]{2,1,0:T(8,128)(2,1)S(1)}, u32[]{:S(2)}, u32[]{:S(2)}) collective-permute-start(bf16[8,64,256]{2,1,0:T(8,128)(2,1)S(1)} %shard_map.98), channel_id=1, source_target_pairs={{0,4},{4,0},{8,12},{12,8},{16,20},{20,16},{24,28},{28,24},{1,5},{5... | collective-permute-start | bytes 786440 | tf_op jit(solution)/shard_map/ppermute | solution.py:466
  64.0 6.8 %collective-permute-start.24 = (bf16[2,64,256]{2,1,0:T(8,128)(2,1)S(1)}, bf16[2,64,256]{2,1,0:T(8,128)(2,1)S(1)}, u32[]{:S(2)}, u32[]{:S(2)}) collective-permute-start(bf16[2,64,256]{2,1,0:T(8,128)(2,1)S(1)} %get-tuple-element.100), channel_id=1, source_target_pairs={{0,26},{1,27},{2,24},{3,25},{4,30},{5,31},{6,28},{7,29},{8,2},{9,3... | collective-permute-start | bytes 196616 | tf_op jit(solution)/shard_map/ppermute | solution.py:381
  67.6 5.2 %collective-permute-start.25 = (bf16[2,64,256]{2,1,0:T(8,128)(2,1)S(1)}, bf16[2,64,256]{2,1,0:T(8,128)(2,1)S(1)}, u32[]{:S(2)}, u32[]{:S(2)}) collective-permute-start(bf16[2,64,256]{2,1,0:T(8,128)(2,1)S(1)} %get-tuple-element.101), channel_id=1, source_target_pairs={{0,27},{1,26},{2,25},{3,24},{4,31},{5,30},{6,29},{7,28},{8,3},{9,2... | collective-permute-start | bytes 196616 | tf_op jit(solution)/shard_map/ppermute | solution.py:381
  67.6 5.8 %collective-permute-start.21 = (bf16[4,64,256]{2,1,0:T(8,128)(2,1)S(1)}, bf16[4,64,256]{2,1,0:T(8,128)(2,1)S(1)}, u32[]{:S(2)}, u32[]{:S(2)}) collective-permute-start(bf16[4,64,256]{2,1,0:T(8,128)(2,1)S(1)} %get-tuple-element.97), channel_id=1, source_target_pairs={{0,24},{4,28},{8,0},{12,4},{16,8},{20,12},{24,16},{28,20},{1,25},{... | collective-permute-start | bytes 393224 | tf_op jit(solution)/shard_map/ppermute | solution.py:474
  69.4 5.0 %collective-permute-start.22 = (bf16[2,64,256]{2,1,0:T(8,128)(2,1)S(1)}, bf16[2,64,256]{2,1,0:T(8,128)(2,1)S(1)}, u32[]{:S(2)}, u32[]{:S(2)}) collective-permute-start(bf16[2,64,256]{2,1,0:T(8,128)(2,1)S(1)} %get-tuple-element.98), channel_id=1, source_target_pairs={{0,2},{1,3},{2,0},{3,1},{4,6},{5,7},{6,4},{7,5},{8,10},{9,11},{10,... | collective-permute-start | bytes 196616 | tf_op jit(solution)/shard_map/ppermute | solution.py:477
  69.9 4.8 %collective-permute-start.23 = (bf16[2,64,256]{2,1,0:T(8,128)(2,1)S(1)}, bf16[2,64,256]{2,1,0:T(8,128)(2,1)S(1)}, u32[]{:S(2)}, u32[]{:S(2)}) collective-permute-start(bf16[2,64,256]{2,1,0:T(8,128)(2,1)S(1)} %get-tuple-element.99), channel_id=1, source_target_pairs={{0,3},{1,2},{2,1},{3,0},{4,7},{5,6},{6,5},{7,4},{8,11},{9,10},{10,... | collective-permute-start | bytes 196616 | tf_op jit(solution)/shard_map/ppermute | solution.py:477
  70.8 4.4 %collective-permute-start.16 = (bf16[64,1024]{1,0:T(8,128)(2,1)S(1)}, bf16[64,1024]{1,0:T(8,128)(2,1)S(1)}, u32[]{:S(2)}, u32[]{:S(2)}) collective-permute-start(bf16[64,1024]{1,0:T(8,128)(2,1)S(1)} %get-tuple-element.90), channel_id=1, source_target_pairs={{0,1},{1,0},{2,3},{3,2},{4,5},{5,4},{6,7},{7,6},{8,9},{9,8},{10,11... | collective-permute-start | bytes 393224 | tf_op jit(solution)/shard_map/ppermute | solution.py:366
  72.8 2.3 %collective-permute-start.17 = (bf16[64,1024]{1,0:T(8,128)(2,1)S(1)}, bf16[64,1024]{1,0:T(8,128)(2,1)S(1)}, u32[]{:S(2)}, u32[]{:S(2)}) collective-permute-start(bf16[64,1024]{1,0:T(8,128)(2,1)S(1)} %get-tuple-element.115), channel_id=1, source_target_pairs={{0,1},{1,0},{2,3},{3,2},{4,5},{5,4},{6,7},{7,6},{8,9},{9,8},{10,11... | collective-permute-start | bytes 393224 | tf_op jit(solution)/shard_map/ppermute | solution.py:367
  74.7 1.4 %collective-permute-start.26 = (bf16[2,64,256]{2,1,0:T(8,128)(2,1)S(1)}, bf16[2,64,256]{2,1,0:T(8,128)(2,1)S(1)}, u32[]{:S(2)}, u32[]{:S(2)}) collective-permute-start(bf16[2,64,256]{2,1,0:T(8,128)(2,1)S(1)} %get-tuple-element.106), channel_id=1, source_target_pairs={{0,1},{1,0},{2,3},{3,2},{4,5},{5,4},{6,7},{7,6},{8,9},{9,8},{10,11... | collective-permute-start | bytes 196616 | tf_op jit(solution)/shard_map/ppermute | solution.py:482
